TPU v7x, 32 devices: a whole 2x2x4 slice. The times are simulated.
32 devices in a mesh: tm: 4 (over z), space: 8 (over y, x, core).
Axes of the slice: x: 2, y: 2, z: 4, core: 2. Of those that a mesh axis runs over, the one named last changes fastest.
Arguments:
- initial: float32 [32, 128, 512], P('space'), may hold values from -6 to 6
- prior: float32 [4, 32, 128, 512], P('tm', 'space'), may hold values from -6 to 6
- conductivity: float32 [32, 128, 512], P('space'), may hold values from 0.1 to 1
Outputs:
- update: float32 [4, 32, 128, 512], P('tm', 'space')
- coarse_end: float32 [4, 16, 64, 256], P('tm', 'space')
All inputs are finite; a program needn't handle non-finite values.
Results may differ from a plain program's by a relative error of at most 0.00002.
Values sent between devices are 32-bit elements; how exact they have to be, the bound alone decides.
No kernel may reach another device: no remote copies, remote signals or barrier semaphores. Data moves between devices by JAX's collectives and lax.ppermute only.
A program may use at most 64 MiB of HBM per device.

v0:
```python
import jax
import jax.numpy as jnp
from jax import lax
from jax.sharding import PartitionSpec as P

FINE_STEPS = 4
COARSE_STEPS = 2


fine_rate = 0.16


def passed_along(block, axis, distance):
    devices = range(lax.axis_size(axis))
    route = [(i - distance, i) for i in devices if i - distance in devices]
    return lax.ppermute(block, axis, route)


def extended(shard, sides, width):
    for axis, dim in sides:
        size, length = (lax.axis_size(axis), shard.shape[dim])
        up = [(i, (i + 1) % size) for i in range(size - 1)]
        down = [(j, i) for i, j in up]
        last = lax.slice_in_dim(shard, length - width, length, axis=dim)
        initial = lax.slice_in_dim(shard, 0, width, axis=dim)
        before = lax.ppermute(last, axis, up)
        after = lax.ppermute(initial, axis, down)
        shard = jnp.concatenate([before, shard, after], axis=dim)
    return shard


def neighbour(field, dim, forward):
    count = field.shape[dim]
    edge_shape = list(field.shape)
    edge_shape[dim] = 1
    zeros = jnp.zeros(edge_shape, field.dtype)
    if forward:
        return jnp.concatenate([lax.slice_in_dim(field, 1, count, axis=dim), zeros], axis=dim)
    return jnp.concatenate([zeros, lax.slice_in_dim(field, 0, count - 1, axis=dim)], axis=dim)


def face_terms(padded_cond):
    center = padded_cond[1:-1]
    return (
        0.5 * (center + padded_cond[2:]),
        0.5 * (center + padded_cond[:-2]),
        0.5 * (center + neighbour(center, 1, True)),
        0.5 * (center + neighbour(center, 1, False)),
        0.5 * (center + neighbour(center, 2, True)),
        0.5 * (center + neighbour(center, 2, False)),
    )


def local_step(padded_state, faces, factor):
    center = padded_state[1:-1]
    flux_sum = faces[0] * (padded_state[2:] - center)
    flux_sum = flux_sum + faces[1] * (padded_state[:-2] - center)
    flux_sum = flux_sum + faces[2] * (neighbour(center, 1, True) - center)
    flux_sum = flux_sum + faces[3] * (neighbour(center, 1, False) - center)
    flux_sum = flux_sum + faces[4] * (neighbour(center, 2, True) - center)
    flux_sum = flux_sum + faces[5] * (neighbour(center, 2, False) - center)
    return center + factor * flux_sum


def restrict(field):
    paired = field[0::2] + field[1::2]
    paired = paired[:, 0::2] + paired[:, 1::2]
    paired = paired[:, :, 0::2] + paired[:, :, 1::2]
    return paired * 0.125


def prolong(field):
    return jnp.repeat(jnp.repeat(jnp.repeat(field, 2, axis=0), 2, axis=1), 2, axis=2)


def shards(initial, prior, conductivity):
    time_index = lax.axis_index("tm")
    time_count = lax.axis_size("tm")
    own_prior = prior[0]
    received_prior = passed_along(prior, "tm", 1)[0]
    opening = jnp.where(time_index == 0, initial, received_prior)
    padded_cond = extended(conductivity, (("space", 0),), 1)
    faces = face_terms(padded_cond)
    fine_state = opening
    for step in range(FINE_STEPS):
        padded_state = extended(fine_state, (("space", 0),), 1)
        fine_state = local_step(padded_state, faces, fine_rate)
    coarse_faces = face_terms(extended(restrict(conductivity), (("space", 0),), 1))

    def coarse(state):
        for step in range(COARSE_STEPS):
            padded_coarse = extended(state, (("space", 0),), 1)
            state = local_step(padded_coarse, coarse_faces, fine_rate * 0.5)
        return state

    predicted = coarse(restrict(opening))
    delta = fine_state - prolong(predicted)
    reduced = restrict(delta)
    anchor = restrict(initial)
    all_reduced = lax.all_gather(reduced[None], "tm", axis=0, tiled=True)
    current = anchor
    propagated_own = jnp.zeros_like(anchor)
    coarse_tail = jnp.zeros_like(anchor)
    for section in range(time_count):
        propagated = coarse(current)
        following = propagated + all_reduced[section]
        propagated_own = jnp.where(time_index == section, propagated, propagated_own)
        coarse_tail = jnp.where(time_index == section, following, coarse_tail)
        current = following
    update = prolong(propagated_own) + delta - own_prior
    return (update[None], coarse_tail[None])


def solution(mesh):
    return jax.shard_map(
        shards,
        mesh=mesh,
        in_specs=(P("space", None, None), P("tm", "space", None, None), P("space", None, None)),
        out_specs=(P("tm", "space", None, None), P("tm", "space", None, None)),
        check_vma=False,
    )
```

profile of v0, /device:TPU:4, one launch (start us, length us, event | category | flops | bytes accessed | tf_op | source)
XLA Modules:
  0.0 320.3 jit_solution(1367705607396505924)
XLA Ops:
  3.3 4.5 %collective-permute-start.6 = (f32[1,4,128,512]{2,3,1,0:T(8,128)}, f32[1,4,128,512]{2,3,1,0:T(8,128)}, u32[]{:S(2)}, u32[]{:S(2)}) collective-permute-start(f32[1,4,128,512]{2,3,1,0:T(8,128)} %copy.59), channel_id=1, source_target_pairs={{0,8},{8,16},{16,24},{1,9},{9,17},{17,25},{2,10},{10,18},{18,26},{... | collective-permute-start | bytes 3145736 | tf_op jit(solution)/shard_map/ppermute | solution.py:16
  8.1 12.6 %slice.508 = f32[2,64,512]{1,2,0:T(8,128)S(1)} slice(f32[2,128,512]{1,2,0:T(8,128)S(1)} %slice_add_fusion.2), slice={[0:2:1], [0:128:2], [0:512:1]} | slice | bytes 524288 | tf_op jit(solution)/shard_map/slice | solution.py:67
  20.8 12.8 %slice.509 = f32[2,64,512]{1,2,0:T(8,128)S(1)} slice(f32[2,128,512]{1,2,0:T(8,128)S(1)} %slice_add_fusion.2), slice={[0:2:1], [1:128:2], [0:512:1]} | slice | bytes 524288 | tf_op jit(solution)/shard_map/slice | solution.py:67
  39.6 12.6 %slice.502 = f32[2,64,512]{1,2,0:T(8,128)S(1)} slice(f32[2,128,512]{1,2,0:T(8,128)S(1)} %slice_add_fusion.3), slice={[0:2:1], [0:128:2], [0:512:1]} | slice | bytes 524288 | tf_op jit(solution)/shard_map/slice | solution.py:67
  52.2 13.3 %slice.503 = f32[2,64,512]{1,2,0:T(8,128)} slice(f32[2,128,512]{1,2,0:T(8,128)S(1)} %slice_add_fusion.3), slice={[0:2:1], [1:128:2], [0:512:1]} | slice | bytes 524288 | tf_op jit(solution)/shard_map/slice | solution.py:67
  67.7 4.5 %collective-permute-start.1 = (f32[1,64,256]{1,2,0:T(8,128)}, f32[1,64,256]{1,2,0:T(8,128)}, u32[]{:S(2)}, u32[]{:S(2)}) collective-permute-start(f32[1,64,256]{1,2,0:T(8,128)} %get-tuple-element.108), channel_id=1, source_target_pairs={{1,0},{2,1},{3,2},{4,3},{5,4},{6,5},{7,6},{9,8},{10,9},{11,10},{12... | collective-permute-start | bytes 196616 | tf_op jit(solution)/shard_map/ppermute | solution.py:27
  79.3 12.6 %slice.578 = f32[2,64,512]{1,2,0:T(8,128)S(1)} slice(f32[2,128,512]{1,2,0:T(8,128)S(1)} %slice_add_fusion.1), slice={[0:2:1], [0:128:2], [0:512:1]} | slice | bytes 524288 | tf_op jit(solution)/shard_map/slice | solution.py:67
  92.0 13.3 %slice.579 = f32[2,64,512]{1,2,0:T(8,128)} slice(f32[2,128,512]{1,2,0:T(8,128)S(1)} %slice_add_fusion.1), slice={[0:2:1], [1:128:2], [0:512:1]} | slice | bytes 524288 | tf_op jit(solution)/shard_map/slice | solution.py:67
  117.5 4.5 %collective-permute-start.7 = (f32[1,128,512]{1,2,0:T(8,128)}, f32[1,128,512]{1,2,0:T(8,128)}, u32[]{:S(2)}, u32[]{:S(2)}) collective-permute-start(f32[1,128,512]{1,2,0:T(8,128)} %get-tuple-element.51), channel_id=1, source_target_pairs={{1,0},{2,1},{3,2},{4,3},{5,4},{6,5},{7,6},{9,8},{10,9},{11,10},{12... | collective-permute-start | bytes 786440 | tf_op jit(solution)/shard_map/ppermute | solution.py:27
  130.7 4.5 %collective-permute-start.19 = (f32[1,64,256]{1,2,0:T(8,128)S(1)}, f32[1,64,256]{1,2,0:T(8,128)S(1)}, u32[]{:S(2)}, u32[]{:S(2)}) collective-permute-start(f32[1,64,256]{1,2,0:T(8,128)S(1)} %get-tuple-element.114), channel_id=1, source_target_pairs={{1,0},{2,1},{3,2},{4,3},{5,4},{6,5},{7,6},{9,8},{10,9},{11,10},{12... | collective-permute-start | bytes 196616 | tf_op jit(solution)/shard_map/ppermute | solution.py:27
  138.6 4.7 %collective-permute-start.8 = (f32[1,128,512]{1,2,0:T(8,128)}, f32[1,128,512]{1,2,0:T(8,128)}, u32[]{:S(2)}, u32[]{:S(2)}) collective-permute-start(f32[1,128,512]{1,2,0:T(8,128)} %get-tuple-element.56), channel_id=1, source_target_pairs={{1,0},{2,1},{3,2},{4,3},{5,4},{6,5},{7,6},{9,8},{10,9},{11,10},{12... | collective-permute-start | bytes 786440 | tf_op jit(solution)/shard_map/ppermute | solution.py:27
  156.4 4.6 %fusion.42 = (f32[4,128,512]{1,2,0:T(8,128)S(1)}, f32[4,128,512]{1,2,0:T(8,128)S(1)}, f32[4,128,512]{1,2,0:T(8,128)S(1)}, f32[4,128,512]{1,2,0:T(8,128)S(1)}, f32[4,128,512]{1,2,0:T(8,128)S(1)}) fusion(f32[4,128,512]{1,2,0:T(8,128)S(1)} %bitcast_select_fusion, f32[1,128,512]{1,2,0:T(8,128)} %collective-permute-done.10, ...), kind=kLoop, calls=%fused_computation.49 | loop fusion | flops 9175040 | bytes 16736256 | tf_op jit(solution)/shard_map/add | solution.py:62
  161.4 4.1 %collective-permute-start.11 = (f32[1,128,512]{1,2,0:T(8,128)S(1)}, f32[1,128,512]{1,2,0:T(8,128)S(1)}, u32[]{:S(2)}, u32[]{:S(2)}) collective-permute-start(f32[1,128,512]{1,2,0:T(8,128)S(1)} %get-tuple-element.44), channel_id=1, source_target_pairs={{1,0},{2,1},{3,2},{4,3},{5,4},{6,5},{7,6},{9,8},{10,9},{11,10},{12... | collective-permute-start | bytes 786440 | tf_op jit(solution)/shard_map/ppermute | solution.py:27
  183.8 3.8 %collective-permute-done.14 = f32[1,128,512]{1,2,0:T(8,128)S(1)} collective-permute-done((f32[1,128,512]{1,2,0:T(8,128)S(1)}, f32[1,128,512]{1,2,0:T(8,128)S(1)}, u32[]{:S(2)}, u32[]{:S(2)}) %collective-permute-start.14) | collective-permute-done | bytes 262176 | tf_op jit(solution)/shard_map/ppermute | solution.py:26
  197.0 4.2 %collective-permute-done.16 = f32[1,128,512]{1,2,0:T(8,128)S(1)} collective-permute-done((f32[1,128,512]{1,2,0:T(8,128)S(1)}, f32[1,128,512]{1,2,0:T(8,128)S(1)}, u32[]{:S(2)}, u32[]{:S(2)}) %collective-permute-start.16) | collective-permute-done | bytes 262176 | tf_op jit(solution)/shard_map/ppermute | solution.py:26
  205.2 12.6 %slice.600 = f32[2,64,512]{1,2,0:T(8,128)S(1)} slice(f32[2,128,512]{1,2,0:T(8,128)S(1)} %slice_add_fusion), slice={[0:2:1], [0:128:2], [0:512:1]} | slice | bytes 524288 | tf_op jit(solution)/shard_map/slice | solution.py:67
  217.9 12.8 %slice.601 = f32[2,64,512]{1,2,0:T(8,128)S(1)} slice(f32[2,128,512]{1,2,0:T(8,128)S(1)} %slice_add_fusion), slice={[0:2:1], [1:128:2], [0:512:1]} | slice | bytes 524288 | tf_op jit(solution)/shard_map/slice | solution.py:67
  231.2 15.2 %all-gather = f32[8,64,256]{2,1,0:T(8,128)S(1)} all-gather(f32[2,64,256]{2,1,0:T(8,128)S(1)} %copy.77), channel_id=2, replica_groups=mesh['tm'=4,'space'=8] {'tm'}, dimensions={0}, use_global_device_ids=true | all-gather | bytes 655360 | tf_op jit(solution)/shard_map/all_gather | solution.py:100
  257.6 4.0 %collective-permute-done.22 = f32[1,64,256]{1,2,0:T(8,128)} collective-permute-done((f32[1,64,256]{1,2,0:T(8,128)}, f32[1,64,256]{1,2,0:T(8,128)}, u32[]{:S(2)}, u32[]{:S(2)}) %collective-permute-start.22) | collective-permute-done | bytes 65568 | tf_op jit(solution)/shard_map/ppermute | solution.py:26
  267.5 5.5 %collective-permute-done.24 = f32[1,64,256]{1,2,0:T(8,128)S(1)} collective-permute-done((f32[1,64,256]{1,2,0:T(8,128)S(1)}, f32[1,64,256]{1,2,0:T(8,128)S(1)}, u32[]{:S(2)}, u32[]{:S(2)}) %collective-permute-start.24) | collective-permute-done | bytes 65568 | tf_op jit(solution)/shard_map/ppermute | solution.py:26
  277.9 5.5 %collective-permute-done.26 = f32[1,64,256]{1,2,0:T(8,128)S(1)} collective-permute-done((f32[1,64,256]{1,2,0:T(8,128)S(1)}, f32[1,64,256]{1,2,0:T(8,128)S(1)}, u32[]{:S(2)}, u32[]{:S(2)}) %collective-permute-start.26) | collective-permute-done | bytes 65568 | tf_op jit(solution)/shard_map/ppermute | solution.py:26
  288.3 5.5 %collective-permute-done.28 = f32[1,64,256]{1,2,0:T(8,128)S(1)} collective-permute-done((f32[1,64,256]{1,2,0:T(8,128)S(1)}, f32[1,64,256]{1,2,0:T(8,128)S(1)}, u32[]{:S(2)}, u32[]{:S(2)}) %collective-permute-start.28) | collective-permute-done | bytes 65568 | tf_op jit(solution)/shard_map/ppermute | solution.py:26
  298.7 5.5 %collective-permute-done.30 = f32[1,64,256]{1,2,0:T(8,128)S(1)} collective-permute-done((f32[1,64,256]{1,2,0:T(8,128)S(1)}, f32[1,64,256]{1,2,0:T(8,128)S(1)}, u32[]{:S(2)}, u32[]{:S(2)}) %collective-permute-start.30) | collective-permute-done | bytes 65568 | tf_op jit(solution)/shard_map/ppermute | solution.py:26
  309.1 4.7 %collective-permute-done.32 = f32[1,64,256]{1,2,0:T(8,128)S(1)} collective-permute-done((f32[1,64,256]{1,2,0:T(8,128)S(1)}, f32[1,64,256]{1,2,0:T(8,128)S(1)}, u32[]{:S(2)}, u32[]{:S(2)}) %collective-permute-start.32) | collective-permute-done | bytes 65568 | tf_op jit(solution)/shard_map/ppermute | solution.py:26
  (213 shorter events, 130.5 us)
Async XLA Ops:
  3.3 74.6 %collective-permute-start.6 = (f32[1,4,128,512]{2,3,1,0:T(8,128)}, f32[1,4,128,512]{2,3,1,0:T(8,128)}, u32[]{:S(2)}, u32[]{:S(2)}) collective-permute-start(f32[1,4,128,512]{2,3,1,0:T(8,128)} %copy.59), channel_id=1, source_target_pairs={{0,8},{8,16},{16,24},{1,9},{9,17},{17,25},{2,10},{10,18},{18,26},{... | collective-permute-start | bytes 3145736 | tf_op jit(solution)/shard_map/ppermute | solution.py:16
  34.7 80.9 %collective-permute-start = (f32[1,64,256]{1,2,0:T(8,128)}, f32[1,64,256]{1,2,0:T(8,128)S(1)}, u32[]{:S(2)}, u32[]{:S(2)}) collective-permute-start(f32[1,64,256]{1,2,0:T(8,128)} %get-tuple-element.117), channel_id=1, source_target_pairs={{1,0},{2,1},{3,2},{4,3},{5,4},{6,5},{7,6},{9,8},{10,9},{11,10},{12... | collective-permute-start | bytes 196616 | tf_op jit(solution)/shard_map/ppermute | solution.py:27
  37.2 80.3 %collective-permute-start.2 = (f32[1,64,256]{1,2,0:T(8,128)}, f32[1,64,256]{1,2,0:T(8,128)}, u32[]{:S(2)}, u32[]{:S(2)}) collective-permute-start(f32[1,64,256]{1,2,0:T(8,128)} %get-tuple-element.116), channel_id=1, source_target_pairs={{0,1},{1,2},{2,3},{3,4},{4,5},{5,6},{6,7},{8,9},{9,10},{10,11},{11... | collective-permute-start | bytes 196616 | tf_op jit(solution)/shard_map/ppermute | solution.py:26
  67.7 59.8 %collective-permute-start.1 = (f32[1,64,256]{1,2,0:T(8,128)}, f32[1,64,256]{1,2,0:T(8,128)}, u32[]{:S(2)}, u32[]{:S(2)}) collective-permute-start(f32[1,64,256]{1,2,0:T(8,128)} %get-tuple-element.108), channel_id=1, source_target_pairs={{1,0},{2,1},{3,2},{4,3},{5,4},{6,5},{7,6},{9,8},{10,9},{11,10},{12... | collective-permute-start | bytes 196616 | tf_op jit(solution)/shard_map/ppermute | solution.py:27
  110.1 12.0 %collective-permute-start.17 = (f32[1,64,256]{1,2,0:T(8,128)S(1)}, f32[1,64,256]{1,2,0:T(8,128)S(1)}, u32[]{:S(2)}, u32[]{:S(2)}) collective-permute-start(f32[1,64,256]{1,2,0:T(8,128)S(1)} %get-tuple-element.126), channel_id=1, source_target_pairs={{1,0},{2,1},{3,2},{4,3},{5,4},{6,5},{7,6},{9,8},{10,9},{11,10},{12... | collective-permute-start | bytes 196616 | tf_op jit(solution)/shard_map/ppermute | solution.py:27
  112.0 12.0 %collective-permute-start.18 = (f32[1,64,256]{1,2,0:T(8,128)S(1)}, f32[1,64,256]{1,2,0:T(8,128)S(1)}, u32[]{:S(2)}, u32[]{:S(2)}) collective-permute-start(f32[1,64,256]{1,2,0:T(8,128)S(1)} %get-tuple-element.127), channel_id=1, source_target_pairs={{0,1},{1,2},{2,3},{3,4},{4,5},{5,6},{6,7},{8,9},{9,10},{10,11},{11... | collective-permute-start | bytes 196616 | tf_op jit(solution)/shard_map/ppermute | solution.py:26
  115.6 11.9 %collective-permute-start.3 = (f32[1,64,256]{1,2,0:T(8,128)S(1)}, f32[1,64,256]{1,2,0:T(8,128)S(1)}, u32[]{:S(2)}, u32[]{:S(2)}) collective-permute-start(f32[1,64,256]{1,2,0:T(8,128)S(1)} %copy-done.27), channel_id=1, source_target_pairs={{0,1},{1,2},{2,3},{3,4},{4,5},{5,6},{6,7},{8,9},{9,10},{10,11},{11... | collective-permute-start | bytes 196616 | tf_op jit(solution)/shard_map/ppermute | solution.py:26
  117.5 36.5 %collective-permute-start.7 = (f32[1,128,512]{1,2,0:T(8,128)}, f32[1,128,512]{1,2,0:T(8,128)}, u32[]{:S(2)}, u32[]{:S(2)}) collective-permute-start(f32[1,128,512]{1,2,0:T(8,128)} %get-tuple-element.51), channel_id=1, source_target_pairs={{1,0},{2,1},{3,2},{4,3},{5,4},{6,5},{7,6},{9,8},{10,9},{11,10},{12... | collective-permute-start | bytes 786440 | tf_op jit(solution)/shard_map/ppermute | solution.py:27
  122.1 34.3 %collective-permute-start.9 = (f32[1,128,512]{1,2,0:T(8,128)}, f32[1,128,512]{1,2,0:T(8,128)}, u32[]{:S(2)}, u32[]{:S(2)}) collective-permute-start(f32[1,128,512]{1,2,0:T(8,128)} %get-tuple-element.50), channel_id=1, source_target_pairs={{0,1},{1,2},{2,3},{3,4},{4,5},{5,6},{6,7},{8,9},{9,10},{10,11},{11... | collective-permute-start | bytes 786440 | tf_op jit(solution)/shard_map/ppermute | solution.py:26
  124.0 32.4 %collective-permute-start.10 = (f32[1,128,512]{1,2,0:T(8,128)}, f32[1,128,512]{1,2,0:T(8,128)}, u32[]{:S(2)}, u32[]{:S(2)}) collective-permute-start(f32[1,128,512]{1,2,0:T(8,128)} %get-tuple-element.57), channel_id=1, source_target_pairs={{0,1},{1,2},{2,3},{3,4},{4,5},{5,6},{6,7},{8,9},{9,10},{10,11},{11... | collective-permute-start | bytes 786440 | tf_op jit(solution)/shard_map/ppermute | solution.py:26
  130.7 8.0 %collective-permute-start.19 = (f32[1,64,256]{1,2,0:T(8,128)S(1)}, f32[1,64,256]{1,2,0:T(8,128)S(1)}, u32[]{:S(2)}, u32[]{:S(2)}) collective-permute-start(f32[1,64,256]{1,2,0:T(8,128)S(1)} %get-tuple-element.114), channel_id=1, source_target_pairs={{1,0},{2,1},{3,2},{4,3},{5,4},{6,5},{7,6},{9,8},{10,9},{11,10},{12... | collective-permute-start | bytes 196616 | tf_op jit(solution)/shard_map/ppermute | solution.py:27
  135.2 8.1 %collective-permute-start.20 = (f32[1,64,256]{1,2,0:T(8,128)S(1)}, f32[1,64,256]{1,2,0:T(8,128)S(1)}, u32[]{:S(2)}, u32[]{:S(2)}) collective-permute-start(f32[1,64,256]{1,2,0:T(8,128)S(1)} %get-tuple-element.115), channel_id=1, source_target_pairs={{0,1},{1,2},{2,3},{3,4},{4,5},{5,6},{6,7},{8,9},{9,10},{10,11},{11... | collective-permute-start | bytes 196616 | tf_op jit(solution)/shard_map/ppermute | solution.py:26
  138.6 17.8 %collective-permute-start.8 = (f32[1,128,512]{1,2,0:T(8,128)}, f32[1,128,512]{1,2,0:T(8,128)}, u32[]{:S(2)}, u32[]{:S(2)}) collective-permute-start(f32[1,128,512]{1,2,0:T(8,128)} %get-tuple-element.56), channel_id=1, source_target_pairs={{1,0},{2,1},{3,2},{4,3},{5,4},{6,5},{7,6},{9,8},{10,9},{11,10},{12... | collective-permute-start | bytes 786440 | tf_op jit(solution)/shard_map/ppermute | solution.py:27
  143.4 104.9 %collective-permute-start.4 = (f32[1,64,256]{1,2,0:T(8,128)}, f32[1,64,256]{1,2,0:T(8,128)}, u32[]{:S(2)}, u32[]{:S(2)}) collective-permute-start(f32[1,64,256]{1,2,0:T(8,128)} %get-tuple-element.98), channel_id=1, source_target_pairs={{1,0},{2,1},{3,2},{4,3},{5,4},{6,5},{7,6},{9,8},{10,9},{11,10},{12... | collective-permute-start | bytes 196616 | tf_op jit(solution)/shard_map/ppermute | solution.py:27
  154.0 94.3 %collective-permute-start.5 = (f32[1,64,256]{1,2,0:T(8,128)}, f32[1,64,256]{1,2,0:T(8,128)}, u32[]{:S(2)}, u32[]{:S(2)}) collective-permute-start(f32[1,64,256]{1,2,0:T(8,128)} %get-tuple-element.99), channel_id=1, source_target_pairs={{0,1},{1,2},{2,3},{3,4},{4,5},{5,6},{6,7},{8,9},{9,10},{10,11},{11... | collective-permute-start | bytes 196616 | tf_op jit(solution)/shard_map/ppermute | solution.py:26
  161.4 9.9 %collective-permute-start.11 = (f32[1,128,512]{1,2,0:T(8,128)S(1)}, f32[1,128,512]{1,2,0:T(8,128)S(1)}, u32[]{:S(2)}, u32[]{:S(2)}) collective-permute-start(f32[1,128,512]{1,2,0:T(8,128)S(1)} %get-tuple-element.44), channel_id=1, source_target_pairs={{1,0},{2,1},{3,2},{4,3},{5,4},{6,5},{7,6},{9,8},{10,9},{11,10},{12... | collective-permute-start | bytes 786440 | tf_op jit(solution)/shard_map/ppermute | solution.py:27
  165.5 8.6 %collective-permute-start.12 = (f32[1,128,512]{1,2,0:T(8,128)S(1)}, f32[1,128,512]{1,2,0:T(8,128)S(1)}, u32[]{:S(2)}, u32[]{:S(2)}) collective-permute-start(f32[1,128,512]{1,2,0:T(8,128)S(1)} %get-tuple-element.45), channel_id=1, source_target_pairs={{0,1},{1,2},{2,3},{3,4},{4,5},{5,6},{6,7},{8,9},{9,10},{10,11},{11... | collective-permute-start | bytes 786440 | tf_op jit(solution)/shard_map/ppermute | solution.py:26
  179.0 8.6 %collective-permute-start.14 = (f32[1,128,512]{1,2,0:T(8,128)S(1)}, f32[1,128,512]{1,2,0:T(8,128)S(1)}, u32[]{:S(2)}, u32[]{:S(2)}) collective-permute-start(f32[1,128,512]{1,2,0:T(8,128)S(1)} %get-tuple-element.39), channel_id=1, source_target_pairs={{0,1},{1,2},{2,3},{3,4},{4,5},{5,6},{6,7},{8,9},{9,10},{10,11},{11... | collective-permute-start | bytes 786440 | tf_op jit(solution)/shard_map/ppermute | solution.py:26
  192.4 8.7 %collective-permute-start.16 = (f32[1,128,512]{1,2,0:T(8,128)S(1)}, f32[1,128,512]{1,2,0:T(8,128)S(1)}, u32[]{:S(2)}, u32[]{:S(2)}) collective-permute-start(f32[1,128,512]{1,2,0:T(8,128)S(1)} %get-tuple-element.33), channel_id=1, source_target_pairs={{0,1},{1,2},{2,3},{3,4},{4,5},{5,6},{6,7},{8,9},{9,10},{10,11},{11... | collective-permute-start | bytes 786440 | tf_op jit(solution)/shard_map/ppermute | solution.py:26
  253.1 8.4 %collective-permute-start.22 = (f32[1,64,256]{1,2,0:T(8,128)}, f32[1,64,256]{1,2,0:T(8,128)}, u32[]{:S(2)}, u32[]{:S(2)}) collective-permute-start(f32[1,64,256]{1,2,0:T(8,128)} %get-tuple-element.97), channel_id=1, source_target_pairs={{0,1},{1,2},{2,3},{3,4},{4,5},{5,6},{6,7},{8,9},{9,10},{10,11},{11... | collective-permute-start | bytes 196616 | tf_op jit(solution)/shard_map/ppermute | solution.py:26
  264.9 8.1 %collective-permute-start.24 = (f32[1,64,256]{1,2,0:T(8,128)S(1)}, f32[1,64,256]{1,2,0:T(8,128)S(1)}, u32[]{:S(2)}, u32[]{:S(2)}) collective-permute-start(f32[1,64,256]{1,2,0:T(8,128)S(1)} %get-tuple-element.87), channel_id=1, source_target_pairs={{0,1},{1,2},{2,3},{3,4},{4,5},{5,6},{6,7},{8,9},{9,10},{10,11},{11... | collective-permute-start | bytes 196616 | tf_op jit(solution)/shard_map/ppermute | solution.py:26
  275.4 8.0 %collective-permute-start.26 = (f32[1,64,256]{1,2,0:T(8,128)S(1)}, f32[1,64,256]{1,2,0:T(8,128)S(1)}, u32[]{:S(2)}, u32[]{:S(2)}) collective-permute-start(f32[1,64,256]{1,2,0:T(8,128)S(1)} %get-tuple-element.85), channel_id=1, source_target_pairs={{0,1},{1,2},{2,3},{3,4},{4,5},{5,6},{6,7},{8,9},{9,10},{10,11},{11... | collective-permute-start | bytes 196616 | tf_op jit(solution)/shard_map/ppermute | solution.py:26
  285.7 8.1 %collective-permute-start.28 = (f32[1,64,256]{1,2,0:T(8,128)S(1)}, f32[1,64,256]{1,2,0:T(8,128)S(1)}, u32[]{:S(2)}, u32[]{:S(2)}) collective-permute-start(f32[1,64,256]{1,2,0:T(8,128)S(1)} %get-tuple-element.75), channel_id=1, source_target_pairs={{0,1},{1,2},{2,3},{3,4},{4,5},{5,6},{6,7},{8,9},{9,10},{10,11},{11... | collective-permute-start | bytes 196616 | tf_op jit(solution)/shard_map/ppermute | solution.py:26
  296.2 8.0 %collective-permute-start.30 = (f32[1,64,256]{1,2,0:T(8,128)S(1)}, f32[1,64,256]{1,2,0:T(8,128)S(1)}, u32[]{:S(2)}, u32[]{:S(2)}) collective-permute-start(f32[1,64,256]{1,2,0:T(8,128)S(1)} %get-tuple-element.73), channel_id=1, source_target_pairs={{0,1},{1,2},{2,3},{3,4},{4,5},{5,6},{6,7},{8,9},{9,10},{10,11},{11... | collective-permute-start | bytes 196616 | tf_op jit(solution)/shard_map/ppermute | solution.py:26
  (37 other events, 250.9 us)
where the time goes:
time: 322 us; the launch traced here: 320 us
  local copies, waits for them, and re-layouts  141 us (44%)
  starting transfers between devices  84.9 us (26%)
  waiting for transfers between devices  50.1 us (16%)
  other arithmetic  26.8 us (8%)
  blocking collectives  15.2 us (5%)
    slice x8, local copies, waits for them, and re-layouts, restrict(): paired = paired[:, 0::2] + paired[:, 1::2]  103 us
    ppermute x16, starting transfers between devices, extended(): after = lax.ppermute(initial, axis, down)  44.1 us
    ppermute x16, waiting for transfers between devices, extended(): before = lax.ppermute(last, axis, up)  41.2 us
    ppermute x16, starting transfers between devices, extended(): before = lax.ppermute(last, axis, up)  36.3 us
    all_gather x1, blocking collectives, shards(): all_reduced = lax.all_gather(reduced[None], 'tm', axis=0, tiled=True)  15.2 us
    add x9, other arithmetic, local_step(): return center + factor * flux_sum  15.1 us
    unnamed x65, local copies, waits for them, and re-layouts  10.2 us
    slice x26, local copies, waits for them, and re-layouts, neighbour(): lax.slice_in_dim(field, 1, count, axis=dim)  9.21 us
  transfers between devices with their start and end apart: 33, of which 13 were waited for; matrix products, arithmetic and copies ran while one was open for 47% of the time, Pallas kernels for 0%

commit v1 on v0

v1 whole, which is shorter than its diff:
```python
import jax
import jax.numpy as jnp
from jax import lax
from jax.experimental import pallas as pl
from jax.experimental.pallas import tpu as pltpu
from jax.sharding import PartitionSpec as P

FINE_STEPS = 4
COARSE_STEPS = 2
FINE_RATE = 0.16
HALF_FINE = 0.5 * FINE_RATE
HALF_COARSE = 0.25 * FINE_RATE
TILE = 16
LANES = 128

VMEM = pl.BlockSpec(memory_space=pltpu.VMEM)
SMEM = pl.BlockSpec(memory_space=pltpu.SMEM)
F32 = jnp.float32


def call(body, out_shapes, operands, specs=None, scratch=(), flops=0):
    operands = list(operands)
    specs = specs or [VMEM] * len(operands)
    return pl.pallas_call(
        body,
        out_shape=[jax.ShapeDtypeStruct(s, F32) for s in out_shapes],
        in_specs=specs,
        out_specs=[VMEM] * len(out_shapes),
        scratch_shapes=list(scratch),
        compiler_params=pltpu.CompilerParams(vmem_limit_bytes=32 * 1024 * 1024),
    )(*operands)


def lane_scratch(rows, columns):
    return pltpu.VMEM((columns // LANES, rows, LANES), F32)


def split3(x):
    hi = x.astype(jnp.bfloat16)
    rest = x - hi.astype(F32)
    mid = rest.astype(jnp.bfloat16)
    low = (rest - mid.astype(F32)).astype(jnp.bfloat16)
    return hi, mid, low


def dot3(x, m):
    parts = [jnp.dot(p, m, preferred_element_type=F32) for p in split3(x)]
    return parts[0] + (parts[1] + parts[2])


def pair_matrix(fine, coarse, value):
    rows = lax.broadcasted_iota(jnp.int32, (fine, coarse), 0)
    cols = lax.broadcasted_iota(jnp.int32, (fine, coarse), 1)
    return jnp.where((rows >> 1) == cols, value, 0.0).astype(jnp.bfloat16)


def repeat_matrix(coarse, fine):
    rows = lax.broadcasted_iota(jnp.int32, (coarse, fine), 0)
    cols = lax.broadcasted_iota(jnp.int32, (coarse, fine), 1)
    return jnp.where(rows == (cols >> 1), 1.0, 0.0).astype(jnp.bfloat16)


def restrict_planes(first, second, scratch, matrix):
    blocks, ny, _ = scratch.shape
    sums = dot3(first + second, matrix)
    parts = []
    for b in range(blocks):
        scratch[b] = sums[:, b * LANES:(b + 1) * LANES]
        parts.append(scratch[b, pl.ds(0, ny // 2, 2), :] + scratch[b, pl.ds(1, ny // 2, 2), :])
    return jnp.concatenate(parts, axis=1)


def rows_above(ref, index, a, size):
    if a == 0:
        return pltpu.roll(ref[index + (slice(0, size),)], 1, 0)
    return ref[index + (slice(a - 1, a + size - 1),)]


def rows_below(ref, index, a, size, ny):
    if a + size == ny:
        return pltpu.roll(ref[index + (slice(a, a + size),)], size - 1, 0)
    return ref[index + (slice(a + 1, a + size + 1),)]


def face_coefficients(k, above, below, half, a, size, ny, nz):
    row = lax.broadcasted_iota(jnp.int32, (size, nz), 0) + a
    col = lax.broadcasted_iota(jnp.int32, (size, nz), 1)
    up_face = half * (k + jnp.where(row == 0, 0.0, above))
    down_face = half * (k + jnp.where(row == ny - 1, 0.0, below))
    right = pltpu.roll(k, nz - 1, 1)
    left = pltpu.roll(k, 1, 1)
    right_face = half * (k + jnp.where(col == nz - 1, 0.0, right))
    left_face = half * (k + jnp.where(col == 0, 0.0, left))
    total = (up_face + down_face) + (right_face + left_face)
    return (
        jnp.where(row == 0, 0.0, up_face),
        jnp.where(row == ny - 1, 0.0, down_face),
        jnp.where(col == nz - 1, 0.0, right_face),
        total,
    )


def prepare_fine(cond):
    nx, ny, nz = cond.shape

    def body(k_ref, kx, up, down, right, diag, coarse, scratch):
        for p in range(nx):
            for a in range(0, ny, TILE):
                s = slice(a, a + TILE)
                k = k_ref[p, s]
                u, d, r, total = face_coefficients(
                    k, rows_above(k_ref, (p,), a, TILE), rows_below(k_ref, (p,), a, TILE, ny),
                    HALF_FINE, a, TILE, ny, nz)
                up[p, s], down[p, s], right[p, s] = u, d, r
                if p > 0:
                    total = total + kx[p - 1, s]
                if p < nx - 1:
                    face = HALF_FINE * (k + k_ref[p + 1, s])
                    kx[p, s] = face
                    total = total + face
                diag[p, s] = 1.0 - total
        matrix = pair_matrix(nz, nz // 2, 0.125)
        for q in range(nx // 2):
            coarse[q] = restrict_planes(k_ref[2 * q], k_ref[2 * q + 1], scratch, matrix)

    full = (nx, ny, nz)
    return call(
        body,
        [(nx - 1, ny, nz), full, full, full, full, (nx // 2, ny // 2, nz // 2)],
        [cond],
        scratch=[lane_scratch(ny, nz // 2)],
    )


def restricted(field):
    nx, ny, nz = field.shape

    def body(f_ref, out, scratch):
        matrix = pair_matrix(nz, nz // 2, 0.125)
        for q in range(nx // 2):
            out[q] = restrict_planes(f_ref[2 * q], f_ref[2 * q + 1], scratch, matrix)

    return call(
        body, [(nx // 2, ny // 2, nz // 2)], [field], scratch=[lane_scratch(ny, nz // 2)]
    )[0]


def fine_step(ends, planes, before, after, cond, cond_before, cond_after, coefficients, last_prior=None):
    nx = len(planes)
    ny, nz = planes[0].shape
    final = last_prior is not None

    def body(*refs):
        ends_ref = refs[0]
        v = refs[1:1 + nx]
        lo, hi, k_ref, k_lo, k_hi, kx, up, down, right, diag = refs[1 + nx:11 + nx]
        rest = refs[11 + nx:]
        has_lo, has_hi = ends_ref[0] > 0, ends_ref[1] > 0
        if final:
            prior_ref, out_ref, jump_ref, scratch = rest
            out = [out_ref.at[p] for p in range(nx)]
        else:
            out = rest
        for p in range(nx):
            for a in range(0, ny, TILE):
                s = slice(a, a + TILE)
                c = v[p][s]
                total = diag[p, s] * c
                total = total + up[p, s] * rows_above(v[p], (), a, TILE)
                total = total + down[p, s] * rows_below(v[p], (), a, TILE, ny)
                r = right[p, s]
                total = total + r * pltpu.roll(c, nz - 1, 1)
                total = total + pltpu.roll(r * c, 1, 1)
                if p > 0:
                    total = total + kx[p - 1, s] * v[p - 1][s]
                else:
                    face = HALF_FINE * (k_ref[p, s] + jnp.where(has_lo, k_lo[0, s], 0.0))
                    total = total + face * (jnp.where(has_lo, lo[s], 0.0) - c)
                if p < nx - 1:
                    total = total + kx[p, s] * v[p + 1][s]
                else:
                    face = HALF_FINE * (k_ref[p, s] + jnp.where(has_hi, k_hi[0, s], 0.0))
                    total = total + face * (jnp.where(has_hi, hi[s], 0.0) - c)
                out[p][s] = total
        if final:
            matrix = pair_matrix(nz, nz // 2, 0.125)
            for q in range(nx // 2):
                jump_ref[q] = restrict_planes(out[2 * q][...], out[2 * q + 1][...], scratch, matrix) - prior_ref[q]

    operands = [ends, *planes, before, after, cond, cond_before, cond_after, *coefficients]
    if final:
        operands.append(last_prior)
        shapes = [(nx, ny, nz), (nx // 2, ny // 2, nz // 2)]
        scratch = [lane_scratch(ny, nz // 2)]
    else:
        shapes = [(ny, nz)] * nx
        scratch = []
    return call(body, shapes, operands, [SMEM] + [VMEM] * (len(operands) - 1), scratch)


def coarse_coefficients(ends, own, before, after):
    nx, ny, nz = own.shape
    planes = nx + 2

    def body(ends_ref, k_own, k_lo, k_hi, kx, up, down, right, diag):
        has_lo, has_hi = ends_ref[0] > 0, ends_ref[1] > 0

        def plane(i):
            if i < 2:
                return jnp.where(has_lo, k_lo[nx - 2 + i], 0.0)
            if i < nx + 2:
                return k_own[i - 2]
            return jnp.where(has_hi, k_hi[i - nx - 2], 0.0)

        for i in range(planes + 1):
            kx[i] = HALF_COARSE * (plane(i) + plane(i + 1))
        for p in range(planes):
            k = plane(p + 1)
            u, d, r, total = face_coefficients(
                k, pltpu.roll(k, 1, 0), pltpu.roll(k, ny - 1, 0), HALF_COARSE, 0, ny, ny, nz)
            up[p], down[p], right[p] = u, d, r
            diag[p] = 1.0 - (total + kx[p] + kx[p + 1])

    full = (planes, ny, nz)
    return call(
        body, [(planes + 1, ny, nz)] + [full] * 4, [ends, own, before, after], [SMEM] + [VMEM] * 3
    )


def coarse_sweep_step(ends, own, before, after, coefficients, jump=None):
    nx, ny, nz = own.shape

    def body(ends_ref, d_own, d_lo, d_hi, kx, up, down, right, diag, *rest):
        has_lo, has_hi = ends_ref[0] > 0, ends_ref[1] > 0

        def step(v, i):
            c = v[1]
            total = diag[i] * c + kx[i] * v[0] + kx[i + 1] * v[2]
            total = total + up[i] * pltpu.roll(c, 1, 0) + down[i] * pltpu.roll(c, ny - 1, 0)
            return total + right[i] * pltpu.roll(c, nz - 1, 1) + pltpu.roll(right[i] * c, 1, 1)

        lo = [jnp.where(has_lo, d_lo[nx - 2 + i], 0.0) for i in range(2)]
        hi = [jnp.where(has_hi, d_hi[i], 0.0) for i in range(2)]
        v = lo + [d_own[i] for i in range(nx)] + hi
        w = [step(v[i:i + 3], i) for i in range(nx + 2)]
        w[0] = jnp.where(has_lo, w[0], 0.0)
        w[-1] = jnp.where(has_hi, w[-1], 0.0)
        for i in range(nx):
            e = step(w[i:i + 3], i + 1)
            rest[-1 if jump is None else -2][i] = e
            if jump is not None:
                rest[-1][i] = e + rest[0][i]

    operands = [ends, own, before, after, *coefficients]
    shapes = [own.shape]
    if jump is not None:
        operands.append(jump)
        shapes.append(own.shape)
    return call(body, shapes, operands, [SMEM] + [VMEM] * (len(operands) - 1))


def finish(fine, prior, correction):
    nx, ny, nz = fine.shape

    def body(f_ref, p_ref, e_ref, update, tail, scratch, wide):
        matrix = pair_matrix(nz, nz // 2, 0.125)
        spread = repeat_matrix(nz // 2, nz)
        for q in range(nx // 2):
            e = e_ref[q]
            tail[q] = e + restrict_planes(f_ref[2 * q], f_ref[2 * q + 1], scratch, matrix)
            row = dot3(e, spread)
            for b in range(nz // LANES):
                s = slice(b * LANES, (b + 1) * LANES)
                wide[b, pl.ds(0, ny // 2, 2), :] = row[:, s]
                wide[b, pl.ds(1, ny // 2, 2), :] = row[:, s]
                for p in (2 * q, 2 * q + 1):
                    update[p, :, s] = (f_ref[p, :, s] + wide[b]) - p_ref[p, :, s]

    return call(
        body,
        [(nx, ny, nz), (nx // 2, ny // 2, nz // 2)],
        [fine, prior, correction],
        scratch=[lane_scratch(ny, nz // 2), lane_scratch(ny, nz)],
    )


def ring(block, axis, distance):
    size = lax.axis_size(axis)
    return lax.ppermute(block, axis, [(i, (i + distance) % size) for i in range(size)])


def from_sides(last, first):
    return ring(last, "space", 1), ring(first, "space", -1)


def shards(initial, prior, conductivity):
    t, times = lax.axis_index("tm"), lax.axis_size("tm")
    s, blocks = lax.axis_index("space"), lax.axis_size("space")
    ends = jnp.stack([s > 0, s < blocks - 1]).astype(jnp.int32)
    own_prior = prior[0]
    nx = initial.shape[0]
    home = times - 1

    opening = jnp.where(t == home, initial, own_prior)
    planes = [opening[p] for p in range(nx)]
    cond_before, cond_after = from_sides(conductivity[nx - 1:], conductivity[:1])

    *coefficients, coarse_cond = prepare_fine(conductivity)
    next_prior = ring(restricted(own_prior), "tm", -1)
    coarse_before, coarse_after = from_sides(coarse_cond, coarse_cond)
    coarse_coef = coarse_coefficients(ends, coarse_cond, coarse_before, coarse_after)

    for step in range(FINE_STEPS):
        before, after = from_sides(planes[-1], planes[0])
        planes = fine_step(
            ends, planes, before, after, conductivity, cond_before, cond_after, coefficients,
            next_prior if step == FINE_STEPS - 1 else None)
    fine, jump = planes

    jumps = [jump] + [
        lax.ppermute(jump, "tm", [(n - 1, home)]) for n in range(1, times - 1)
    ]
    own_fine = ring(fine, "tm", 1)
    state = jump
    correction = jnp.zeros_like(jump)
    for n in range(1, times):
        before, after = from_sides(state, state)
        swept = coarse_sweep_step(
            ends, state, before, after, coarse_coef, jumps[n] if n < home else None)
        if n < home:
            e, state = swept
            arrived = lax.ppermute(e, "tm", [(home, n)])
        else:
            arrived = swept[0]
        correction = jnp.where(t == n, arrived, correction)
    update, tail = finish(own_fine, own_prior, correction)
    return update[None], tail[None]


def solution(mesh):
    return jax.shard_map(
        shards,
        mesh=mesh,
        in_specs=(P("space", None, None), P("tm", "space", None, None), P("space", None, None)),
        out_specs=(P("tm", "space", None, None), P("tm", "space", None, None)),
        check_vma=False,
    )
```

time: 322 us -> 107 us (0.33)
  the two profiles are of different devices: /device:TPU:4 before, /device:TPU:19 now
where the time goes in v1:
time: 107 us
  waiting for transfers between devices  54.5 us (51%)
  starting transfers between devices  23.2 us (22%)
  Pallas kernels  16.5 us (15%)
  local copies, waits for them, and re-layouts  10.2 us (10%)
  other arithmetic  1.54 us (1%)
    ppermute x20, waiting for transfers between devices, ring(): lax.ppermute(block, axis, [(i, (i + distance) % size) for i in range(size)])  37.1 us
    ppermute x20, starting transfers between devices, ring(): lax.ppermute(block, axis, [(i, (i + distance) % size) for i in range(size)])  20 us
    ppermute x2, waiting for transfers between devices, shards(): arrived = lax.ppermute(e, 'tm', [(home, n)])  17.4 us
    pallas_call x11, Pallas kernels, call(): pl.pallas_call(body, out_shape=[jax.ShapeDtypeStruct(s, F32) for s in out...  16.5 us
    unnamed x28, local copies, waits for them, and re-layouts  8.37 us
  transfers between devices with their start and end apart: 24, of which 17 were waited for; matrix products, arithmetic and copies ran while one was open for 1% of the time, Pallas kernels for 5%

profile of v1, /device:TPU:19, one launch (start us, length us, event | category | flops | bytes accessed | tf_op | source)
XLA Modules:
  0.0 106.8 jit_solution(2964050528609400845)
XLA Ops:
  0.6 1.4 %broadcast_select_fusion = f32[4,128,512]{2,1,0:T(8,128)S(1)} fusion(f32[4,128,512]{2,1,0:T(8,128)} %param.3, pred[]{:T(512)S(6)} %eq.10, f32[1,4,128,512]{3,2,1,0:T(8,128)} %param.4), kind=kLoop, calls=%fused_computation | loop fusion | flops 262144 | bytes 3145729 | tf_op jit(solution)/shard_map/jit(_where)/select_n | solution.py:304
  3.1 1.8 %collective-permute-start = (f32[128,512]{1,0:T(8,128)}, f32[128,512]{1,0:T(8,128)}, u32[]{:S(2)}, u32[]{:S(2)}) collective-permute-start(f32[128,512]{1,0:T(8,128)} %get-tuple-element.66.refs_4_), channel_id=1, source_target_pairs={{0,1},{1,2},{2,3},{3,4},{4,5},{5,6},{6,7},{7,0},{8,9},{9,10},{10,1... | collective-permute-start | bytes 786440 | tf_op jit(solution)/shard_map/ppermute | solution.py:289
  5.7 2.6 %collective-permute-start.2 = (f32[1,128,512]{2,1,0:T(8,128)}, f32[1,128,512]{2,1,0:T(8,128)S(1)}, u32[]{:S(2)}, u32[]{:S(2)}) collective-permute-start(f32[1,128,512]{2,1,0:T(8,128)} %get-tuple-element.65), channel_id=1, source_target_pairs={{0,1},{1,2},{2,3},{3,4},{4,5},{5,6},{6,7},{7,0},{8,9},{9,10},{10,1... | collective-permute-start | bytes 786440 | tf_op jit(solution)/shard_map/ppermute | solution.py:289
  12.4 2.3 %collective-permute-done.1.refs_6_ = f32[128,512]{1,0:T(8,128)} collective-permute-done((f32[128,512]{1,0:T(8,128)}, f32[128,512]{1,0:T(8,128)}, u32[]{:S(2)}, u32[]{:S(2)}) %collective-permute-start.1) | collective-permute-done | bytes 262176 | tf_op jit(solution)/shard_map/ppermute | solution.py:289
  16.1 2.5 %collective-permute-done.3.refs_9_ = f32[1,128,512]{2,1,0:T(8,128)} collective-permute-done((f32[1,128,512]{2,1,0:T(8,128)}, f32[1,128,512]{2,1,0:T(8,128)}, u32[]{:S(2)}, u32[]{:S(2)}) %collective-permute-start.3) | collective-permute-done | bytes 262176 | tf_op jit(solution)/shard_map/ppermute | solution.py:289
  24.1 2.3 %shard_map.51 = (f32[128,512]{1,0:T(8,128)S(1)}, f32[128,512]{1,0:T(8,128)S(1)}, f32[128,512]{1,0:T(8,128)S(1)}, f32[128,512]{1,0:T(8,128)S(1)}) custom-call(s32[2]{0:T(128)S(1)} %add_convert_fusion.refs_0_.ends_ref, f32[128,512]{1,0:T(8,128)} %get-tuple-element.69.refs_1_, f32[128,512]{1,0:T(8,128)S(1)} %copy-done.13, f32[128,512]{1,0:T(8,128)S(1)} %copy-done.12, ...), custom_call_target="tpu_custom_call" | custom-call | tf_op jit(solution)/shard_map/pallas_call | solution.py:24
  27.3 6.0 %collective-permute-done.4.refs_5_ = f32[128,512]{1,0:T(8,128)S(1)} collective-permute-done((f32[128,512]{1,0:T(8,128)S(1)}, f32[128,512]{1,0:T(8,128)S(1)}, u32[]{:S(2)}, u32[]{:S(2)}) %collective-permute-start.4) | collective-permute-done | bytes 262176 | tf_op jit(solution)/shard_map/ppermute | solution.py:289
  34.0 1.9 %shard_map.52 = (f32[128,512]{1,0:T(8,128)S(1)}, f32[128,512]{1,0:T(8,128)S(1)}, f32[128,512]{1,0:T(8,128)S(1)}, f32[128,512]{1,0:T(8,128)S(1)}) custom-call(s32[2]{0:T(128)S(1)} %add_convert_fusion.refs_0_.ends_ref, f32[128,512]{1,0:T(8,128)S(1)} %get-tuple-element.38.refs_1_, f32[128,512]{1,0:T(8,128)S(1)} %get-tuple-element.39.refs_2_, ...), custom_call_target="tpu_custom_call" | custom-call | tf_op jit(solution)/shard_map/pallas_call | solution.py:24
  35.9 2.8 %collective-permute-start.6 = (f32[128,512]{1,0:T(8,128)S(1)}, f32[128,512]{1,0:T(8,128)S(1)}, u32[]{:S(2)}, u32[]{:S(2)}) collective-permute-start(f32[128,512]{1,0:T(8,128)S(1)} %get-tuple-element.45.refs_4_), channel_id=1, source_target_pairs={{0,1},{1,2},{2,3},{3,4},{4,5},{5,6},{6,7},{7,0},{8,9},{9,10},{10,1... | collective-permute-start | bytes 786440 | tf_op jit(solution)/shard_map/ppermute | solution.py:289
  38.7 5.4 %collective-permute-done.6.refs_5_ = f32[128,512]{1,0:T(8,128)S(1)} collective-permute-done((f32[128,512]{1,0:T(8,128)S(1)}, f32[128,512]{1,0:T(8,128)S(1)}, u32[]{:S(2)}, u32[]{:S(2)}) %collective-permute-start.6) | collective-permute-done | bytes 262176 | tf_op jit(solution)/shard_map/ppermute | solution.py:289
  45.4 2.3 %shard_map.53 = (f32[128,512]{1,0:T(8,128)S(1)}, f32[128,512]{1,0:T(8,128)S(1)}, f32[128,512]{1,0:T(8,128)S(1)}, f32[128,512]{1,0:T(8,128)S(1)}) custom-call(s32[2]{0:T(128)S(1)} %add_convert_fusion.refs_0_.ends_ref, f32[128,512]{1,0:T(8,128)S(1)} %get-tuple-element.42.refs_1_, f32[128,512]{1,0:T(8,128)S(1)} %get-tuple-element.43.refs_2_, ...), custom_call_target="tpu_custom_call" | custom-call | tf_op jit(solution)/shard_map/pallas_call | solution.py:24
  47.7 2.1 %collective-permute-start.8 = (f32[128,512]{1,0:T(8,128)S(1)}, f32[128,512]{1,0:T(8,128)S(1)}, u32[]{:S(2)}, u32[]{:S(2)}) collective-permute-start(f32[128,512]{1,0:T(8,128)S(1)} %get-tuple-element.49.refs_4_), channel_id=1, source_target_pairs={{0,1},{1,2},{2,3},{3,4},{4,5},{5,6},{6,7},{7,0},{8,9},{9,10},{10,1... | collective-permute-start | bytes 786440 | tf_op jit(solution)/shard_map/ppermute | solution.py:289
  50.5 4.0 %collective-permute-done.10.refs_15_ = f32[2,64,256]{2,1,0:T(8,128)S(1)} collective-permute-done((f32[2,64,256]{2,1,0:T(8,128)S(1)}, f32[2,64,256]{2,1,0:T(8,128)S(1)}, u32[]{:S(2)}, u32[]{:S(2)}) %collective-permute-start.10) | collective-permute-done | bytes 131104 | tf_op jit(solution)/shard_map/ppermute | solution.py:289
  54.5 1.9 %collective-permute-done.9.refs_6_ = f32[128,512]{1,0:T(8,128)S(1)} collective-permute-done((f32[128,512]{1,0:T(8,128)S(1)}, f32[128,512]{1,0:T(8,128)S(1)}, u32[]{:S(2)}, u32[]{:S(2)}) %collective-permute-start.9) | collective-permute-done | bytes 262176 | tf_op jit(solution)/shard_map/ppermute | solution.py:289
  56.5 3.2 %shard_map.55 = (f32[4,128,512]{2,1,0:T(8,128)}, f32[2,64,256]{2,1,0:T(8,128)S(1)}) custom-call(s32[2]{0:T(128)S(1)} %add_convert_fusion.refs_0_.ends_ref, f32[128,512]{1,0:T(8,128)S(1)} %get-tuple-element.46.refs_1_, f32[128,512]{1,0:T(8,128)S(1)} %get-tuple-element.47.refs_2_, f32[128,512]{1,0:T(8,128)S(1)} %get-tuple-element.48.refs_3_, ...), custom_call_target="tpu_custom_call" | custom-call | tf_op jit(solution)/shard_map/pallas_call | solution.py:24
  59.7 1.6 %collective-permute-start.11 = (f32[4,128,512]{2,1,0:T(8,128)}, f32[4,128,512]{2,1,0:T(8,128)S(1)}, u32[]{:S(2)}, u32[]{:S(2)}) collective-permute-start(f32[4,128,512]{2,1,0:T(8,128)} %get-tuple-element.50), channel_id=1, source_target_pairs={{0,8},{8,16},{16,24},{24,0},{1,9},{9,17},{17,25},{25,1},{2,10},{10... | collective-permute-start | bytes 3145736 | tf_op jit(solution)/shard_map/ppermute | solution.py:289
  61.3 3.5 %collective-permute-start.14 = (f32[2,64,256]{2,1,0:T(8,128)S(1)}, f32[2,64,256]{2,1,0:T(8,128)S(1)}, u32[]{:S(2)}, u32[]{:S(2)}) collective-permute-start(f32[2,64,256]{2,1,0:T(8,128)S(1)} %get-tuple-element.52.k_own), channel_id=1, source_target_pairs={{0,1},{1,2},{2,3},{3,4},{4,5},{5,6},{6,7},{7,0},{8,9},{9,10},{10,1... | collective-permute-start | bytes 393224 | tf_op jit(solution)/shard_map/ppermute | solution.py:289
  64.9 2.6 %collective-permute-start.12 = (f32[2,64,256]{2,1,0:T(8,128)S(1)}, f32[2,64,256]{2,1,0:T(8,128)S(1)}, u32[]{:S(2)}, u32[]{:S(2)}) collective-permute-start(f32[2,64,256]{2,1,0:T(8,128)S(1)} %get-tuple-element.51.d_own), channel_id=1, source_target_pairs={{0,1},{1,2},{2,3},{3,4},{4,5},{5,6},{6,7},{7,0},{8,9},{9,10},{10,1... | collective-permute-start | bytes 393224 | tf_op jit(solution)/shard_map/ppermute | solution.py:289
  68.2 2.0 %collective-permute-done.15.k_hi = f32[2,64,256]{2,1,0:T(8,128)S(1)} collective-permute-done((f32[2,64,256]{2,1,0:T(8,128)S(1)}, f32[2,64,256]{2,1,0:T(8,128)S(1)}, u32[]{:S(2)}, u32[]{:S(2)}) %collective-permute-start.15) | collective-permute-done | bytes 131104 | tf_op jit(solution)/shard_map/ppermute | solution.py:289
  74.3 2.8 %collective-permute-done.17.d_lo = f32[2,64,256]{2,1,0:T(8,128)S(1)} collective-permute-done((f32[2,64,256]{2,1,0:T(8,128)S(1)}, f32[2,64,256]{2,1,0:T(8,128)S(1)}, u32[]{:S(2)}, u32[]{:S(2)}) %collective-permute-start.17) | collective-permute-done | bytes 131104 | tf_op jit(solution)/shard_map/ppermute | solution.py:289
  77.1 2.3 %collective-permute-done.18.d_hi = f32[2,64,256]{2,1,0:T(8,128)S(1)} collective-permute-done((f32[2,64,256]{2,1,0:T(8,128)S(1)}, f32[2,64,256]{2,1,0:T(8,128)S(1)}, u32[]{:S(2)}, u32[]{:S(2)}) %collective-permute-start.18) | collective-permute-done | bytes 131104 | tf_op jit(solution)/shard_map/ppermute | solution.py:289
  84.5 2.2 %collective-permute-done.21.d_hi = f32[2,64,256]{2,1,0:T(8,128)S(1)} collective-permute-done((f32[2,64,256]{2,1,0:T(8,128)S(1)}, f32[2,64,256]{2,1,0:T(8,128)S(1)}, u32[]{:S(2)}, u32[]{:S(2)}) %collective-permute-start.21) | collective-permute-done | bytes 131104 | tf_op jit(solution)/shard_map/ppermute | solution.py:289
  87.6 17.4 %collective-permute-done.22 = f32[2,64,256]{2,1,0:T(8,128)S(1)} collective-permute-done((f32[2,64,256]{2,1,0:T(8,128)S(1)}, f32[2,64,256]{2,1,0:T(8,128)S(1)}, u32[]{:S(2)}, u32[]{:S(2)}) %collective-permute-start.22) | collective-permute-done | bytes 131104 | tf_op jit(solution)/shard_map/ppermute | solution.py:332
  105.0 1.8 %shard_map.60 = (f32[4,128,512]{2,1,0:T(8,128)}, f32[2,64,256]{2,1,0:T(8,128)}) custom-call(f32[4,128,512]{2,1,0:T(8,128)S(1)} %collective-permute-done.11.f_ref, f32[4,128,512]{2,1,0:T(8,128)S(1)} %bitcast.15, f32[2,64,256]{2,1,0:T(8,128)S(1)} %select_select_fusion.e_ref), custom_call_target="tpu_custom_call" | custom-call | tf_op jit(solution)/shard_map/pallas_call | solution.py:24
  (68 shorter events, 27.1 us)
Async XLA Ops:
  3.1 9.3 %collective-permute-start = (f32[128,512]{1,0:T(8,128)}, f32[128,512]{1,0:T(8,128)}, u32[]{:S(2)}, u32[]{:S(2)}) collective-permute-start(f32[128,512]{1,0:T(8,128)} %get-tuple-element.66.refs_4_), channel_id=1, source_target_pairs={{0,1},{1,2},{2,3},{3,4},{4,5},{5,6},{6,7},{7,0},{8,9},{9,10},{10,1... | collective-permute-start | bytes 786440 | tf_op jit(solution)/shard_map/ppermute | solution.py:289
  4.9 9.9 %collective-permute-start.1 = (f32[128,512]{1,0:T(8,128)}, f32[128,512]{1,0:T(8,128)}, u32[]{:S(2)}, u32[]{:S(2)}) collective-permute-start(f32[128,512]{1,0:T(8,128)} %get-tuple-element.69.refs_1_), channel_id=1, source_target_pairs={{0,7},{1,0},{2,1},{3,2},{4,3},{5,4},{6,5},{7,6},{8,15},{9,8},{10,9... | collective-permute-start | bytes 786440 | tf_op jit(solution)/shard_map/ppermute | solution.py:289
  5.7 10.4 %collective-permute-start.2 = (f32[1,128,512]{2,1,0:T(8,128)}, f32[1,128,512]{2,1,0:T(8,128)S(1)}, u32[]{:S(2)}, u32[]{:S(2)}) collective-permute-start(f32[1,128,512]{2,1,0:T(8,128)} %get-tuple-element.65), channel_id=1, source_target_pairs={{0,1},{1,2},{2,3},{3,4},{4,5},{5,6},{6,7},{7,0},{8,9},{9,10},{10,1... | collective-permute-start | bytes 786440 | tf_op jit(solution)/shard_map/ppermute | solution.py:289
  8.4 10.2 %collective-permute-start.3 = (f32[1,128,512]{2,1,0:T(8,128)}, f32[1,128,512]{2,1,0:T(8,128)}, u32[]{:S(2)}, u32[]{:S(2)}) collective-permute-start(f32[1,128,512]{2,1,0:T(8,128)} %get-tuple-element.64), channel_id=1, source_target_pairs={{0,7},{1,0},{2,1},{3,2},{4,3},{5,4},{6,5},{7,6},{8,15},{9,8},{10,9... | collective-permute-start | bytes 786440 | tf_op jit(solution)/shard_map/ppermute | solution.py:289
  26.4 6.9 %collective-permute-start.4 = (f32[128,512]{1,0:T(8,128)S(1)}, f32[128,512]{1,0:T(8,128)S(1)}, u32[]{:S(2)}, u32[]{:S(2)}) collective-permute-start(f32[128,512]{1,0:T(8,128)S(1)} %get-tuple-element.41.refs_4_), channel_id=1, source_target_pairs={{0,1},{1,2},{2,3},{3,4},{4,5},{5,6},{6,7},{7,0},{8,9},{9,10},{10,1... | collective-permute-start | bytes 786440 | tf_op jit(solution)/shard_map/ppermute | solution.py:289
  27.3 6.7 %collective-permute-start.5 = (f32[128,512]{1,0:T(8,128)S(1)}, f32[128,512]{1,0:T(8,128)S(1)}, u32[]{:S(2)}, u32[]{:S(2)}) collective-permute-start(f32[128,512]{1,0:T(8,128)S(1)} %get-tuple-element.38.refs_1_), channel_id=1, source_target_pairs={{0,7},{1,0},{2,1},{3,2},{4,3},{5,4},{6,5},{7,6},{8,15},{9,8},{10,9... | collective-permute-start | bytes 786440 | tf_op jit(solution)/shard_map/ppermute | solution.py:289
  35.9 8.2 %collective-permute-start.6 = (f32[128,512]{1,0:T(8,128)S(1)}, f32[128,512]{1,0:T(8,128)S(1)}, u32[]{:S(2)}, u32[]{:S(2)}) collective-permute-start(f32[128,512]{1,0:T(8,128)S(1)} %get-tuple-element.45.refs_4_), channel_id=1, source_target_pairs={{0,1},{1,2},{2,3},{3,4},{4,5},{5,6},{6,7},{7,0},{8,9},{9,10},{10,1... | collective-permute-start | bytes 786440 | tf_op jit(solution)/shard_map/ppermute | solution.py:289
  38.7 6.7 %collective-permute-start.7 = (f32[128,512]{1,0:T(8,128)S(1)}, f32[128,512]{1,0:T(8,128)S(1)}, u32[]{:S(2)}, u32[]{:S(2)}) collective-permute-start(f32[128,512]{1,0:T(8,128)S(1)} %get-tuple-element.42.refs_1_), channel_id=1, source_target_pairs={{0,7},{1,0},{2,1},{3,2},{4,3},{5,4},{6,5},{7,6},{8,15},{9,8},{10,9... | collective-permute-start | bytes 786440 | tf_op jit(solution)/shard_map/ppermute | solution.py:289
  47.7 6.9 %collective-permute-start.8 = (f32[128,512]{1,0:T(8,128)S(1)}, f32[128,512]{1,0:T(8,128)S(1)}, u32[]{:S(2)}, u32[]{:S(2)}) collective-permute-start(f32[128,512]{1,0:T(8,128)S(1)} %get-tuple-element.49.refs_4_), channel_id=1, source_target_pairs={{0,1},{1,2},{2,3},{3,4},{4,5},{5,6},{6,7},{7,0},{8,9},{9,10},{10,1... | collective-permute-start | bytes 786440 | tf_op jit(solution)/shard_map/ppermute | solution.py:289
  49.8 6.7 %collective-permute-start.9 = (f32[128,512]{1,0:T(8,128)S(1)}, f32[128,512]{1,0:T(8,128)S(1)}, u32[]{:S(2)}, u32[]{:S(2)}) collective-permute-start(f32[128,512]{1,0:T(8,128)S(1)} %get-tuple-element.46.refs_1_), channel_id=1, source_target_pairs={{0,7},{1,0},{2,1},{3,2},{4,3},{5,4},{6,5},{7,6},{8,15},{9,8},{10,9... | collective-permute-start | bytes 786440 | tf_op jit(solution)/shard_map/ppermute | solution.py:289
  50.2 4.2 %collective-permute-start.10 = (f32[2,64,256]{2,1,0:T(8,128)S(1)}, f32[2,64,256]{2,1,0:T(8,128)S(1)}, u32[]{:S(2)}, u32[]{:S(2)}) collective-permute-start(f32[2,64,256]{2,1,0:T(8,128)S(1)} %shard_map.54), channel_id=1, source_target_pairs={{0,24},{8,0},{16,8},{24,16},{1,25},{9,1},{17,9},{25,17},{2,26},{10... | collective-permute-start | bytes 393224 | tf_op jit(solution)/shard_map/ppermute | solution.py:289
  59.7 45.2 %collective-permute-start.11 = (f32[4,128,512]{2,1,0:T(8,128)}, f32[4,128,512]{2,1,0:T(8,128)S(1)}, u32[]{:S(2)}, u32[]{:S(2)}) collective-permute-start(f32[4,128,512]{2,1,0:T(8,128)} %get-tuple-element.50), channel_id=1, source_target_pairs={{0,8},{8,16},{16,24},{24,0},{1,9},{9,17},{17,25},{25,1},{2,10},{10... | collective-permute-start | bytes 3145736 | tf_op jit(solution)/shard_map/ppermute | solution.py:289
  61.3 6.2 %collective-permute-start.14 = (f32[2,64,256]{2,1,0:T(8,128)S(1)}, f32[2,64,256]{2,1,0:T(8,128)S(1)}, u32[]{:S(2)}, u32[]{:S(2)}) collective-permute-start(f32[2,64,256]{2,1,0:T(8,128)S(1)} %get-tuple-element.52.k_own), channel_id=1, source_target_pairs={{0,1},{1,2},{2,3},{3,4},{4,5},{5,6},{6,7},{7,0},{8,9},{9,10},{10,1... | collective-permute-start | bytes 393224 | tf_op jit(solution)/shard_map/ppermute | solution.py:289
  64.9 5.3 %collective-permute-start.15 = (f32[2,64,256]{2,1,0:T(8,128)S(1)}, f32[2,64,256]{2,1,0:T(8,128)S(1)}, u32[]{:S(2)}, u32[]{:S(2)}) collective-permute-start(f32[2,64,256]{2,1,0:T(8,128)S(1)} %get-tuple-element.52.k_own), channel_id=1, source_target_pairs={{0,7},{1,0},{2,1},{3,2},{4,3},{5,4},{6,5},{7,6},{8,15},{9,8},{10,9... | collective-permute-start | bytes 393224 | tf_op jit(solution)/shard_map/ppermute | solution.py:289
  64.9 6.8 %collective-permute-start.12 = (f32[2,64,256]{2,1,0:T(8,128)S(1)}, f32[2,64,256]{2,1,0:T(8,128)S(1)}, u32[]{:S(2)}, u32[]{:S(2)}) collective-permute-start(f32[2,64,256]{2,1,0:T(8,128)S(1)} %get-tuple-element.51.d_own), channel_id=1, source_target_pairs={{0,1},{1,2},{2,3},{3,4},{4,5},{5,6},{6,7},{7,0},{8,9},{9,10},{10,1... | collective-permute-start | bytes 393224 | tf_op jit(solution)/shard_map/ppermute | solution.py:289
  67.5 5.3 %collective-permute-start.13 = (f32[2,64,256]{2,1,0:T(8,128)S(1)}, f32[2,64,256]{2,1,0:T(8,128)S(1)}, u32[]{:S(2)}, u32[]{:S(2)}) collective-permute-start(f32[2,64,256]{2,1,0:T(8,128)S(1)} %get-tuple-element.51.d_own), channel_id=1, source_target_pairs={{0,7},{1,0},{2,1},{3,2},{4,3},{5,4},{6,5},{7,6},{8,15},{9,8},{10,9... | collective-permute-start | bytes 393224 | tf_op jit(solution)/shard_map/ppermute | solution.py:289
  67.5 5.3 %collective-permute-start.16 = (f32[2,64,256]{2,1,0:T(8,128)S(1)}, f32[2,64,256]{2,1,0:T(8,128)S(1)}, u32[]{:S(2)}, u32[]{:S(2)}) collective-permute-start(f32[2,64,256]{2,1,0:T(8,128)S(1)} %get-tuple-element.51.d_own), channel_id=1, source_target_pairs={{0,24},{1,25},{2,26},{3,27},{4,28},{5,29},{6,30},{7,31}} | collective-permute-start | bytes 393224 | tf_op jit(solution)/shard_map/ppermute | solution.py:321
  71.0 3.3 %collective-permute-start.19 = (f32[2,64,256]{2,1,0:T(8,128)S(1)}, f32[2,64,256]{2,1,0:T(8,128)S(1)}, u32[]{:S(2)}, u32[]{:S(2)}) collective-permute-start(f32[2,64,256]{2,1,0:T(8,128)S(1)} %get-tuple-element.51.d_own), channel_id=1, source_target_pairs={{8,24},{9,25},{10,26},{11,27},{12,28},{13,29},{14,30},{15,31}} | collective-permute-start | bytes 393224 | tf_op jit(solution)/shard_map/ppermute | solution.py:321
  73.7 3.4 %collective-permute-start.17 = (f32[2,64,256]{2,1,0:T(8,128)S(1)}, f32[2,64,256]{2,1,0:T(8,128)S(1)}, u32[]{:S(2)}, u32[]{:S(2)}) collective-permute-start(f32[2,64,256]{2,1,0:T(8,128)S(1)} %get-tuple-element.58.d_own), channel_id=1, source_target_pairs={{0,1},{1,2},{2,3},{3,4},{4,5},{5,6},{6,7},{7,0},{8,9},{9,10},{10,1... | collective-permute-start | bytes 393224 | tf_op jit(solution)/shard_map/ppermute | solution.py:289
  74.1 5.3 %collective-permute-start.18 = (f32[2,64,256]{2,1,0:T(8,128)S(1)}, f32[2,64,256]{2,1,0:T(8,128)S(1)}, u32[]{:S(2)}, u32[]{:S(2)}) collective-permute-start(f32[2,64,256]{2,1,0:T(8,128)S(1)} %get-tuple-element.58.d_own), channel_id=1, source_target_pairs={{0,7},{1,0},{2,1},{3,2},{4,3},{5,4},{6,5},{7,6},{8,15},{9,8},{10,9... | collective-permute-start | bytes 393224 | tf_op jit(solution)/shard_map/ppermute | solution.py:289
  80.2 4.2 %collective-permute-start.20 = (f32[2,64,256]{2,1,0:T(8,128)S(1)}, f32[2,64,256]{2,1,0:T(8,128)S(1)}, u32[]{:S(2)}, u32[]{:S(2)}) collective-permute-start(f32[2,64,256]{2,1,0:T(8,128)S(1)} %get-tuple-element.59.d_own), channel_id=1, source_target_pairs={{0,1},{1,2},{2,3},{3,4},{4,5},{5,6},{6,7},{7,0},{8,9},{9,10},{10,1... | collective-permute-start | bytes 393224 | tf_op jit(solution)/shard_map/ppermute | solution.py:289
  81.4 5.3 %collective-permute-start.21 = (f32[2,64,256]{2,1,0:T(8,128)S(1)}, f32[2,64,256]{2,1,0:T(8,128)S(1)}, u32[]{:S(2)}, u32[]{:S(2)}) collective-permute-start(f32[2,64,256]{2,1,0:T(8,128)S(1)} %get-tuple-element.59.d_own), channel_id=1, source_target_pairs={{0,7},{1,0},{2,1},{3,2},{4,3},{5,4},{6,5},{7,6},{8,15},{9,8},{10,9... | collective-permute-start | bytes 393224 | tf_op jit(solution)/shard_map/ppermute | solution.py:289
  81.4 6.1 %collective-permute-start.23 = (f32[2,64,256]{2,1,0:T(8,128)S(1)}, f32[2,64,256]{2,1,0:T(8,128)S(1)}, u32[]{:S(2)}, u32[]{:S(2)}) collective-permute-start(f32[2,64,256]{2,1,0:T(8,128)S(1)} %get-tuple-element.61), channel_id=1, source_target_pairs={{24,8},{25,9},{26,10},{27,11},{28,12},{29,13},{30,14},{31,15}} | collective-permute-start | bytes 393224 | tf_op jit(solution)/shard_map/ppermute | solution.py:332
  82.1 22.9 %collective-permute-start.22 = (f32[2,64,256]{2,1,0:T(8,128)S(1)}, f32[2,64,256]{2,1,0:T(8,128)S(1)}, u32[]{:S(2)}, u32[]{:S(2)}) collective-permute-start(f32[2,64,256]{2,1,0:T(8,128)S(1)} %get-tuple-element.60), channel_id=1, source_target_pairs={{24,16},{25,17},{26,18},{27,19},{28,20},{29,21},{30,22},{31,23}} | collective-permute-start | bytes 393224 | tf_op jit(solution)/shard_map/ppermute | solution.py:332
  (14 other events, 68.2 us)

commit v2 on v1

--- a/solution.py
+++ b/solution.py
@@ -5,8 +5,6 @@
 from jax.experimental.pallas import tpu as pltpu
 from jax.sharding import PartitionSpec as P
 
-FINE_STEPS = 4
-COARSE_STEPS = 2
 FINE_RATE = 0.16
 HALF_FINE = 0.5 * FINE_RATE
 HALF_COARSE = 0.25 * FINE_RATE
@@ -27,7 +25,7 @@
         in_specs=specs,
         out_specs=[VMEM] * len(out_shapes),
         scratch_shapes=list(scratch),
-        compiler_params=pltpu.CompilerParams(vmem_limit_bytes=32 * 1024 * 1024),
+        compiler_params=pltpu.CompilerParams(vmem_limit_bytes=8 * 1024 * 1024),
     )(*operands)
 
 
@@ -145,56 +143,162 @@
     )[0]
 
 
-def fine_step(ends, planes, before, after, cond, cond_before, cond_after, coefficients, last_prior=None):
-    nx = len(planes)
-    ny, nz = planes[0].shape
-    final = last_prior is not None
-
-    def body(*refs):
-        ends_ref = refs[0]
-        v = refs[1:1 + nx]
-        lo, hi, k_ref, k_lo, k_hi, kx, up, down, right, diag = refs[1 + nx:11 + nx]
-        rest = refs[11 + nx:]
-        has_lo, has_hi = ends_ref[0] > 0, ends_ref[1] > 0
-        if final:
-            prior_ref, out_ref, jump_ref, scratch = rest
-            out = [out_ref.at[p] for p in range(nx)]
-        else:
-            out = rest
+def gather_openings(place, initial, prior, cond, slots):
+    nx, ny, nz = initial.shape
+    half, rows = nx // 2, ny // slots
+
+    def body(place_ref, i_ref, p_ref, k_ref, low, high, on, off, sems):
+        even = place_ref[2]
+        own, far = even * half, (1 - even) * half
+        start = pl.multiple_of(place_ref[3] * rows, rows)
+
+        def opening(ref):
+            copies = [
+                pltpu.make_async_copy(ref.at[pl.ds(0, half)], low, sems.at[0]),
+                pltpu.make_async_copy(ref.at[pl.ds(half, half)], high, sems.at[1]),
+                pltpu.make_async_copy(k_ref.at[pl.ds(own, half)], on, sems.at[2]),
+                pltpu.make_async_copy(
+                    k_ref.at[pl.ds(far, half), pl.ds(start, rows)], off, sems.at[3]),
+            ]
+            for c in copies:
+                c.start()
+            for c in copies:
+                c.wait()
+
+        pl.when(place_ref[4] > 0)(lambda: opening(i_ref))
+        pl.when(place_ref[4] == 0)(lambda: opening(p_ref))
+
+    plane = (half, ny, nz)
+    return call(
+        body, [plane, plane, plane, (half, rows, nz)], [place, initial, prior, cond],
+        [SMEM] + [pl.BlockSpec(memory_space=pl.ANY)] * 3, [pltpu.SemaphoreType.DMA((4,))])
+
+
+def ghost_coefficients(place, cond, on, quarters):
+    nx, ny, nz = cond.shape
+    half, rows, _ = quarters[0].shape
+    slots = len(quarters)
+
+    def body(place_ref, k_ref, on_ref, *refs):
+        parts = refs[:slots]
+        kx, up, down, right, diag, far, sides = refs[slots:]
+        even = place_ref[2] > 0
+        has_lo, has_hi = place_ref[0] > 0, place_ref[1] > 0
+        for j in range(slots):
+            slot = lax.rem(place_ref[3] + (slots - j), slots)
+            far[:, pl.ds(pl.multiple_of(slot * rows, rows), rows)] = parts[j][...]
+        for p in range(half):
+            for a in range(0, ny, TILE):
+                s = slice(a, a + TILE)
+                x, y = far[p, s], on_ref[p, s]
+                sides[p, s] = jnp.where(has_lo, jnp.where(even, x, y), 0.0)
+                sides[half + p, s] = jnp.where(has_hi, jnp.where(even, y, x), 0.0)
+        for side, near, next_, inner in ((0, half - 1, half - 2, 0), (1, half, half + 1, nx - 1)):
+            for a in range(0, ny, TILE):
+                s = slice(a, a + TILE)
+                k = sides[near, s]
+                u, d, r, total = face_coefficients(
+                    k, rows_above(sides, (near,), a, TILE), rows_below(sides, (near,), a, TILE, ny),
+                    HALF_FINE, a, TILE, ny, nz)
+                outer = HALF_FINE * (k + sides[next_, s])
+                face = HALF_FINE * (k + k_ref[inner, s])
+                kx[2 * side, s], kx[2 * side + 1, s] = outer, face
+                up[side, s], down[side, s], right[side, s] = u, d, r
+                diag[side, s] = 1.0 - ((total + outer) + face)
+
+    two = (2, ny, nz)
+    return call(
+        body, [(4, ny, nz), two, two, two, two], [place, cond, on, *quarters],
+        [SMEM] + [VMEM] * (2 + slots),
+        [pltpu.VMEM((half, ny, nz), F32), pltpu.VMEM((2 * half, ny, nz), F32)])
+
+
+def row_step(v, up, down, right, diag, a, ny, nz):
+    ref, index = v
+    s = slice(a, a + TILE)
+    c = ref[index + (s,)]
+    total = diag * c
+    total = total + up * rows_above(ref, index, a, TILE)
+    total = total + down * rows_below(ref, index, a, TILE, ny)
+    total = total + right * pltpu.roll(c, nz - 1, 1)
+    return c, total + pltpu.roll(right * c, 1, 1)
+
+
+def half_step(low, high, coefficients):
+    half, ny, nz = low.shape
+    nx = 2 * half
+
+    def body(low_ref, high_ref, kx, up, down, right, diag, out):
+        planes = [(low_ref, (p,)) for p in range(half)] + [(high_ref, (p,)) for p in range(half)]
         for p in range(nx):
             for a in range(0, ny, TILE):
                 s = slice(a, a + TILE)
-                c = v[p][s]
-                total = diag[p, s] * c
-                total = total + up[p, s] * rows_above(v[p], (), a, TILE)
-                total = total + down[p, s] * rows_below(v[p], (), a, TILE, ny)
-                r = right[p, s]
-                total = total + r * pltpu.roll(c, nz - 1, 1)
-                total = total + pltpu.roll(r * c, 1, 1)
+                c, total = row_step(planes[p], up[p, s], down[p, s], right[p, s], diag[p, s], a, ny, nz)
                 if p > 0:
-                    total = total + kx[p - 1, s] * v[p - 1][s]
+                    ref, index = planes[p - 1]
+                    total = total + kx[p - 1, s] * ref[index + (s,)]
+                if p < nx - 1:
+                    ref, index = planes[p + 1]
+                    total = total + kx[p, s] * ref[index + (s,)]
+                out[p, s] = total
+
+    return call(body, [(nx, ny, nz)], [low, high, *coefficients])[0]
+
+
+def two_steps(place, low, high, before, after, started, coefficients, ghosts, last_prior=None, extra=()):
+    half, ny, nz = low.shape
+    nx = 2 * half
+    final = last_prior is not None
+
+    def body(place_ref, low_ref, high_ref, lo, hi, part, kx, up, down, right, diag, gx, gup, gdown, gright, gdiag, *rest):
+        has_lo, has_hi = place_ref[0] > 0, place_ref[1] > 0
+        rest = rest[len(extra):]
+        if final:
+            prior_ref, out_ref, jump_ref, mid, scratch = rest
+            out = [out_ref.at[p] for p in range(nx)]
+        else:
+            low_out, high_out, mid = rest
+            out = [low_out.at[p] for p in range(half)] + [high_out.at[p] for p in range(half)]
+        for a in range(0, ny, TILE):
+            s = slice(a, a + TILE)
+            for side, ref, near, far, inner, has, own, place_in in (
+                (0, lo, half - 1, half - 2, low_ref[0, s], has_lo, 0, 0),
+                (1, hi, 0, 1, high_ref[half - 1, s], has_hi, nx - 1, nx + 1),
+            ):
+                c, total = row_step(
+                    (ref, (near,)), gup[side, s], gdown[side, s], gright[side, s], gdiag[side, s], a, ny, nz)
+                total = total + gx[2 * side, s] * ref[far, s] + gx[2 * side + 1, s] * inner
+                mid[place_in, s] = jnp.where(has, total, 0.0)
+                mid[own + 1, s] = part[own, s] + gx[2 * side + 1, s] * (jnp.where(has, c, 0.0) - inner)
+            for p in range(1, nx - 1):
+                mid[p + 1, s] = part[p, s]
+        for p in range(nx):
+            for a in range(0, ny, TILE):
+                s = slice(a, a + TILE)
+                c, total = row_step(
+                    (mid, (p + 1,)), up[p, s], down[p, s], right[p, s], diag[p, s], a, ny, nz)
+                if p > 0:
+                    total = total + kx[p - 1, s] * mid[p, s]
                 else:
-                    face = HALF_FINE * (k_ref[p, s] + jnp.where(has_lo, k_lo[0, s], 0.0))
-                    total = total + face * (jnp.where(has_lo, lo[s], 0.0) - c)
+                    total = total + gx[1, s] * (mid[p, s] - c)
                 if p < nx - 1:
-                    total = total + kx[p, s] * v[p + 1][s]
+                    total = total + kx[p, s] * mid[p + 2, s]
                 else:
-                    face = HALF_FINE * (k_ref[p, s] + jnp.where(has_hi, k_hi[0, s], 0.0))
-                    total = total + face * (jnp.where(has_hi, hi[s], 0.0) - c)
+                    total = total + gx[3, s] * (mid[p + 2, s] - c)
                 out[p][s] = total
         if final:
             matrix = pair_matrix(nz, nz // 2, 0.125)
-            for q in range(nx // 2):
+            for q in range(half):
                 jump_ref[q] = restrict_planes(out[2 * q][...], out[2 * q + 1][...], scratch, matrix) - prior_ref[q]
 
-    operands = [ends, *planes, before, after, cond, cond_before, cond_after, *coefficients]
+    operands = [place, low, high, before, after, started, *coefficients, *ghosts, *extra]
+    scratch = [pltpu.VMEM((nx + 2, ny, nz), F32)]
     if final:
         operands.append(last_prior)
-        shapes = [(nx, ny, nz), (nx // 2, ny // 2, nz // 2)]
-        scratch = [lane_scratch(ny, nz // 2)]
+        shapes = [(nx, ny, nz), (half, ny // 2, nz // 2)]
+        scratch.append(lane_scratch(ny, nz // 2))
     else:
-        shapes = [(ny, nz)] * nx
-        scratch = []
+        shapes = [low.shape, high.shape]
     return call(body, shapes, operands, [SMEM] + [VMEM] * (len(operands) - 1), scratch)
 
 
@@ -293,29 +397,37 @@
     return ring(last, "space", 1), ring(first, "space", -1)
 
 
+def swapped(block, axis, offset):
+    size = lax.axis_size(axis)
+    pairs = [(i % size, (i + 1) % size) for i in range(offset, size + offset, 2)]
+    return lax.ppermute(block, axis, pairs + [(j, i) for i, j in pairs])
+
+
 def shards(initial, prior, conductivity):
     t, times = lax.axis_index("tm"), lax.axis_size("tm")
     s, blocks = lax.axis_index("space"), lax.axis_size("space")
-    ends = jnp.stack([s > 0, s < blocks - 1]).astype(jnp.int32)
     own_prior = prior[0]
-    nx = initial.shape[0]
     home = times - 1
-
-    opening = jnp.where(t == home, initial, own_prior)
-    planes = [opening[p] for p in range(nx)]
-    cond_before, cond_after = from_sides(conductivity[nx - 1:], conductivity[:1])
+    place = jnp.stack([s > 0, s < blocks - 1, s % 2 == 0, t, t == home]).astype(jnp.int32)
+
+    low, high, on, off = gather_openings(place, initial, own_prior, conductivity, times)
+    off = swapped(off, "space", 1)
+    before, after = from_sides(high, low)
+    on = swapped(on, "space", 0)
+    quarters = [off] + [ring(off, "tm", j) for j in range(1, times)]
 
     *coefficients, coarse_cond = prepare_fine(conductivity)
+    started = half_step(low, high, coefficients)
     next_prior = ring(restricted(own_prior), "tm", -1)
     coarse_before, coarse_after = from_sides(coarse_cond, coarse_cond)
-    coarse_coef = coarse_coefficients(ends, coarse_cond, coarse_before, coarse_after)
-
-    for step in range(FINE_STEPS):
-        before, after = from_sides(planes[-1], planes[0])
-        planes = fine_step(
-            ends, planes, before, after, conductivity, cond_before, cond_after, coefficients,
-            next_prior if step == FINE_STEPS - 1 else None)
-    fine, jump = planes
+    ghosts = ghost_coefficients(place, conductivity, on, quarters)
+    low, high = two_steps(place, low, high, before, after, started, coefficients, ghosts)
+
+    before, after = from_sides(high, low)
+    started = half_step(low, high, coefficients)
+    coarse_coef = coarse_coefficients(place, coarse_cond, coarse_before, coarse_after)
+    fine, jump = two_steps(
+        place, low, high, before, after, started, coefficients, ghosts, next_prior, coarse_coef[:1])
 
     jumps = [jump] + [
         lax.ppermute(jump, "tm", [(n - 1, home)]) for n in range(1, times - 1)
@@ -326,7 +438,7 @@
     for n in range(1, times):
         before, after = from_sides(state, state)
         swept = coarse_sweep_step(
-            ends, state, before, after, coarse_coef, jumps[n] if n < home else None)
+            place, state, before, after, coarse_coef, jumps[n] if n < home else None)
         if n < home:
             e, state = swept
             arrived = lax.ppermute(e, "tm", [(home, n)])

time: 107 us -> 115 us (1.075)
  the two profiles are of different devices: /device:TPU:19 before, /device:TPU:16 now
where the time goes in v2:
time: 115 us; the launch traced here: 114 us
  waiting for transfers between devices  65.8 us (57%)
  starting transfers between devices  24.5 us (21%)
  Pallas kernels  18.4 us (16%)
  local copies, waits for them, and re-layouts  3.77 us (3%)
    ppermute x17, waiting for transfers between devices, ring(): lax.ppermute(block, axis, [(i, (i + distance) % size) for i in range(size)])  27 us
    ppermute x2, waiting for transfers between devices, shards(): arrived = lax.ppermute(e, 'tm', [(home, n)])  25.8 us
    ppermute x17, starting transfers between devices, ring(): lax.ppermute(block, axis, [(i, (i + distance) % size) for i in range(size)])  20.1 us
    pallas_call x13, Pallas kernels, call(): pl.pallas_call(body, out_shape=[jax.ShapeDtypeStruct(s, F32) for s in out...  18.4 us
    ppermute x2, waiting for transfers between devices, swapped(): return lax.ppermute(block, axis, pairs + [(j, i) for i, j in pairs])  13 us
    unnamed x10, local copies, waits for them, and re-layouts  3.69 us
    ppermute x2, starting transfers between devices, shards(): arrived = lax.ppermute(e, 'tm', [(home, n)])  2.6 us
  transfers between devices with their start and end apart: 23, of which 10 were waited for; matrix products, arithmetic and copies ran while one was open for 1% of the time, Pallas kernels for 9%

profile of v2, /device:TPU:16, one launch (start us, length us, event | category | flops | bytes accessed | tf_op | source)
XLA Modules:
  0.0 114.3 jit_solution(10082431737824840266)
XLA Ops:
  5.8 2.2 %collective-permute-start.1 = (f32[2,128,512]{2,1,0:T(8,128)S(1)}, f32[2,128,512]{2,1,0:T(8,128)S(1)}, u32[]{:S(2)}, u32[]{:S(2)}) collective-permute-start(f32[2,128,512]{2,1,0:T(8,128)S(1)} %get-tuple-element.32.low_ref), channel_id=1, source_target_pairs={{0,7},{1,0},{2,1},{3,2},{4,3},{5,4},{6,5},{7,6},{8,15},{9,8},{10,9... | collective-permute-start | bytes 1572872 | tf_op jit(solution)/shard_map/ppermute | solution.py:393
  8.3 13.0 %collective-permute-done.3.refs_0_ = f32[2,32,512]{2,1,0:T(8,128)S(1)} collective-permute-done((f32[2,32,512]{2,1,0:T(8,128)S(1)}, f32[2,32,512]{2,1,0:T(8,128)S(1)}, u32[]{:S(2)}, u32[]{:S(2)}) %collective-permute-start.3) | collective-permute-done | bytes 131104 | tf_op jit(solution)/shard_map/ppermute | solution.py:403
  21.4 1.6 %collective-permute-start.4 = (f32[2,32,512]{2,1,0:T(8,128)S(1)}, f32[2,32,512]{2,1,0:T(8,128)S(1)}, u32[]{:S(2)}, u32[]{:S(2)}) collective-permute-start(f32[2,32,512]{2,1,0:T(8,128)S(1)} %collective-permute-done.3.refs_0_), channel_id=1, source_target_pairs={{0,8},{8,16},{16,24},{24,0},{1,9},{9,17},{17,25},{25,1},{2,10},{10... | collective-permute-start | bytes 393224 | tf_op jit(solution)/shard_map/ppermute | solution.py:393
  23.3 3.7 %collective-permute-done.4.refs_1_ = f32[2,32,512]{2,1,0:T(8,128)S(1)} collective-permute-done((f32[2,32,512]{2,1,0:T(8,128)S(1)}, f32[2,32,512]{2,1,0:T(8,128)S(1)}, u32[]{:S(2)}, u32[]{:S(2)}) %collective-permute-start.4) | collective-permute-done | bytes 131104 | tf_op jit(solution)/shard_map/ppermute | solution.py:393
  29.6 2.5 %collective-permute-done.5.refs_2_ = f32[2,32,512]{2,1,0:T(8,128)S(1)} collective-permute-done((f32[2,32,512]{2,1,0:T(8,128)S(1)}, f32[2,32,512]{2,1,0:T(8,128)S(1)}, u32[]{:S(2)}, u32[]{:S(2)}) %collective-permute-start.5) | collective-permute-done | bytes 131104 | tf_op jit(solution)/shard_map/ppermute | solution.py:393
  32.1 2.8 %collective-permute-done.6.refs_3_ = f32[2,32,512]{2,1,0:T(8,128)S(1)} collective-permute-done((f32[2,32,512]{2,1,0:T(8,128)S(1)}, f32[2,32,512]{2,1,0:T(8,128)S(1)}, u32[]{:S(2)}, u32[]{:S(2)}) %collective-permute-start.6) | collective-permute-done | bytes 131104 | tf_op jit(solution)/shard_map/ppermute | solution.py:393
  36.2 2.3 %shard_map.54 = (f32[2,128,512]{2,1,0:T(8,128)S(1)}, f32[2,128,512]{2,1,0:T(8,128)S(1)}) custom-call(s32[5]{0:T(128)S(1)} %stack.39.place_ref.ends_ref, f32[2,128,512]{2,1,0:T(8,128)S(1)} %get-tuple-element.32.low_ref, f32[2,128,512]{2,1,0:T(8,128)S(1)} %get-tuple-element.33.high_ref, f32[2,128,512]{2,1,0:T(8,128)S(1)} %collective-permute-done.lo, ...), custom_call_target="tpu_custom_call" | custom-call | tf_op jit(solution)/shard_map/pallas_call | solution.py:22
  38.9 2.3 %collective-permute-start.8 = (f32[2,128,512]{2,1,0:T(8,128)S(1)}, f32[2,128,512]{2,1,0:T(8,128)S(1)}, u32[]{:S(2)}, u32[]{:S(2)}) collective-permute-start(f32[2,128,512]{2,1,0:T(8,128)S(1)} %get-tuple-element.46.low_ref), channel_id=1, source_target_pairs={{0,7},{1,0},{2,1},{3,2},{4,3},{5,4},{6,5},{7,6},{8,15},{9,8},{10,9... | collective-permute-start | bytes 1572872 | tf_op jit(solution)/shard_map/ppermute | solution.py:393
  42.2 2.5 %collective-permute-start.11 = (f32[2,64,256]{2,1,0:T(8,128)S(1)}, f32[2,64,256]{2,1,0:T(8,128)S(1)}, u32[]{:S(2)}, u32[]{:S(2)}) collective-permute-start(f32[2,64,256]{2,1,0:T(8,128)S(1)} %shard_map.57), channel_id=1, source_target_pairs={{0,24},{8,0},{16,8},{24,16},{1,25},{9,1},{17,9},{25,17},{2,26},{10... | collective-permute-start | bytes 393224 | tf_op jit(solution)/shard_map/ppermute | solution.py:393
  44.7 9.9 %collective-permute-done.10.k_hi = f32[2,64,256]{2,1,0:T(8,128)S(1)} collective-permute-done((f32[2,64,256]{2,1,0:T(8,128)S(1)}, f32[2,64,256]{2,1,0:T(8,128)S(1)}, u32[]{:S(2)}, u32[]{:S(2)}) %collective-permute-start.10) | collective-permute-done | bytes 131104 | tf_op jit(solution)/shard_map/ppermute | solution.py:393
  57.2 3.5 %shard_map.58 = (f32[4,128,512]{2,1,0:T(8,128)}, f32[2,64,256]{2,1,0:T(8,128)S(1)}) custom-call(s32[5]{0:T(128)S(1)} %stack.39.place_ref.ends_ref, f32[2,128,512]{2,1,0:T(8,128)S(1)} %get-tuple-element.46.low_ref, f32[2,128,512]{2,1,0:T(8,128)S(1)} %get-tuple-element.47.high_ref, f32[2,128,512]{2,1,0:T(8,128)S(1)} %collective-permute-done.7.lo, ...), custom_call_target="tpu_custom_call" | custom-call | tf_op jit(solution)/shard_map/pallas_call | solution.py:22
  60.7 1.4 %collective-permute-start.12 = (f32[4,128,512]{2,1,0:T(8,128)}, f32[4,128,512]{2,1,0:T(8,128)S(1)}, u32[]{:S(2)}, u32[]{:S(2)}) collective-permute-start(f32[4,128,512]{2,1,0:T(8,128)} %get-tuple-element.50), channel_id=1, source_target_pairs={{0,8},{8,16},{16,24},{24,0},{1,9},{9,17},{17,25},{25,1},{2,10},{10... | collective-permute-start | bytes 3145736 | tf_op jit(solution)/shard_map/ppermute | solution.py:393
  62.2 1.7 %collective-permute-start.13 = (f32[2,64,256]{2,1,0:T(8,128)S(1)}, f32[2,64,256]{2,1,0:T(8,128)S(1)}, u32[]{:S(2)}, u32[]{:S(2)}) collective-permute-start(f32[2,64,256]{2,1,0:T(8,128)S(1)} %get-tuple-element.51.d_own), channel_id=1, source_target_pairs={{0,1},{1,2},{2,3},{3,4},{4,5},{5,6},{6,7},{7,0},{8,9},{9,10},{10,1... | collective-permute-start | bytes 393224 | tf_op jit(solution)/shard_map/ppermute | solution.py:393
  66.1 2.2 %collective-permute-done.13.d_lo = f32[2,64,256]{2,1,0:T(8,128)S(1)} collective-permute-done((f32[2,64,256]{2,1,0:T(8,128)S(1)}, f32[2,64,256]{2,1,0:T(8,128)S(1)}, u32[]{:S(2)}, u32[]{:S(2)}) %collective-permute-start.13) | collective-permute-done | bytes 131104 | tf_op jit(solution)/shard_map/ppermute | solution.py:393
  68.3 1.5 %shard_map.59 = (f32[2,64,256]{2,1,0:T(8,128)}, f32[2,64,256]{2,1,0:T(8,128)S(1)}) custom-call(s32[5]{0:T(128)S(1)} %stack.39.place_ref.ends_ref, f32[2,64,256]{2,1,0:T(8,128)S(1)} %get-tuple-element.51.d_own, f32[2,64,256]{2,1,0:T(8,128)S(1)} %collective-permute-done.13.d_lo, f32[2,64,256]{2,1,0:T(8,128)S(1)} %collective-permute-done.14.d_hi, ...), custom_call_target="tpu_custom_call" | custom-call | tf_op jit(solution)/shard_map/pallas_call | solution.py:22
  70.4 2.1 %collective-permute-start.17 = (f32[2,64,256]{2,1,0:T(8,128)S(1)}, f32[2,64,256]{2,1,0:T(8,128)S(1)}, u32[]{:S(2)}, u32[]{:S(2)}) collective-permute-start(f32[2,64,256]{2,1,0:T(8,128)S(1)} %get-tuple-element.56.d_own), channel_id=1, source_target_pairs={{0,7},{1,0},{2,1},{3,2},{4,3},{5,4},{6,5},{7,6},{8,15},{9,8},{10,9... | collective-permute-start | bytes 393224 | tf_op jit(solution)/shard_map/ppermute | solution.py:393
  72.5 4.0 %collective-permute-done.16.d_lo = f32[2,64,256]{2,1,0:T(8,128)S(1)} collective-permute-done((f32[2,64,256]{2,1,0:T(8,128)S(1)}, f32[2,64,256]{2,1,0:T(8,128)S(1)}, u32[]{:S(2)}, u32[]{:S(2)}) %collective-permute-start.16) | collective-permute-done | bytes 131104 | tf_op jit(solution)/shard_map/ppermute | solution.py:393
  76.5 1.6 %shard_map.60 = (f32[2,64,256]{2,1,0:T(8,128)}, f32[2,64,256]{2,1,0:T(8,128)}) custom-call(s32[5]{0:T(128)S(1)} %stack.39.place_ref.ends_ref, f32[2,64,256]{2,1,0:T(8,128)S(1)} %get-tuple-element.56.d_own, f32[2,64,256]{2,1,0:T(8,128)S(1)} %collective-permute-done.16.d_lo, f32[2,64,256]{2,1,0:T(8,128)S(1)} %collective-permute-done.17.d_hi, ...), custom_call_target="tpu_custom_call" | custom-call | tf_op jit(solution)/shard_map/pallas_call | solution.py:22
  78.1 1.9 %collective-permute-start.19 = (f32[2,64,256]{2,1,0:T(8,128)}, f32[2,64,256]{2,1,0:T(8,128)}, u32[]{:S(2)}, u32[]{:S(2)}) collective-permute-start(f32[2,64,256]{2,1,0:T(8,128)} %get-tuple-element.57.d_own), channel_id=1, source_target_pairs={{0,1},{1,2},{2,3},{3,4},{4,5},{5,6},{6,7},{7,0},{8,9},{9,10},{10,1... | collective-permute-start | bytes 393224 | tf_op jit(solution)/shard_map/ppermute | solution.py:393
  80.7 1.3 %collective-permute-start.22 = (f32[2,64,256]{2,1,0:T(8,128)}, f32[2,64,256]{2,1,0:T(8,128)}, u32[]{:S(2)}, u32[]{:S(2)}) collective-permute-start(f32[2,64,256]{2,1,0:T(8,128)} %get-tuple-element.59), channel_id=1, source_target_pairs={{24,8},{25,9},{26,10},{27,11},{28,12},{29,13},{30,14},{31,15}} | collective-permute-start | bytes 393224 | tf_op jit(solution)/shard_map/ppermute | solution.py:444
  82.0 1.3 %collective-permute-start.21 = (f32[2,64,256]{2,1,0:T(8,128)}, f32[2,64,256]{2,1,0:T(8,128)}, u32[]{:S(2)}, u32[]{:S(2)}) collective-permute-start(f32[2,64,256]{2,1,0:T(8,128)} %get-tuple-element.58), channel_id=1, source_target_pairs={{24,16},{25,17},{26,18},{27,19},{28,20},{29,21},{30,22},{31,23}} | collective-permute-start | bytes 393224 | tf_op jit(solution)/shard_map/ppermute | solution.py:444
  84.4 1.3 %shard_map.61 = f32[2,64,256]{2,1,0:T(8,128)S(1)} custom-call(s32[5]{0:T(128)S(1)} %stack.39.place_ref.ends_ref, f32[2,64,256]{2,1,0:T(8,128)} %get-tuple-element.57.d_own, f32[2,64,256]{2,1,0:T(8,128)} %collective-permute-done.19.d_lo, f32[2,64,256]{2,1,0:T(8,128)} %collective-permute-done.20.d_hi, f32[5,64,256]{2,1,0:T(8,128)S(1)} %get-tuple-element.49.rest_0_.kx, ...), custom_call_target="tpu_custom_call" | custom-call | tf_op jit(solution)/shard_map/pallas_call | solution.py:22
  85.8 25.8 %collective-permute-done.21 = f32[2,64,256]{2,1,0:T(8,128)} collective-permute-done((f32[2,64,256]{2,1,0:T(8,128)}, f32[2,64,256]{2,1,0:T(8,128)}, u32[]{:S(2)}, u32[]{:S(2)}) %collective-permute-start.21) | collective-permute-done | bytes 131104 | tf_op jit(solution)/shard_map/ppermute | solution.py:444
  112.5 1.8 %shard_map.62 = (f32[4,128,512]{2,1,0:T(8,128)}, f32[2,64,256]{2,1,0:T(8,128)}) custom-call(f32[4,128,512]{2,1,0:T(8,128)S(1)} %collective-permute-done.12.f_ref, f32[4,128,512]{2,1,0:T(8,128)S(1)} %bitcast.10, f32[2,64,256]{2,1,0:T(8,128)S(1)} %select_select_fusion.e_ref), custom_call_target="tpu_custom_call" | custom-call | tf_op jit(solution)/shard_map/pallas_call | solution.py:22
  (47 shorter events, 19.2 us)
Async XLA Ops:
  5.2 29.7 %collective-permute-start.2 = (f32[2,128,512]{2,1,0:T(8,128)S(1)}, f32[2,128,512]{2,1,0:T(8,128)S(1)}, u32[]{:S(2)}, u32[]{:S(2)}) collective-permute-start(f32[2,128,512]{2,1,0:T(8,128)S(1)} %get-tuple-element.39), channel_id=1, source_target_pairs={{0,1},{2,3},{4,5},{6,7},{1,0},{3,2},{5,4},{7,6},{8,9},{10,11},{12,... | collective-permute-start | bytes 1572872 | tf_op jit(solution)/shard_map/ppermute | solution.py:403
  5.3 30.8 %collective-permute-start = (f32[2,128,512]{2,1,0:T(8,128)S(1)}, f32[2,128,512]{2,1,0:T(8,128)S(1)}, u32[]{:S(2)}, u32[]{:S(2)}) collective-permute-start(f32[2,128,512]{2,1,0:T(8,128)S(1)} %get-tuple-element.33.high_ref), channel_id=1, source_target_pairs={{0,1},{1,2},{2,3},{3,4},{4,5},{5,6},{6,7},{7,0},{8,9},{9,10},{10,1... | collective-permute-start | bytes 1572872 | tf_op jit(solution)/shard_map/ppermute | solution.py:393
  5.8 30.4 %collective-permute-start.1 = (f32[2,128,512]{2,1,0:T(8,128)S(1)}, f32[2,128,512]{2,1,0:T(8,128)S(1)}, u32[]{:S(2)}, u32[]{:S(2)}) collective-permute-start(f32[2,128,512]{2,1,0:T(8,128)S(1)} %get-tuple-element.32.low_ref), channel_id=1, source_target_pairs={{0,7},{1,0},{2,1},{3,2},{4,3},{5,4},{6,5},{7,6},{8,15},{9,8},{10,9... | collective-permute-start | bytes 1572872 | tf_op jit(solution)/shard_map/ppermute | solution.py:393
  8.0 13.4 %collective-permute-start.3 = (f32[2,32,512]{2,1,0:T(8,128)S(1)}, f32[2,32,512]{2,1,0:T(8,128)S(1)}, u32[]{:S(2)}, u32[]{:S(2)}) collective-permute-start(f32[2,32,512]{2,1,0:T(8,128)S(1)} %get-tuple-element.40), channel_id=1, source_target_pairs={{1,2},{3,4},{5,6},{7,0},{2,1},{4,3},{6,5},{0,7},{9,10},{11,12},{13... | collective-permute-start | bytes 393224 | tf_op jit(solution)/shard_map/ppermute | solution.py:403
  21.4 5.6 %collective-permute-start.4 = (f32[2,32,512]{2,1,0:T(8,128)S(1)}, f32[2,32,512]{2,1,0:T(8,128)S(1)}, u32[]{:S(2)}, u32[]{:S(2)}) collective-permute-start(f32[2,32,512]{2,1,0:T(8,128)S(1)} %collective-permute-done.3.refs_0_), channel_id=1, source_target_pairs={{0,8},{8,16},{16,24},{24,0},{1,9},{9,17},{17,25},{25,1},{2,10},{10... | collective-permute-start | bytes 393224 | tf_op jit(solution)/shard_map/ppermute | solution.py:393
  23.0 9.2 %collective-permute-start.5 = (f32[2,32,512]{2,1,0:T(8,128)S(1)}, f32[2,32,512]{2,1,0:T(8,128)S(1)}, u32[]{:S(2)}, u32[]{:S(2)}) collective-permute-start(f32[2,32,512]{2,1,0:T(8,128)S(1)} %collective-permute-done.3.refs_0_), channel_id=1, source_target_pairs={{0,16},{8,24},{16,0},{24,8},{1,17},{9,25},{17,1},{25,9},{2,18},{10... | collective-permute-start | bytes 393224 | tf_op jit(solution)/shard_map/ppermute | solution.py:393
  27.0 7.9 %collective-permute-start.6 = (f32[2,32,512]{2,1,0:T(8,128)S(1)}, f32[2,32,512]{2,1,0:T(8,128)S(1)}, u32[]{:S(2)}, u32[]{:S(2)}) collective-permute-start(f32[2,32,512]{2,1,0:T(8,128)S(1)} %collective-permute-done.3.refs_0_), channel_id=1, source_target_pairs={{0,24},{8,0},{16,8},{24,16},{1,25},{9,1},{17,9},{25,17},{2,26},{10... | collective-permute-start | bytes 393224 | tf_op jit(solution)/shard_map/ppermute | solution.py:393
  28.6 6.4 %copy-start.1 = (f32[4,128,512]{2,1,0:T(8,128)S(1)}, f32[4,128,512]{2,1,0:T(8,128)}, u32[]{:S(2)}) copy-start(f32[4,128,512]{2,1,0:T(8,128)} %k_ref.5) | copy-start | bytes 3145732
  38.5 18.7 %collective-permute-start.7 = (f32[2,128,512]{2,1,0:T(8,128)S(1)}, f32[2,128,512]{2,1,0:T(8,128)S(1)}, u32[]{:S(2)}, u32[]{:S(2)}) collective-permute-start(f32[2,128,512]{2,1,0:T(8,128)S(1)} %get-tuple-element.47.high_ref), channel_id=1, source_target_pairs={{0,1},{1,2},{2,3},{3,4},{4,5},{5,6},{6,7},{7,0},{8,9},{9,10},{10,1... | collective-permute-start | bytes 1572872 | tf_op jit(solution)/shard_map/ppermute | solution.py:393
  38.9 18.4 %collective-permute-start.8 = (f32[2,128,512]{2,1,0:T(8,128)S(1)}, f32[2,128,512]{2,1,0:T(8,128)S(1)}, u32[]{:S(2)}, u32[]{:S(2)}) collective-permute-start(f32[2,128,512]{2,1,0:T(8,128)S(1)} %get-tuple-element.46.low_ref), channel_id=1, source_target_pairs={{0,7},{1,0},{2,1},{3,2},{4,3},{5,4},{6,5},{7,6},{8,15},{9,8},{10,9... | collective-permute-start | bytes 1572872 | tf_op jit(solution)/shard_map/ppermute | solution.py:393
  41.2 13.4 %collective-permute-start.10 = (f32[2,64,256]{2,1,0:T(8,128)S(1)}, f32[2,64,256]{2,1,0:T(8,128)S(1)}, u32[]{:S(2)}, u32[]{:S(2)}) collective-permute-start(f32[2,64,256]{2,1,0:T(8,128)S(1)} %get-tuple-element.48.k_own), channel_id=1, source_target_pairs={{0,7},{1,0},{2,1},{3,2},{4,3},{5,4},{6,5},{7,6},{8,15},{9,8},{10,9... | collective-permute-start | bytes 393224 | tf_op jit(solution)/shard_map/ppermute | solution.py:393
  41.2 14.2 %collective-permute-start.9 = (f32[2,64,256]{2,1,0:T(8,128)S(1)}, f32[2,64,256]{2,1,0:T(8,128)S(1)}, u32[]{:S(2)}, u32[]{:S(2)}) collective-permute-start(f32[2,64,256]{2,1,0:T(8,128)S(1)} %get-tuple-element.48.k_own), channel_id=1, source_target_pairs={{0,1},{1,2},{2,3},{3,4},{4,5},{5,6},{6,7},{7,0},{8,9},{9,10},{10,1... | collective-permute-start | bytes 393224 | tf_op jit(solution)/shard_map/ppermute | solution.py:393
  42.2 15.0 %collective-permute-start.11 = (f32[2,64,256]{2,1,0:T(8,128)S(1)}, f32[2,64,256]{2,1,0:T(8,128)S(1)}, u32[]{:S(2)}, u32[]{:S(2)}) collective-permute-start(f32[2,64,256]{2,1,0:T(8,128)S(1)} %shard_map.57), channel_id=1, source_target_pairs={{0,24},{8,0},{16,8},{24,16},{1,25},{9,1},{17,9},{25,17},{2,26},{10... | collective-permute-start | bytes 393224 | tf_op jit(solution)/shard_map/ppermute | solution.py:393
  60.7 51.7 %collective-permute-start.12 = (f32[4,128,512]{2,1,0:T(8,128)}, f32[4,128,512]{2,1,0:T(8,128)S(1)}, u32[]{:S(2)}, u32[]{:S(2)}) collective-permute-start(f32[4,128,512]{2,1,0:T(8,128)} %get-tuple-element.50), channel_id=1, source_target_pairs={{0,8},{8,16},{16,24},{24,0},{1,9},{9,17},{17,25},{25,1},{2,10},{10... | collective-permute-start | bytes 3145736 | tf_op jit(solution)/shard_map/ppermute | solution.py:393
  62.2 6.2 %collective-permute-start.13 = (f32[2,64,256]{2,1,0:T(8,128)S(1)}, f32[2,64,256]{2,1,0:T(8,128)S(1)}, u32[]{:S(2)}, u32[]{:S(2)}) collective-permute-start(f32[2,64,256]{2,1,0:T(8,128)S(1)} %get-tuple-element.51.d_own), channel_id=1, source_target_pairs={{0,1},{1,2},{2,3},{3,4},{4,5},{5,6},{6,7},{7,0},{8,9},{9,10},{10,1... | collective-permute-start | bytes 393224 | tf_op jit(solution)/shard_map/ppermute | solution.py:393
  63.9 4.4 %collective-permute-start.14 = (f32[2,64,256]{2,1,0:T(8,128)S(1)}, f32[2,64,256]{2,1,0:T(8,128)S(1)}, u32[]{:S(2)}, u32[]{:S(2)}) collective-permute-start(f32[2,64,256]{2,1,0:T(8,128)S(1)} %get-tuple-element.51.d_own), channel_id=1, source_target_pairs={{0,7},{1,0},{2,1},{3,2},{4,3},{5,4},{6,5},{7,6},{8,15},{9,8},{10,9... | collective-permute-start | bytes 393224 | tf_op jit(solution)/shard_map/ppermute | solution.py:393
  64.8 3.5 %collective-permute-start.15 = (f32[2,64,256]{2,1,0:T(8,128)S(1)}, f32[2,64,256]{2,1,0:T(8,128)S(1)}, u32[]{:S(2)}, u32[]{:S(2)}) collective-permute-start(f32[2,64,256]{2,1,0:T(8,128)S(1)} %get-tuple-element.51.d_own), channel_id=1, source_target_pairs={{0,24},{1,25},{2,26},{3,27},{4,28},{5,29},{6,30},{7,31}} | collective-permute-start | bytes 393224 | tf_op jit(solution)/shard_map/ppermute | solution.py:433
  65.5 7.0 %collective-permute-start.18 = (f32[2,64,256]{2,1,0:T(8,128)S(1)}, f32[2,64,256]{2,1,0:T(8,128)S(1)}, u32[]{:S(2)}, u32[]{:S(2)}) collective-permute-start(f32[2,64,256]{2,1,0:T(8,128)S(1)} %get-tuple-element.51.d_own), channel_id=1, source_target_pairs={{8,24},{9,25},{10,26},{11,27},{12,28},{13,29},{14,30},{15,31}} | collective-permute-start | bytes 393224 | tf_op jit(solution)/shard_map/ppermute | solution.py:433
  69.9 6.6 %collective-permute-start.16 = (f32[2,64,256]{2,1,0:T(8,128)S(1)}, f32[2,64,256]{2,1,0:T(8,128)S(1)}, u32[]{:S(2)}, u32[]{:S(2)}) collective-permute-start(f32[2,64,256]{2,1,0:T(8,128)S(1)} %get-tuple-element.56.d_own), channel_id=1, source_target_pairs={{0,1},{1,2},{2,3},{3,4},{4,5},{5,6},{6,7},{7,0},{8,9},{9,10},{10,1... | collective-permute-start | bytes 393224 | tf_op jit(solution)/shard_map/ppermute | solution.py:393
  70.4 6.1 %collective-permute-start.17 = (f32[2,64,256]{2,1,0:T(8,128)S(1)}, f32[2,64,256]{2,1,0:T(8,128)S(1)}, u32[]{:S(2)}, u32[]{:S(2)}) collective-permute-start(f32[2,64,256]{2,1,0:T(8,128)S(1)} %get-tuple-element.56.d_own), channel_id=1, source_target_pairs={{0,7},{1,0},{2,1},{3,2},{4,3},{5,4},{6,5},{7,6},{8,15},{9,8},{10,9... | collective-permute-start | bytes 393224 | tf_op jit(solution)/shard_map/ppermute | solution.py:393
  78.1 6.4 %collective-permute-start.19 = (f32[2,64,256]{2,1,0:T(8,128)}, f32[2,64,256]{2,1,0:T(8,128)}, u32[]{:S(2)}, u32[]{:S(2)}) collective-permute-start(f32[2,64,256]{2,1,0:T(8,128)} %get-tuple-element.57.d_own), channel_id=1, source_target_pairs={{0,1},{1,2},{2,3},{3,4},{4,5},{5,6},{6,7},{7,0},{8,9},{9,10},{10,1... | collective-permute-start | bytes 393224 | tf_op jit(solution)/shard_map/ppermute | solution.py:393
  79.9 4.5 %collective-permute-start.20 = (f32[2,64,256]{2,1,0:T(8,128)}, f32[2,64,256]{2,1,0:T(8,128)}, u32[]{:S(2)}, u32[]{:S(2)}) collective-permute-start(f32[2,64,256]{2,1,0:T(8,128)} %get-tuple-element.57.d_own), channel_id=1, source_target_pairs={{0,7},{1,0},{2,1},{3,2},{4,3},{5,4},{6,5},{7,6},{8,15},{9,8},{10,9... | collective-permute-start | bytes 393224 | tf_op jit(solution)/shard_map/ppermute | solution.py:393
  80.7 5.1 %collective-permute-start.22 = (f32[2,64,256]{2,1,0:T(8,128)}, f32[2,64,256]{2,1,0:T(8,128)}, u32[]{:S(2)}, u32[]{:S(2)}) collective-permute-start(f32[2,64,256]{2,1,0:T(8,128)} %get-tuple-element.59), channel_id=1, source_target_pairs={{24,8},{25,9},{26,10},{27,11},{28,12},{29,13},{30,14},{31,15}} | collective-permute-start | bytes 393224 | tf_op jit(solution)/shard_map/ppermute | solution.py:444
  82.0 29.5 %collective-permute-start.21 = (f32[2,64,256]{2,1,0:T(8,128)}, f32[2,64,256]{2,1,0:T(8,128)}, u32[]{:S(2)}, u32[]{:S(2)}) collective-permute-start(f32[2,64,256]{2,1,0:T(8,128)} %get-tuple-element.58), channel_id=1, source_target_pairs={{24,16},{25,17},{26,18},{27,19},{28,20},{29,21},{30,22},{31,23}} | collective-permute-start | bytes 393224 | tf_op jit(solution)/shard_map/ppermute | solution.py:444
  (4 other events, 9.2 us)

commit v3 on v1

v3 whole, which is shorter than its diff:
```python
import jax
import jax.numpy as jnp
from jax import lax
from jax.experimental import pallas as pl
from jax.experimental.pallas import tpu as pltpu
from jax.sharding import PartitionSpec as P

FINE_RATE = 0.16
HALF_FINE = 0.5 * FINE_RATE
HALF_COARSE = 0.25 * FINE_RATE
TILE = 8
OVERLAP = 8
LANES = 128

VMEM = pl.BlockSpec(memory_space=pltpu.VMEM)
SMEM = pl.BlockSpec(memory_space=pltpu.SMEM)
HBM = pl.BlockSpec(memory_space=pltpu.HBM)
F32 = jnp.float32


def call(body, out_shapes, operands, specs=None, scratch=()):
    operands = list(operands)
    specs = specs or [VMEM] * len(operands)
    operands = [
        pltpu.with_memory_space_constraint(x, pltpu.HBM) if spec is HBM else x for x, spec in zip(operands, specs)
    ]
    return pl.pallas_call(
        body,
        out_shape=[jax.ShapeDtypeStruct(s, F32) for s in out_shapes],
        in_specs=specs,
        out_specs=[VMEM] * len(out_shapes),
        scratch_shapes=list(scratch),
        compiler_params=pltpu.CompilerParams(vmem_limit_bytes=8 * 1024 * 1024),
    )(*operands)


def lane_scratch(rows, columns):
    return pltpu.VMEM((columns // LANES, rows, LANES), F32)


def split3(x):
    hi = x.astype(jnp.bfloat16)
    rest = x - hi.astype(F32)
    mid = rest.astype(jnp.bfloat16)
    low = (rest - mid.astype(F32)).astype(jnp.bfloat16)
    return hi, mid, low


def dot3(x, m):
    parts = [jnp.dot(p, m, preferred_element_type=F32) for p in split3(x)]
    return parts[0] + (parts[1] + parts[2])


def pair_matrix(fine, coarse, value):
    rows = lax.broadcasted_iota(jnp.int32, (fine, coarse), 0)
    cols = lax.broadcasted_iota(jnp.int32, (fine, coarse), 1)
    return jnp.where((rows >> 1) == cols, value, 0.0).astype(jnp.bfloat16)


def repeat_matrix(coarse, fine):
    rows = lax.broadcasted_iota(jnp.int32, (coarse, fine), 0)
    cols = lax.broadcasted_iota(jnp.int32, (coarse, fine), 1)
    return jnp.where(rows == (cols >> 1), 1.0, 0.0).astype(jnp.bfloat16)


def restrict_planes(first, second, scratch, matrix):
    blocks, ny, _ = scratch.shape
    sums = dot3(first + second, matrix)
    parts = []
    for b in range(blocks):
        scratch[b] = sums[:, b * LANES:(b + 1) * LANES]
        parts.append(scratch[b, pl.ds(0, ny // 2, 2), :] + scratch[b, pl.ds(1, ny // 2, 2), :])
    return jnp.concatenate(parts, axis=1)


class Field:
    def __init__(self, pieces, ny):
        self.pieces, self.ny = pieces, ny

    def find(self, row):
        for piece in self.pieces:
            if piece[0] <= row < piece[1]:
                return piece
        return None

    def rows(self, a, size):
        first, end, ref, index, base = self.find(a)
        return ref[index + (slice(a - base, a - base + size),)]

    def tile(self, a):
        return self.rows(a, TILE)

    def edge(self, a, row, shift, at):
        moved = pltpu.roll(self.tile(a), shift, 0)
        if self.find(row) is None:
            return moved
        place = lax.broadcasted_iota(jnp.int32, moved.shape, 0)
        return jnp.where(place == at, self.rows(row, 1), moved)

    def above(self, a):
        if self.find(a - 1) == self.find(a):
            return self.rows(a - 1, TILE)
        return self.edge(a, a - 1, 1, 0)

    def below(self, a):
        if self.find(a + TILE) == self.find(a):
            return self.rows(a + 1, TILE)
        return self.edge(a, a + TILE, TILE - 1, TILE - 1)


def plane(ref, index, ny):
    return Field([(0, ny, ref, index, 0)], ny)


def face_coefficients(k, above, below, half, a, size, ny, nz):
    row = lax.broadcasted_iota(jnp.int32, (size, nz), 0) + a
    col = lax.broadcasted_iota(jnp.int32, (size, nz), 1)
    up_face = half * (k + jnp.where(row == 0, 0.0, above))
    down_face = half * (k + jnp.where(row == ny - 1, 0.0, below))
    right = pltpu.roll(k, nz - 1, 1)
    left = pltpu.roll(k, 1, 1)
    right_face = half * (k + jnp.where(col == nz - 1, 0.0, right))
    left_face = half * (k + jnp.where(col == 0, 0.0, left))
    total = (up_face + down_face) + (right_face + left_face)
    return (
        jnp.where(row == 0, 0.0, up_face),
        jnp.where(row == ny - 1, 0.0, down_face),
        jnp.where(col == nz - 1, 0.0, right_face),
        total,
    )


def prepare_fine(cond):
    nx, ny, nz = cond.shape

    def body(k_ref, kx, up, down, right, diag):
        for p in range(nx):
            for a in range(0, ny, TILE):
                s = slice(a, a + TILE)
                k = k_ref[p, s]
                u, d, r, total = face_coefficients(
                    k, plane(k_ref, (p,), ny).above(a), plane(k_ref, (p,), ny).below(a),
                    HALF_FINE, a, TILE, ny, nz)
                up[p, s], down[p, s], right[p, s] = u, d, r
                if p > 0:
                    total = total + kx[p - 1, s]
                if p < nx - 1:
                    face = HALF_FINE * (k + k_ref[p + 1, s])
                    kx[p, s] = face
                    total = total + face
                diag[p, s] = 1.0 - total
    full = (nx, ny, nz)
    return call(body, [(nx - 1, ny, nz), full, full, full, full], [cond])


def restricted(field):
    nx, ny, nz = field.shape

    def body(f_ref, out, scratch):
        matrix = pair_matrix(nz, nz // 2, 0.125)
        for q in range(nx // 2):
            out[q] = restrict_planes(f_ref[2 * q], f_ref[2 * q + 1], scratch, matrix)

    return call(
        body, [(nx // 2, ny // 2, nz // 2)], [field], scratch=[lane_scratch(ny, nz // 2)]
    )[0]


def packed(half, nz, at, count):
    step = count // (2 * half)
    return [
        (slice(i * step, (i + 1) * step),
         (i // 2, slice(at, at + step), slice(i % 2 * nz // 2, (i % 2 + 1) * nz // 2)))
        for i in range(2 * half)
    ]


def row_copies(source, out, base, rows, at, sems, first_sem):
    start, end = rows
    return [
        pltpu.make_async_copy(
            source.at[base + p, pl.ds(start, end - start)], out.at[p, pl.ds(at, end - start)], sems.at[first_sem + p])
        for p in range(out.shape[0])
    ]


def run(copies):
    for c in copies:
        c.start()
    for c in copies:
        c.wait()


def chosen(flag, body, this, other):
    pl.when(flag > 0)(lambda: body(this))
    pl.when(flag == 0)(lambda: body(other))


def first_messages(place, initial, prior, cond, end):
    nx, ny, nz = cond.shape
    half = nx // 2

    def body(place_ref, i_ref, p_ref, k_ref, down, up, sems):
        def copy(ref):
            copies = []
            for out, base in ((down, 0), (up, half)):
                for source, at in ((k_ref, 0), (ref, end)):
                    copies += row_copies(source, out, base, (0, end), at, sems, len(copies))
            run(copies)

        chosen(place_ref[3], copy, i_ref, p_ref)

    return call(
        body, [(half, 2 * end, nz)] * 2, [place, initial, prior, cond], [SMEM, HBM, HBM, HBM],
        [pltpu.SemaphoreType.DMA((4 * half,))])


def second_messages(cond, end, after):
    nx, ny, nz = cond.shape
    half, rows = nx // 2, ny - end
    extra = ny // 2 // (2 * half)

    def body(k_ref, after_ref, down, up, cond_out, coarse, scratch, sems):
        whole = [pltpu.make_async_copy(k_ref.at[p], cond_out.at[p], sems.at[p]) for p in range(nx)]
        run(whole)
        matrix = pair_matrix(nz, nz // 2, 0.125)
        for q in range(half):
            coarse[q] = restrict_planes(cond_out[2 * q], cond_out[2 * q + 1], scratch, matrix)
            down[q, :rows] = cond_out[q, end:]
            up[q, :rows] = cond_out[half + q, end:]
        for source, to in packed(half, nz, rows, ny // 2):
            down[to] = coarse[half - 1, source]
            up[to] = coarse[0, source]

    return call(
        body, [(half, rows + extra, nz)] * 2 + [(nx, ny, nz), (half, ny // 2, nz // 2)],
        [cond, after], [HBM, VMEM], [lane_scratch(ny, nz // 2), pltpu.SemaphoreType.DMA((nx,))])


def rows_from(field, start, after):
    nx, ny, nz = field.shape

    def body(ref, after_ref, out, sems):
        run(row_copies(ref, out, 0, (start, ny), 0, sems, 0))

    return call(body, [(nx, ny - start, nz)], [field, after], [HBM, VMEM], [pltpu.SemaphoreType.DMA((nx,))])[0]


def third_messages(place, initial, received, start):
    nx, ny, nz = initial.shape
    half = nx // 2

    def body(place_ref, i_ref, r_ref, down, up, sems):
        def copy(rows_of):
            ref, rows = rows_of
            run(row_copies(ref, down, 0, rows, 0, sems, 0) + row_copies(ref, up, half, rows, 0, sems, half))

        chosen(place_ref[4], copy, (i_ref, (start, ny)), (r_ref, (0, ny - start)))

    return call(
        body, [(half, ny - start, nz)] * 2, [place, initial, received], [SMEM, HBM, VMEM],
        [pltpu.SemaphoreType.DMA((nx,))])


def ghost_coefficients(place, cond, before, after, spans, window):
    nx, ny, nz = cond.shape
    half, count = nx // 2, len(spans)
    w0, w1 = window

    def body(place_ref, k_ref, *refs):
        lo = fields(spans, refs[:count], half, ny)
        hi = fields(spans, refs[count:2 * count], half, ny)
        kx, up, down, right, diag = refs[2 * count:]
        for side, near, far, inner, has in (
            (0, lo[half - 1], lo[half - 2], 0, place_ref[0] > 0),
            (1, hi[0], hi[1], nx - 1, place_ref[1] > 0),
        ):
            for a in range(w0, w1, TILE):
                s, d = slice(a, a + TILE), slice(a - w0, a - w0 + TILE)
                k = jnp.where(has, near.tile(a), 0.0)
                above, below = (jnp.where(has, x, 0.0) for x in (near.above(a), near.below(a)))
                u, v, r, total = face_coefficients(k, above, below, HALF_FINE, a, TILE, ny, nz)
                outer = HALF_FINE * (k + jnp.where(has, far.tile(a), 0.0))
                face = HALF_FINE * (k + k_ref[inner, s])
                kx[2 * side, d], kx[2 * side + 1, d] = outer, face
                up[side, d], down[side, d], right[side, d] = u, v, r
                diag[side, d] = 1.0 - ((total + outer) + face)

    rows = w1 - w0
    return call(
        body, [(4, rows, nz)] + [(2, rows, nz)] * 4, [place, cond, *before, *after],
        [SMEM] + [VMEM] * (1 + 2 * count))


def row_step(v, up, down, right, diag, a):
    c = v.tile(a)
    nz = c.shape[1]
    total = diag * c
    total = total + up * v.above(a)
    total = total + down * v.below(a)
    total = total + right * pltpu.roll(c, nz - 1, 1)
    return c, total + pltpu.roll(right * c, 1, 1)


def fields(spans, refs, half, ny):
    return [
        Field([(a, b, ref, (p,), base) for (a, b, base), ref in zip(spans, refs)], ny)
        for p in range(half)
    ]


def half_step(low, high, spans, window, coefficients):
    half, nz = low[0].shape[0], low[0].shape[2]
    nx, ny, count = 2 * half, coefficients[1].shape[1], len(spans)
    w0, w1 = window

    def body(*refs):
        kx, up, down, right, diag, out = refs[2 * count:]
        v = fields(spans, refs[:count], half, ny) + fields(spans, refs[count:2 * count], half, ny)
        for p in range(nx):
            for a in range(w0, w1, TILE):
                s = slice(a, a + TILE)
                _, total = row_step(v[p], up[p, s], down[p, s], right[p, s], diag[p, s], a)
                if p > 0:
                    total = total + kx[p - 1, s] * v[p - 1].tile(a)
                if p < nx - 1:
                    total = total + kx[p, s] * v[p + 1].tile(a)
                out[p, a - w0:a - w0 + TILE] = total

    return call(body, [(nx, w1 - w0, nz)], [*low, *high, *coefficients])[0]


def two_steps(place, low, high, spans, before, after, side_spans, started, window, result, coefficients, ghosts, final=False):
    half, nz = low[0].shape[0], low[0].shape[2]
    nx, ny = 2 * half, coefficients[1].shape[1]
    n, m = len(spans), len(side_spans)
    (w0, w1), (r0, r1) = window, result
    counts = [n, n, m, m]

    def body(place_ref, *refs):
        groups, at = [], 0
        for c in counts:
            groups.append(refs[at:at + c])
            at += c
        part, kx, up, down, right, diag, gx, gup, gdown, gright, gdiag, *rest = refs[at:]
        v = fields(spans, groups[0], half, ny) + fields(spans, groups[1], half, ny)
        lo = fields(side_spans, groups[2], half, ny)
        hi = fields(side_spans, groups[3], half, ny)
        has_lo, has_hi = place_ref[0] > 0, place_ref[1] > 0
        if final:
            out_ref, coarse_out, mid, scratch = rest
            out = [out_ref.at[p] for p in range(nx)]
        else:
            low_out, high_out, mid = rest
            out = [low_out.at[p] for p in range(half)] + [high_out.at[p] for p in range(half)]
        for a in range(w0, w1, TILE):
            s, d = slice(a, a + TILE), slice(a - w0, a - w0 + TILE)
            for side, near, far, has, own, ghost in (
                (0, lo[half - 1], lo[half - 2], has_lo, 0, 0),
                (1, hi[0], hi[1], has_hi, nx - 1, nx + 1),
            ):
                inner = v[own].tile(a)
                c, total = row_step(near, gup[side, d], gdown[side, d], gright[side, d], gdiag[side, d], a)
                total = total + gx[2 * side, d] * far.tile(a) + gx[2 * side + 1, d] * inner
                mid[ghost, d] = jnp.where(has, total, 0.0)
                mid[own + 1, d] = part[own, d] + gx[2 * side + 1, d] * (jnp.where(has, c, 0.0) - inner)
            for p in range(1, nx - 1):
                mid[p + 1, d] = part[p, d]
        w = [Field([(w0, w1, mid, (p,), w0)], ny) for p in range(nx + 2)]
        for p in range(nx):
            for a in range(r0, r1, TILE):
                s, d = slice(a, a + TILE), slice(a - w0, a - w0 + TILE)
                c, total = row_step(w[p + 1], up[p, s], down[p, s], right[p, s], diag[p, s], a)
                if p > 0:
                    total = total + kx[p - 1, s] * w[p].tile(a)
                else:
                    total = total + gx[1, d] * (w[p].tile(a) - c)
                if p < nx - 1:
                    total = total + kx[p, s] * w[p + 2].tile(a)
                else:
                    total = total + gx[3, d] * (w[p + 2].tile(a) - c)
                out[p][a - r0:a - r0 + TILE] = total
        if final:
            matrix = pair_matrix(nz, nz // 2, 0.125)
            for q in range(half):
                coarse_out[q] = restrict_planes(out[2 * q][...], out[2 * q + 1][...], scratch, matrix)

    operands = [place, *low, *high, *before, *after, started, *coefficients, *ghosts]
    scratch = [pltpu.VMEM((nx + 2, w1 - w0, nz), F32)]
    shapes = [(half, r1 - r0, nz)] * 2
    if final:
        scratch.append(lane_scratch(r1 - r0, nz // 2))
        shapes = [(nx, r1 - r0, nz), (half, (r1 - r0) // 2, nz // 2)]
    return call(body, shapes, operands, [SMEM] + [VMEM] * (len(operands) - 1), scratch)


def coarse_coefficients(place, own, before, after, spans):
    nx, ny, nz = own.shape
    planes, count = nx + 2, len(spans)

    def body(place_ref, k_own, *refs):
        sides = refs[:count], refs[count:2 * count]
        kx, up, down, right, diag, k_near, k_far, total, scratch = refs[2 * count:]
        matrix = pair_matrix(2 * nz, nz, 0.125)
        for i, (side, has) in enumerate(zip(sides, (place_ref[0] > 0, place_ref[1] > 0))):
            for (a, b, base), ref in zip(spans, side):
                total[a:b] = ref[0, a - base:b - base] + ref[1, a - base:b - base]
            near = restrict_planes(total[...], 0.0, scratch, matrix)
            k_near[i] = jnp.where(has, near, 0.0)
            last = side[-1]
            for rows, at in packed(nx, 2 * nz, last.shape[1] - ny // (2 * nx), ny):
                k_far[i, rows] = jnp.where(has, last[at], 0.0)

        def plane(i):
            if i == 0:
                return k_far[0]
            if i == 1:
                return k_near[0]
            if i < nx + 2:
                return k_own[i - 2]
            return k_near[1] if i == nx + 2 else k_far[1]

        for i in range(planes + 1):
            kx[i] = HALF_COARSE * (plane(i) + plane(i + 1))
        for p in range(planes):
            k = plane(p + 1)
            u, d, r, total = face_coefficients(
                k, pltpu.roll(k, 1, 0), pltpu.roll(k, ny - 1, 0), HALF_COARSE, 0, ny, ny, nz)
            up[p], down[p], right[p] = u, d, r
            diag[p] = 1.0 - (total + kx[p] + kx[p + 1])

    full = (planes, ny, nz)
    return call(
        body, [(planes + 1, ny, nz)] + [full] * 4, [place, own, *before, *after],
        [SMEM] + [VMEM] * (1 + 2 * count),
        [pltpu.VMEM((2, ny, nz), F32), pltpu.VMEM((2, ny, nz), F32),
         pltpu.VMEM((2 * ny, 2 * nz), F32), lane_scratch(2 * ny, nz)])


def sweep_step(place, own, before, after, coefficients, first, jumps=(), later=0):
    nx, ny, nz = own.shape

    def body(place_ref, d_own, d_lo, d_hi, kx, up, down, right, diag, *rest):
        live = place_ref[3] > 0 if first else True
        has_lo = jnp.logical_and(place_ref[0] > 0, live)
        has_hi = jnp.logical_and(place_ref[1] > 0, live)

        def step(v, i):
            c = v[1]
            total = diag[i] * c + kx[i] * v[0] + kx[i + 1] * v[2]
            total = total + up[i] * pltpu.roll(c, 1, 0) + down[i] * pltpu.roll(c, ny - 1, 0)
            return total + right[i] * pltpu.roll(c, nz - 1, 1) + pltpu.roll(right[i] * c, 1, 1)

        lo = [jnp.where(has_lo, d_lo[nx - 2 + i], 0.0) for i in range(2)]
        hi = [jnp.where(has_hi, d_hi[i], 0.0) for i in range(2)]
        block = [jnp.where(live, d_own[i], 0.0) if first else d_own[i] for i in range(nx)]
        v = lo + block + hi
        w = [step(v[i:i + 3], i) for i in range(nx + 2)]
        w[0] = jnp.where(has_lo, w[0], 0.0)
        w[-1] = jnp.where(has_hi, w[-1], 0.0)
        for i in range(nx):
            e = step(w[i:i + 3], i + 1)
            if jumps:
                e = e + jnp.where(place_ref[2] >= later, joined(rest[0][i], rest[1][i]), 0.0)
            rest[-1][i] = e

    operands = [place, own, before, after, *coefficients]
    operands += jumps
    return call(body, [own.shape], operands, [SMEM] + [VMEM] * (len(operands) - 1))[0]


def jumps_of(moved, own, next_prior, own_prior):
    nx, rows, nz = moved.shape

    def body(a_ref, b_ref, next_ref, own_ref, out):
        for p in range(nx):
            out[p, :rows] = a_ref[p] - next_ref[p, :rows]
            out[p, rows:] = b_ref[p] - own_ref[p, rows:]

    return call(body, [own_prior.shape], [moved, own, next_prior, own_prior])[0]


def joined(upper, lower):
    rows = upper.shape[-2]
    row = lax.broadcasted_iota(jnp.int32, upper.shape, upper.ndim - 2)
    return jnp.where(row < rows // 2, upper, lower)


def finish(moved, own, prior, correction):
    nx, ny, nz = prior.shape
    rows = moved.shape[1]

    def body(moved_ref, own_ref, p_ref, e_ref, update, tail, scratch, wide):
        matrix = pair_matrix(nz, nz // 2, 0.125)
        spread = repeat_matrix(nz // 2, nz)
        for i, ref in enumerate((own_ref, moved_ref)):
            r0 = rows * (1 - i)
            r, c = slice(r0, r0 + rows), slice(r0 // 2, (r0 + rows) // 2)
            for q in range(nx // 2):
                e = e_ref[q, c]
                tail[q, c] = e + restrict_planes(ref[2 * q], ref[2 * q + 1], scratch, matrix)
                row = dot3(e, spread)
                for b in range(nz // LANES):
                    s = slice(b * LANES, (b + 1) * LANES)
                    wide[b, pl.ds(0, rows // 2, 2), :] = row[:, s]
                    wide[b, pl.ds(1, rows // 2, 2), :] = row[:, s]
                    for p in (2 * q, 2 * q + 1):
                        update[p, r, s] = (ref[p, :, s] + wide[b]) - p_ref[p, r, s]

    return call(
        body,
        [(nx, ny, nz), (nx // 2, ny // 2, nz // 2)],
        [moved, own, prior, correction],
        scratch=[lane_scratch(rows, nz // 2), lane_scratch(rows, nz)],
    )


def ring(block, axis, distance):
    size = lax.axis_size(axis)
    return lax.ppermute(block, axis, [(i, (i + distance) % size) for i in range(size)])


def from_sides(last, first):
    return ring(last, "space", 1), ring(first, "space", -1)


def shards(initial, prior, conductivity):
    t, times = lax.axis_index("tm"), lax.axis_size("tm")
    s, blocks = lax.axis_index("space"), lax.axis_size("space")
    own_prior = prior[0]
    home = times - 1
    place = jnp.stack([s > 0, s < blocks - 1, t, t == home, t == 0]).astype(jnp.int32)
    ny = initial.shape[1]
    cut, wide = ny // 2, ny // 2 + OVERLAP
    windows = [(0, wide), (cut - OVERLAP, ny)]
    results = [(0, cut), (cut, ny)]

    down, up = first_messages(place, initial, own_prior, conductivity, wide)
    before, after = ([x] for x in from_sides(up, down))
    received = ring(rows_from(own_prior, windows[1][0], up), "tm", 1)
    down_2, up_2, cond, coarse_cond = second_messages(conductivity, wide, up)
    before_2, after_2 = from_sides(up_2, down_2)
    down_3, up_3 = third_messages(place, initial, received, windows[1][0])
    before_3, after_3 = from_sides(up_3, down_3)

    coefficients = prepare_fine(cond)
    cond_spans = [(0, wide, 0), (wide, ny, wide)]
    cond_before, cond_after = (before[0], before_2), (after[0], after_2)
    low, high = [[down], [down_3]], [[up], [up_3]]
    before, after = [before, [before_3]], [after, [after_3]]
    spans = [[(0, wide, -wide)], [(*windows[1], windows[1][0])]]
    started = [half_step(low[i], high[i], spans[i], windows[i], coefficients) for i in range(2)]
    own_coarse = restricted(own_prior)
    next_coarse = ring(own_coarse, "tm", -1)

    ghosts, middle = [], []
    for i in range(2):
        there = slice(0, i + 1)
        ghosts.append(ghost_coefficients(
            place, cond, cond_before[there], cond_after[there], cond_spans[there], windows[i]))
        middle.append(two_steps(
            place, low[i], high[i], spans[i], before[i], after[i], spans[i],
            started[i], windows[i], windows[i], coefficients, ghosts[i]))
    coarse_coef = coarse_coefficients(place, coarse_cond, cond_before, cond_after, cond_spans)
    sides = [from_sides(b, a) for a, b in middle]
    spans = [[(*w, w[0])] for w in windows]
    ended = []
    for i in range(2):
        a, b = middle[i]
        part = half_step([a], [b], spans[i], windows[i], coefficients)
        ended.append(two_steps(
            place, [a], [b], spans[i], [sides[i][0]], [sides[i][1]], spans[i],
            part, windows[i], results[i], coefficients, ghosts[i], True))
    (moved, moved_coarse), (own_fine, fine_coarse) = ended

    jump = jumps_of(moved_coarse, fine_coarse, next_coarse, own_coarse)
    shifted = [jump] + [ring(jump, "tm", -j) for j in range(1, times)]
    state = joined(shifted[0], shifted[1])
    for j in range(home):
        before, after = from_sides(state, state)
        if j == 0:
            before, after, moved, *shifted[2:] = lax.optimization_barrier((before, after, moved, *shifted[2:]))
            moved = ring(moved, "tm", 1)
        more = (shifted[j + 1:j + 3], home - j - 1) if j < home - 1 else ()
        state = sweep_step(place, state, before, after, coarse_coef, j == 0, *more)
    update, tail = finish(moved, own_fine, own_prior, state)
    return update[None], tail[None]


def solution(mesh):
    return jax.shard_map(
        shards,
        mesh=mesh,
        in_specs=(P("space", None, None), P("tm", "space", None, None), P("space", None, None)),
        out_specs=(P("tm", "space", None, None), P("tm", "space", None, None)),
        check_vma=False,
    )
```

time: 107 us -> 85.1 us (0.80)
  the two profiles are of different devices: /device:TPU:19 before, /device:TPU:0 now
where the time goes in v3:
time: 85.1 us; the launch traced here: 84.9 us
  starting transfers between devices  31.9 us (37%)
  waiting for transfers between devices  27.8 us (33%)
  Pallas kernels  24.2 us (28%)
  between operations  0.88 us (1%)
    ppermute x22, starting transfers between devices, ring(): lax.ppermute(block, axis, [(i, (i + distance) % size) for i in range(size)])  31.9 us
    ppermute x22, waiting for transfers between devices, ring(): lax.ppermute(block, axis, [(i, (i + distance) % size) for i in range(size)])  27.8 us
    pallas_call x22, Pallas kernels, call(): pl.pallas_call(body, out_shape=[jax.ShapeDtypeStruct(s, F32) for s in out...  24.2 us
  transfers between devices with their start and end apart: 22, of which 7 were waited for; matrix products, arithmetic and copies ran while one was open for 0% of the time, Pallas kernels for 22%

profile of v3, /device:TPU:0, one launch (start us, length us, event | category | flops | bytes accessed | tf_op | source)
XLA Modules:
  0.0 84.9 jit_solution(17774276203001480218)
XLA Ops:
  0.7 2.0 %shard_map.50 = (f32[2,144,512]{2,1,0:T(8,128)S(1)}, f32[2,144,512]{2,1,0:T(8,128)S(1)}) custom-call(s32[5]{0:T(128)S(1)} %stack.39.place_ref, f32[4,128,512]{2,1,0:T(8,128)} %i_ref.3, f32[4,128,512]{2,1,0:T(8,128)} %bitcast.8, f32[4,128,512]{2,1,0:T(8,128)} %k_ref.3), custom_call_target="tpu_custom_call" | custom-call | tf_op jit(solution)/shard_map/pallas_call | solution.py:27
  3.9 3.1 %collective-permute-start.4 = (f32[4,72,512]{2,1,0:T(8,128)S(1)}, f32[4,72,512]{2,1,0:T(8,128)S(1)}, u32[]{:S(2)}, u32[]{:S(2)}) collective-permute-start(f32[4,72,512]{2,1,0:T(8,128)S(1)} %shard_map.58), channel_id=1, source_target_pairs={{0,8},{8,16},{16,24},{24,0},{1,9},{9,17},{17,25},{25,1},{2,10},{10... | collective-permute-start | bytes 1769480 | tf_op jit(solution)/shard_map/ppermute | solution.py:520
  6.9 2.6 %collective-permute-start.1 = (f32[2,144,512]{2,1,0:T(8,128)S(1)}, f32[2,144,512]{2,1,0:T(8,128)S(1)}, u32[]{:S(2)}, u32[]{:S(2)}) collective-permute-start(f32[2,144,512]{2,1,0:T(8,128)S(1)} %get-tuple-element.45.refs_0_), channel_id=1, source_target_pairs={{0,7},{1,0},{2,1},{3,2},{4,3},{5,4},{6,5},{7,6},{8,15},{9,8},{10,9... | collective-permute-start | bytes 1769480 | tf_op jit(solution)/shard_map/ppermute | solution.py:520
  9.6 1.7 %shard_map.51 = (f32[2,72,512]{2,1,0:T(8,128)S(1)}, f32[2,72,512]{2,1,0:T(8,128)S(1)}, f32[4,128,512]{2,1,0:T(8,128)S(1)}, f32[2,64,256]{2,1,0:T(8,128)S(1)}) custom-call(f32[4,128,512]{2,1,0:T(8,128)} %k_ref.3, f32[2,144,512]{2,1,0:T(8,128)S(1)} %get-tuple-element.46.after_ref.refs_1_), custom_call_target="tpu_custom_call" | custom-call | tf_op jit(solution)/shard_map/pallas_call | solution.py:27
  11.4 2.6 %collective-permute-start.8 = (f32[2,72,512]{2,1,0:T(8,128)S(1)}, f32[2,72,512]{2,1,0:T(8,128)S(1)}, u32[]{:S(2)}, u32[]{:S(2)}) collective-permute-start(f32[2,72,512]{2,1,0:T(8,128)S(1)} %get-tuple-element.64), channel_id=1, source_target_pairs={{0,7},{1,0},{2,1},{3,2},{4,3},{5,4},{6,5},{7,6},{8,15},{9,8},{10,9... | collective-permute-start | bytes 884744 | tf_op jit(solution)/shard_map/ppermute | solution.py:520
  14.0 8.3 %collective-permute-done.4.r_ref = f32[4,72,512]{2,1,0:T(8,128)S(1)} collective-permute-done((f32[4,72,512]{2,1,0:T(8,128)S(1)}, f32[4,72,512]{2,1,0:T(8,128)S(1)}, u32[]{:S(2)}, u32[]{:S(2)}) %collective-permute-start.4) | collective-permute-done | bytes 589856 | tf_op jit(solution)/shard_map/ppermute | solution.py:520
  22.3 1.7 %shard_map.59 = (f32[2,72,512]{2,1,0:T(8,128)S(1)}, f32[2,72,512]{2,1,0:T(8,128)S(1)}) custom-call(s32[5]{0:T(128)S(1)} %stack.39.place_ref, f32[4,128,512]{2,1,0:T(8,128)} %i_ref.3, f32[4,72,512]{2,1,0:T(8,128)S(1)} %collective-permute-done.4.r_ref), custom_call_target="tpu_custom_call" | custom-call | tf_op jit(solution)/shard_map/pallas_call | solution.py:27
  24.1 2.6 %collective-permute-start.6 = (f32[2,72,512]{2,1,0:T(8,128)S(1)}, f32[2,72,512]{2,1,0:T(8,128)S(1)}, u32[]{:S(2)}, u32[]{:S(2)}) collective-permute-start(f32[2,72,512]{2,1,0:T(8,128)S(1)} %get-tuple-element.61.refs_0_), channel_id=1, source_target_pairs={{0,7},{1,0},{2,1},{3,2},{4,3},{5,4},{6,5},{7,6},{8,15},{9,8},{10,9... | collective-permute-start | bytes 884744 | tf_op jit(solution)/shard_map/ppermute | solution.py:520
  30.9 2.6 %collective-permute-start.3 = (f32[2,72,512]{2,1,0:T(8,128)S(1)}, f32[2,72,512]{2,1,0:T(8,128)S(1)}, u32[]{:S(2)}, u32[]{:S(2)}) collective-permute-start(f32[2,72,512]{2,1,0:T(8,128)S(1)} %get-tuple-element.58.refs_0_), channel_id=1, source_target_pairs={{0,7},{1,0},{2,1},{3,2},{4,3},{5,4},{6,5},{7,6},{8,15},{9,8},{10,9... | collective-permute-start | bytes 884744 | tf_op jit(solution)/shard_map/ppermute | solution.py:520
  34.4 1.6 %collective-permute-done.6.refs_3_ = f32[2,72,512]{2,1,0:T(8,128)S(1)} collective-permute-done((f32[2,72,512]{2,1,0:T(8,128)S(1)}, f32[2,72,512]{2,1,0:T(8,128)S(1)}, u32[]{:S(2)}, u32[]{:S(2)}) %collective-permute-start.6) | collective-permute-done | bytes 294944 | tf_op jit(solution)/shard_map/ppermute | solution.py:520
  38.6 1.8 %collective-permute-start.10 = (f32[2,72,512]{2,1,0:T(8,128)S(1)}, f32[2,72,512]{2,1,0:T(8,128)S(1)}, u32[]{:S(2)}, u32[]{:S(2)}) collective-permute-start(f32[2,72,512]{2,1,0:T(8,128)S(1)} %get-tuple-element.70.refs_0_), channel_id=1, source_target_pairs={{0,7},{1,0},{2,1},{3,2},{4,3},{5,4},{6,5},{7,6},{8,15},{9,8},{10,9... | collective-permute-start | bytes 884744 | tf_op jit(solution)/shard_map/ppermute | solution.py:520
  40.9 2.1 %collective-permute-start.11 = (f32[2,64,256]{2,1,0:T(8,128)S(1)}, f32[2,64,256]{2,1,0:T(8,128)S(1)}, u32[]{:S(2)}, u32[]{:S(2)}) collective-permute-start(f32[2,64,256]{2,1,0:T(8,128)S(1)} %shard_map.65.own_ref), channel_id=1, source_target_pairs={{0,24},{8,0},{16,8},{24,16},{1,25},{9,1},{17,9},{25,17},{2,26},{10... | collective-permute-start | bytes 393224 | tf_op jit(solution)/shard_map/ppermute | solution.py:520
  43.9 1.9 %shard_map.57 = (f32[4,64,512]{2,1,0:T(8,128)S(1)}, f32[2,32,256]{2,1,0:T(8,128)S(1)}) custom-call(s32[5]{0:T(128)S(1)} %stack.39.place_ref, f32[2,72,512]{2,1,0:T(8,128)S(1)} %get-tuple-element.58.refs_0_, f32[2,72,512]{2,1,0:T(8,128)S(1)} %get-tuple-element.59.refs_1_, f32[2,72,512]{2,1,0:T(8,128)S(1)} %collective-permute-done.2.refs_2_, ...), custom_call_target="tpu_custom_call" | custom-call | tf_op jit(solution)/shard_map/pallas_call | solution.py:27
  45.8 2.1 %collective-permute-done.9.refs_2_ = f32[2,72,512]{2,1,0:T(8,128)S(1)} collective-permute-done((f32[2,72,512]{2,1,0:T(8,128)S(1)}, f32[2,72,512]{2,1,0:T(8,128)S(1)}, u32[]{:S(2)}, u32[]{:S(2)}) %collective-permute-start.9) | collective-permute-done | bytes 294944 | tf_op jit(solution)/shard_map/ppermute | solution.py:520
  48.0 1.9 %shard_map.64 = (f32[4,64,512]{2,1,0:T(8,128)S(1)}, f32[2,32,256]{2,1,0:T(8,128)S(1)}) custom-call(s32[5]{0:T(128)S(1)} %stack.39.place_ref, f32[2,72,512]{2,1,0:T(8,128)S(1)} %get-tuple-element.70.refs_0_, f32[2,72,512]{2,1,0:T(8,128)S(1)} %get-tuple-element.71.refs_1_, f32[2,72,512]{2,1,0:T(8,128)S(1)} %collective-permute-done.9.refs_2_, ...), custom_call_target="tpu_custom_call" | custom-call | tf_op jit(solution)/shard_map/pallas_call | solution.py:27
  49.9 2.1 %collective-permute-start.12 = (f32[2,64,256]{2,1,0:T(8,128)S(1)}, f32[2,64,256]{2,1,0:T(8,128)S(1)}, u32[]{:S(2)}, u32[]{:S(2)}) collective-permute-start(f32[2,64,256]{2,1,0:T(8,128)S(1)} %shard_map.66), channel_id=1, source_target_pairs={{0,24},{8,0},{16,8},{24,16},{1,25},{9,1},{17,9},{25,17},{2,26},{10... | collective-permute-start | bytes 393224 | tf_op jit(solution)/shard_map/ppermute | solution.py:520
  53.0 1.6 %collective-permute-start.16 = (f32[2,64,256]{2,1,0:T(8,128)S(1)}, f32[2,64,256]{2,1,0:T(8,128)S(1)}, u32[]{:S(2)}, u32[]{:S(2)}) collective-permute-start(f32[2,64,256]{2,1,0:T(8,128)S(1)} %shard_map.66), channel_id=1, source_target_pairs={{0,8},{8,16},{16,24},{24,0},{1,9},{9,17},{17,25},{25,1},{2,10},{10... | collective-permute-start | bytes 393224 | tf_op jit(solution)/shard_map/ppermute | solution.py:520
  56.1 2.6 %collective-permute-start.14 = (f32[2,64,256]{2,1,0:T(8,128)S(1)}, f32[2,64,256]{2,1,0:T(8,128)S(1)}, u32[]{:S(2)}, u32[]{:S(2)}) collective-permute-start(f32[2,64,256]{2,1,0:T(8,128)S(1)} %broadcast_select_fusion.d_own), channel_id=1, source_target_pairs={{0,7},{1,0},{2,1},{3,2},{4,3},{5,4},{6,5},{7,6},{8,15},{9,8},{10,9... | collective-permute-start | bytes 393224 | tf_op jit(solution)/shard_map/ppermute | solution.py:520
  58.8 6.7 %collective-permute-done.15.rest_1_.rest_0_ = f32[2,64,256]{2,1,0:T(8,128)S(1)} collective-permute-done((f32[2,64,256]{2,1,0:T(8,128)S(1)}, f32[2,64,256]{2,1,0:T(8,128)S(1)}, u32[]{:S(2)}, u32[]{:S(2)}) %collective-permute-start.15) | collective-permute-done | bytes 131104 | tf_op jit(solution)/shard_map/ppermute | solution.py:520
  67.8 2.6 %collective-permute-start.19 = (f32[2,64,256]{2,1,0:T(8,128)S(1)}, f32[2,64,256]{2,1,0:T(8,128)S(1)}, u32[]{:S(2)}, u32[]{:S(2)}) collective-permute-start(f32[2,64,256]{2,1,0:T(8,128)S(1)} %shard_map.68.d_own), channel_id=1, source_target_pairs={{0,7},{1,0},{2,1},{3,2},{4,3},{5,4},{6,5},{7,6},{8,15},{9,8},{10,9... | collective-permute-start | bytes 393224 | tf_op jit(solution)/shard_map/ppermute | solution.py:520
  70.5 3.6 %collective-permute-done.18.d_lo = f32[2,64,256]{2,1,0:T(8,128)S(1)} collective-permute-done((f32[2,64,256]{2,1,0:T(8,128)S(1)}, f32[2,64,256]{2,1,0:T(8,128)S(1)}, u32[]{:S(2)}, u32[]{:S(2)}) %collective-permute-start.18) | collective-permute-done | bytes 131104 | tf_op jit(solution)/shard_map/ppermute | solution.py:520
  75.0 2.6 %collective-permute-start.21 = (f32[2,64,256]{2,1,0:T(8,128)S(1)}, f32[2,64,256]{2,1,0:T(8,128)S(1)}, u32[]{:S(2)}, u32[]{:S(2)}) collective-permute-start(f32[2,64,256]{2,1,0:T(8,128)S(1)} %shard_map.69.d_own), channel_id=1, source_target_pairs={{0,7},{1,0},{2,1},{3,2},{4,3},{5,4},{6,5},{7,6},{8,15},{9,8},{10,9... | collective-permute-start | bytes 393224 | tf_op jit(solution)/shard_map/ppermute | solution.py:520
  77.7 4.0 %collective-permute-done.20.d_lo = f32[2,64,256]{2,1,0:T(8,128)S(1)} collective-permute-done((f32[2,64,256]{2,1,0:T(8,128)S(1)}, f32[2,64,256]{2,1,0:T(8,128)S(1)}, u32[]{:S(2)}, u32[]{:S(2)}) %collective-permute-start.20) | collective-permute-done | bytes 131104 | tf_op jit(solution)/shard_map/ppermute | solution.py:520
  82.6 2.3 %shard_map.71 = (f32[4,128,512]{2,1,0:T(8,128)}, f32[2,64,256]{2,1,0:T(8,128)}) custom-call(f32[4,64,512]{2,1,0:T(8,128)S(1)} %collective-permute-done.17.moved_ref, f32[4,64,512]{2,1,0:T(8,128)S(1)} %get-tuple-element.75.own_ref, f32[4,128,512]{2,1,0:T(8,128)S(1)} %bitcast.11, f32[2,64,256]{2,1,0:T(8,128)S(1)} %shard_map.70.e_ref), custom_call_target="tpu_custom_call" | custom-call | tf_op jit(solution)/shard_map/pallas_call | solution.py:27
  (47 shorter events, 17.2 us)
Async XLA Ops:
  3.9 18.4 %collective-permute-start.4 = (f32[4,72,512]{2,1,0:T(8,128)S(1)}, f32[4,72,512]{2,1,0:T(8,128)S(1)}, u32[]{:S(2)}, u32[]{:S(2)}) collective-permute-start(f32[4,72,512]{2,1,0:T(8,128)S(1)} %shard_map.58), channel_id=1, source_target_pairs={{0,8},{8,16},{16,24},{24,0},{1,9},{9,17},{17,25},{25,1},{2,10},{10... | collective-permute-start | bytes 1769480 | tf_op jit(solution)/shard_map/ppermute | solution.py:520
  6.9 17.1 %collective-permute-start = (f32[2,144,512]{2,1,0:T(8,128)S(1)}, f32[2,144,512]{2,1,0:T(8,128)S(1)}, u32[]{:S(2)}, u32[]{:S(2)}) collective-permute-start(f32[2,144,512]{2,1,0:T(8,128)S(1)} %get-tuple-element.46.after_ref.refs_1_), channel_id=1, source_target_pairs={{0,1},{1,2},{2,3},{3,4},{4,5},{5,6},{6,7},{7,0},{8,9},{9,10},{10,1... | collective-permute-start | bytes 1769480 | tf_op jit(solution)/shard_map/ppermute | solution.py:520
  6.9 21.5 %collective-permute-start.1 = (f32[2,144,512]{2,1,0:T(8,128)S(1)}, f32[2,144,512]{2,1,0:T(8,128)S(1)}, u32[]{:S(2)}, u32[]{:S(2)}) collective-permute-start(f32[2,144,512]{2,1,0:T(8,128)S(1)} %get-tuple-element.45.refs_0_), channel_id=1, source_target_pairs={{0,7},{1,0},{2,1},{3,2},{4,3},{5,4},{6,5},{7,6},{8,15},{9,8},{10,9... | collective-permute-start | bytes 1769480 | tf_op jit(solution)/shard_map/ppermute | solution.py:520
  11.3 19.6 %collective-permute-start.7 = (f32[2,72,512]{2,1,0:T(8,128)S(1)}, f32[2,72,512]{2,1,0:T(8,128)S(1)}, u32[]{:S(2)}, u32[]{:S(2)}) collective-permute-start(f32[2,72,512]{2,1,0:T(8,128)S(1)} %get-tuple-element.63), channel_id=1, source_target_pairs={{0,1},{1,2},{2,3},{3,4},{4,5},{5,6},{6,7},{7,0},{8,9},{9,10},{10,1... | collective-permute-start | bytes 884744 | tf_op jit(solution)/shard_map/ppermute | solution.py:520
  11.4 22.1 %collective-permute-start.8 = (f32[2,72,512]{2,1,0:T(8,128)S(1)}, f32[2,72,512]{2,1,0:T(8,128)S(1)}, u32[]{:S(2)}, u32[]{:S(2)}) collective-permute-start(f32[2,72,512]{2,1,0:T(8,128)S(1)} %get-tuple-element.64), channel_id=1, source_target_pairs={{0,7},{1,0},{2,1},{3,2},{4,3},{5,4},{6,5},{7,6},{8,15},{9,8},{10,9... | collective-permute-start | bytes 884744 | tf_op jit(solution)/shard_map/ppermute | solution.py:520
  24.0 10.4 %collective-permute-start.5 = (f32[2,72,512]{2,1,0:T(8,128)S(1)}, f32[2,72,512]{2,1,0:T(8,128)S(1)}, u32[]{:S(2)}, u32[]{:S(2)}) collective-permute-start(f32[2,72,512]{2,1,0:T(8,128)S(1)} %get-tuple-element.62.refs_1_), channel_id=1, source_target_pairs={{0,1},{1,2},{2,3},{3,4},{4,5},{5,6},{6,7},{7,0},{8,9},{9,10},{10,1... | collective-permute-start | bytes 884744 | tf_op jit(solution)/shard_map/ppermute | solution.py:520
  24.1 11.9 %collective-permute-start.6 = (f32[2,72,512]{2,1,0:T(8,128)S(1)}, f32[2,72,512]{2,1,0:T(8,128)S(1)}, u32[]{:S(2)}, u32[]{:S(2)}) collective-permute-start(f32[2,72,512]{2,1,0:T(8,128)S(1)} %get-tuple-element.61.refs_0_), channel_id=1, source_target_pairs={{0,7},{1,0},{2,1},{3,2},{4,3},{5,4},{6,5},{7,6},{8,15},{9,8},{10,9... | collective-permute-start | bytes 884744 | tf_op jit(solution)/shard_map/ppermute | solution.py:520
  30.8 13.1 %collective-permute-start.2 = (f32[2,72,512]{2,1,0:T(8,128)S(1)}, f32[2,72,512]{2,1,0:T(8,128)S(1)}, u32[]{:S(2)}, u32[]{:S(2)}) collective-permute-start(f32[2,72,512]{2,1,0:T(8,128)S(1)} %get-tuple-element.59.refs_1_), channel_id=1, source_target_pairs={{0,1},{1,2},{2,3},{3,4},{4,5},{5,6},{6,7},{7,0},{8,9},{9,10},{10,1... | collective-permute-start | bytes 884744 | tf_op jit(solution)/shard_map/ppermute | solution.py:520
  30.9 13.1 %collective-permute-start.3 = (f32[2,72,512]{2,1,0:T(8,128)S(1)}, f32[2,72,512]{2,1,0:T(8,128)S(1)}, u32[]{:S(2)}, u32[]{:S(2)}) collective-permute-start(f32[2,72,512]{2,1,0:T(8,128)S(1)} %get-tuple-element.58.refs_0_), channel_id=1, source_target_pairs={{0,7},{1,0},{2,1},{3,2},{4,3},{5,4},{6,5},{7,6},{8,15},{9,8},{10,9... | collective-permute-start | bytes 884744 | tf_op jit(solution)/shard_map/ppermute | solution.py:520
  36.0 4.4 %copy-start = (f32[1,4,128,512]{3,2,1,0:T(8,128)S(1)}, f32[1,4,128,512]{3,2,1,0:T(8,128)}, u32[]{:S(2)}) copy-start(f32[1,4,128,512]{3,2,1,0:T(8,128)} %param.4) | copy-start | bytes 3145732
  37.5 10.5 %collective-permute-start.9 = (f32[2,72,512]{2,1,0:T(8,128)S(1)}, f32[2,72,512]{2,1,0:T(8,128)S(1)}, u32[]{:S(2)}, u32[]{:S(2)}) collective-permute-start(f32[2,72,512]{2,1,0:T(8,128)S(1)} %get-tuple-element.71.refs_1_), channel_id=1, source_target_pairs={{0,1},{1,2},{2,3},{3,4},{4,5},{5,6},{6,7},{7,0},{8,9},{9,10},{10,1... | collective-permute-start | bytes 884744 | tf_op jit(solution)/shard_map/ppermute | solution.py:520
  38.6 9.4 %collective-permute-start.10 = (f32[2,72,512]{2,1,0:T(8,128)S(1)}, f32[2,72,512]{2,1,0:T(8,128)S(1)}, u32[]{:S(2)}, u32[]{:S(2)}) collective-permute-start(f32[2,72,512]{2,1,0:T(8,128)S(1)} %get-tuple-element.70.refs_0_), channel_id=1, source_target_pairs={{0,7},{1,0},{2,1},{3,2},{4,3},{5,4},{6,5},{7,6},{8,15},{9,8},{10,9... | collective-permute-start | bytes 884744 | tf_op jit(solution)/shard_map/ppermute | solution.py:520
  40.9 9.0 %collective-permute-start.11 = (f32[2,64,256]{2,1,0:T(8,128)S(1)}, f32[2,64,256]{2,1,0:T(8,128)S(1)}, u32[]{:S(2)}, u32[]{:S(2)}) collective-permute-start(f32[2,64,256]{2,1,0:T(8,128)S(1)} %shard_map.65.own_ref), channel_id=1, source_target_pairs={{0,24},{8,0},{16,8},{24,16},{1,25},{9,1},{17,9},{25,17},{2,26},{10... | collective-permute-start | bytes 393224 | tf_op jit(solution)/shard_map/ppermute | solution.py:520
  49.9 6.1 %collective-permute-start.12 = (f32[2,64,256]{2,1,0:T(8,128)S(1)}, f32[2,64,256]{2,1,0:T(8,128)S(1)}, u32[]{:S(2)}, u32[]{:S(2)}) collective-permute-start(f32[2,64,256]{2,1,0:T(8,128)S(1)} %shard_map.66), channel_id=1, source_target_pairs={{0,24},{8,0},{16,8},{24,16},{1,25},{9,1},{17,9},{25,17},{2,26},{10... | collective-permute-start | bytes 393224 | tf_op jit(solution)/shard_map/ppermute | solution.py:520
  52.0 13.4 %collective-permute-start.15 = (f32[2,64,256]{2,1,0:T(8,128)S(1)}, f32[2,64,256]{2,1,0:T(8,128)S(1)}, u32[]{:S(2)}, u32[]{:S(2)}) collective-permute-start(f32[2,64,256]{2,1,0:T(8,128)S(1)} %shard_map.66), channel_id=1, source_target_pairs={{0,16},{8,24},{16,0},{24,8},{1,17},{9,25},{17,1},{25,9},{2,18},{10... | collective-permute-start | bytes 393224 | tf_op jit(solution)/shard_map/ppermute | solution.py:520
  53.0 12.4 %collective-permute-start.16 = (f32[2,64,256]{2,1,0:T(8,128)S(1)}, f32[2,64,256]{2,1,0:T(8,128)S(1)}, u32[]{:S(2)}, u32[]{:S(2)}) collective-permute-start(f32[2,64,256]{2,1,0:T(8,128)S(1)} %shard_map.66), channel_id=1, source_target_pairs={{0,8},{8,16},{16,24},{24,0},{1,9},{9,17},{17,25},{25,1},{2,10},{10... | collective-permute-start | bytes 393224 | tf_op jit(solution)/shard_map/ppermute | solution.py:520
  56.1 9.4 %collective-permute-start.13 = (f32[2,64,256]{2,1,0:T(8,128)S(1)}, f32[2,64,256]{2,1,0:T(8,128)S(1)}, u32[]{:S(2)}, u32[]{:S(2)}) collective-permute-start(f32[2,64,256]{2,1,0:T(8,128)S(1)} %broadcast_select_fusion.d_own), channel_id=1, source_target_pairs={{0,1},{1,2},{2,3},{3,4},{4,5},{5,6},{6,7},{7,0},{8,9},{9,10},{10,1... | collective-permute-start | bytes 393224 | tf_op jit(solution)/shard_map/ppermute | solution.py:520
  56.1 9.3 %collective-permute-start.14 = (f32[2,64,256]{2,1,0:T(8,128)S(1)}, f32[2,64,256]{2,1,0:T(8,128)S(1)}, u32[]{:S(2)}, u32[]{:S(2)}) collective-permute-start(f32[2,64,256]{2,1,0:T(8,128)S(1)} %broadcast_select_fusion.d_own), channel_id=1, source_target_pairs={{0,7},{1,0},{2,1},{3,2},{4,3},{5,4},{6,5},{7,6},{8,15},{9,8},{10,9... | collective-permute-start | bytes 393224 | tf_op jit(solution)/shard_map/ppermute | solution.py:520
  65.4 17.1 %collective-permute-start.17 = (f32[4,64,512]{2,1,0:T(8,128)S(1)}, f32[4,64,512]{2,1,0:T(8,128)S(1)}, u32[]{:S(2)}, u32[]{:S(2)}) collective-permute-start(f32[4,64,512]{2,1,0:T(8,128)S(1)} %get-tuple-element.74), channel_id=1, source_target_pairs={{0,8},{8,16},{16,24},{24,0},{1,9},{9,17},{17,25},{25,1},{2,10},{10... | collective-permute-start | bytes 1572872 | tf_op jit(solution)/shard_map/ppermute | solution.py:520
  67.8 6.3 %collective-permute-start.18 = (f32[2,64,256]{2,1,0:T(8,128)S(1)}, f32[2,64,256]{2,1,0:T(8,128)S(1)}, u32[]{:S(2)}, u32[]{:S(2)}) collective-permute-start(f32[2,64,256]{2,1,0:T(8,128)S(1)} %shard_map.68.d_own), channel_id=1, source_target_pairs={{0,1},{1,2},{2,3},{3,4},{4,5},{5,6},{6,7},{7,0},{8,9},{9,10},{10,1... | collective-permute-start | bytes 393224 | tf_op jit(solution)/shard_map/ppermute | solution.py:520
  67.8 6.2 %collective-permute-start.19 = (f32[2,64,256]{2,1,0:T(8,128)S(1)}, f32[2,64,256]{2,1,0:T(8,128)S(1)}, u32[]{:S(2)}, u32[]{:S(2)}) collective-permute-start(f32[2,64,256]{2,1,0:T(8,128)S(1)} %shard_map.68.d_own), channel_id=1, source_target_pairs={{0,7},{1,0},{2,1},{3,2},{4,3},{5,4},{6,5},{7,6},{8,15},{9,8},{10,9... | collective-permute-start | bytes 393224 | tf_op jit(solution)/shard_map/ppermute | solution.py:520
  75.0 6.7 %collective-permute-start.20 = (f32[2,64,256]{2,1,0:T(8,128)S(1)}, f32[2,64,256]{2,1,0:T(8,128)S(1)}, u32[]{:S(2)}, u32[]{:S(2)}) collective-permute-start(f32[2,64,256]{2,1,0:T(8,128)S(1)} %shard_map.69.d_own), channel_id=1, source_target_pairs={{0,1},{1,2},{2,3},{3,4},{4,5},{5,6},{6,7},{7,0},{8,9},{9,10},{10,1... | collective-permute-start | bytes 393224 | tf_op jit(solution)/shard_map/ppermute | solution.py:520
  75.0 6.6 %collective-permute-start.21 = (f32[2,64,256]{2,1,0:T(8,128)S(1)}, f32[2,64,256]{2,1,0:T(8,128)S(1)}, u32[]{:S(2)}, u32[]{:S(2)}) collective-permute-start(f32[2,64,256]{2,1,0:T(8,128)S(1)} %shard_map.69.d_own), channel_id=1, source_target_pairs={{0,7},{1,0},{2,1},{3,2},{4,3},{5,4},{6,5},{7,6},{8,15},{9,8},{10,9... | collective-permute-start | bytes 393224 | tf_op jit(solution)/shard_map/ppermute | solution.py:520

commit v4 on v3

--- a/solution.py
+++ b/solution.py
@@ -18,7 +18,7 @@
 F32 = jnp.float32
 
 
-def call(body, out_shapes, operands, specs=None, scratch=()):
+def call(body, out_shapes, operands, specs=None, scratch=(), out_specs=None):
     operands = list(operands)
     specs = specs or [VMEM] * len(operands)
     operands = [
@@ -28,7 +28,7 @@
         body,
         out_shape=[jax.ShapeDtypeStruct(s, F32) for s in out_shapes],
         in_specs=specs,
-        out_specs=[VMEM] * len(out_shapes),
+        out_specs=out_specs or [VMEM] * len(out_shapes),
         scratch_shapes=list(scratch),
         compiler_params=pltpu.CompilerParams(vmem_limit_bytes=8 * 1024 * 1024),
     )(*operands)
@@ -196,23 +196,23 @@
     pl.when(flag == 0)(lambda: body(other))
 
 
-def first_messages(place, initial, prior, cond, end):
+def first_messages(place, initial, prior, cond, end, start):
     nx, ny, nz = cond.shape
     half = nx // 2
 
-    def body(place_ref, i_ref, p_ref, k_ref, down, up, sems):
+    def body(place_ref, i_ref, p_ref, k_ref, down, up, rows, sems):
         def copy(ref):
             copies = []
             for out, base in ((down, 0), (up, half)):
                 for source, at in ((k_ref, 0), (ref, end)):
                     copies += row_copies(source, out, base, (0, end), at, sems, len(copies))
-            run(copies)
+            run(copies + row_copies(p_ref, rows, 0, (start, ny), 0, sems, len(copies)))
 
         chosen(place_ref[3], copy, i_ref, p_ref)
 
     return call(
-        body, [(half, 2 * end, nz)] * 2, [place, initial, prior, cond], [SMEM, HBM, HBM, HBM],
-        [pltpu.SemaphoreType.DMA((4 * half,))])
+        body, [(half, 2 * end, nz)] * 2 + [(nx, ny - start, nz)], [place, initial, prior, cond], [SMEM, HBM, HBM, HBM],
+        [pltpu.SemaphoreType.DMA((4 * half + nx,))])
 
 
 def second_messages(cond, end, after):
@@ -235,15 +235,6 @@
     return call(
         body, [(half, rows + extra, nz)] * 2 + [(nx, ny, nz), (half, ny // 2, nz // 2)],
         [cond, after], [HBM, VMEM], [lane_scratch(ny, nz // 2), pltpu.SemaphoreType.DMA((nx,))])
-
-
-def rows_from(field, start, after):
-    nx, ny, nz = field.shape
-
-    def body(ref, after_ref, out, sems):
-        run(row_copies(ref, out, 0, (start, ny), 0, sems, 0))
-
-    return call(body, [(nx, ny - start, nz)], [field, after], [HBM, VMEM], [pltpu.SemaphoreType.DMA((nx,))])[0]
 
 
 def third_messages(place, initial, received, start):
@@ -309,13 +300,14 @@
     ]
 
 
-def half_step(low, high, spans, window, coefficients):
+def half_step(low, high, spans, window, coefficients, ahead=()):
     half, nz = low[0].shape[0], low[0].shape[2]
     nx, ny, count = 2 * half, coefficients[1].shape[1], len(spans)
     w0, w1 = window
 
     def body(*refs):
-        kx, up, down, right, diag, out = refs[2 * count:]
+        kx, up, down, right, diag = refs[2 * count:2 * count + 5]
+        out = refs[-1]
         v = fields(spans, refs[:count], half, ny) + fields(spans, refs[count:2 * count], half, ny)
         for p in range(nx):
             for a in range(w0, w1, TILE):
@@ -327,7 +319,7 @@
                     total = total + kx[p, s] * v[p + 1].tile(a)
                 out[p, a - w0:a - w0 + TILE] = total
 
-    return call(body, [(nx, w1 - w0, nz)], [*low, *high, *coefficients])[0]
+    return call(body, [(nx, w1 - w0, nz)], [*low, *high, *coefficients, *ahead])[0]
 
 
 def two_steps(place, low, high, spans, before, after, side_spans, started, window, result, coefficients, ghosts, final=False):
@@ -437,10 +429,11 @@
          pltpu.VMEM((2 * ny, 2 * nz), F32), lane_scratch(2 * ny, nz)])
 
 
-def sweep_step(place, own, before, after, coefficients, first, jumps=(), later=0):
+def sweep_step(place, own, on, off, coefficients, first, jumps=(), later=0):
     nx, ny, nz = own.shape
 
-    def body(place_ref, d_own, d_lo, d_hi, kx, up, down, right, diag, *rest):
+    def body(place_ref, d_own, d_on, d_off, kx, up, down, right, diag, *rest):
+        even = place_ref[5] > 0
         live = place_ref[3] > 0 if first else True
         has_lo = jnp.logical_and(place_ref[0] > 0, live)
         has_hi = jnp.logical_and(place_ref[1] > 0, live)
@@ -451,8 +444,8 @@
             total = total + up[i] * pltpu.roll(c, 1, 0) + down[i] * pltpu.roll(c, ny - 1, 0)
             return total + right[i] * pltpu.roll(c, nz - 1, 1) + pltpu.roll(right[i] * c, 1, 1)
 
-        lo = [jnp.where(has_lo, d_lo[nx - 2 + i], 0.0) for i in range(2)]
-        hi = [jnp.where(has_hi, d_hi[i], 0.0) for i in range(2)]
+        lo = [jnp.where(has_lo, jnp.where(even, d_off[nx - 2 + i], d_on[nx - 2 + i]), 0.0) for i in range(2)]
+        hi = [jnp.where(has_hi, jnp.where(even, d_on[i], d_off[i]), 0.0) for i in range(2)]
         block = [jnp.where(live, d_own[i], 0.0) if first else d_own[i] for i in range(nx)]
         v = lo + block + hi
         w = [step(v[i:i + 3], i) for i in range(nx + 2)]
@@ -464,7 +457,7 @@
                 e = e + jnp.where(place_ref[2] >= later, joined(rest[0][i], rest[1][i]), 0.0)
             rest[-1][i] = e
 
-    operands = [place, own, before, after, *coefficients]
+    operands = [place, own, on, off, *coefficients]
     operands += jumps
     return call(body, [own.shape], operands, [SMEM] + [VMEM] * (len(operands) - 1))[0]
 
@@ -490,29 +483,36 @@
     nx, ny, nz = prior.shape
     rows = moved.shape[1]
 
-    def body(moved_ref, own_ref, p_ref, e_ref, update, tail, scratch, wide):
+    def body(moved_ref, own_ref, p_ref, e_ref, update, tail, out, wide, scratch, sems):
+        parts = ((moved_ref, slice(0, rows)), (own_ref, slice(rows, ny)))
+        spread = repeat_matrix(nz // 2, nz)
+        copies = []
+        for q in range(nx // 2):
+            row = dot3(e_ref[q], spread)
+            for b in range(nz // LANES):
+                s = slice(b * LANES, (b + 1) * LANES)
+                wide[b, pl.ds(0, ny // 2, 2), :] = row[:, s]
+                wide[b, pl.ds(1, ny // 2, 2), :] = row[:, s]
+            for p in (2 * q, 2 * q + 1):
+                for ref, r in parts:
+                    for b in range(nz // LANES):
+                        s = slice(b * LANES, (b + 1) * LANES)
+                        out[p, r, s] = (ref[p, :, s] + wide[b, r]) - p_ref[p, r, s]
+                copies.append(pltpu.make_async_copy(out.at[p], update.at[p], sems.at[p]))
+                copies[-1].start()
         matrix = pair_matrix(nz, nz // 2, 0.125)
-        spread = repeat_matrix(nz // 2, nz)
-        for i, ref in enumerate((own_ref, moved_ref)):
-            r0 = rows * (1 - i)
-            r, c = slice(r0, r0 + rows), slice(r0 // 2, (r0 + rows) // 2)
-            for q in range(nx // 2):
-                e = e_ref[q, c]
-                tail[q, c] = e + restrict_planes(ref[2 * q], ref[2 * q + 1], scratch, matrix)
-                row = dot3(e, spread)
-                for b in range(nz // LANES):
-                    s = slice(b * LANES, (b + 1) * LANES)
-                    wide[b, pl.ds(0, rows // 2, 2), :] = row[:, s]
-                    wide[b, pl.ds(1, rows // 2, 2), :] = row[:, s]
-                    for p in (2 * q, 2 * q + 1):
-                        update[p, r, s] = (ref[p, :, s] + wide[b]) - p_ref[p, r, s]
+        for q in range(nx // 2):
+            for ref, r in parts:
+                c = slice(r.start // 2, r.stop // 2)
+                tail[q, c] = e_ref[q, c] + restrict_planes(ref[2 * q], ref[2 * q + 1], scratch, matrix)
+        for c in copies:
+            c.wait()
 
     return call(
-        body,
-        [(nx, ny, nz), (nx // 2, ny // 2, nz // 2)],
-        [moved, own, prior, correction],
-        scratch=[lane_scratch(rows, nz // 2), lane_scratch(rows, nz)],
-    )
+        body, [prior.shape, correction.shape], [moved, own, prior, correction],
+        scratch=[pltpu.VMEM(prior.shape, F32), lane_scratch(ny, nz), lane_scratch(rows, nz // 2),
+                 pltpu.SemaphoreType.DMA((nx,))],
+        out_specs=[HBM, VMEM])
 
 
 def ring(block, axis, distance):
@@ -522,6 +522,12 @@
 
 def from_sides(last, first):
     return ring(last, "space", 1), ring(first, "space", -1)
+
+
+def swapped(block, axis, offset):
+    size = lax.axis_size(axis)
+    pairs = [(i % size, (i + 1) % size) for i in range(offset, size + offset, 2)]
+    return lax.ppermute(block, axis, pairs + [(j, i) for i, j in pairs])
 
 
 def shards(initial, prior, conductivity):
@@ -529,15 +535,15 @@
     s, blocks = lax.axis_index("space"), lax.axis_size("space")
     own_prior = prior[0]
     home = times - 1
-    place = jnp.stack([s > 0, s < blocks - 1, t, t == home, t == 0]).astype(jnp.int32)
+    place = jnp.stack([s > 0, s < blocks - 1, t, t == home, t == 0, s % 2 == 0]).astype(jnp.int32)
     ny = initial.shape[1]
     cut, wide = ny // 2, ny // 2 + OVERLAP
     windows = [(0, wide), (cut - OVERLAP, ny)]
     results = [(0, cut), (cut, ny)]
 
-    down, up = first_messages(place, initial, own_prior, conductivity, wide)
+    down, up, lower_prior = first_messages(place, initial, own_prior, conductivity, wide, windows[1][0])
     before, after = ([x] for x in from_sides(up, down))
-    received = ring(rows_from(own_prior, windows[1][0], up), "tm", 1)
+    received = ring(lower_prior, "tm", 1)
     down_2, up_2, cond, coarse_cond = second_messages(conductivity, wide, up)
     before_2, after_2 = from_sides(up_2, down_2)
     down_3, up_3 = third_messages(place, initial, received, windows[1][0])
@@ -567,22 +573,23 @@
     ended = []
     for i in range(2):
         a, b = middle[i]
-        part = half_step([a], [b], spans[i], windows[i], coefficients)
+        part = half_step([a], [b], spans[i], windows[i], coefficients, coarse_coef[:i])
         ended.append(two_steps(
             place, [a], [b], spans[i], [sides[i][0]], [sides[i][1]], spans[i],
             part, windows[i], results[i], coefficients, ghosts[i], True))
     (moved, moved_coarse), (own_fine, fine_coarse) = ended
 
     jump = jumps_of(moved_coarse, fine_coarse, next_coarse, own_coarse)
-    shifted = [jump] + [ring(jump, "tm", -j) for j in range(1, times)]
+    lower = ring(jump[:, jump.shape[1] // 2:], "tm", -home)
+    shifted = [jump] + [ring(jump, "tm", -j) for j in range(1, home)] + [jnp.concatenate([lower, lower], axis=1)]
     state = joined(shifted[0], shifted[1])
     for j in range(home):
-        before, after = from_sides(state, state)
+        off, on = swapped(state, "space", 1), swapped(state, "space", 0)
         if j == 0:
-            before, after, moved, *shifted[2:] = lax.optimization_barrier((before, after, moved, *shifted[2:]))
+            *_, moved = lax.optimization_barrier((on, off, lower, *shifted[2:home], moved))
             moved = ring(moved, "tm", 1)
         more = (shifted[j + 1:j + 3], home - j - 1) if j < home - 1 else ()
-        state = sweep_step(place, state, before, after, coarse_coef, j == 0, *more)
+        state = sweep_step(place, state, on, off, coarse_coef, j == 0, *more)
     update, tail = finish(moved, own_fine, own_prior, state)
     return update[None], tail[None]
 

time: 85.1 us -> 80.9 us (0.951)
  starting transfers between devices: 31.9 us -> 29.1 us
  Pallas kernels: 24.2 us -> 22.8 us
    ppermute x22 -> x16, waiting for transfers between devices: 27.8 us -> 19.7 us  [ring(): lax.ppermute(block, axis, [(i, (i + distance) % size) for i in range(size)])]
    ppermute x22 -> x16, starting transfers between devices: 31.9 us -> 23.8 us  [ring(): lax.ppermute(block, axis, [(i, (i + distance) % size) for i in range(size)])]
    ppermute x0 -> x6, waiting for transfers between devices: none -> 7.94 us  [swapped(): return lax.ppermute(block, axis, pairs + [(j, i) for i, j in pairs])]
    ppermute x0 -> x6, starting transfers between devices: none -> 5.31 us  [swapped(): return lax.ppermute(block, axis, pairs + [(j, i) for i, j in pairs])]
    pallas_call x22 -> x21, Pallas kernels: 24.2 us -> 22.8 us  [call(): pl.pallas_call(body, out_shape=[jax.ShapeDtypeStruct(s, F32) for s in out...]
  transfers between devices with their start and end apart: 22 -> 22, of which waited for: 7 -> 8; matrix products, arithmetic and copies ran while one was open for 0% -> 0% of each run, Pallas kernels for 22% -> 23%
where the time goes in v4:
time: 80.9 us; the launch traced here: 80.6 us
  starting transfers between devices  29.1 us (36%)
  waiting for transfers between devices  27.6 us (34%)
  Pallas kernels  22.8 us (28%)
  between operations  0.87 us (1%)
    ppermute x16, starting transfers between devices, ring(): lax.ppermute(block, axis, [(i, (i + distance) % size) for i in range(size)])  23.8 us
    pallas_call x21, Pallas kernels, call(): pl.pallas_call(body, out_shape=[jax.ShapeDtypeStruct(s, F32) for s in out...  22.8 us
    ppermute x16, waiting for transfers between devices, ring(): lax.ppermute(block, axis, [(i, (i + distance) % size) for i in range(size)])  19.7 us
    ppermute x6, waiting for transfers between devices, swapped(): return lax.ppermute(block, axis, pairs + [(j, i) for i, j in pairs])  7.94 us
    ppermute x6, starting transfers between devices, swapped(): return lax.ppermute(block, axis, pairs + [(j, i) for i, j in pairs])  5.31 us
  transfers between devices with their start and end apart: 22, of which 8 were waited for; matrix products, arithmetic and copies ran while one was open for 0% of the time, Pallas kernels for 23%

profile of v4, /device:TPU:0, one launch (start us, length us, event | category | flops | bytes accessed | tf_op | source)
XLA Modules:
  0.0 80.6 jit_solution(6885432044038139367)
XLA Ops:
  0.7 2.2 %shard_map.50 = (f32[2,144,512]{2,1,0:T(8,128)S(1)}, f32[2,144,512]{2,1,0:T(8,128)S(1)}, f32[4,72,512]{2,1,0:T(8,128)S(1)}) custom-call(s32[6]{0:T(128)S(1)} %stack.47.place_ref, f32[4,128,512]{2,1,0:T(8,128)} %i_ref.3, f32[4,128,512]{2,1,0:T(8,128)} %bitcast.9, f32[4,128,512]{2,1,0:T(8,128)} %k_ref.3), custom_call_target="tpu_custom_call" | custom-call | tf_op jit(solution)/shard_map/pallas_call | solution.py:27
  2.9 3.1 %collective-permute-start.4 = (f32[4,72,512]{2,1,0:T(8,128)S(1)}, f32[4,72,512]{2,1,0:T(8,128)S(1)}, u32[]{:S(2)}, u32[]{:S(2)}) collective-permute-start(f32[4,72,512]{2,1,0:T(8,128)S(1)} %get-tuple-element.58), channel_id=1, source_target_pairs={{0,8},{8,16},{16,24},{24,0},{1,9},{9,17},{17,25},{25,1},{2,10},{10... | collective-permute-start | bytes 1769480 | tf_op jit(solution)/shard_map/ppermute | solution.py:520
  6.0 2.6 %collective-permute-start.1 = (f32[2,144,512]{2,1,0:T(8,128)S(1)}, f32[2,144,512]{2,1,0:T(8,128)S(1)}, u32[]{:S(2)}, u32[]{:S(2)}) collective-permute-start(f32[2,144,512]{2,1,0:T(8,128)S(1)} %get-tuple-element.42.refs_0_), channel_id=1, source_target_pairs={{0,7},{1,0},{2,1},{3,2},{4,3},{5,4},{6,5},{7,6},{8,15},{9,8},{10,9... | collective-permute-start | bytes 1769480 | tf_op jit(solution)/shard_map/ppermute | solution.py:520
  8.7 1.7 %shard_map.51 = (f32[2,72,512]{2,1,0:T(8,128)S(1)}, f32[2,72,512]{2,1,0:T(8,128)S(1)}, f32[4,128,512]{2,1,0:T(8,128)S(1)}, f32[2,64,256]{2,1,0:T(8,128)S(1)}) custom-call(f32[4,128,512]{2,1,0:T(8,128)} %k_ref.3, f32[2,144,512]{2,1,0:T(8,128)S(1)} %get-tuple-element.43.after_ref.refs_1_), custom_call_target="tpu_custom_call" | custom-call | tf_op jit(solution)/shard_map/pallas_call | solution.py:27
  10.4 2.6 %collective-permute-start.8 = (f32[2,72,512]{2,1,0:T(8,128)S(1)}, f32[2,72,512]{2,1,0:T(8,128)S(1)}, u32[]{:S(2)}, u32[]{:S(2)}) collective-permute-start(f32[2,72,512]{2,1,0:T(8,128)S(1)} %get-tuple-element.62), channel_id=1, source_target_pairs={{0,7},{1,0},{2,1},{3,2},{4,3},{5,4},{6,5},{7,6},{8,15},{9,8},{10,9... | collective-permute-start | bytes 884744 | tf_op jit(solution)/shard_map/ppermute | solution.py:520
  13.1 8.3 %collective-permute-done.4.r_ref = f32[4,72,512]{2,1,0:T(8,128)S(1)} collective-permute-done((f32[4,72,512]{2,1,0:T(8,128)S(1)}, f32[4,72,512]{2,1,0:T(8,128)S(1)}, u32[]{:S(2)}, u32[]{:S(2)}) %collective-permute-start.4) | collective-permute-done | bytes 589856 | tf_op jit(solution)/shard_map/ppermute | solution.py:520
  21.3 1.7 %shard_map.58 = (f32[2,72,512]{2,1,0:T(8,128)S(1)}, f32[2,72,512]{2,1,0:T(8,128)S(1)}) custom-call(s32[6]{0:T(128)S(1)} %stack.47.place_ref, f32[4,128,512]{2,1,0:T(8,128)} %i_ref.3, f32[4,72,512]{2,1,0:T(8,128)S(1)} %collective-permute-done.4.r_ref), custom_call_target="tpu_custom_call" | custom-call | tf_op jit(solution)/shard_map/pallas_call | solution.py:27
  23.1 2.6 %collective-permute-start.6 = (f32[2,72,512]{2,1,0:T(8,128)S(1)}, f32[2,72,512]{2,1,0:T(8,128)S(1)}, u32[]{:S(2)}, u32[]{:S(2)}) collective-permute-start(f32[2,72,512]{2,1,0:T(8,128)S(1)} %get-tuple-element.59.refs_0_), channel_id=1, source_target_pairs={{0,7},{1,0},{2,1},{3,2},{4,3},{5,4},{6,5},{7,6},{8,15},{9,8},{10,9... | collective-permute-start | bytes 884744 | tf_op jit(solution)/shard_map/ppermute | solution.py:520
  28.3 1.4 %shard_map.55 = (f32[2,72,512]{2,1,0:T(8,128)S(1)}, f32[2,72,512]{2,1,0:T(8,128)S(1)}) custom-call(s32[6]{0:T(128)S(1)} %stack.47.place_ref, f32[2,144,512]{2,1,0:T(8,128)S(1)} %get-tuple-element.42.refs_0_, f32[2,144,512]{2,1,0:T(8,128)S(1)} %get-tuple-element.43.after_ref.refs_1_, f32[2,144,512]{2,1,0:T(8,128)S(1)} %collective-permute-done.refs_0_.refs_2_, ...), custom_call_target="tpu_custom_call" | custom-call | tf_op jit(solution)/shard_map/pallas_call | solution.py:27
  29.8 2.6 %collective-permute-start.3 = (f32[2,72,512]{2,1,0:T(8,128)S(1)}, f32[2,72,512]{2,1,0:T(8,128)S(1)}, u32[]{:S(2)}, u32[]{:S(2)}) collective-permute-start(f32[2,72,512]{2,1,0:T(8,128)S(1)} %get-tuple-element.55.refs_0_), channel_id=1, source_target_pairs={{0,7},{1,0},{2,1},{3,2},{4,3},{5,4},{6,5},{7,6},{8,15},{9,8},{10,9... | collective-permute-start | bytes 884744 | tf_op jit(solution)/shard_map/ppermute | solution.py:520
  33.4 1.7 %collective-permute-done.6.refs_3_ = f32[2,72,512]{2,1,0:T(8,128)S(1)} collective-permute-done((f32[2,72,512]{2,1,0:T(8,128)S(1)}, f32[2,72,512]{2,1,0:T(8,128)S(1)}, u32[]{:S(2)}, u32[]{:S(2)}) %collective-permute-start.6) | collective-permute-done | bytes 294944 | tf_op jit(solution)/shard_map/ppermute | solution.py:520
  37.6 1.8 %collective-permute-start.10 = (f32[2,72,512]{2,1,0:T(8,128)S(1)}, f32[2,72,512]{2,1,0:T(8,128)S(1)}, u32[]{:S(2)}, u32[]{:S(2)}) collective-permute-start(f32[2,72,512]{2,1,0:T(8,128)S(1)} %get-tuple-element.68.refs_0_), channel_id=1, source_target_pairs={{0,7},{1,0},{2,1},{3,2},{4,3},{5,4},{6,5},{7,6},{8,15},{9,8},{10,9... | collective-permute-start | bytes 884744 | tf_op jit(solution)/shard_map/ppermute | solution.py:520
  39.9 2.1 %collective-permute-start.11 = (f32[2,64,256]{2,1,0:T(8,128)S(1)}, f32[2,64,256]{2,1,0:T(8,128)S(1)}, u32[]{:S(2)}, u32[]{:S(2)}) collective-permute-start(f32[2,64,256]{2,1,0:T(8,128)S(1)} %shard_map.65.own_ref), channel_id=1, source_target_pairs={{0,24},{8,0},{16,8},{24,16},{1,25},{9,1},{17,9},{25,17},{2,26},{10... | collective-permute-start | bytes 393224 | tf_op jit(solution)/shard_map/ppermute | solution.py:520
  44.0 1.9 %shard_map.57 = (f32[4,64,512]{2,1,0:T(8,128)S(1)}, f32[2,32,256]{2,1,0:T(8,128)S(1)}) custom-call(s32[6]{0:T(128)S(1)} %stack.47.place_ref, f32[2,72,512]{2,1,0:T(8,128)S(1)} %get-tuple-element.55.refs_0_, f32[2,72,512]{2,1,0:T(8,128)S(1)} %get-tuple-element.56.refs_1_, f32[2,72,512]{2,1,0:T(8,128)S(1)} %collective-permute-done.2.refs_2_, ...), custom_call_target="tpu_custom_call" | custom-call | tf_op jit(solution)/shard_map/pallas_call | solution.py:27
  47.0 1.8 %shard_map.64 = (f32[4,64,512]{2,1,0:T(8,128)S(1)}, f32[2,32,256]{2,1,0:T(8,128)S(1)}) custom-call(s32[6]{0:T(128)S(1)} %stack.47.place_ref, f32[2,72,512]{2,1,0:T(8,128)S(1)} %get-tuple-element.68.refs_0_, f32[2,72,512]{2,1,0:T(8,128)S(1)} %get-tuple-element.69.refs_1_, f32[2,72,512]{2,1,0:T(8,128)S(1)} %collective-permute-done.9.refs_2_, ...), custom_call_target="tpu_custom_call" | custom-call | tf_op jit(solution)/shard_map/pallas_call | solution.py:27
  48.9 2.1 %collective-permute-start.12 = (f32[2,64,256]{2,1,0:T(8,128)S(1)}, f32[2,64,256]{2,1,0:T(8,128)S(1)}, u32[]{:S(2)}, u32[]{:S(2)}) collective-permute-start(f32[2,64,256]{2,1,0:T(8,128)S(1)} %shard_map.66), channel_id=1, source_target_pairs={{0,24},{8,0},{16,8},{24,16},{1,25},{9,1},{17,9},{25,17},{2,26},{10... | collective-permute-start | bytes 393224 | tf_op jit(solution)/shard_map/ppermute | solution.py:520
  52.0 3.1 %collective-permute-done.12.rest_0_ = f32[2,64,256]{2,1,0:T(8,128)S(1)} collective-permute-done((f32[2,64,256]{2,1,0:T(8,128)S(1)}, f32[2,64,256]{2,1,0:T(8,128)S(1)}, u32[]{:S(2)}, u32[]{:S(2)}) %collective-permute-start.12) | collective-permute-done | bytes 131104 | tf_op jit(solution)/shard_map/ppermute | solution.py:520
  56.2 1.6 %collective-permute-start.15 = (f32[2,32,256]{2,1,0:T(8,128)S(1)}, f32[2,32,256]{2,1,0:T(8,128)S(1)}, u32[]{:S(2)}, u32[]{:S(2)}) collective-permute-start(f32[2,32,256]{2,1,0:T(8,128)S(1)} %slice.4), channel_id=1, source_target_pairs={{0,8},{8,16},{16,24},{24,0},{1,9},{9,17},{17,25},{25,1},{2,10},{10... | collective-permute-start | bytes 196616 | tf_op jit(solution)/shard_map/ppermute | solution.py:520
  57.8 5.2 %collective-permute-done.15 = f32[2,32,256]{2,1,0:T(8,128)S(1)} collective-permute-done((f32[2,32,256]{2,1,0:T(8,128)S(1)}, f32[2,32,256]{2,1,0:T(8,128)S(1)}, u32[]{:S(2)}, u32[]{:S(2)}) %collective-permute-start.15) | collective-permute-done | bytes 65568 | tf_op jit(solution)/shard_map/ppermute | solution.py:520
  64.4 2.2 %collective-permute-start.19 = (f32[2,64,256]{2,1,0:T(8,128)S(1)}, f32[2,64,256]{2,1,0:T(8,128)S(1)}, u32[]{:S(2)}, u32[]{:S(2)}) collective-permute-start(f32[2,64,256]{2,1,0:T(8,128)S(1)} %shard_map.67.d_own), channel_id=1, source_target_pairs={{1,2},{3,4},{5,6},{7,0},{2,1},{4,3},{6,5},{0,7},{9,10},{11,12},{13... | collective-permute-start | bytes 393224 | tf_op jit(solution)/shard_map/ppermute | solution.py:530
  66.6 3.8 %collective-permute-done.19.d_off = f32[2,64,256]{2,1,0:T(8,128)S(1)} collective-permute-done((f32[2,64,256]{2,1,0:T(8,128)S(1)}, f32[2,64,256]{2,1,0:T(8,128)S(1)}, u32[]{:S(2)}, u32[]{:S(2)}) %collective-permute-start.19) | collective-permute-done | bytes 131104 | tf_op jit(solution)/shard_map/ppermute | solution.py:530
  71.6 1.6 %collective-permute-start.21 = (f32[2,64,256]{2,1,0:T(8,128)S(1)}, f32[2,64,256]{2,1,0:T(8,128)S(1)}, u32[]{:S(2)}, u32[]{:S(2)}) collective-permute-start(f32[2,64,256]{2,1,0:T(8,128)S(1)} %shard_map.68.d_own), channel_id=1, source_target_pairs={{1,2},{3,4},{5,6},{7,0},{2,1},{4,3},{6,5},{0,7},{9,10},{11,12},{13... | collective-permute-start | bytes 393224 | tf_op jit(solution)/shard_map/ppermute | solution.py:530
  73.2 4.1 %collective-permute-done.21.d_off = f32[2,64,256]{2,1,0:T(8,128)S(1)} collective-permute-done((f32[2,64,256]{2,1,0:T(8,128)S(1)}, f32[2,64,256]{2,1,0:T(8,128)S(1)}, u32[]{:S(2)}, u32[]{:S(2)}) %collective-permute-start.21) | collective-permute-done | bytes 131104 | tf_op jit(solution)/shard_map/ppermute | solution.py:530
  78.5 2.1 %shard_map.70 = (f32[4,128,512]{2,1,0:T(8,128)}, f32[2,64,256]{2,1,0:T(8,128)}) custom-call(f32[4,64,512]{2,1,0:T(8,128)S(1)} %collective-permute-done.17.moved_ref, f32[4,64,512]{2,1,0:T(8,128)S(1)} %get-tuple-element.75.own_ref, f32[4,128,512]{2,1,0:T(8,128)S(1)} %bitcast.11, f32[2,64,256]{2,1,0:T(8,128)S(1)} %shard_map.69.e_ref), custom_call_target="tpu_custom_call" | custom-call | tf_op jit(solution)/shard_map/pallas_call | solution.py:27
  (48 shorter events, 15.6 us)
Async XLA Ops:
  2.9 18.4 %collective-permute-start.4 = (f32[4,72,512]{2,1,0:T(8,128)S(1)}, f32[4,72,512]{2,1,0:T(8,128)S(1)}, u32[]{:S(2)}, u32[]{:S(2)}) collective-permute-start(f32[4,72,512]{2,1,0:T(8,128)S(1)} %get-tuple-element.58), channel_id=1, source_target_pairs={{0,8},{8,16},{16,24},{24,0},{1,9},{9,17},{17,25},{25,1},{2,10},{10... | collective-permute-start | bytes 1769480 | tf_op jit(solution)/shard_map/ppermute | solution.py:520
  6.0 17.1 %collective-permute-start = (f32[2,144,512]{2,1,0:T(8,128)S(1)}, f32[2,144,512]{2,1,0:T(8,128)S(1)}, u32[]{:S(2)}, u32[]{:S(2)}) collective-permute-start(f32[2,144,512]{2,1,0:T(8,128)S(1)} %get-tuple-element.43.after_ref.refs_1_), channel_id=1, source_target_pairs={{0,1},{1,2},{2,3},{3,4},{4,5},{5,6},{6,7},{7,0},{8,9},{9,10},{10,1... | collective-permute-start | bytes 1769480 | tf_op jit(solution)/shard_map/ppermute | solution.py:520
  6.0 21.5 %collective-permute-start.1 = (f32[2,144,512]{2,1,0:T(8,128)S(1)}, f32[2,144,512]{2,1,0:T(8,128)S(1)}, u32[]{:S(2)}, u32[]{:S(2)}) collective-permute-start(f32[2,144,512]{2,1,0:T(8,128)S(1)} %get-tuple-element.42.refs_0_), channel_id=1, source_target_pairs={{0,7},{1,0},{2,1},{3,2},{4,3},{5,4},{6,5},{7,6},{8,15},{9,8},{10,9... | collective-permute-start | bytes 1769480 | tf_op jit(solution)/shard_map/ppermute | solution.py:520
  10.4 19.5 %collective-permute-start.7 = (f32[2,72,512]{2,1,0:T(8,128)S(1)}, f32[2,72,512]{2,1,0:T(8,128)S(1)}, u32[]{:S(2)}, u32[]{:S(2)}) collective-permute-start(f32[2,72,512]{2,1,0:T(8,128)S(1)} %get-tuple-element.61), channel_id=1, source_target_pairs={{0,1},{1,2},{2,3},{3,4},{4,5},{5,6},{6,7},{7,0},{8,9},{9,10},{10,1... | collective-permute-start | bytes 884744 | tf_op jit(solution)/shard_map/ppermute | solution.py:520
  10.4 22.0 %collective-permute-start.8 = (f32[2,72,512]{2,1,0:T(8,128)S(1)}, f32[2,72,512]{2,1,0:T(8,128)S(1)}, u32[]{:S(2)}, u32[]{:S(2)}) collective-permute-start(f32[2,72,512]{2,1,0:T(8,128)S(1)} %get-tuple-element.62), channel_id=1, source_target_pairs={{0,7},{1,0},{2,1},{3,2},{4,3},{5,4},{6,5},{7,6},{8,15},{9,8},{10,9... | collective-permute-start | bytes 884744 | tf_op jit(solution)/shard_map/ppermute | solution.py:520
  23.0 10.3 %collective-permute-start.5 = (f32[2,72,512]{2,1,0:T(8,128)S(1)}, f32[2,72,512]{2,1,0:T(8,128)S(1)}, u32[]{:S(2)}, u32[]{:S(2)}) collective-permute-start(f32[2,72,512]{2,1,0:T(8,128)S(1)} %get-tuple-element.60.refs_1_), channel_id=1, source_target_pairs={{0,1},{1,2},{2,3},{3,4},{4,5},{5,6},{6,7},{7,0},{8,9},{9,10},{10,1... | collective-permute-start | bytes 884744 | tf_op jit(solution)/shard_map/ppermute | solution.py:520
  23.1 12.0 %collective-permute-start.6 = (f32[2,72,512]{2,1,0:T(8,128)S(1)}, f32[2,72,512]{2,1,0:T(8,128)S(1)}, u32[]{:S(2)}, u32[]{:S(2)}) collective-permute-start(f32[2,72,512]{2,1,0:T(8,128)S(1)} %get-tuple-element.59.refs_0_), channel_id=1, source_target_pairs={{0,7},{1,0},{2,1},{3,2},{4,3},{5,4},{6,5},{7,6},{8,15},{9,8},{10,9... | collective-permute-start | bytes 884744 | tf_op jit(solution)/shard_map/ppermute | solution.py:520
  29.8 14.3 %collective-permute-start.2 = (f32[2,72,512]{2,1,0:T(8,128)S(1)}, f32[2,72,512]{2,1,0:T(8,128)S(1)}, u32[]{:S(2)}, u32[]{:S(2)}) collective-permute-start(f32[2,72,512]{2,1,0:T(8,128)S(1)} %get-tuple-element.56.refs_1_), channel_id=1, source_target_pairs={{0,1},{1,2},{2,3},{3,4},{4,5},{5,6},{6,7},{7,0},{8,9},{9,10},{10,1... | collective-permute-start | bytes 884744 | tf_op jit(solution)/shard_map/ppermute | solution.py:520
  29.8 14.2 %collective-permute-start.3 = (f32[2,72,512]{2,1,0:T(8,128)S(1)}, f32[2,72,512]{2,1,0:T(8,128)S(1)}, u32[]{:S(2)}, u32[]{:S(2)}) collective-permute-start(f32[2,72,512]{2,1,0:T(8,128)S(1)} %get-tuple-element.55.refs_0_), channel_id=1, source_target_pairs={{0,7},{1,0},{2,1},{3,2},{4,3},{5,4},{6,5},{7,6},{8,15},{9,8},{10,9... | collective-permute-start | bytes 884744 | tf_op jit(solution)/shard_map/ppermute | solution.py:520
  35.1 4.3 %copy-start = (f32[1,4,128,512]{3,2,1,0:T(8,128)S(1)}, f32[1,4,128,512]{3,2,1,0:T(8,128)}, u32[]{:S(2)}) copy-start(f32[1,4,128,512]{3,2,1,0:T(8,128)} %param.4) | copy-start | bytes 3145732
  36.5 10.5 %collective-permute-start.9 = (f32[2,72,512]{2,1,0:T(8,128)S(1)}, f32[2,72,512]{2,1,0:T(8,128)S(1)}, u32[]{:S(2)}, u32[]{:S(2)}) collective-permute-start(f32[2,72,512]{2,1,0:T(8,128)S(1)} %get-tuple-element.69.refs_1_), channel_id=1, source_target_pairs={{0,1},{1,2},{2,3},{3,4},{4,5},{5,6},{6,7},{7,0},{8,9},{9,10},{10,1... | collective-permute-start | bytes 884744 | tf_op jit(solution)/shard_map/ppermute | solution.py:520
  37.6 9.4 %collective-permute-start.10 = (f32[2,72,512]{2,1,0:T(8,128)S(1)}, f32[2,72,512]{2,1,0:T(8,128)S(1)}, u32[]{:S(2)}, u32[]{:S(2)}) collective-permute-start(f32[2,72,512]{2,1,0:T(8,128)S(1)} %get-tuple-element.68.refs_0_), channel_id=1, source_target_pairs={{0,7},{1,0},{2,1},{3,2},{4,3},{5,4},{6,5},{7,6},{8,15},{9,8},{10,9... | collective-permute-start | bytes 884744 | tf_op jit(solution)/shard_map/ppermute | solution.py:520
  39.9 8.9 %collective-permute-start.11 = (f32[2,64,256]{2,1,0:T(8,128)S(1)}, f32[2,64,256]{2,1,0:T(8,128)S(1)}, u32[]{:S(2)}, u32[]{:S(2)}) collective-permute-start(f32[2,64,256]{2,1,0:T(8,128)S(1)} %shard_map.65.own_ref), channel_id=1, source_target_pairs={{0,24},{8,0},{16,8},{24,16},{1,25},{9,1},{17,9},{25,17},{2,26},{10... | collective-permute-start | bytes 393224 | tf_op jit(solution)/shard_map/ppermute | solution.py:520
  48.9 6.2 %collective-permute-start.12 = (f32[2,64,256]{2,1,0:T(8,128)S(1)}, f32[2,64,256]{2,1,0:T(8,128)S(1)}, u32[]{:S(2)}, u32[]{:S(2)}) collective-permute-start(f32[2,64,256]{2,1,0:T(8,128)S(1)} %shard_map.66), channel_id=1, source_target_pairs={{0,24},{8,0},{16,8},{24,16},{1,25},{9,1},{17,9},{25,17},{2,26},{10... | collective-permute-start | bytes 393224 | tf_op jit(solution)/shard_map/ppermute | solution.py:520
  51.0 12.1 %collective-permute-start.16 = (f32[2,64,256]{2,1,0:T(8,128)S(1)}, f32[2,64,256]{2,1,0:T(8,128)S(1)}, u32[]{:S(2)}, u32[]{:S(2)}) collective-permute-start(f32[2,64,256]{2,1,0:T(8,128)S(1)} %shard_map.66), channel_id=1, source_target_pairs={{0,16},{8,24},{16,0},{24,8},{1,17},{9,25},{17,1},{25,9},{2,18},{10... | collective-permute-start | bytes 393224 | tf_op jit(solution)/shard_map/ppermute | solution.py:520
  55.1 8.0 %collective-permute-start.13 = (f32[2,64,256]{2,1,0:T(8,128)S(1)}, f32[2,64,256]{2,1,0:T(8,128)S(1)}, u32[]{:S(2)}, u32[]{:S(2)}) collective-permute-start(f32[2,64,256]{2,1,0:T(8,128)S(1)} %broadcast_select_fusion.d_own), channel_id=1, source_target_pairs={{0,1},{2,3},{4,5},{6,7},{1,0},{3,2},{5,4},{7,6},{8,9},{10,11},{12,... | collective-permute-start | bytes 393224 | tf_op jit(solution)/shard_map/ppermute | solution.py:530
  55.2 7.9 %collective-permute-start.14 = (f32[2,64,256]{2,1,0:T(8,128)S(1)}, f32[2,64,256]{2,1,0:T(8,128)S(1)}, u32[]{:S(2)}, u32[]{:S(2)}) collective-permute-start(f32[2,64,256]{2,1,0:T(8,128)S(1)} %broadcast_select_fusion.d_own), channel_id=1, source_target_pairs={{1,2},{3,4},{5,6},{7,0},{2,1},{4,3},{6,5},{0,7},{9,10},{11,12},{13... | collective-permute-start | bytes 393224 | tf_op jit(solution)/shard_map/ppermute | solution.py:530
  56.2 6.8 %collective-permute-start.15 = (f32[2,32,256]{2,1,0:T(8,128)S(1)}, f32[2,32,256]{2,1,0:T(8,128)S(1)}, u32[]{:S(2)}, u32[]{:S(2)}) collective-permute-start(f32[2,32,256]{2,1,0:T(8,128)S(1)} %slice.4), channel_id=1, source_target_pairs={{0,8},{8,16},{16,24},{24,0},{1,9},{9,17},{17,25},{25,1},{2,10},{10... | collective-permute-start | bytes 196616 | tf_op jit(solution)/shard_map/ppermute | solution.py:520
  63.1 15.4 %collective-permute-start.17 = (f32[4,64,512]{2,1,0:T(8,128)S(1)}, f32[4,64,512]{2,1,0:T(8,128)S(1)}, u32[]{:S(2)}, u32[]{:S(2)}) collective-permute-start(f32[4,64,512]{2,1,0:T(8,128)S(1)} %get-tuple-element.74), channel_id=1, source_target_pairs={{0,8},{8,16},{16,24},{24,0},{1,9},{9,17},{17,25},{25,1},{2,10},{10... | collective-permute-start | bytes 1572872 | tf_op jit(solution)/shard_map/ppermute | solution.py:520
  64.3 2.3 %collective-permute-start.18 = (f32[2,64,256]{2,1,0:T(8,128)S(1)}, f32[2,64,256]{2,1,0:T(8,128)S(1)}, u32[]{:S(2)}, u32[]{:S(2)}) collective-permute-start(f32[2,64,256]{2,1,0:T(8,128)S(1)} %shard_map.67.d_own), channel_id=1, source_target_pairs={{0,1},{2,3},{4,5},{6,7},{1,0},{3,2},{5,4},{7,6},{8,9},{10,11},{12,... | collective-permute-start | bytes 393224 | tf_op jit(solution)/shard_map/ppermute | solution.py:530
  64.4 6.0 %collective-permute-start.19 = (f32[2,64,256]{2,1,0:T(8,128)S(1)}, f32[2,64,256]{2,1,0:T(8,128)S(1)}, u32[]{:S(2)}, u32[]{:S(2)}) collective-permute-start(f32[2,64,256]{2,1,0:T(8,128)S(1)} %shard_map.67.d_own), channel_id=1, source_target_pairs={{1,2},{3,4},{5,6},{7,0},{2,1},{4,3},{6,5},{0,7},{9,10},{11,12},{13... | collective-permute-start | bytes 393224 | tf_op jit(solution)/shard_map/ppermute | solution.py:530
  71.3 1.9 %collective-permute-start.20 = (f32[2,64,256]{2,1,0:T(8,128)S(1)}, f32[2,64,256]{2,1,0:T(8,128)S(1)}, u32[]{:S(2)}, u32[]{:S(2)}) collective-permute-start(f32[2,64,256]{2,1,0:T(8,128)S(1)} %shard_map.68.d_own), channel_id=1, source_target_pairs={{0,1},{2,3},{4,5},{6,7},{1,0},{3,2},{5,4},{7,6},{8,9},{10,11},{12,... | collective-permute-start | bytes 393224 | tf_op jit(solution)/shard_map/ppermute | solution.py:530
  71.6 5.8 %collective-permute-start.21 = (f32[2,64,256]{2,1,0:T(8,128)S(1)}, f32[2,64,256]{2,1,0:T(8,128)S(1)}, u32[]{:S(2)}, u32[]{:S(2)}) collective-permute-start(f32[2,64,256]{2,1,0:T(8,128)S(1)} %shard_map.68.d_own), channel_id=1, source_target_pairs={{1,2},{3,4},{5,6},{7,0},{2,1},{4,3},{6,5},{0,7},{9,10},{11,12},{13... | collective-permute-start | bytes 393224 | tf_op jit(solution)/shard_map/ppermute | solution.py:530

commit v5 on v4

--- a/solution.py
+++ b/solution.py
@@ -1,3 +1,5 @@
+from typing import Any, NamedTuple
+
 import jax
 import jax.numpy as jnp
 from jax import lax
@@ -13,9 +15,23 @@
 LANES = 128
 
 VMEM = pl.BlockSpec(memory_space=pltpu.VMEM)
-SMEM = pl.BlockSpec(memory_space=pltpu.SMEM)
 HBM = pl.BlockSpec(memory_space=pltpu.HBM)
 F32 = jnp.float32
+
+
+class Here(NamedTuple):
+    t: Any
+    first: Any
+    last: Any
+    has_lo: Any
+    has_hi: Any
+    even: Any
+
+
+def here():
+    t, s = lax.axis_index("tm"), lax.axis_index("space")
+    times, blocks = lax.axis_size("tm"), lax.axis_size("space")
+    return Here(t, t == 0, t == times - 1, s > 0, s < blocks - 1, lax.rem(s, 2) == 0)
 
 
 def call(body, out_shapes, operands, specs=None, scratch=(), out_specs=None):
@@ -74,42 +90,43 @@
 
 
 class Field:
-    def __init__(self, pieces, ny):
-        self.pieces, self.ny = pieces, ny
-
-    def find(self, row):
-        for piece in self.pieces:
-            if piece[0] <= row < piece[1]:
-                return piece
+    def __init__(self, pieces, edges):
+        self.pieces, self.edges, self.moved = pieces, edges, {}
+
+    def tile(self, a):
+        for first, end, ref, index, base in self.pieces:
+            if first <= a and a + TILE <= end:
+                return ref[index + (slice(a - base, a - base + TILE),)]
         return None
 
-    def rows(self, a, size):
-        first, end, ref, index, base = self.find(a)
-        return ref[index + (slice(a - base, a - base + size),)]
-
-    def tile(self, a):
-        return self.rows(a, TILE)
-
-    def edge(self, a, row, shift, at):
-        moved = pltpu.roll(self.tile(a), shift, 0)
-        if self.find(row) is None:
-            return moved
-        place = lax.broadcasted_iota(jnp.int32, moved.shape, 0)
-        return jnp.where(place == at, self.rows(row, 1), moved)
+    def rolled(self, a, shift):
+        if (a, shift) not in self.moved:
+            tile = self.tile(a)
+            self.moved[a, shift] = None if tile is None else pltpu.roll(tile, shift, 0)
+        return self.moved[a, shift]
+
+    def neighbour(self, a, other, shift, edge):
+        own, next_ = self.rolled(a, shift), self.rolled(other, shift)
+        return own if next_ is None else jnp.where(edge, next_, own)
 
     def above(self, a):
-        if self.find(a - 1) == self.find(a):
-            return self.rows(a - 1, TILE)
-        return self.edge(a, a - 1, 1, 0)
+        return self.neighbour(a, a - TILE, 1, self.edges[0])
 
     def below(self, a):
-        if self.find(a + TILE) == self.find(a):
-            return self.rows(a + 1, TILE)
-        return self.edge(a, a + TILE, TILE - 1, TILE - 1)
-
-
-def plane(ref, index, ny):
-    return Field([(0, ny, ref, index, 0)], ny)
+        return self.neighbour(a, a + TILE, TILE - 1, self.edges[1])
+
+
+def edges(nz):
+    row = lax.broadcasted_iota(jnp.int32, (TILE, nz), 0)
+    return row == 0, row == TILE - 1
+
+
+def fields(spans, refs, planes, nz):
+    e = edges(nz)
+    return [
+        Field([(a, b, ref, (p,), base) for (a, b, base), ref in zip(spans, refs)], e)
+        for p in range(planes)
+    ]
 
 
 def face_coefficients(k, above, below, half, a, size, ny, nz):
@@ -134,13 +151,13 @@
     nx, ny, nz = cond.shape
 
     def body(k_ref, kx, up, down, right, diag):
+        planes = fields([(0, ny, 0)], [k_ref], nx, nz)
         for p in range(nx):
             for a in range(0, ny, TILE):
                 s = slice(a, a + TILE)
                 k = k_ref[p, s]
                 u, d, r, total = face_coefficients(
-                    k, plane(k_ref, (p,), ny).above(a), plane(k_ref, (p,), ny).below(a),
-                    HALF_FINE, a, TILE, ny, nz)
+                    k, planes[p].above(a), planes[p].below(a), HALF_FINE, a, TILE, ny, nz)
                 up[p, s], down[p, s], right[p, s] = u, d, r
                 if p > 0:
                     total = total + kx[p - 1, s]
@@ -192,27 +209,36 @@
 
 
 def chosen(flag, body, this, other):
-    pl.when(flag > 0)(lambda: body(this))
-    pl.when(flag == 0)(lambda: body(other))
-
-
-def first_messages(place, initial, prior, cond, end, start):
+    pl.when(flag)(lambda: body(this))
+    pl.when(jnp.logical_not(flag))(lambda: body(other))
+
+
+def first_messages(initial, prior, cond, end):
     nx, ny, nz = cond.shape
     half = nx // 2
 
-    def body(place_ref, i_ref, p_ref, k_ref, down, up, rows, sems):
+    def body(i_ref, p_ref, k_ref, down, up, sems):
         def copy(ref):
             copies = []
             for out, base in ((down, 0), (up, half)):
                 for source, at in ((k_ref, 0), (ref, end)):
                     copies += row_copies(source, out, base, (0, end), at, sems, len(copies))
-            run(copies + row_copies(p_ref, rows, 0, (start, ny), 0, sems, len(copies)))
-
-        chosen(place_ref[3], copy, i_ref, p_ref)
-
-    return call(
-        body, [(half, 2 * end, nz)] * 2 + [(nx, ny - start, nz)], [place, initial, prior, cond], [SMEM, HBM, HBM, HBM],
-        [pltpu.SemaphoreType.DMA((4 * half + nx,))])
+            run(copies)
+
+        chosen(here().last, copy, i_ref, p_ref)
+
+    return call(
+        body, [(half, 2 * end, nz)] * 2, [initial, prior, cond], [HBM, HBM, HBM],
+        [pltpu.SemaphoreType.DMA((4 * half,))])
+
+
+def rows_from(field, start):
+    nx, ny, nz = field.shape
+
+    def body(ref, out, sems):
+        run(row_copies(ref, out, 0, (start, ny), 0, sems, 0))
+
+    return call(body, [(nx, ny - start, nz)], [field], [HBM], [pltpu.SemaphoreType.DMA((nx,))])[0]
 
 
 def second_messages(cond, end, after):
@@ -237,34 +263,35 @@
         [cond, after], [HBM, VMEM], [lane_scratch(ny, nz // 2), pltpu.SemaphoreType.DMA((nx,))])
 
 
-def third_messages(place, initial, received, start):
+def third_messages(initial, received, start, after):
     nx, ny, nz = initial.shape
     half = nx // 2
 
-    def body(place_ref, i_ref, r_ref, down, up, sems):
+    def body(i_ref, r_ref, after_ref, down, up, sems):
         def copy(rows_of):
             ref, rows = rows_of
             run(row_copies(ref, down, 0, rows, 0, sems, 0) + row_copies(ref, up, half, rows, 0, sems, half))
 
-        chosen(place_ref[4], copy, (i_ref, (start, ny)), (r_ref, (0, ny - start)))
-
-    return call(
-        body, [(half, ny - start, nz)] * 2, [place, initial, received], [SMEM, HBM, VMEM],
+        chosen(here().first, copy, (i_ref, (start, ny)), (r_ref, (0, ny - start)))
+
+    return call(
+        body, [(half, ny - start, nz)] * 2, [initial, received, after], [HBM, VMEM, VMEM],
         [pltpu.SemaphoreType.DMA((nx,))])
 
 
-def ghost_coefficients(place, cond, before, after, spans, window):
+def ghost_coefficients(cond, before, after, spans, window):
     nx, ny, nz = cond.shape
     half, count = nx // 2, len(spans)
     w0, w1 = window
 
-    def body(place_ref, k_ref, *refs):
-        lo = fields(spans, refs[:count], half, ny)
-        hi = fields(spans, refs[count:2 * count], half, ny)
+    def body(k_ref, *refs):
+        me = here()
+        lo = fields(spans, refs[:count], half, nz)
+        hi = fields(spans, refs[count:2 * count], half, nz)
         kx, up, down, right, diag = refs[2 * count:]
         for side, near, far, inner, has in (
-            (0, lo[half - 1], lo[half - 2], 0, place_ref[0] > 0),
-            (1, hi[0], hi[1], nx - 1, place_ref[1] > 0),
+            (0, lo[half - 1], lo[half - 2], 0, me.has_lo),
+            (1, hi[0], hi[1], nx - 1, me.has_hi),
         ):
             for a in range(w0, w1, TILE):
                 s, d = slice(a, a + TILE), slice(a - w0, a - w0 + TILE)
@@ -279,8 +306,8 @@
 
     rows = w1 - w0
     return call(
-        body, [(4, rows, nz)] + [(2, rows, nz)] * 4, [place, cond, *before, *after],
-        [SMEM] + [VMEM] * (1 + 2 * count))
+        body, [(4, rows, nz)] + [(2, rows, nz)] * 4, [cond, *before, *after],
+        [VMEM] * (1 + 2 * count))
 
 
 def row_step(v, up, down, right, diag, a):
@@ -293,13 +320,6 @@
     return c, total + pltpu.roll(right * c, 1, 1)
 
 
-def fields(spans, refs, half, ny):
-    return [
-        Field([(a, b, ref, (p,), base) for (a, b, base), ref in zip(spans, refs)], ny)
-        for p in range(half)
-    ]
-
-
 def half_step(low, high, spans, window, coefficients, ahead=()):
     half, nz = low[0].shape[0], low[0].shape[2]
     nx, ny, count = 2 * half, coefficients[1].shape[1], len(spans)
@@ -308,7 +328,7 @@
     def body(*refs):
         kx, up, down, right, diag = refs[2 * count:2 * count + 5]
         out = refs[-1]
-        v = fields(spans, refs[:count], half, ny) + fields(spans, refs[count:2 * count], half, ny)
+        v = fields(spans, refs[:count], half, nz) + fields(spans, refs[count:2 * count], half, nz)
         for p in range(nx):
             for a in range(w0, w1, TILE):
                 s = slice(a, a + TILE)
@@ -322,23 +342,23 @@
     return call(body, [(nx, w1 - w0, nz)], [*low, *high, *coefficients, *ahead])[0]
 
 
-def two_steps(place, low, high, spans, before, after, side_spans, started, window, result, coefficients, ghosts, final=False):
+def two_steps(low, high, spans, before, after, side_spans, started, window, result, coefficients, ghosts, final=False):
     half, nz = low[0].shape[0], low[0].shape[2]
     nx, ny = 2 * half, coefficients[1].shape[1]
     n, m = len(spans), len(side_spans)
     (w0, w1), (r0, r1) = window, result
     counts = [n, n, m, m]
 
-    def body(place_ref, *refs):
+    def body(*refs):
         groups, at = [], 0
         for c in counts:
             groups.append(refs[at:at + c])
             at += c
         part, kx, up, down, right, diag, gx, gup, gdown, gright, gdiag, *rest = refs[at:]
-        v = fields(spans, groups[0], half, ny) + fields(spans, groups[1], half, ny)
-        lo = fields(side_spans, groups[2], half, ny)
-        hi = fields(side_spans, groups[3], half, ny)
-        has_lo, has_hi = place_ref[0] > 0, place_ref[1] > 0
+        v = fields(spans, groups[0], half, nz) + fields(spans, groups[1], half, nz)
+        lo = fields(side_spans, groups[2], half, nz)
+        hi = fields(side_spans, groups[3], half, nz)
+        has_lo, has_hi = here().has_lo, here().has_hi
         if final:
             out_ref, coarse_out, mid, scratch = rest
             out = [out_ref.at[p] for p in range(nx)]
@@ -358,7 +378,7 @@
                 mid[own + 1, d] = part[own, d] + gx[2 * side + 1, d] * (jnp.where(has, c, 0.0) - inner)
             for p in range(1, nx - 1):
                 mid[p + 1, d] = part[p, d]
-        w = [Field([(w0, w1, mid, (p,), w0)], ny) for p in range(nx + 2)]
+        w = fields([(w0, w1, w0)], [mid], nx + 2, nz)
         for p in range(nx):
             for a in range(r0, r1, TILE):
                 s, d = slice(a, a + TILE), slice(a - w0, a - w0 + TILE)
@@ -377,24 +397,24 @@
             for q in range(half):
                 coarse_out[q] = restrict_planes(out[2 * q][...], out[2 * q + 1][...], scratch, matrix)
 
-    operands = [place, *low, *high, *before, *after, started, *coefficients, *ghosts]
+    operands = [*low, *high, *before, *after, started, *coefficients, *ghosts]
     scratch = [pltpu.VMEM((nx + 2, w1 - w0, nz), F32)]
     shapes = [(half, r1 - r0, nz)] * 2
     if final:
         scratch.append(lane_scratch(r1 - r0, nz // 2))
         shapes = [(nx, r1 - r0, nz), (half, (r1 - r0) // 2, nz // 2)]
-    return call(body, shapes, operands, [SMEM] + [VMEM] * (len(operands) - 1), scratch)
-
-
-def coarse_coefficients(place, own, before, after, spans):
+    return call(body, shapes, operands, [VMEM] * len(operands), scratch)
+
+
+def coarse_coefficients(own, before, after, spans):
     nx, ny, nz = own.shape
     planes, count = nx + 2, len(spans)
 
-    def body(place_ref, k_own, *refs):
+    def body(k_own, *refs):
         sides = refs[:count], refs[count:2 * count]
         kx, up, down, right, diag, k_near, k_far, total, scratch = refs[2 * count:]
         matrix = pair_matrix(2 * nz, nz, 0.125)
-        for i, (side, has) in enumerate(zip(sides, (place_ref[0] > 0, place_ref[1] > 0))):
+        for i, (side, has) in enumerate(zip(sides, (here().has_lo, here().has_hi))):
             for (a, b, base), ref in zip(spans, side):
                 total[a:b] = ref[0, a - base:b - base] + ref[1, a - base:b - base]
             near = restrict_planes(total[...], 0.0, scratch, matrix)
@@ -423,43 +443,63 @@
 
     full = (planes, ny, nz)
     return call(
-        body, [(planes + 1, ny, nz)] + [full] * 4, [place, own, *before, *after],
-        [SMEM] + [VMEM] * (1 + 2 * count),
+        body, [(planes + 1, ny, nz)] + [full] * 4, [own, *before, *after],
+        [VMEM] * (1 + 2 * count),
         [pltpu.VMEM((2, ny, nz), F32), pltpu.VMEM((2, ny, nz), F32),
          pltpu.VMEM((2 * ny, 2 * nz), F32), lane_scratch(2 * ny, nz)])
 
 
-def sweep_step(place, own, on, off, coefficients, first, jumps=(), later=0):
+def sweep_step(own, on, off, coefficients, first, jumps=(), later=0):
     nx, ny, nz = own.shape
 
-    def body(place_ref, d_own, d_on, d_off, kx, up, down, right, diag, *rest):
-        even = place_ref[5] > 0
-        live = place_ref[3] > 0 if first else True
-        has_lo = jnp.logical_and(place_ref[0] > 0, live)
-        has_hi = jnp.logical_and(place_ref[1] > 0, live)
-
-        def step(v, i):
-            c = v[1]
-            total = diag[i] * c + kx[i] * v[0] + kx[i + 1] * v[2]
-            total = total + up[i] * pltpu.roll(c, 1, 0) + down[i] * pltpu.roll(c, ny - 1, 0)
-            return total + right[i] * pltpu.roll(c, nz - 1, 1) + pltpu.roll(right[i] * c, 1, 1)
-
-        lo = [jnp.where(has_lo, jnp.where(even, d_off[nx - 2 + i], d_on[nx - 2 + i]), 0.0) for i in range(2)]
-        hi = [jnp.where(has_hi, jnp.where(even, d_on[i], d_off[i]), 0.0) for i in range(2)]
-        block = [jnp.where(live, d_own[i], 0.0) if first else d_own[i] for i in range(nx)]
-        v = lo + block + hi
-        w = [step(v[i:i + 3], i) for i in range(nx + 2)]
-        w[0] = jnp.where(has_lo, w[0], 0.0)
-        w[-1] = jnp.where(has_hi, w[-1], 0.0)
+    def body(d_own, d_on, d_off, kx, up, down, right, diag, *rest):
+        out, v_ref, w_ref = rest[-3:]
+        me = here()
+        even, has_lo, has_hi = me.even, me.has_lo, me.has_hi
+        if first:
+            has_lo, has_hi = (jnp.logical_and(x, me.last) for x in (has_lo, has_hi))
+        tiles = [(a, slice(a, a + TILE)) for a in range(0, ny, TILE)]
+        for a, s in tiles:
+            for i in range(2):
+                near = nx - 2 + i
+                v_ref[i, s] = jnp.where(has_lo, jnp.where(even, d_off[near, s], d_on[near, s]), 0.0)
+                v_ref[nx + 2 + i, s] = jnp.where(has_hi, jnp.where(even, d_on[i, s], d_off[i, s]), 0.0)
+            for i in range(nx):
+                v_ref[2 + i, s] = jnp.where(me.last, d_own[i, s], 0.0) if first else d_own[i, s]
+        v = fields([(0, ny, 0)], [v_ref], nx + 4, nz)
+        w = fields([(0, ny, 0)], [w_ref], nx + 2, nz)
+
+        def step(planes, i, a, s):
+            _, total = row_step(planes[i + 1], up[i, s], down[i, s], right[i, s], diag[i, s], a)
+            return total + kx[i, s] * planes[i].tile(a) + kx[i + 1, s] * planes[i + 2].tile(a)
+
+        for i in range(nx + 2):
+            for a, s in tiles:
+                total = step(v, i, a, s)
+                if i == 0:
+                    total = jnp.where(has_lo, total, 0.0)
+                if i == nx + 1:
+                    total = jnp.where(has_hi, total, 0.0)
+                w_ref[i, s] = total
         for i in range(nx):
-            e = step(w[i:i + 3], i + 1)
-            if jumps:
-                e = e + jnp.where(place_ref[2] >= later, joined(rest[0][i], rest[1][i]), 0.0)
-            rest[-1][i] = e
-
-    operands = [place, own, on, off, *coefficients]
-    operands += jumps
-    return call(body, [own.shape], operands, [SMEM] + [VMEM] * (len(operands) - 1))[0]
+            for a, s in tiles:
+                _, e = row_step(w[i + 1], up[i + 1, s], down[i + 1, s], right[i + 1, s], diag[i + 1, s], a)
+                e = e + kx[i + 1, s] * w[i].tile(a) + kx[i + 2, s] * w[i + 2].tile(a)
+                if jumps:
+                    jump = rest[0 if a < ny // 2 else 1][i, s]
+                    e = e + jnp.where(me.t >= later, jump, 0.0)
+                out[i, s] = e
+
+    operands = [own, on, off, *coefficients, *jumps]
+    return call(
+        body, [own.shape], operands, [VMEM] * len(operands),
+        [pltpu.VMEM((nx + 4, ny, nz), F32), pltpu.VMEM((nx + 2, ny, nz), F32)])[0]
+
+
+def joined(upper, lower):
+    rows = upper.shape[-2]
+    row = lax.broadcasted_iota(jnp.int32, upper.shape, upper.ndim - 2)
+    return jnp.where(row < rows // 2, upper, lower)
 
 
 def jumps_of(moved, own, next_prior, own_prior):
@@ -471,12 +511,6 @@
             out[p, rows:] = b_ref[p] - own_ref[p, rows:]
 
     return call(body, [own_prior.shape], [moved, own, next_prior, own_prior])[0]
-
-
-def joined(upper, lower):
-    rows = upper.shape[-2]
-    row = lax.broadcasted_iota(jnp.int32, upper.shape, upper.ndim - 2)
-    return jnp.where(row < rows // 2, upper, lower)
 
 
 def finish(moved, own, prior, correction):
@@ -535,18 +569,17 @@
     s, blocks = lax.axis_index("space"), lax.axis_size("space")
     own_prior = prior[0]
     home = times - 1
-    place = jnp.stack([s > 0, s < blocks - 1, t, t == home, t == 0, s % 2 == 0]).astype(jnp.int32)
     ny = initial.shape[1]
     cut, wide = ny // 2, ny // 2 + OVERLAP
     windows = [(0, wide), (cut - OVERLAP, ny)]
     results = [(0, cut), (cut, ny)]
 
-    down, up, lower_prior = first_messages(place, initial, own_prior, conductivity, wide, windows[1][0])
+    down, up = first_messages(initial, own_prior, conductivity, wide)
     before, after = ([x] for x in from_sides(up, down))
-    received = ring(lower_prior, "tm", 1)
+    received = ring(rows_from(own_prior, windows[1][0]), "tm", 1)
     down_2, up_2, cond, coarse_cond = second_messages(conductivity, wide, up)
     before_2, after_2 = from_sides(up_2, down_2)
-    down_3, up_3 = third_messages(place, initial, received, windows[1][0])
+    down_3, up_3 = third_messages(initial, received, windows[1][0], before[0])
     before_3, after_3 = from_sides(up_3, down_3)
 
     coefficients = prepare_fine(cond)
@@ -563,11 +596,11 @@
     for i in range(2):
         there = slice(0, i + 1)
         ghosts.append(ghost_coefficients(
-            place, cond, cond_before[there], cond_after[there], cond_spans[there], windows[i]))
+            cond, cond_before[there], cond_after[there], cond_spans[there], windows[i]))
         middle.append(two_steps(
-            place, low[i], high[i], spans[i], before[i], after[i], spans[i],
+            low[i], high[i], spans[i], before[i], after[i], spans[i],
             started[i], windows[i], windows[i], coefficients, ghosts[i]))
-    coarse_coef = coarse_coefficients(place, coarse_cond, cond_before, cond_after, cond_spans)
+    coarse_coef = coarse_coefficients(coarse_cond, cond_before, cond_after, cond_spans)
     sides = [from_sides(b, a) for a, b in middle]
     spans = [[(*w, w[0])] for w in windows]
     ended = []
@@ -575,7 +608,7 @@
         a, b = middle[i]
         part = half_step([a], [b], spans[i], windows[i], coefficients, coarse_coef[:i])
         ended.append(two_steps(
-            place, [a], [b], spans[i], [sides[i][0]], [sides[i][1]], spans[i],
+            [a], [b], spans[i], [sides[i][0]], [sides[i][1]], spans[i],
             part, windows[i], results[i], coefficients, ghosts[i], True))
     (moved, moved_coarse), (own_fine, fine_coarse) = ended
 
@@ -589,7 +622,7 @@
             *_, moved = lax.optimization_barrier((on, off, lower, *shifted[2:home], moved))
             moved = ring(moved, "tm", 1)
         more = (shifted[j + 1:j + 3], home - j - 1) if j < home - 1 else ()
-        state = sweep_step(place, state, on, off, coarse_coef, j == 0, *more)
+        state = sweep_step(state, on, off, coarse_coef, j == 0, *more)
     update, tail = finish(moved, own_fine, own_prior, state)
     return update[None], tail[None]
 

time: 80.9 us -> 78.2 us (0.967)
  waiting for transfers between devices: 27.6 us -> 34.1 us
  Pallas kernels: 22.8 us -> 16.4 us
  starting transfers between devices: 29.1 us -> 26.5 us
    pallas_call x21 -> x22, Pallas kernels: 22.8 us -> 16.4 us  [call(): pl.pallas_call(body, out_shape=[jax.ShapeDtypeStruct(s, F32) for s in out...]
    ppermute x16, waiting for transfers between devices: 19.7 us -> 23.2 us  [ring(): lax.ppermute(block, axis, [(i, (i + distance) % size) for i in range(size)])]
    ppermute x6, waiting for transfers between devices: 7.94 us -> 11 us  [swapped(): return lax.ppermute(block, axis, pairs + [(j, i) for i, j in pairs])]
    ppermute x16, starting transfers between devices: 23.8 us -> 22.4 us  [ring(): lax.ppermute(block, axis, [(i, (i + distance) % size) for i in range(size)])]
    ppermute x6, starting transfers between devices: 5.31 us -> 4.09 us  [swapped(): return lax.ppermute(block, axis, pairs + [(j, i) for i, j in pairs])]
  transfers between devices with their start and end apart: 22 -> 22, of which waited for: 8 -> 10; matrix products, arithmetic and copies ran while one was open for 0% -> 0% of each run, Pallas kernels for 23% -> 17%
where the time goes in v5:
time: 78.2 us; the launch traced here: 78 us
  waiting for transfers between devices  34.1 us (44%)
  starting transfers between devices  26.5 us (34%)
  Pallas kernels  16.4 us (21%)
  between operations  0.88 us (1%)
    ppermute x16, waiting for transfers between devices, ring(): lax.ppermute(block, axis, [(i, (i + distance) % size) for i in range(size)])  23.2 us
    ppermute x16, starting transfers between devices, ring(): lax.ppermute(block, axis, [(i, (i + distance) % size) for i in range(size)])  22.4 us
    pallas_call x22, Pallas kernels, call(): pl.pallas_call(body, out_shape=[jax.ShapeDtypeStruct(s, F32) for s in out...  16.4 us
    ppermute x6, waiting for transfers between devices, swapped(): return lax.ppermute(block, axis, pairs + [(j, i) for i, j in pairs])  11 us
    ppermute x6, starting transfers between devices, swapped(): return lax.ppermute(block, axis, pairs + [(j, i) for i, j in pairs])  4.09 us
  transfers between devices with their start and end apart: 22, of which 10 were waited for; matrix products, arithmetic and copies ran while one was open for 0% of the time, Pallas kernels for 17%

profile of v5, /device:TPU:0, one launch (start us, length us, event | category | flops | bytes accessed | tf_op | source)
XLA Modules:
  0.0 78.0 jit_solution(4769896520141046389)
XLA Ops:
  0.6 1.4 %shard_map.50 = (f32[2,144,512]{2,1,0:T(8,128)S(1)}, f32[2,144,512]{2,1,0:T(8,128)S(1)}) custom-call(f32[4,128,512]{2,1,0:T(8,128)} %i_ref.3, f32[4,128,512]{2,1,0:T(8,128)} %bitcast.3, f32[4,128,512]{2,1,0:T(8,128)} %k_ref.3), custom_call_target="tpu_custom_call" | custom-call | tf_op jit(solution)/shard_map/pallas_call | solution.py:43
  2.6 1.2 %shard_map.58 = f32[4,72,512]{2,1,0:T(8,128)S(1)} custom-call(f32[4,128,512]{2,1,0:T(8,128)} %bitcast.4), custom_call_target="tpu_custom_call" | custom-call | tf_op jit(solution)/shard_map/pallas_call | solution.py:43
  3.7 2.6 %collective-permute-start.4 = (f32[4,72,512]{2,1,0:T(8,128)S(1)}, f32[4,72,512]{2,1,0:T(8,128)S(1)}, u32[]{:S(2)}, u32[]{:S(2)}) collective-permute-start(f32[4,72,512]{2,1,0:T(8,128)S(1)} %shard_map.58), channel_id=1, source_target_pairs={{0,8},{8,16},{16,24},{24,0},{1,9},{9,17},{17,25},{25,1},{2,10},{10... | collective-permute-start | bytes 1769480 | tf_op jit(solution)/shard_map/ppermute | solution.py:554
  6.4 2.3 %collective-permute-start.1 = (f32[2,144,512]{2,1,0:T(8,128)S(1)}, f32[2,144,512]{2,1,0:T(8,128)S(1)}, u32[]{:S(2)}, u32[]{:S(2)}) collective-permute-start(f32[2,144,512]{2,1,0:T(8,128)S(1)} %get-tuple-element.41.refs_0_), channel_id=1, source_target_pairs={{0,7},{1,0},{2,1},{3,2},{4,3},{5,4},{6,5},{7,6},{8,15},{9,8},{10,9... | collective-permute-start | bytes 1769480 | tf_op jit(solution)/shard_map/ppermute | solution.py:554
  8.7 1.7 %shard_map.51 = (f32[2,72,512]{2,1,0:T(8,128)S(1)}, f32[2,72,512]{2,1,0:T(8,128)S(1)}, f32[4,128,512]{2,1,0:T(8,128)S(1)}, f32[2,64,256]{2,1,0:T(8,128)S(1)}) custom-call(f32[4,128,512]{2,1,0:T(8,128)} %k_ref.3, f32[2,144,512]{2,1,0:T(8,128)S(1)} %get-tuple-element.42.after_ref.refs_1_), custom_call_target="tpu_custom_call" | custom-call | tf_op jit(solution)/shard_map/pallas_call | solution.py:43
  10.5 2.6 %collective-permute-start.8 = (f32[2,72,512]{2,1,0:T(8,128)S(1)}, f32[2,72,512]{2,1,0:T(8,128)S(1)}, u32[]{:S(2)}, u32[]{:S(2)}) collective-permute-start(f32[2,72,512]{2,1,0:T(8,128)S(1)} %get-tuple-element.60), channel_id=1, source_target_pairs={{0,7},{1,0},{2,1},{3,2},{4,3},{5,4},{6,5},{7,6},{8,15},{9,8},{10,9... | collective-permute-start | bytes 884744 | tf_op jit(solution)/shard_map/ppermute | solution.py:554
  14.2 7.5 %collective-permute-done.4.r_ref = f32[4,72,512]{2,1,0:T(8,128)S(1)} collective-permute-done((f32[4,72,512]{2,1,0:T(8,128)S(1)}, f32[4,72,512]{2,1,0:T(8,128)S(1)}, u32[]{:S(2)}, u32[]{:S(2)}) %collective-permute-start.4) | collective-permute-done | bytes 589856 | tf_op jit(solution)/shard_map/ppermute | solution.py:554
  21.7 1.2 %shard_map.59 = (f32[2,72,512]{2,1,0:T(8,128)S(1)}, f32[2,72,512]{2,1,0:T(8,128)S(1)}) custom-call(f32[4,128,512]{2,1,0:T(8,128)} %i_ref.3, f32[4,72,512]{2,1,0:T(8,128)S(1)} %collective-permute-done.4.r_ref, f32[2,144,512]{2,1,0:T(8,128)S(1)} %collective-permute-done.refs_0_.refs_2_.after_ref), custom_call_target="tpu_custom_call" | custom-call | tf_op jit(solution)/shard_map/pallas_call | solution.py:43
  23.6 2.0 %collective-permute-start.6 = (f32[2,72,512]{2,1,0:T(8,128)S(1)}, f32[2,72,512]{2,1,0:T(8,128)S(1)}, u32[]{:S(2)}, u32[]{:S(2)}) collective-permute-start(f32[2,72,512]{2,1,0:T(8,128)S(1)} %get-tuple-element.57.refs_0_), channel_id=1, source_target_pairs={{0,7},{1,0},{2,1},{3,2},{4,3},{5,4},{6,5},{7,6},{8,15},{9,8},{10,9... | collective-permute-start | bytes 884744 | tf_op jit(solution)/shard_map/ppermute | solution.py:554
  28.4 2.6 %collective-permute-start.3 = (f32[2,72,512]{2,1,0:T(8,128)S(1)}, f32[2,72,512]{2,1,0:T(8,128)S(1)}, u32[]{:S(2)}, u32[]{:S(2)}) collective-permute-start(f32[2,72,512]{2,1,0:T(8,128)S(1)} %get-tuple-element.54.refs_0_), channel_id=1, source_target_pairs={{0,7},{1,0},{2,1},{3,2},{4,3},{5,4},{6,5},{7,6},{8,15},{9,8},{10,9... | collective-permute-start | bytes 884744 | tf_op jit(solution)/shard_map/ppermute | solution.py:554
  31.3 1.7 %collective-permute-done.6.refs_3_ = f32[2,72,512]{2,1,0:T(8,128)S(1)} collective-permute-done((f32[2,72,512]{2,1,0:T(8,128)S(1)}, f32[2,72,512]{2,1,0:T(8,128)S(1)}, u32[]{:S(2)}, u32[]{:S(2)}) %collective-permute-start.6) | collective-permute-done | bytes 294944 | tf_op jit(solution)/shard_map/ppermute | solution.py:554
  33.7 1.6 %collective-permute-start.9 = (f32[2,72,512]{2,1,0:T(8,128)S(1)}, f32[2,72,512]{2,1,0:T(8,128)S(1)}, u32[]{:S(2)}, u32[]{:S(2)}) collective-permute-start(f32[2,72,512]{2,1,0:T(8,128)S(1)} %get-tuple-element.67.refs_1_), channel_id=1, source_target_pairs={{0,1},{1,2},{2,3},{3,4},{4,5},{5,6},{6,7},{7,0},{8,9},{9,10},{10,1... | collective-permute-start | bytes 884744 | tf_op jit(solution)/shard_map/ppermute | solution.py:554
  35.3 1.3 %collective-permute-start.10 = (f32[2,72,512]{2,1,0:T(8,128)S(1)}, f32[2,72,512]{2,1,0:T(8,128)S(1)}, u32[]{:S(2)}, u32[]{:S(2)}) collective-permute-start(f32[2,72,512]{2,1,0:T(8,128)S(1)} %get-tuple-element.66.refs_0_), channel_id=1, source_target_pairs={{0,7},{1,0},{2,1},{3,2},{4,3},{5,4},{6,5},{7,6},{8,15},{9,8},{10,9... | collective-permute-start | bytes 884744 | tf_op jit(solution)/shard_map/ppermute | solution.py:554
  37.1 2.7 %collective-permute-start.11 = (f32[2,64,256]{2,1,0:T(8,128)S(1)}, f32[2,64,256]{2,1,0:T(8,128)S(1)}, u32[]{:S(2)}, u32[]{:S(2)}) collective-permute-start(f32[2,64,256]{2,1,0:T(8,128)S(1)} %shard_map.66.own_ref), channel_id=1, source_target_pairs={{0,24},{8,0},{16,8},{24,16},{1,25},{9,1},{17,9},{25,17},{2,26},{10... | collective-permute-start | bytes 393224 | tf_op jit(solution)/shard_map/ppermute | solution.py:554
  42.3 2.5 %collective-permute-done.9.refs_2_ = f32[2,72,512]{2,1,0:T(8,128)S(1)} collective-permute-done((f32[2,72,512]{2,1,0:T(8,128)S(1)}, f32[2,72,512]{2,1,0:T(8,128)S(1)}, u32[]{:S(2)}, u32[]{:S(2)}) %collective-permute-start.9) | collective-permute-done | bytes 294944 | tf_op jit(solution)/shard_map/ppermute | solution.py:554
  44.9 1.1 %shard_map.65 = (f32[4,64,512]{2,1,0:T(8,128)S(1)}, f32[2,32,256]{2,1,0:T(8,128)S(1)}) custom-call(f32[2,72,512]{2,1,0:T(8,128)S(1)} %get-tuple-element.66.refs_0_, f32[2,72,512]{2,1,0:T(8,128)S(1)} %get-tuple-element.67.refs_1_, f32[2,72,512]{2,1,0:T(8,128)S(1)} %collective-permute-done.9.refs_2_, f32[2,72,512]{2,1,0:T(8,128)S(1)} %collective-permute-done.10.refs_3_, ...), custom_call_target="tpu_custom_call" | custom-call | tf_op jit(solution)/shard_map/pallas_call | solution.py:43
  46.0 3.0 %collective-permute-start.12 = (f32[2,64,256]{2,1,0:T(8,128)S(1)}, f32[2,64,256]{2,1,0:T(8,128)S(1)}, u32[]{:S(2)}, u32[]{:S(2)}) collective-permute-start(f32[2,64,256]{2,1,0:T(8,128)S(1)} %shard_map.67), channel_id=1, source_target_pairs={{0,24},{8,0},{16,8},{24,16},{1,25},{9,1},{17,9},{25,17},{2,26},{10... | collective-permute-start | bytes 393224 | tf_op jit(solution)/shard_map/ppermute | solution.py:554
  49.0 3.8 %collective-permute-done.12.rest_0_ = f32[2,64,256]{2,1,0:T(8,128)S(1)} collective-permute-done((f32[2,64,256]{2,1,0:T(8,128)S(1)}, f32[2,64,256]{2,1,0:T(8,128)S(1)}, u32[]{:S(2)}, u32[]{:S(2)}) %collective-permute-start.12) | collective-permute-done | bytes 131104 | tf_op jit(solution)/shard_map/ppermute | solution.py:554
  53.3 1.6 %collective-permute-start.14 = (f32[2,64,256]{2,1,0:T(8,128)S(1)}, f32[2,64,256]{2,1,0:T(8,128)S(1)}, u32[]{:S(2)}, u32[]{:S(2)}) collective-permute-start(f32[2,64,256]{2,1,0:T(8,128)S(1)} %broadcast_select_fusion.d_own), channel_id=1, source_target_pairs={{1,2},{3,4},{5,6},{7,0},{2,1},{4,3},{6,5},{0,7},{9,10},{11,12},{13... | collective-permute-start | bytes 393224 | tf_op jit(solution)/shard_map/ppermute | solution.py:564
  55.2 6.3 %collective-permute-done.15 = f32[2,32,256]{2,1,0:T(8,128)S(1)} collective-permute-done((f32[2,32,256]{2,1,0:T(8,128)S(1)}, f32[2,32,256]{2,1,0:T(8,128)S(1)}, u32[]{:S(2)}, u32[]{:S(2)}) %collective-permute-start.15) | collective-permute-done | bytes 65568 | tf_op jit(solution)/shard_map/ppermute | solution.py:554
  62.0 1.3 %collective-permute-start.19 = (f32[2,64,256]{2,1,0:T(8,128)S(1)}, f32[2,64,256]{2,1,0:T(8,128)S(1)}, u32[]{:S(2)}, u32[]{:S(2)}) collective-permute-start(f32[2,64,256]{2,1,0:T(8,128)S(1)} %shard_map.68.d_own), channel_id=1, source_target_pairs={{1,2},{3,4},{5,6},{7,0},{2,1},{4,3},{6,5},{0,7},{9,10},{11,12},{13... | collective-permute-start | bytes 393224 | tf_op jit(solution)/shard_map/ppermute | solution.py:564
  63.4 5.2 %collective-permute-done.19.d_off = f32[2,64,256]{2,1,0:T(8,128)S(1)} collective-permute-done((f32[2,64,256]{2,1,0:T(8,128)S(1)}, f32[2,64,256]{2,1,0:T(8,128)S(1)}, u32[]{:S(2)}, u32[]{:S(2)}) %collective-permute-start.19) | collective-permute-done | bytes 131104 | tf_op jit(solution)/shard_map/ppermute | solution.py:564
  70.4 5.0 %collective-permute-done.21.d_off = f32[2,64,256]{2,1,0:T(8,128)S(1)} collective-permute-done((f32[2,64,256]{2,1,0:T(8,128)S(1)}, f32[2,64,256]{2,1,0:T(8,128)S(1)}, u32[]{:S(2)}, u32[]{:S(2)}) %collective-permute-start.21) | collective-permute-done | bytes 131104 | tf_op jit(solution)/shard_map/ppermute | solution.py:564
  76.0 2.0 %shard_map.71 = (f32[4,128,512]{2,1,0:T(8,128)}, f32[2,64,256]{2,1,0:T(8,128)}) custom-call(f32[4,64,512]{2,1,0:T(8,128)S(1)} %collective-permute-done.17.moved_ref, f32[4,64,512]{2,1,0:T(8,128)S(1)} %get-tuple-element.73.own_ref, f32[4,128,512]{2,1,0:T(8,128)S(1)} %bitcast.6, f32[2,64,256]{2,1,0:T(8,128)S(1)} %shard_map.70.e_ref), custom_call_target="tpu_custom_call" | custom-call | tf_op jit(solution)/shard_map/pallas_call | solution.py:43
  (48 shorter events, 12.7 us)
Async XLA Ops:
  2.1 12.1 %collective-permute-start = (f32[2,144,512]{2,1,0:T(8,128)S(1)}, f32[2,144,512]{2,1,0:T(8,128)S(1)}, u32[]{:S(2)}, u32[]{:S(2)}) collective-permute-start(f32[2,144,512]{2,1,0:T(8,128)S(1)} %get-tuple-element.42.after_ref.refs_1_), channel_id=1, source_target_pairs={{0,1},{1,2},{2,3},{3,4},{4,5},{5,6},{6,7},{7,0},{8,9},{9,10},{10,1... | collective-permute-start | bytes 1769480 | tf_op jit(solution)/shard_map/ppermute | solution.py:554
  3.7 18.0 %collective-permute-start.4 = (f32[4,72,512]{2,1,0:T(8,128)S(1)}, f32[4,72,512]{2,1,0:T(8,128)S(1)}, u32[]{:S(2)}, u32[]{:S(2)}) collective-permute-start(f32[4,72,512]{2,1,0:T(8,128)S(1)} %shard_map.58), channel_id=1, source_target_pairs={{0,8},{8,16},{16,24},{24,0},{1,9},{9,17},{17,25},{25,1},{2,10},{10... | collective-permute-start | bytes 1769480 | tf_op jit(solution)/shard_map/ppermute | solution.py:554
  6.4 20.9 %collective-permute-start.1 = (f32[2,144,512]{2,1,0:T(8,128)S(1)}, f32[2,144,512]{2,1,0:T(8,128)S(1)}, u32[]{:S(2)}, u32[]{:S(2)}) collective-permute-start(f32[2,144,512]{2,1,0:T(8,128)S(1)} %get-tuple-element.41.refs_0_), channel_id=1, source_target_pairs={{0,7},{1,0},{2,1},{3,2},{4,3},{5,4},{6,5},{7,6},{8,15},{9,8},{10,9... | collective-permute-start | bytes 1769480 | tf_op jit(solution)/shard_map/ppermute | solution.py:554
  10.4 17.9 %collective-permute-start.7 = (f32[2,72,512]{2,1,0:T(8,128)S(1)}, f32[2,72,512]{2,1,0:T(8,128)S(1)}, u32[]{:S(2)}, u32[]{:S(2)}) collective-permute-start(f32[2,72,512]{2,1,0:T(8,128)S(1)} %get-tuple-element.59), channel_id=1, source_target_pairs={{0,1},{1,2},{2,3},{3,4},{4,5},{5,6},{6,7},{7,0},{8,9},{9,10},{10,1... | collective-permute-start | bytes 884744 | tf_op jit(solution)/shard_map/ppermute | solution.py:554
  10.5 20.5 %collective-permute-start.8 = (f32[2,72,512]{2,1,0:T(8,128)S(1)}, f32[2,72,512]{2,1,0:T(8,128)S(1)}, u32[]{:S(2)}, u32[]{:S(2)}) collective-permute-start(f32[2,72,512]{2,1,0:T(8,128)S(1)} %get-tuple-element.60), channel_id=1, source_target_pairs={{0,7},{1,0},{2,1},{3,2},{4,3},{5,4},{6,5},{7,6},{8,15},{9,8},{10,9... | collective-permute-start | bytes 884744 | tf_op jit(solution)/shard_map/ppermute | solution.py:554
  22.9 8.5 %collective-permute-start.5 = (f32[2,72,512]{2,1,0:T(8,128)S(1)}, f32[2,72,512]{2,1,0:T(8,128)S(1)}, u32[]{:S(2)}, u32[]{:S(2)}) collective-permute-start(f32[2,72,512]{2,1,0:T(8,128)S(1)} %get-tuple-element.58.refs_1_), channel_id=1, source_target_pairs={{0,1},{1,2},{2,3},{3,4},{4,5},{5,6},{6,7},{7,0},{8,9},{9,10},{10,1... | collective-permute-start | bytes 884744 | tf_op jit(solution)/shard_map/ppermute | solution.py:554
  23.6 9.4 %collective-permute-start.6 = (f32[2,72,512]{2,1,0:T(8,128)S(1)}, f32[2,72,512]{2,1,0:T(8,128)S(1)}, u32[]{:S(2)}, u32[]{:S(2)}) collective-permute-start(f32[2,72,512]{2,1,0:T(8,128)S(1)} %get-tuple-element.57.refs_0_), channel_id=1, source_target_pairs={{0,7},{1,0},{2,1},{3,2},{4,3},{5,4},{6,5},{7,6},{8,15},{9,8},{10,9... | collective-permute-start | bytes 884744 | tf_op jit(solution)/shard_map/ppermute | solution.py:554
  28.3 12.9 %collective-permute-start.2 = (f32[2,72,512]{2,1,0:T(8,128)S(1)}, f32[2,72,512]{2,1,0:T(8,128)S(1)}, u32[]{:S(2)}, u32[]{:S(2)}) collective-permute-start(f32[2,72,512]{2,1,0:T(8,128)S(1)} %get-tuple-element.55.refs_1_), channel_id=1, source_target_pairs={{0,1},{1,2},{2,3},{3,4},{4,5},{5,6},{6,7},{7,0},{8,9},{9,10},{10,1... | collective-permute-start | bytes 884744 | tf_op jit(solution)/shard_map/ppermute | solution.py:554
  28.4 12.8 %collective-permute-start.3 = (f32[2,72,512]{2,1,0:T(8,128)S(1)}, f32[2,72,512]{2,1,0:T(8,128)S(1)}, u32[]{:S(2)}, u32[]{:S(2)}) collective-permute-start(f32[2,72,512]{2,1,0:T(8,128)S(1)} %get-tuple-element.54.refs_0_), channel_id=1, source_target_pairs={{0,7},{1,0},{2,1},{3,2},{4,3},{5,4},{6,5},{7,6},{8,15},{9,8},{10,9... | collective-permute-start | bytes 884744 | tf_op jit(solution)/shard_map/ppermute | solution.py:554
  33.0 3.6 %copy-start = (f32[1,4,128,512]{3,2,1,0:T(8,128)S(1)}, f32[1,4,128,512]{3,2,1,0:T(8,128)}, u32[]{:S(2)}) copy-start(f32[1,4,128,512]{3,2,1,0:T(8,128)} %param.4) | copy-start | bytes 3145732
  33.7 11.2 %collective-permute-start.9 = (f32[2,72,512]{2,1,0:T(8,128)S(1)}, f32[2,72,512]{2,1,0:T(8,128)S(1)}, u32[]{:S(2)}, u32[]{:S(2)}) collective-permute-start(f32[2,72,512]{2,1,0:T(8,128)S(1)} %get-tuple-element.67.refs_1_), channel_id=1, source_target_pairs={{0,1},{1,2},{2,3},{3,4},{4,5},{5,6},{6,7},{7,0},{8,9},{9,10},{10,1... | collective-permute-start | bytes 884744 | tf_op jit(solution)/shard_map/ppermute | solution.py:554
  35.3 9.5 %collective-permute-start.10 = (f32[2,72,512]{2,1,0:T(8,128)S(1)}, f32[2,72,512]{2,1,0:T(8,128)S(1)}, u32[]{:S(2)}, u32[]{:S(2)}) collective-permute-start(f32[2,72,512]{2,1,0:T(8,128)S(1)} %get-tuple-element.66.refs_0_), channel_id=1, source_target_pairs={{0,7},{1,0},{2,1},{3,2},{4,3},{5,4},{6,5},{7,6},{8,15},{9,8},{10,9... | collective-permute-start | bytes 884744 | tf_op jit(solution)/shard_map/ppermute | solution.py:554
  37.1 8.9 %collective-permute-start.11 = (f32[2,64,256]{2,1,0:T(8,128)S(1)}, f32[2,64,256]{2,1,0:T(8,128)S(1)}, u32[]{:S(2)}, u32[]{:S(2)}) collective-permute-start(f32[2,64,256]{2,1,0:T(8,128)S(1)} %shard_map.66.own_ref), channel_id=1, source_target_pairs={{0,24},{8,0},{16,8},{24,16},{1,25},{9,1},{17,9},{25,17},{2,26},{10... | collective-permute-start | bytes 393224 | tf_op jit(solution)/shard_map/ppermute | solution.py:554
  46.0 6.8 %collective-permute-start.12 = (f32[2,64,256]{2,1,0:T(8,128)S(1)}, f32[2,64,256]{2,1,0:T(8,128)S(1)}, u32[]{:S(2)}, u32[]{:S(2)}) collective-permute-start(f32[2,64,256]{2,1,0:T(8,128)S(1)} %shard_map.67), channel_id=1, source_target_pairs={{0,24},{8,0},{16,8},{24,16},{1,25},{9,1},{17,9},{25,17},{2,26},{10... | collective-permute-start | bytes 393224 | tf_op jit(solution)/shard_map/ppermute | solution.py:554
  49.0 12.5 %collective-permute-start.16 = (f32[2,64,256]{2,1,0:T(8,128)S(1)}, f32[2,64,256]{2,1,0:T(8,128)S(1)}, u32[]{:S(2)}, u32[]{:S(2)}) collective-permute-start(f32[2,64,256]{2,1,0:T(8,128)S(1)} %shard_map.67), channel_id=1, source_target_pairs={{0,16},{8,24},{16,0},{24,8},{1,17},{9,25},{17,1},{25,9},{2,18},{10... | collective-permute-start | bytes 393224 | tf_op jit(solution)/shard_map/ppermute | solution.py:554
  52.9 8.6 %collective-permute-start.13 = (f32[2,64,256]{2,1,0:T(8,128)S(1)}, f32[2,64,256]{2,1,0:T(8,128)S(1)}, u32[]{:S(2)}, u32[]{:S(2)}) collective-permute-start(f32[2,64,256]{2,1,0:T(8,128)S(1)} %broadcast_select_fusion.d_own), channel_id=1, source_target_pairs={{0,1},{2,3},{4,5},{6,7},{1,0},{3,2},{5,4},{7,6},{8,9},{10,11},{12,... | collective-permute-start | bytes 393224 | tf_op jit(solution)/shard_map/ppermute | solution.py:564
  53.3 8.2 %collective-permute-start.14 = (f32[2,64,256]{2,1,0:T(8,128)S(1)}, f32[2,64,256]{2,1,0:T(8,128)S(1)}, u32[]{:S(2)}, u32[]{:S(2)}) collective-permute-start(f32[2,64,256]{2,1,0:T(8,128)S(1)} %broadcast_select_fusion.d_own), channel_id=1, source_target_pairs={{1,2},{3,4},{5,6},{7,0},{2,1},{4,3},{6,5},{0,7},{9,10},{11,12},{13... | collective-permute-start | bytes 393224 | tf_op jit(solution)/shard_map/ppermute | solution.py:564
  54.9 6.6 %collective-permute-start.15 = (f32[2,32,256]{2,1,0:T(8,128)S(1)}, f32[2,32,256]{2,1,0:T(8,128)S(1)}, u32[]{:S(2)}, u32[]{:S(2)}) collective-permute-start(f32[2,32,256]{2,1,0:T(8,128)S(1)} %slice.4), channel_id=1, source_target_pairs={{0,8},{8,16},{16,24},{24,0},{1,9},{9,17},{17,25},{25,1},{2,10},{10... | collective-permute-start | bytes 196616 | tf_op jit(solution)/shard_map/ppermute | solution.py:554
  61.5 14.5 %collective-permute-start.17 = (f32[4,64,512]{2,1,0:T(8,128)S(1)}, f32[4,64,512]{2,1,0:T(8,128)S(1)}, u32[]{:S(2)}, u32[]{:S(2)}) collective-permute-start(f32[4,64,512]{2,1,0:T(8,128)S(1)} %get-tuple-element.72), channel_id=1, source_target_pairs={{0,8},{8,16},{16,24},{24,0},{1,9},{9,17},{17,25},{25,1},{2,10},{10... | collective-permute-start | bytes 1572872 | tf_op jit(solution)/shard_map/ppermute | solution.py:554
  62.0 1.4 %collective-permute-start.18 = (f32[2,64,256]{2,1,0:T(8,128)S(1)}, f32[2,64,256]{2,1,0:T(8,128)S(1)}, u32[]{:S(2)}, u32[]{:S(2)}) collective-permute-start(f32[2,64,256]{2,1,0:T(8,128)S(1)} %shard_map.68.d_own), channel_id=1, source_target_pairs={{0,1},{2,3},{4,5},{6,7},{1,0},{3,2},{5,4},{7,6},{8,9},{10,11},{12,... | collective-permute-start | bytes 393224 | tf_op jit(solution)/shard_map/ppermute | solution.py:564
  62.0 6.6 %collective-permute-start.19 = (f32[2,64,256]{2,1,0:T(8,128)S(1)}, f32[2,64,256]{2,1,0:T(8,128)S(1)}, u32[]{:S(2)}, u32[]{:S(2)}) collective-permute-start(f32[2,64,256]{2,1,0:T(8,128)S(1)} %shard_map.68.d_own), channel_id=1, source_target_pairs={{1,2},{3,4},{5,6},{7,0},{2,1},{4,3},{6,5},{0,7},{9,10},{11,12},{13... | collective-permute-start | bytes 393224 | tf_op jit(solution)/shard_map/ppermute | solution.py:564
  69.0 1.4 %collective-permute-start.20 = (f32[2,64,256]{2,1,0:T(8,128)S(1)}, f32[2,64,256]{2,1,0:T(8,128)S(1)}, u32[]{:S(2)}, u32[]{:S(2)}) collective-permute-start(f32[2,64,256]{2,1,0:T(8,128)S(1)} %shard_map.69.d_own), channel_id=1, source_target_pairs={{0,1},{2,3},{4,5},{6,7},{1,0},{3,2},{5,4},{7,6},{8,9},{10,11},{12,... | collective-permute-start | bytes 393224 | tf_op jit(solution)/shard_map/ppermute | solution.py:564
  69.1 6.4 %collective-permute-start.21 = (f32[2,64,256]{2,1,0:T(8,128)S(1)}, f32[2,64,256]{2,1,0:T(8,128)S(1)}, u32[]{:S(2)}, u32[]{:S(2)}) collective-permute-start(f32[2,64,256]{2,1,0:T(8,128)S(1)} %shard_map.69.d_own), channel_id=1, source_target_pairs={{1,2},{3,4},{5,6},{7,0},{2,1},{4,3},{6,5},{0,7},{9,10},{11,12},{13... | collective-permute-start | bytes 393224 | tf_op jit(solution)/shard_map/ppermute | solution.py:564

commit v6 on v5

v6 whole, which is shorter than its diff:
```python
from typing import Any, NamedTuple

import jax
import jax.numpy as jnp
from jax import lax
from jax.experimental import pallas as pl
from jax.experimental.pallas import tpu as pltpu
from jax.sharding import PartitionSpec as P

FINE_RATE = 0.16
HALF_FINE = 0.5 * FINE_RATE
HALF_COARSE = 0.25 * FINE_RATE
TILE = 8
OVERLAP = 8
CUT = (5, 8)
LANES = 128

VMEM = pl.BlockSpec(memory_space=pltpu.VMEM)
HBM = pl.BlockSpec(memory_space=pltpu.HBM)
F32 = jnp.float32


class Here(NamedTuple):
    t: Any
    first: Any
    last: Any
    has_lo: Any
    has_hi: Any
    even: Any


def here():
    t, s = lax.axis_index("tm"), lax.axis_index("space")
    times, blocks = lax.axis_size("tm"), lax.axis_size("space")
    return Here(t, t == 0, t == times - 1, s > 0, s < blocks - 1, lax.rem(s, 2) == 0)


def call(body, out_shapes, operands, specs=None, scratch=(), out_specs=None):
    operands = list(operands)
    specs = specs or [VMEM] * len(operands)
    operands = [
        pltpu.with_memory_space_constraint(x, pltpu.HBM) if spec is HBM else x for x, spec in zip(operands, specs)
    ]
    return pl.pallas_call(
        body,
        out_shape=[jax.ShapeDtypeStruct(s, F32) for s in out_shapes],
        in_specs=specs,
        out_specs=out_specs or [VMEM] * len(out_shapes),
        scratch_shapes=list(scratch),
        compiler_params=pltpu.CompilerParams(vmem_limit_bytes=8 * 1024 * 1024),
    )(*operands)


def lane_scratch(rows, columns):
    return pltpu.VMEM((columns // LANES, rows, LANES), F32)


def split3(x):
    hi = x.astype(jnp.bfloat16)
    rest = x - hi.astype(F32)
    mid = rest.astype(jnp.bfloat16)
    low = (rest - mid.astype(F32)).astype(jnp.bfloat16)
    return hi, mid, low


def dot3(x, m):
    parts = [jnp.dot(p, m, preferred_element_type=F32) for p in split3(x)]
    return parts[0] + (parts[1] + parts[2])


def pair_matrix(fine, coarse, value):
    rows = lax.broadcasted_iota(jnp.int32, (fine, coarse), 0)
    cols = lax.broadcasted_iota(jnp.int32, (fine, coarse), 1)
    return jnp.where((rows >> 1) == cols, value, 0.0).astype(jnp.bfloat16)


def repeat_matrix(coarse, fine):
    rows = lax.broadcasted_iota(jnp.int32, (coarse, fine), 0)
    cols = lax.broadcasted_iota(jnp.int32, (coarse, fine), 1)
    return jnp.where(rows == (cols >> 1), 1.0, 0.0).astype(jnp.bfloat16)


def restrict_planes(first, second, scratch, matrix):
    blocks, ny, _ = scratch.shape
    sums = dot3(first + second, matrix)
    parts = []
    for b in range(blocks):
        scratch[b] = sums[:, b * LANES:(b + 1) * LANES]
        parts.append(scratch[b, pl.ds(0, ny // 2, 2), :] + scratch[b, pl.ds(1, ny // 2, 2), :])
    return jnp.concatenate(parts, axis=1)


class Field:
    def __init__(self, pieces, edges):
        self.pieces, self.edges, self.moved = pieces, edges, {}

    def tile(self, a):
        for first, end, ref, index, base in self.pieces:
            if first <= a and a + TILE <= end:
                return ref[index + (slice(a - base, a - base + TILE),)]
        return None

    def rolled(self, a, shift):
        if (a, shift) not in self.moved:
            tile = self.tile(a)
            self.moved[a, shift] = None if tile is None else pltpu.roll(tile, shift, 0)
        return self.moved[a, shift]

    def neighbour(self, a, other, shift, edge):
        own, next_ = self.rolled(a, shift), self.rolled(other, shift)
        return own if next_ is None else jnp.where(edge, next_, own)

    def above(self, a):
        return self.neighbour(a, a - TILE, 1, self.edges[0])

    def below(self, a):
        return self.neighbour(a, a + TILE, TILE - 1, self.edges[1])


def edges(nz):
    row = lax.broadcasted_iota(jnp.int32, (TILE, nz), 0)
    return row == 0, row == TILE - 1


def fields(spans, refs, planes, nz):
    e = edges(nz)
    return [
        Field([(a, b, ref, (p,), base) for (a, b, base), ref in zip(spans, refs)], e)
        for p in range(planes)
    ]


def face_coefficients(k, above, below, half, a, size, ny, nz):
    row = lax.broadcasted_iota(jnp.int32, (size, nz), 0) + a
    col = lax.broadcasted_iota(jnp.int32, (size, nz), 1)
    up_face = half * (k + jnp.where(row == 0, 0.0, above))
    down_face = half * (k + jnp.where(row == ny - 1, 0.0, below))
    right = pltpu.roll(k, nz - 1, 1)
    left = pltpu.roll(k, 1, 1)
    right_face = half * (k + jnp.where(col == nz - 1, 0.0, right))
    left_face = half * (k + jnp.where(col == 0, 0.0, left))
    total = (up_face + down_face) + (right_face + left_face)
    return (
        jnp.where(row == 0, 0.0, up_face),
        jnp.where(row == ny - 1, 0.0, down_face),
        jnp.where(col == nz - 1, 0.0, right_face),
        total,
    )


def prepare_fine(cond):
    nx, ny, nz = cond.shape

    def body(k_ref, kx, up, down, right, diag):
        planes = fields([(0, ny, 0)], [k_ref], nx, nz)
        for p in range(nx):
            for a in range(0, ny, TILE):
                s = slice(a, a + TILE)
                k = k_ref[p, s]
                u, d, r, total = face_coefficients(
                    k, planes[p].above(a), planes[p].below(a), HALF_FINE, a, TILE, ny, nz)
                up[p, s], down[p, s], right[p, s] = u, d, r
                if p > 0:
                    total = total + kx[p - 1, s]
                if p < nx - 1:
                    face = HALF_FINE * (k + k_ref[p + 1, s])
                    kx[p, s] = face
                    total = total + face
                diag[p, s] = 1.0 - total
    full = (nx, ny, nz)
    return call(body, [(nx - 1, ny, nz), full, full, full, full], [cond])


def restricted(field):
    nx, ny, nz = field.shape

    def body(f_ref, out, scratch):
        matrix = pair_matrix(nz, nz // 2, 0.125)
        for q in range(nx // 2):
            out[q] = restrict_planes(f_ref[2 * q], f_ref[2 * q + 1], scratch, matrix)

    return call(
        body, [(nx // 2, ny // 2, nz // 2)], [field], scratch=[lane_scratch(ny, nz // 2)]
    )[0]


def row_copies(source, out, rows, at, sems, first_sem, planes):
    start, end = rows
    return [
        pltpu.make_async_copy(
            source.at[p, pl.ds(start, end - start)], out.at[i, pl.ds(at, end - start)], sems.at[first_sem + i])
        for i, p in enumerate(planes)
    ]


def run(copies):
    for c in copies:
        c.start()
    for c in copies:
        c.wait()


def chosen(flag, body, this, other):
    pl.when(flag)(lambda: body(this))
    pl.when(jnp.logical_not(flag))(lambda: body(other))


def first_block(initial, prior, cond, end):
    nx, ny, nz = cond.shape

    def body(i_ref, p_ref, k_hbm, k_ref, v_ref, down, up, sems):
        def copy(ref):
            run(row_copies(k_hbm, k_ref, (0, ny), 0, sems, 0, range(nx))
                + row_copies(ref, v_ref, (0, end), 0, sems, nx, range(nx)))

        chosen(here().last, copy, i_ref, p_ref)
        k = fields([(0, ny, 0)], [k_ref], nx, nz)
        v = fields([(0, end, 0)], [v_ref], nx, nz)
        for out, own, inner in ((down, 0, 1), (up, nx - 1, nx - 2)):
            for a in range(0, ny, TILE):
                own_k = k[own].tile(a)
                out[a:a + TILE] = own_k
                if a >= end:
                    continue
                u, d, r, total = face_coefficients(
                    own_k, k[own].above(a), k[own].below(a), HALF_FINE, a, TILE, ny, nz)
                face = HALF_FINE * (own_k + k[inner].tile(a))
                c, stepped = row_step(v[own], u, d, r, 1.0 - (total + face), a)
                out[ny + a:ny + a + TILE] = c
                out[ny + end + a:ny + end + a + TILE] = stepped + face * v[inner].tile(a)

    return call(
        body, [cond.shape, (nx, end, nz)] + [(ny + 2 * end, nz)] * 2, [initial, prior, cond], [HBM, HBM, HBM],
        [pltpu.SemaphoreType.DMA((2 * nx,))])


def rows_from(field, start):
    nx, ny, nz = field.shape

    def body(ref, out, sems):
        run(row_copies(ref, out, (start, ny), 0, sems, 0, range(nx)))

    return call(body, [(nx, ny - start, nz)], [field], [HBM], [pltpu.SemaphoreType.DMA((nx,))])[0]


def coarse_and_initial(cond, initial, start):
    nx, ny, nz = cond.shape

    def body(k_ref, i_ref, coarse, rows, scratch, sems):
        copies = row_copies(i_ref, rows, (start, ny), 0, sems, 0, range(nx))
        for c in copies:
            c.start()
        matrix = pair_matrix(nz, nz // 2, 0.125)
        for q in range(nx // 2):
            coarse[q] = restrict_planes(k_ref[2 * q], k_ref[2 * q + 1], scratch, matrix)
        for c in copies:
            c.wait()

    return call(
        body, [(nx // 2, ny // 2, nz // 2), (nx, ny - start, nz)], [cond, initial], [VMEM, HBM],
        [lane_scratch(ny, nz // 2), pltpu.SemaphoreType.DMA((nx,))])


def row_step(v, up, down, right, diag, a):
    c = v.tile(a)
    nz = c.shape[1]
    total = diag * c
    total = total + up * v.above(a)
    total = total + down * v.below(a)
    total = total + right * pltpu.roll(c, nz - 1, 1)
    return c, total + pltpu.roll(right * c, 1, 1)


def block_step(planes, p, coefficients, a):
    kx, up, down, right, diag = coefficients
    s = slice(a, a + TILE)
    c, total = row_step(planes[p], up[p, s], down[p, s], right[p, s], diag[p, s], a)
    if p > 0:
        total = total + kx[p - 1, s] * planes[p - 1].tile(a)
    if p < len(planes) - 1:
        total = total + kx[p, s] * planes[p + 1].tile(a)
    return c, total


def half_step(state, window, coefficients, ahead=()):
    nx, rows, nz = state.shape
    w0, w1 = window

    def body(v_ref, *refs):
        v, out = fields([(w0, w1, w0)], [v_ref], nx, nz), refs[-1]
        for p in range(nx):
            for a in range(w0, w1, TILE):
                out[p, a - w0:a - w0 + TILE] = block_step(v, p, refs[:5], a)[1]

    return call(body, [state.shape], [state, *coefficients, *ahead])[0]


def lower_start(initial, received, window, coefficients, coarse, after):
    nx, rows, nz = received.shape
    w0, w1 = window
    extra = coarse.shape[1] // 2

    def body(i_ref, r_ref, *refs):
        coarse_ref, _, state, part, down, up = refs[5:]
        first = here().first
        for p in range(nx):
            for a in range(0, rows, TILE):
                s = slice(a, a + TILE)
                state[p, s] = jnp.where(first, i_ref[p, s], r_ref[p, s])
        edge_messages(state, part, down, up, refs[:5], window)
        for out, q in ((down, 0), (up, coarse.shape[0] - 1)):
            for i in range(2):
                out[2 * rows:, i * nz // 2:(i + 1) * nz // 2] = coarse_ref[q, i * extra:(i + 1) * extra]

    return call(
        body, [received.shape] * 2 + [(2 * rows + extra, nz)] * 2,
        [initial, received, *coefficients, coarse, after])


def edge_messages(state, part, down, up, coefficients, window):
    nx, rows, nz = state.shape
    w0, w1 = window
    v = fields([(w0, w1, w0)], [state], nx, nz)
    for p in range(nx):
        out = down if p == 0 else up if p == nx - 1 else None
        if part is None and out is None:
            continue
        for a in range(w0, w1, TILE):
            d = slice(a - w0, a - w0 + TILE)
            c, total = block_step(v, p, coefficients, a)
            if part is not None:
                part[p, d] = total
            if out is not None:
                out[d] = c
                out[slice(rows + d.start, rows + d.stop)] = total


def two_steps(state, started, before, after, conds, cond, window, result, coefficients, final=False):
    nx, rows, nz = state.shape
    ny = cond.shape[1]
    (w0, w1), (r0, r1) = window, result
    sides = [before, after]

    def body(v_ref, part, k_ref, *refs):
        k_sides, messages, coef, rest = refs[:2], refs[2:6], refs[6:11], refs[11:]
        out, rest = rest[0], rest[1:]
        mid = rest[-2] if final else rest[-1]
        me = here()
        owns = ((0, 0, me.has_lo), (1, nx - 1, me.has_hi))

        def face(side, own, has, s):
            return HALF_FINE * (k_ref[own, s] + jnp.where(has, k_sides[side][s], 0.0))

        for side, own, has in owns:
            (_, v_at), (_, p_at) = sides[side]
            near, half_done = messages[2 * side:2 * side + 2]
            for a in range(w0, w1, TILE):
                s, d = slice(a, a + TILE), slice(a - w0, a - w0 + TILE)
                theirs = jnp.where(has, near[slice(v_at + d.start, v_at + d.stop)], 0.0)
                flow = face(side, own, has, s) * (theirs - v_ref[own, d])
                mid[2 + side, d] = part[own, d] + flow
                mid[side, d] = jnp.where(has, half_done[slice(p_at + d.start, p_at + d.stop)] - flow, 0.0)
        span = [(w0, w1, w0)]
        edge = fields(span, [mid], 4, nz)
        w = fields(span, [part], nx, nz)
        w[0], w[nx - 1] = edge[2], edge[3]
        for p in range(nx):
            for a in range(r0, r1, TILE):
                c, total = block_step(w, p, coef, a)
                for side, own, has in owns:
                    if p == own:
                        s = slice(a, a + TILE)
                        total = total + face(side, own, has, s) * (edge[side].tile(a) - c)
                out[p, a - r0:a - r0 + TILE] = total
        if final:
            matrix = pair_matrix(nz, nz // 2, 0.125)
            for q in range(nx // 2):
                rest[0][q] = restrict_planes(out[2 * q], out[2 * q + 1], rest[-1], matrix)
        else:
            edge_messages(out, None, rest[0], rest[1], coef, window)

    shape = (nx, r1 - r0, nz)
    scratch = [pltpu.VMEM((4, w1 - w0, nz), F32)]
    if final:
        shapes = [shape, (nx // 2, (r1 - r0) // 2, nz // 2)]
        scratch.append(lane_scratch(r1 - r0, nz // 2))
    else:
        shapes = [shape, (2 * rows, nz), (2 * rows, nz)]
    messages = [array for side in sides for array, _ in side]
    return call(body, shapes, [state, started, cond, *conds, *messages, *coefficients], scratch=scratch)


def coarse_coefficients(own, before, after, at):
    nx, ny, nz = own.shape

    def body(k_own, lo, hi, kx, up, down, right, diag):
        me = here()

        def side(ref, has):
            k = jnp.concatenate([ref[at:, :nz], ref[at:, nz:]], axis=0)
            return jnp.where(has, k, 0.0)

        planes = [side(lo, me.has_lo)] + [k_own[p] for p in range(nx)] + [side(hi, me.has_hi)]
        for i in range(nx + 1):
            kx[i] = HALF_COARSE * (planes[i] + planes[i + 1])
        for p in range(nx):
            k = k_own[p]
            u, d, r, total = face_coefficients(
                k, pltpu.roll(k, 1, 0), pltpu.roll(k, ny - 1, 0), HALF_COARSE, 0, ny, ny, nz)
            up[p], down[p], right[p] = u, d, r
            if p > 0:
                total = total + kx[p]
            if p < nx - 1:
                total = total + kx[p + 1]
            diag[p] = 1.0 - total

    full = (nx, ny, nz)
    return call(body, [(nx + 1, ny, nz)] + [full] * 4, [own, before, after])


def sweep_messages(state, part, on, off, coefficients):
    nx, ny, nz = state.shape
    kx, up, down, right, diag = coefficients
    even = here().even
    v = fields([(0, ny, 0)], [state], nx, nz)
    for a in range(0, ny, TILE):
        s = slice(a, a + TILE)
        both = []
        for p in range(nx):
            c, total = row_step(v[p], up[p, s], down[p, s], right[p, s], diag[p, s], a)
            if p > 0:
                total = total + kx[p, s] * v[p - 1].tile(a)
            if p < nx - 1:
                total = total + kx[p + 1, s] * v[p + 1].tile(a)
            part[p, s] = total
            both.append((c, total))
        for i in range(2):
            d = slice(i * ny + a, i * ny + a + TILE)
            on[d] = jnp.where(even, both[-1][i], both[0][i])
            off[d] = jnp.where(even, both[0][i], both[-1][i])


def sweep_start(upper, lower, cut, coefficients):
    nx, ny, nz = upper.shape

    def body(a_ref, b_ref, *refs):
        last = here().last
        state = refs[5]
        for p in range(nx):
            for a in range(0, ny, TILE):
                s = slice(a, a + TILE)
                state[p, s] = jnp.where(last, (a_ref if a < cut else b_ref)[p, s], 0.0)
        sweep_messages(*refs[5:], refs[:5])

    return call(body, [upper.shape] * 2 + [(2 * ny, nz)] * 2, [upper, lower, *coefficients])


def sweep_step(state, part, on, off, cut, coefficients, jumps=(), later=0):
    nx, ny, nz = state.shape

    def body(v_ref, part_ref, on_ref, off_ref, *refs):
        coef, rest = refs[:5], refs[5:]
        kx, up, down, right, diag = coef
        jump_refs, rest = rest[:len(jumps)], rest[len(jumps):]
        out, mid = rest[0], rest[-1]
        me = here()
        for a in range(0, ny, TILE):
            s = slice(a, a + TILE)
            for i, (own, has) in enumerate(((0, me.has_lo), (nx - 1, me.has_hi))):
                refs_of = (off_ref, on_ref) if i == 0 else (on_ref, off_ref)
                theirs, half_done = (
                    jnp.where(has, jnp.where(me.even, *(r[slice(j * ny + a, j * ny + a + TILE)] for r in refs_of)), 0.0)
                    for j in range(2)
                )
                flow = kx[i * nx, s] * (theirs - v_ref[own, s])
                mid[1 + own, s] = part_ref[own, s] + flow
                mid[i * (nx + 1), s] = jnp.where(has, half_done - flow, 0.0)
            for p in range(1, nx - 1):
                mid[1 + p, s] = part_ref[p, s]
        w = fields([(0, ny, 0)], [mid], nx + 2, nz)
        for p in range(nx):
            for a in range(0, ny, TILE):
                s = slice(a, a + TILE)
                c, e = row_step(w[p + 1], up[p, s], down[p, s], right[p, s], diag[p, s], a)
                for i, q in ((p, p), (p + 1, p + 2)):
                    other = w[q].tile(a)
                    e = e + kx[i, s] * (other - c if i in (0, nx) else other)
                if jumps:
                    jump = jump_refs[0 if a < cut else 1][p, s]
                    e = e + jnp.where(me.t >= later, jump, 0.0)
                out[p, s] = e
        if jumps:
            sweep_messages(out, *rest[1:4], coef)

    shapes = [state.shape]
    if jumps:
        shapes += [state.shape] + [on.shape] * 2
    return call(
        body, shapes, [state, part, on, off, *coefficients, *jumps], scratch=[pltpu.VMEM((nx + 2, ny, nz), F32)])


def jumps_of(moved, own, next_prior, own_prior):
    nx, rows, nz = moved.shape

    def body(a_ref, b_ref, next_ref, own_ref, out):
        for p in range(nx):
            out[p, :rows] = a_ref[p] - next_ref[p, :rows]
            out[p, rows:] = b_ref[p] - own_ref[p, rows:]

    return call(body, [own_prior.shape], [moved, own, next_prior, own_prior])[0]


def finish(moved, own, prior, correction):
    nx, ny, nz = prior.shape
    rows = moved.shape[1]

    def body(moved_ref, own_ref, p_ref, e_ref, update, tail, out, wide, upper, lower, sems):
        parts = ((moved_ref, slice(0, rows), upper), (own_ref, slice(rows, ny), lower))
        spread = repeat_matrix(nz // 2, nz)
        copies = []
        for q in range(nx // 2):
            row = dot3(e_ref[q], spread)
            for b in range(nz // LANES):
                s = slice(b * LANES, (b + 1) * LANES)
                wide[b, pl.ds(0, ny // 2, 2), :] = row[:, s]
                wide[b, pl.ds(1, ny // 2, 2), :] = row[:, s]
            for p in (2 * q, 2 * q + 1):
                for ref, r, _ in parts:
                    for b in range(nz // LANES):
                        s = slice(b * LANES, (b + 1) * LANES)
                        out[p, r, s] = (ref[p, :, s] + wide[b, r]) - p_ref[p, r, s]
                copies.append(pltpu.make_async_copy(out.at[p], update.at[p], sems.at[p]))
                copies[-1].start()
        matrix = pair_matrix(nz, nz // 2, 0.125)
        for q in range(nx // 2):
            for ref, r, scratch in parts:
                c = slice(r.start // 2, r.stop // 2)
                tail[q, c] = e_ref[q, c] + restrict_planes(ref[2 * q], ref[2 * q + 1], scratch, matrix)
        for c in copies:
            c.wait()

    return call(
        body, [prior.shape, correction.shape], [moved, own, prior, correction],
        scratch=[pltpu.VMEM(prior.shape, F32), lane_scratch(ny, nz), lane_scratch(rows, nz // 2),
                 lane_scratch(ny - rows, nz // 2), pltpu.SemaphoreType.DMA((nx,))],
        out_specs=[HBM, VMEM])


def ring(block, axis, distance):
    size = lax.axis_size(axis)
    return lax.ppermute(block, axis, [(i, (i + distance) % size) for i in range(size)])


def from_sides(last, first):
    return ring(last, "space", 1), ring(first, "space", -1)


def swapped(block, axis, offset):
    size = lax.axis_size(axis)
    pairs = [(i % size, (i + 1) % size) for i in range(offset, size + offset, 2)]
    return lax.ppermute(block, axis, pairs + [(j, i) for i, j in pairs])


def shards(initial, prior, conductivity):
    times = lax.axis_size("tm")
    own_prior = prior[0]
    home = times - 1
    ny = initial.shape[1]
    cut = ny * CUT[0] // CUT[1]
    wide = cut + OVERLAP
    windows = [(0, wide), (cut - OVERLAP, ny)]
    results = [(0, cut), (cut, ny)]
    start = windows[1][0]

    received = ring(rows_from(own_prior, start), "tm", 1)
    cond, upper, down, up = first_block(initial, own_prior, conductivity, wide)
    before, after = from_sides(up, down)
    coefficients = prepare_fine(cond)
    coarse_cond, initial_rows = coarse_and_initial(cond, initial, start)
    lower, lower_part, down, up = lower_start(initial_rows, received, windows[1], coefficients, coarse_cond, before)
    before_2, after_2 = from_sides(up, down)
    own_coarse = restricted(own_prior)
    next_coarse = ring(own_coarse, "tm", -1)

    conds = (before, after)
    rows = ny - start
    sides = [
        [[(x, at), (x, at + size)] for x in pair]
        for pair, at, size in ((conds, ny, wide), ((before_2, after_2), 0, rows))
    ]
    parts = [half_step(upper, windows[0], coefficients), lower_part]
    middle = [
        two_steps(state, parts[i], *sides[i], conds, cond, windows[i], windows[i], coefficients)
        for i, state in enumerate((upper, lower))
    ]
    coarse_coef = coarse_coefficients(coarse_cond, before_2, after_2, 2 * rows)
    received = [from_sides(up, down) for _, down, up in middle]
    ended = []
    for i, (state, _, _) in enumerate(middle):
        part = half_step(state, windows[i], coefficients, coarse_coef[:i])
        side = [[(x, 0), (x, x.shape[0] // 2)] for x in received[i]]
        ended.append(two_steps(state, part, *side, conds, cond, windows[i], results[i], coefficients, True))
    (moved, moved_coarse), (own_fine, fine_coarse) = ended

    jump = jumps_of(moved_coarse, fine_coarse, next_coarse, own_coarse)
    half_cut = cut // 2
    lower = ring(jump[:, half_cut:], "tm", -home)
    shifted = [jump] + [ring(jump, "tm", -j) for j in range(1, home)]
    shifted.append(jnp.concatenate([jump[:, :half_cut], lower], axis=1))
    sweep = sweep_start(shifted[0], shifted[1], half_cut, coarse_coef)
    for j in range(home):
        state, part, on, off = sweep
        off, on = swapped(off, "space", 1), swapped(on, "space", 0)
        if j == 0:
            *_, moved = lax.optimization_barrier((on, off, lower, *shifted[2:home], moved))
            moved = ring(moved, "tm", 1)
        more = (shifted[j + 1:j + 3], home - j - 1) if j < home - 1 else ()
        sweep = sweep_step(state, part, on, off, half_cut, coarse_coef, *more)
    update, tail = finish(moved, own_fine, own_prior, sweep[0])
    return update[None], tail[None]


def solution(mesh):
    return jax.shard_map(
        shards,
        mesh=mesh,
        in_specs=(P("space", None, None), P("tm", "space", None, None), P("space", None, None)),
        out_specs=(P("tm", "space", None, None), P("tm", "space", None, None)),
        check_vma=False,
    )
```

time: 78.2 us -> 77.5 us (level)
  waiting for transfers between devices: 34.1 us -> 37.2 us
  Pallas kernels: 16.4 us -> 14.4 us
  starting transfers between devices: 26.5 us -> 24.9 us
    ppermute x16 -> x14, waiting for transfers between devices: 23.2 us -> 27.6 us  [ring(): lax.ppermute(block, axis, [(i, (i + distance) % size) for i in range(size)])]
    ppermute x16 -> x14, starting transfers between devices: 22.4 us -> 18.3 us  [ring(): lax.ppermute(block, axis, [(i, (i + distance) % size) for i in range(size)])]
    ppermute x6, starting transfers between devices: 4.09 us -> 6.62 us  [swapped(): return lax.ppermute(block, axis, pairs + [(j, i) for i, j in pairs])]
    pallas_call x22 -> x20, Pallas kernels: 16.4 us -> 14.4 us  [call(): pl.pallas_call(body, out_shape=[jax.ShapeDtypeStruct(s, F32) for s in out...]
    ppermute x6, waiting for transfers between devices: 11 us -> 9.57 us  [swapped(): return lax.ppermute(block, axis, pairs + [(j, i) for i, j in pairs])]
  transfers between devices with their start and end apart: 22 -> 20, of which waited for: 10 -> 12; matrix products, arithmetic and copies ran while one was open for 0% -> 0% of each run, Pallas kernels for 17% -> 12%
where the time goes in v6:
time: 77.5 us; the launch traced here: 77.3 us
  waiting for transfers between devices  37.2 us (48%)
  starting transfers between devices  24.9 us (32%)
  Pallas kernels  14.4 us (19%)
  between operations  0.85 us (1%)
    ppermute x14, waiting for transfers between devices, ring(): lax.ppermute(block, axis, [(i, (i + distance) % size) for i in range(size)])  27.6 us
    ppermute x14, starting transfers between devices, ring(): lax.ppermute(block, axis, [(i, (i + distance) % size) for i in range(size)])  18.3 us
    pallas_call x20, Pallas kernels, call(): pl.pallas_call(body, out_shape=[jax.ShapeDtypeStruct(s, F32) for s in out...  14.4 us
    ppermute x6, waiting for transfers between devices, swapped(): return lax.ppermute(block, axis, pairs + [(j, i) for i, j in pairs])  9.57 us
    ppermute x6, starting transfers between devices, swapped(): return lax.ppermute(block, axis, pairs + [(j, i) for i, j in pairs])  6.62 us
  transfers between devices with their start and end apart: 20, of which 12 were waited for; matrix products, arithmetic and copies ran while one was open for 0% of the time, Pallas kernels for 12%

profile of v6, /device:TPU:0, one launch (start us, length us, event | category | flops | bytes accessed | tf_op | source)
XLA Modules:
  0.0 77.3 jit_solution(12693549550146948202)
XLA Ops:
  0.6 2.8 %shard_map.50 = (f32[4,128,512]{2,1,0:T(8,128)S(1)}, f32[4,88,512]{2,1,0:T(8,128)S(1)}, f32[304,512]{1,0:T(8,128)S(1)}, f32[304,512]{1,0:T(8,128)S(1)}) custom-call(f32[4,128,512]{2,1,0:T(8,128)} %i_ref.3, f32[4,128,512]{2,1,0:T(8,128)} %bitcast.3, f32[4,128,512]{2,1,0:T(8,128)} %k_hbm.1), custom_call_target="tpu_custom_call" | custom-call | tf_op jit(solution)/shard_map/pallas_call | solution.py:44
  3.9 1.1 %shard_map.57 = f32[4,56,512]{2,1,0:T(8,128)S(1)} custom-call(f32[4,128,512]{2,1,0:T(8,128)} %bitcast.4), custom_call_target="tpu_custom_call" | custom-call | tf_op jit(solution)/shard_map/pallas_call | solution.py:44
  5.0 2.6 %collective-permute-start.4 = (f32[4,56,512]{2,1,0:T(8,128)S(1)}, f32[4,56,512]{2,1,0:T(8,128)S(1)}, u32[]{:S(2)}, u32[]{:S(2)}) collective-permute-start(f32[4,56,512]{2,1,0:T(8,128)S(1)} %shard_map.57), channel_id=1, source_target_pairs={{0,8},{8,16},{16,24},{24,0},{1,9},{9,17},{17,25},{25,1},{2,10},{10... | collective-permute-start | bytes 1376264 | tf_op jit(solution)/shard_map/ppermute | solution.py:551
  7.7 2.3 %collective-permute-start.1 = (f32[304,512]{1,0:T(8,128)S(1)}, f32[304,512]{1,0:T(8,128)S(1)}, u32[]{:S(2)}, u32[]{:S(2)}) collective-permute-start(f32[304,512]{1,0:T(8,128)S(1)} %get-tuple-element.55), channel_id=1, source_target_pairs={{0,7},{1,0},{2,1},{3,2},{4,3},{5,4},{6,5},{7,6},{8,15},{9,8},{10,9... | collective-permute-start | bytes 1867784 | tf_op jit(solution)/shard_map/ppermute | solution.py:551
  10.9 1.1 %shard_map.56 = (f32[2,64,256]{2,1,0:T(8,128)S(1)}, f32[4,56,512]{2,1,0:T(8,128)S(1)}) custom-call(f32[4,128,512]{2,1,0:T(8,128)S(1)} %get-tuple-element.48.k_ref, f32[4,128,512]{2,1,0:T(8,128)} %i_ref.3), custom_call_target="tpu_custom_call" | custom-call | tf_op jit(solution)/shard_map/pallas_call | solution.py:44
  12.0 8.2 %collective-permute-done.4.r_ref = f32[4,56,512]{2,1,0:T(8,128)S(1)} collective-permute-done((f32[4,56,512]{2,1,0:T(8,128)S(1)}, f32[4,56,512]{2,1,0:T(8,128)S(1)}, u32[]{:S(2)}, u32[]{:S(2)}) %collective-permute-start.4) | collective-permute-done | bytes 458784 | tf_op jit(solution)/shard_map/ppermute | solution.py:551
  21.3 2.0 %collective-permute-start.6 = (f32[144,512]{1,0:T(8,128)S(1)}, f32[144,512]{1,0:T(8,128)S(1)}, u32[]{:S(2)}, u32[]{:S(2)}) collective-permute-start(f32[144,512]{1,0:T(8,128)S(1)} %get-tuple-element.65), channel_id=1, source_target_pairs={{0,7},{1,0},{2,1},{3,2},{4,3},{5,4},{6,5},{7,6},{8,15},{9,8},{10,9... | collective-permute-start | bytes 884744 | tf_op jit(solution)/shard_map/ppermute | solution.py:551
  24.7 2.6 %collective-permute-start.3 = (f32[176,512]{1,0:T(8,128)S(1)}, f32[176,512]{1,0:T(8,128)S(1)}, u32[]{:S(2)}, u32[]{:S(2)}) collective-permute-start(f32[176,512]{1,0:T(8,128)S(1)} %get-tuple-element.58), channel_id=1, source_target_pairs={{0,7},{1,0},{2,1},{3,2},{4,3},{5,4},{6,5},{7,6},{8,15},{9,8},{10,9... | collective-permute-start | bytes 1081352 | tf_op jit(solution)/shard_map/ppermute | solution.py:551
  28.1 2.6 %collective-permute-done.6.refs_4_.refs_5_.hi = f32[144,512]{1,0:T(8,128)S(1)} collective-permute-done((f32[144,512]{1,0:T(8,128)S(1)}, f32[144,512]{1,0:T(8,128)S(1)}, u32[]{:S(2)}, u32[]{:S(2)}) %collective-permute-start.6) | collective-permute-done | bytes 294944 | tf_op jit(solution)/shard_map/ppermute | solution.py:551
  31.3 1.6 %collective-permute-start.7 = (f32[112,512]{1,0:T(8,128)S(1)}, f32[112,512]{1,0:T(8,128)S(1)}, u32[]{:S(2)}, u32[]{:S(2)}) collective-permute-start(f32[112,512]{1,0:T(8,128)S(1)} %get-tuple-element.68), channel_id=1, source_target_pairs={{0,1},{1,2},{2,3},{3,4},{4,5},{5,6},{6,7},{7,0},{8,9},{9,10},{10,1... | collective-permute-start | bytes 688136 | tf_op jit(solution)/shard_map/ppermute | solution.py:551
  32.9 1.3 %collective-permute-start.8 = (f32[112,512]{1,0:T(8,128)S(1)}, f32[112,512]{1,0:T(8,128)S(1)}, u32[]{:S(2)}, u32[]{:S(2)}) collective-permute-start(f32[112,512]{1,0:T(8,128)S(1)} %get-tuple-element.69), channel_id=1, source_target_pairs={{0,7},{1,0},{2,1},{3,2},{4,3},{5,4},{6,5},{7,6},{8,15},{9,8},{10,9... | collective-permute-start | bytes 688136 | tf_op jit(solution)/shard_map/ppermute | solution.py:551
  34.7 2.5 %collective-permute-start.9 = (f32[2,64,256]{2,1,0:T(8,128)S(1)}, f32[2,64,256]{2,1,0:T(8,128)S(1)}, u32[]{:S(2)}, u32[]{:S(2)}) collective-permute-start(f32[2,64,256]{2,1,0:T(8,128)S(1)} %shard_map.63.own_ref), channel_id=1, source_target_pairs={{0,24},{8,0},{16,8},{24,16},{1,25},{9,1},{17,9},{25,17},{2,26},{10... | collective-permute-start | bytes 393224 | tf_op jit(solution)/shard_map/ppermute | solution.py:551
  38.4 1.1 %shard_map.55 = (f32[4,80,512]{2,1,0:T(8,128)S(1)}, f32[2,40,256]{2,1,0:T(8,128)S(1)}) custom-call(f32[4,88,512]{2,1,0:T(8,128)S(1)} %get-tuple-element.56.v_ref, f32[4,88,512]{2,1,0:T(8,128)S(1)} %shard_map.54.part, f32[4,128,512]{2,1,0:T(8,128)S(1)} %get-tuple-element.48.k_ref, f32[304,512]{1,0:T(8,128)S(1)} %collective-permute-done.refs_0_.refs_2_.refs_3_.refs_6_, ...), custom_call_target="tpu_custom_call" | custom-call | tf_op jit(solution)/shard_map/pallas_call | solution.py:44
  39.5 1.8 %collective-permute-done.7.refs_2_.refs_3_ = f32[112,512]{1,0:T(8,128)S(1)} collective-permute-done((f32[112,512]{1,0:T(8,128)S(1)}, f32[112,512]{1,0:T(8,128)S(1)}, u32[]{:S(2)}, u32[]{:S(2)}) %collective-permute-start.7) | collective-permute-done | bytes 229408 | tf_op jit(solution)/shard_map/ppermute | solution.py:551
  42.9 1.9 %collective-permute-start.10 = (f32[2,64,256]{2,1,0:T(8,128)S(1)}, f32[2,64,256]{2,1,0:T(8,128)S(1)}, u32[]{:S(2)}, u32[]{:S(2)}) collective-permute-start(f32[2,64,256]{2,1,0:T(8,128)S(1)} %shard_map.64.a_ref), channel_id=1, source_target_pairs={{0,24},{8,0},{16,8},{24,16},{1,25},{9,1},{17,9},{25,17},{2,26},{10... | collective-permute-start | bytes 393224 | tf_op jit(solution)/shard_map/ppermute | solution.py:551
  44.8 3.7 %collective-permute-done.10.b_ref.refs_5_ = f32[2,64,256]{2,1,0:T(8,128)S(1)} collective-permute-done((f32[2,64,256]{2,1,0:T(8,128)S(1)}, f32[2,64,256]{2,1,0:T(8,128)S(1)}, u32[]{:S(2)}, u32[]{:S(2)}) %collective-permute-start.10) | collective-permute-done | bytes 131104 | tf_op jit(solution)/shard_map/ppermute | solution.py:551
  48.7 1.7 %collective-permute-start.11 = (f32[128,256]{1,0:T(8,128)S(1)}, f32[128,256]{1,0:T(8,128)S(1)}, u32[]{:S(2)}, u32[]{:S(2)}) collective-permute-start(f32[128,256]{1,0:T(8,128)S(1)} %get-tuple-element.75), channel_id=1, source_target_pairs={{0,1},{2,3},{4,5},{6,7},{1,0},{3,2},{5,4},{7,6},{8,9},{10,11},{12,... | collective-permute-start | bytes 393224 | tf_op jit(solution)/shard_map/ppermute | solution.py:561
  50.4 2.3 %collective-permute-start.12 = (f32[128,256]{1,0:T(8,128)S(1)}, f32[128,256]{1,0:T(8,128)S(1)}, u32[]{:S(2)}, u32[]{:S(2)}) collective-permute-start(f32[128,256]{1,0:T(8,128)S(1)} %get-tuple-element.76), channel_id=1, source_target_pairs={{1,2},{3,4},{5,6},{7,0},{2,1},{4,3},{6,5},{0,7},{9,10},{11,12},{13... | collective-permute-start | bytes 393224 | tf_op jit(solution)/shard_map/ppermute | solution.py:561
  52.7 5.9 %collective-permute-done.13 = f32[2,24,256]{2,1,0:T(8,128)S(1)} collective-permute-done((f32[2,24,256]{2,1,0:T(8,128)S(1)}, f32[2,24,256]{2,1,0:T(8,128)S(1)}, u32[]{:S(2)}, u32[]{:S(2)}) %collective-permute-start.13) | collective-permute-done | bytes 49184 | tf_op jit(solution)/shard_map/ppermute | solution.py:551
  59.1 1.5 %collective-permute-start.17 = (f32[128,256]{1,0:T(8,128)S(1)}, f32[128,256]{1,0:T(8,128)S(1)}, u32[]{:S(2)}, u32[]{:S(2)}) collective-permute-start(f32[128,256]{1,0:T(8,128)S(1)} %get-tuple-element.85), channel_id=1, source_target_pairs={{1,2},{3,4},{5,6},{7,0},{2,1},{4,3},{6,5},{0,7},{9,10},{11,12},{13... | collective-permute-start | bytes 393224 | tf_op jit(solution)/shard_map/ppermute | solution.py:561
  60.6 4.7 %collective-permute-done.17.off_ref = f32[128,256]{1,0:T(8,128)S(1)} collective-permute-done((f32[128,256]{1,0:T(8,128)S(1)}, f32[128,256]{1,0:T(8,128)S(1)}, u32[]{:S(2)}, u32[]{:S(2)}) %collective-permute-start.17) | collective-permute-done | bytes 131104 | tf_op jit(solution)/shard_map/ppermute | solution.py:561
  66.9 4.5 %collective-permute-done.19.off_ref = f32[128,256]{1,0:T(8,128)S(1)} collective-permute-done((f32[128,256]{1,0:T(8,128)S(1)}, f32[128,256]{1,0:T(8,128)S(1)}, u32[]{:S(2)}, u32[]{:S(2)}) %collective-permute-start.19) | collective-permute-done | bytes 131104 | tf_op jit(solution)/shard_map/ppermute | solution.py:561
  71.6 3.7 %collective-permute-done.15.moved_ref = f32[4,80,512]{2,1,0:T(8,128)S(1)} collective-permute-done((f32[4,80,512]{2,1,0:T(8,128)S(1)}, f32[4,80,512]{2,1,0:T(8,128)S(1)}, u32[]{:S(2)}, u32[]{:S(2)}) %collective-permute-start.15) | collective-permute-done | bytes 655392 | tf_op jit(solution)/shard_map/ppermute | solution.py:551
  75.3 2.0 %shard_map.69 = (f32[4,128,512]{2,1,0:T(8,128)}, f32[2,64,256]{2,1,0:T(8,128)}) custom-call(f32[4,80,512]{2,1,0:T(8,128)S(1)} %collective-permute-done.15.moved_ref, f32[4,48,512]{2,1,0:T(8,128)S(1)} %get-tuple-element.79.own_ref, f32[4,128,512]{2,1,0:T(8,128)S(1)} %bitcast.6, f32[2,64,256]{2,1,0:T(8,128)S(1)} %shard_map.68.e_ref), custom_call_target="tpu_custom_call" | custom-call | tf_op jit(solution)/shard_map/pallas_call | solution.py:44
  (41 shorter events, 10.9 us)
Async XLA Ops:
  3.4 16.8 %collective-permute-start = (f32[304,512]{1,0:T(8,128)S(1)}, f32[304,512]{1,0:T(8,128)S(1)}, u32[]{:S(2)}, u32[]{:S(2)}) collective-permute-start(f32[304,512]{1,0:T(8,128)S(1)} %get-tuple-element.54), channel_id=1, source_target_pairs={{0,1},{1,2},{2,3},{3,4},{4,5},{5,6},{6,7},{7,0},{8,9},{9,10},{10,1... | collective-permute-start | bytes 1867784 | tf_op jit(solution)/shard_map/ppermute | solution.py:551
  5.0 15.1 %collective-permute-start.4 = (f32[4,56,512]{2,1,0:T(8,128)S(1)}, f32[4,56,512]{2,1,0:T(8,128)S(1)}, u32[]{:S(2)}, u32[]{:S(2)}) collective-permute-start(f32[4,56,512]{2,1,0:T(8,128)S(1)} %shard_map.57), channel_id=1, source_target_pairs={{0,8},{8,16},{16,24},{24,0},{1,9},{9,17},{17,25},{25,1},{2,10},{10... | collective-permute-start | bytes 1376264 | tf_op jit(solution)/shard_map/ppermute | solution.py:551
  7.7 16.1 %collective-permute-start.1 = (f32[304,512]{1,0:T(8,128)S(1)}, f32[304,512]{1,0:T(8,128)S(1)}, u32[]{:S(2)}, u32[]{:S(2)}) collective-permute-start(f32[304,512]{1,0:T(8,128)S(1)} %get-tuple-element.55), channel_id=1, source_target_pairs={{0,7},{1,0},{2,1},{3,2},{4,3},{5,4},{6,5},{7,6},{8,15},{9,8},{10,9... | collective-permute-start | bytes 1867784 | tf_op jit(solution)/shard_map/ppermute | solution.py:551
  20.5 7.6 %collective-permute-start.5 = (f32[144,512]{1,0:T(8,128)S(1)}, f32[144,512]{1,0:T(8,128)S(1)}, u32[]{:S(2)}, u32[]{:S(2)}) collective-permute-start(f32[144,512]{1,0:T(8,128)S(1)} %get-tuple-element.64), channel_id=1, source_target_pairs={{0,1},{1,2},{2,3},{3,4},{4,5},{5,6},{6,7},{7,0},{8,9},{9,10},{10,1... | collective-permute-start | bytes 884744 | tf_op jit(solution)/shard_map/ppermute | solution.py:551
  21.3 9.4 %collective-permute-start.6 = (f32[144,512]{1,0:T(8,128)S(1)}, f32[144,512]{1,0:T(8,128)S(1)}, u32[]{:S(2)}, u32[]{:S(2)}) collective-permute-start(f32[144,512]{1,0:T(8,128)S(1)} %get-tuple-element.65), channel_id=1, source_target_pairs={{0,7},{1,0},{2,1},{3,2},{4,3},{5,4},{6,5},{7,6},{8,15},{9,8},{10,9... | collective-permute-start | bytes 884744 | tf_op jit(solution)/shard_map/ppermute | solution.py:551
  24.7 13.5 %collective-permute-start.2 = (f32[176,512]{1,0:T(8,128)S(1)}, f32[176,512]{1,0:T(8,128)S(1)}, u32[]{:S(2)}, u32[]{:S(2)}) collective-permute-start(f32[176,512]{1,0:T(8,128)S(1)} %get-tuple-element.57), channel_id=1, source_target_pairs={{0,1},{1,2},{2,3},{3,4},{4,5},{5,6},{6,7},{7,0},{8,9},{9,10},{10,1... | collective-permute-start | bytes 1081352 | tf_op jit(solution)/shard_map/ppermute | solution.py:551
  24.7 13.7 %collective-permute-start.3 = (f32[176,512]{1,0:T(8,128)S(1)}, f32[176,512]{1,0:T(8,128)S(1)}, u32[]{:S(2)}, u32[]{:S(2)}) collective-permute-start(f32[176,512]{1,0:T(8,128)S(1)} %get-tuple-element.58), channel_id=1, source_target_pairs={{0,7},{1,0},{2,1},{3,2},{4,3},{5,4},{6,5},{7,6},{8,15},{9,8},{10,9... | collective-permute-start | bytes 1081352 | tf_op jit(solution)/shard_map/ppermute | solution.py:551
  30.7 3.5 %copy-start = (f32[1,4,128,512]{3,2,1,0:T(8,128)S(1)}, f32[1,4,128,512]{3,2,1,0:T(8,128)}, u32[]{:S(2)}) copy-start(f32[1,4,128,512]{3,2,1,0:T(8,128)} %param.4) | copy-start | bytes 3145732
  31.3 10.0 %collective-permute-start.7 = (f32[112,512]{1,0:T(8,128)S(1)}, f32[112,512]{1,0:T(8,128)S(1)}, u32[]{:S(2)}, u32[]{:S(2)}) collective-permute-start(f32[112,512]{1,0:T(8,128)S(1)} %get-tuple-element.68), channel_id=1, source_target_pairs={{0,1},{1,2},{2,3},{3,4},{4,5},{5,6},{6,7},{7,0},{8,9},{9,10},{10,1... | collective-permute-start | bytes 688136 | tf_op jit(solution)/shard_map/ppermute | solution.py:551
  32.9 9.1 %collective-permute-start.8 = (f32[112,512]{1,0:T(8,128)S(1)}, f32[112,512]{1,0:T(8,128)S(1)}, u32[]{:S(2)}, u32[]{:S(2)}) collective-permute-start(f32[112,512]{1,0:T(8,128)S(1)} %get-tuple-element.69), channel_id=1, source_target_pairs={{0,7},{1,0},{2,1},{3,2},{4,3},{5,4},{6,5},{7,6},{8,15},{9,8},{10,9... | collective-permute-start | bytes 688136 | tf_op jit(solution)/shard_map/ppermute | solution.py:551
  34.7 8.2 %collective-permute-start.9 = (f32[2,64,256]{2,1,0:T(8,128)S(1)}, f32[2,64,256]{2,1,0:T(8,128)S(1)}, u32[]{:S(2)}, u32[]{:S(2)}) collective-permute-start(f32[2,64,256]{2,1,0:T(8,128)S(1)} %shard_map.63.own_ref), channel_id=1, source_target_pairs={{0,24},{8,0},{16,8},{24,16},{1,25},{9,1},{17,9},{25,17},{2,26},{10... | collective-permute-start | bytes 393224 | tf_op jit(solution)/shard_map/ppermute | solution.py:551
  42.9 5.7 %collective-permute-start.10 = (f32[2,64,256]{2,1,0:T(8,128)S(1)}, f32[2,64,256]{2,1,0:T(8,128)S(1)}, u32[]{:S(2)}, u32[]{:S(2)}) collective-permute-start(f32[2,64,256]{2,1,0:T(8,128)S(1)} %shard_map.64.a_ref), channel_id=1, source_target_pairs={{0,24},{8,0},{16,8},{24,16},{1,25},{9,1},{17,9},{25,17},{2,26},{10... | collective-permute-start | bytes 393224 | tf_op jit(solution)/shard_map/ppermute | solution.py:551
  44.8 13.9 %collective-permute-start.14 = (f32[2,64,256]{2,1,0:T(8,128)S(1)}, f32[2,64,256]{2,1,0:T(8,128)S(1)}, u32[]{:S(2)}, u32[]{:S(2)}) collective-permute-start(f32[2,64,256]{2,1,0:T(8,128)S(1)} %shard_map.64.a_ref), channel_id=1, source_target_pairs={{0,16},{8,24},{16,0},{24,8},{1,17},{9,25},{17,1},{25,9},{2,18},{10... | collective-permute-start | bytes 393224 | tf_op jit(solution)/shard_map/ppermute | solution.py:551
  48.7 10.0 %collective-permute-start.11 = (f32[128,256]{1,0:T(8,128)S(1)}, f32[128,256]{1,0:T(8,128)S(1)}, u32[]{:S(2)}, u32[]{:S(2)}) collective-permute-start(f32[128,256]{1,0:T(8,128)S(1)} %get-tuple-element.75), channel_id=1, source_target_pairs={{0,1},{2,3},{4,5},{6,7},{1,0},{3,2},{5,4},{7,6},{8,9},{10,11},{12,... | collective-permute-start | bytes 393224 | tf_op jit(solution)/shard_map/ppermute | solution.py:561
  50.4 8.2 %collective-permute-start.12 = (f32[128,256]{1,0:T(8,128)S(1)}, f32[128,256]{1,0:T(8,128)S(1)}, u32[]{:S(2)}, u32[]{:S(2)}) collective-permute-start(f32[128,256]{1,0:T(8,128)S(1)} %get-tuple-element.76), channel_id=1, source_target_pairs={{1,2},{3,4},{5,6},{7,0},{2,1},{4,3},{6,5},{0,7},{9,10},{11,12},{13... | collective-permute-start | bytes 393224 | tf_op jit(solution)/shard_map/ppermute | solution.py:561
  52.7 5.9 %collective-permute-start.13 = (f32[2,24,256]{2,1,0:T(8,128)S(1)}, f32[2,24,256]{2,1,0:T(8,128)S(1)}, u32[]{:S(2)}, u32[]{:S(2)}) collective-permute-start(f32[2,24,256]{2,1,0:T(8,128)S(1)} %slice.8), channel_id=1, source_target_pairs={{0,8},{8,16},{16,24},{24,0},{1,9},{9,17},{17,25},{25,1},{2,10},{10... | collective-permute-start | bytes 147464 | tf_op jit(solution)/shard_map/ppermute | solution.py:551
  58.6 16.6 %collective-permute-start.15 = (f32[4,80,512]{2,1,0:T(8,128)S(1)}, f32[4,80,512]{2,1,0:T(8,128)S(1)}, u32[]{:S(2)}, u32[]{:S(2)}) collective-permute-start(f32[4,80,512]{2,1,0:T(8,128)S(1)} %get-tuple-element.78), channel_id=1, source_target_pairs={{0,8},{8,16},{16,24},{24,0},{1,9},{9,17},{17,25},{25,1},{2,10},{10... | collective-permute-start | bytes 1966088 | tf_op jit(solution)/shard_map/ppermute | solution.py:551
  59.0 1.6 %collective-permute-start.16 = (f32[128,256]{1,0:T(8,128)S(1)}, f32[128,256]{1,0:T(8,128)S(1)}, u32[]{:S(2)}, u32[]{:S(2)}) collective-permute-start(f32[128,256]{1,0:T(8,128)S(1)} %get-tuple-element.84), channel_id=1, source_target_pairs={{0,1},{2,3},{4,5},{6,7},{1,0},{3,2},{5,4},{7,6},{8,9},{10,11},{12,... | collective-permute-start | bytes 393224 | tf_op jit(solution)/shard_map/ppermute | solution.py:561
  59.1 6.2 %collective-permute-start.17 = (f32[128,256]{1,0:T(8,128)S(1)}, f32[128,256]{1,0:T(8,128)S(1)}, u32[]{:S(2)}, u32[]{:S(2)}) collective-permute-start(f32[128,256]{1,0:T(8,128)S(1)} %get-tuple-element.85), channel_id=1, source_target_pairs={{1,2},{3,4},{5,6},{7,0},{2,1},{4,3},{6,5},{0,7},{9,10},{11,12},{13... | collective-permute-start | bytes 393224 | tf_op jit(solution)/shard_map/ppermute | solution.py:561
  65.5 1.4 %collective-permute-start.18 = (f32[128,256]{1,0:T(8,128)S(1)}, f32[128,256]{1,0:T(8,128)S(1)}, u32[]{:S(2)}, u32[]{:S(2)}) collective-permute-start(f32[128,256]{1,0:T(8,128)S(1)} %get-tuple-element.88), channel_id=1, source_target_pairs={{0,1},{2,3},{4,5},{6,7},{1,0},{3,2},{5,4},{7,6},{8,9},{10,11},{12,... | collective-permute-start | bytes 393224 | tf_op jit(solution)/shard_map/ppermute | solution.py:561
  65.6 5.9 %collective-permute-start.19 = (f32[128,256]{1,0:T(8,128)S(1)}, f32[128,256]{1,0:T(8,128)S(1)}, u32[]{:S(2)}, u32[]{:S(2)}) collective-permute-start(f32[128,256]{1,0:T(8,128)S(1)} %get-tuple-element.89), channel_id=1, source_target_pairs={{1,2},{3,4},{5,6},{7,0},{2,1},{4,3},{6,5},{0,7},{9,10},{11,12},{13... | collective-permute-start | bytes 393224 | tf_op jit(solution)/shard_map/ppermute | solution.py:561

commit v7 on v6

--- a/solution.py
+++ b/solution.py
@@ -35,7 +35,7 @@
     return Here(t, t == 0, t == times - 1, s > 0, s < blocks - 1, lax.rem(s, 2) == 0)
 
 
-def call(body, out_shapes, operands, specs=None, scratch=(), out_specs=None):
+def call(body, out_shapes, operands, specs=None, scratch=(), out_specs=None, aliases=None):
     operands = list(operands)
     specs = specs or [VMEM] * len(operands)
     operands = [
@@ -47,6 +47,7 @@
         in_specs=specs,
         out_specs=out_specs or [VMEM] * len(out_shapes),
         scratch_shapes=list(scratch),
+        input_output_aliases=aliases or {},
         compiler_params=pltpu.CompilerParams(vmem_limit_bytes=8 * 1024 * 1024),
     )(*operands)
 
@@ -510,40 +511,78 @@
     return call(body, [own_prior.shape], [moved, own, next_prior, own_prior])[0]
 
 
-def finish(moved, own, prior, correction):
+def prolonged(e_ref, rows, q, spread, wide):
+    row = dot3(e_ref[q, rows], spread)
+    count = row.shape[0]
+    for b in range(wide.shape[0]):
+        s = slice(b * LANES, (b + 1) * LANES)
+        wide[b, pl.ds(0, count, 2), :] = row[:, s]
+        wide[b, pl.ds(1, count, 2), :] = row[:, s]
+
+
+def finish_lower(fine, coarse, prior, correction):
     nx, ny, nz = prior.shape
-    rows = moved.shape[1]
-
-    def body(moved_ref, own_ref, p_ref, e_ref, update, tail, out, wide, upper, lower, sems):
-        parts = ((moved_ref, slice(0, rows), upper), (own_ref, slice(rows, ny), lower))
+    rows = fine.shape[1]
+    cut = ny - rows
+
+    def body(f_ref, c_ref, p_ref, e_ref, update, tail, rest, out, tail_out, upper, lower, sems):
         spread = repeat_matrix(nz // 2, nz)
         copies = []
         for q in range(nx // 2):
-            row = dot3(e_ref[q], spread)
-            for b in range(nz // LANES):
-                s = slice(b * LANES, (b + 1) * LANES)
-                wide[b, pl.ds(0, ny // 2, 2), :] = row[:, s]
-                wide[b, pl.ds(1, ny // 2, 2), :] = row[:, s]
+            tail_out[q] = e_ref[q, cut // 2:] + c_ref[q]
+            copies.append(pltpu.make_async_copy(
+                tail_out.at[q], tail.at[q, pl.ds(cut // 2, rows // 2)], sems.at[nx + q]))
+            copies[-1].start()
+        for q in range(nx // 2):
+            prolonged(e_ref, slice(cut // 2, ny // 2), q, spread, lower)
             for p in (2 * q, 2 * q + 1):
-                for ref, r, _ in parts:
-                    for b in range(nz // LANES):
-                        s = slice(b * LANES, (b + 1) * LANES)
-                        out[p, r, s] = (ref[p, :, s] + wide[b, r]) - p_ref[p, r, s]
-                copies.append(pltpu.make_async_copy(out.at[p], update.at[p], sems.at[p]))
+                for b in range(nz // LANES):
+                    s = slice(b * LANES, (b + 1) * LANES)
+                    out[p, :, s] = (f_ref[p, :, s] + lower[b]) - p_ref[p, cut:, s]
+                copies.append(pltpu.make_async_copy(out.at[p], update.at[p, pl.ds(cut, rows)], sems.at[p]))
                 copies[-1].start()
+        for q in range(nx // 2):
+            prolonged(e_ref, slice(0, cut // 2), q, spread, upper)
+            for p in (2 * q, 2 * q + 1):
+                for b in range(nz // LANES):
+                    s = slice(b * LANES, (b + 1) * LANES)
+                    rest[p, :, s] = upper[b] - p_ref[p, :cut, s]
+        for c in copies:
+            c.wait()
+
+    return call(
+        body, [prior.shape, correction.shape, (nx, cut, nz)], [fine, coarse, prior, correction],
+        scratch=[pltpu.VMEM(fine.shape, F32), pltpu.VMEM(coarse.shape, F32), lane_scratch(cut, nz),
+                 lane_scratch(rows, nz), pltpu.SemaphoreType.DMA((nx + nx // 2,))],
+        out_specs=[HBM, HBM, VMEM])
+
+
+def finish_upper(fine, correction, rest, update, tail):
+    nx, rows, nz = fine.shape
+
+    def body(f_ref, e_ref, rest_ref, *refs):
+        update, tail, out, tail_out, scratch, sems = refs[2:]
+        copies = []
+        for p in range(nx):
+            for a in range(0, rows, TILE):
+                s = slice(a, a + TILE)
+                out[p, s] = f_ref[p, s] + rest_ref[p, s]
+            copies.append(pltpu.make_async_copy(out.at[p], update.at[p, pl.ds(0, rows)], sems.at[p]))
+            copies[-1].start()
         matrix = pair_matrix(nz, nz // 2, 0.125)
         for q in range(nx // 2):
-            for ref, r, scratch in parts:
-                c = slice(r.start // 2, r.stop // 2)
-                tail[q, c] = e_ref[q, c] + restrict_planes(ref[2 * q], ref[2 * q + 1], scratch, matrix)
+            tail_out[q] = e_ref[q, :rows // 2] + restrict_planes(f_ref[2 * q], f_ref[2 * q + 1], scratch, matrix)
+            copies.append(pltpu.make_async_copy(tail_out.at[q], tail.at[q, pl.ds(0, rows // 2)], sems.at[nx + q]))
+            copies[-1].start()
         for c in copies:
             c.wait()
 
     return call(
-        body, [prior.shape, correction.shape], [moved, own, prior, correction],
-        scratch=[pltpu.VMEM(prior.shape, F32), lane_scratch(ny, nz), lane_scratch(rows, nz // 2),
-                 lane_scratch(ny - rows, nz // 2), pltpu.SemaphoreType.DMA((nx,))],
-        out_specs=[HBM, VMEM])
+        body, [update.shape, tail.shape], [fine, correction, rest, update, tail],
+        [VMEM] * 3 + [HBM] * 2,
+        [pltpu.VMEM(fine.shape, F32), pltpu.VMEM((nx // 2, rows // 2, nz // 2), F32), lane_scratch(rows, nz // 2),
+         pltpu.SemaphoreType.DMA((nx + nx // 2,))],
+        [HBM, HBM], {3: 0, 4: 1})
 
 
 def ring(block, axis, distance):
@@ -616,7 +655,8 @@
             moved = ring(moved, "tm", 1)
         more = (shifted[j + 1:j + 3], home - j - 1) if j < home - 1 else ()
         sweep = sweep_step(state, part, on, off, half_cut, coarse_coef, *more)
-    update, tail = finish(moved, own_fine, own_prior, sweep[0])
+    update, tail, rest = finish_lower(own_fine, fine_coarse, own_prior, sweep[0])
+    update, tail = finish_upper(moved, sweep[0], rest, update, tail)
     return update[None], tail[None]
 
 

time: 77.5 us -> 76.7 us (0.990)
  waiting for transfers between devices: 37.2 us -> 36 us
    ppermute x14, waiting for transfers between devices: 27.6 us -> 26.4 us  [ring(): lax.ppermute(block, axis, [(i, (i + distance) % size) for i in range(size)])]
    pallas_call x20 -> x21, Pallas kernels: 14.4 us -> 14.7 us  [call(): pl.pallas_call(body, out_shape=[jax.ShapeDtypeStruct(s, F32) for s in out...]
  transfers between devices with their start and end apart: 20 -> 20, of which waited for: 12 -> 12; matrix products, arithmetic and copies ran while one was open for 0% -> 0% of each run, Pallas kernels for 12% -> 14%
where the time goes in v7:
time: 76.7 us; the launch traced here: 76.5 us
  waiting for transfers between devices  36 us (47%)
  starting transfers between devices  24.9 us (32%)
  Pallas kernels  14.7 us (19%)
  between operations  0.86 us (1%)
    ppermute x14, waiting for transfers between devices, ring(): lax.ppermute(block, axis, [(i, (i + distance) % size) for i in range(size)])  26.4 us
    ppermute x14, starting transfers between devices, ring(): lax.ppermute(block, axis, [(i, (i + distance) % size) for i in range(size)])  18.3 us
    pallas_call x21, Pallas kernels, call(): pl.pallas_call(body, out_shape=[jax.ShapeDtypeStruct(s, F32) for s in out...  14.7 us
    ppermute x6, waiting for transfers between devices, swapped(): return lax.ppermute(block, axis, pairs + [(j, i) for i, j in pairs])  9.57 us
    ppermute x6, starting transfers between devices, swapped(): return lax.ppermute(block, axis, pairs + [(j, i) for i, j in pairs])  6.62 us
  transfers between devices with their start and end apart: 20, of which 12 were waited for; matrix products, arithmetic and copies ran while one was open for 0% of the time, Pallas kernels for 14%

profile of v7, /device:TPU:0, one launch (start us, length us, event | category | flops | bytes accessed | tf_op | source)
XLA Modules:
  0.0 76.5 jit_solution(13821810435945095602)
XLA Ops:
  0.6 2.8 %shard_map.50 = (f32[4,128,512]{2,1,0:T(8,128)S(1)}, f32[4,88,512]{2,1,0:T(8,128)S(1)}, f32[304,512]{1,0:T(8,128)S(1)}, f32[304,512]{1,0:T(8,128)S(1)}) custom-call(f32[4,128,512]{2,1,0:T(8,128)} %i_ref.3, f32[4,128,512]{2,1,0:T(8,128)} %bitcast.3, f32[4,128,512]{2,1,0:T(8,128)} %k_hbm.1), custom_call_target="tpu_custom_call" | custom-call | tf_op jit(solution)/shard_map/pallas_call | solution.py:44
  3.9 1.1 %shard_map.57 = f32[4,56,512]{2,1,0:T(8,128)S(1)} custom-call(f32[4,128,512]{2,1,0:T(8,128)} %bitcast.4), custom_call_target="tpu_custom_call" | custom-call | tf_op jit(solution)/shard_map/pallas_call | solution.py:44
  5.0 2.6 %collective-permute-start.4 = (f32[4,56,512]{2,1,0:T(8,128)S(1)}, f32[4,56,512]{2,1,0:T(8,128)S(1)}, u32[]{:S(2)}, u32[]{:S(2)}) collective-permute-start(f32[4,56,512]{2,1,0:T(8,128)S(1)} %shard_map.57), channel_id=1, source_target_pairs={{0,8},{8,16},{16,24},{24,0},{1,9},{9,17},{17,25},{25,1},{2,10},{10... | collective-permute-start | bytes 1376264 | tf_op jit(solution)/shard_map/ppermute | solution.py:590
  7.7 2.3 %collective-permute-start.1 = (f32[304,512]{1,0:T(8,128)S(1)}, f32[304,512]{1,0:T(8,128)S(1)}, u32[]{:S(2)}, u32[]{:S(2)}) collective-permute-start(f32[304,512]{1,0:T(8,128)S(1)} %get-tuple-element.58), channel_id=1, source_target_pairs={{0,7},{1,0},{2,1},{3,2},{4,3},{5,4},{6,5},{7,6},{8,15},{9,8},{10,9... | collective-permute-start | bytes 1867784 | tf_op jit(solution)/shard_map/ppermute | solution.py:590
  10.9 1.1 %shard_map.56 = (f32[2,64,256]{2,1,0:T(8,128)S(1)}, f32[4,56,512]{2,1,0:T(8,128)S(1)}) custom-call(f32[4,128,512]{2,1,0:T(8,128)S(1)} %get-tuple-element.51.k_ref, f32[4,128,512]{2,1,0:T(8,128)} %i_ref.3), custom_call_target="tpu_custom_call" | custom-call | tf_op jit(solution)/shard_map/pallas_call | solution.py:44
  12.0 8.2 %collective-permute-done.4.r_ref = f32[4,56,512]{2,1,0:T(8,128)S(1)} collective-permute-done((f32[4,56,512]{2,1,0:T(8,128)S(1)}, f32[4,56,512]{2,1,0:T(8,128)S(1)}, u32[]{:S(2)}, u32[]{:S(2)}) %collective-permute-start.4) | collective-permute-done | bytes 458784 | tf_op jit(solution)/shard_map/ppermute | solution.py:590
  21.3 2.0 %collective-permute-start.6 = (f32[144,512]{1,0:T(8,128)S(1)}, f32[144,512]{1,0:T(8,128)S(1)}, u32[]{:S(2)}, u32[]{:S(2)}) collective-permute-start(f32[144,512]{1,0:T(8,128)S(1)} %get-tuple-element.68), channel_id=1, source_target_pairs={{0,7},{1,0},{2,1},{3,2},{4,3},{5,4},{6,5},{7,6},{8,15},{9,8},{10,9... | collective-permute-start | bytes 884744 | tf_op jit(solution)/shard_map/ppermute | solution.py:590
  24.7 2.6 %collective-permute-start.3 = (f32[176,512]{1,0:T(8,128)S(1)}, f32[176,512]{1,0:T(8,128)S(1)}, u32[]{:S(2)}, u32[]{:S(2)}) collective-permute-start(f32[176,512]{1,0:T(8,128)S(1)} %get-tuple-element.61), channel_id=1, source_target_pairs={{0,7},{1,0},{2,1},{3,2},{4,3},{5,4},{6,5},{7,6},{8,15},{9,8},{10,9... | collective-permute-start | bytes 1081352 | tf_op jit(solution)/shard_map/ppermute | solution.py:590
  28.1 2.6 %collective-permute-done.6.refs_4_.refs_5_.hi = f32[144,512]{1,0:T(8,128)S(1)} collective-permute-done((f32[144,512]{1,0:T(8,128)S(1)}, f32[144,512]{1,0:T(8,128)S(1)}, u32[]{:S(2)}, u32[]{:S(2)}) %collective-permute-start.6) | collective-permute-done | bytes 294944 | tf_op jit(solution)/shard_map/ppermute | solution.py:590
  31.3 1.6 %collective-permute-start.7 = (f32[112,512]{1,0:T(8,128)S(1)}, f32[112,512]{1,0:T(8,128)S(1)}, u32[]{:S(2)}, u32[]{:S(2)}) collective-permute-start(f32[112,512]{1,0:T(8,128)S(1)} %get-tuple-element.71), channel_id=1, source_target_pairs={{0,1},{1,2},{2,3},{3,4},{4,5},{5,6},{6,7},{7,0},{8,9},{9,10},{10,1... | collective-permute-start | bytes 688136 | tf_op jit(solution)/shard_map/ppermute | solution.py:590
  32.9 1.3 %collective-permute-start.8 = (f32[112,512]{1,0:T(8,128)S(1)}, f32[112,512]{1,0:T(8,128)S(1)}, u32[]{:S(2)}, u32[]{:S(2)}) collective-permute-start(f32[112,512]{1,0:T(8,128)S(1)} %get-tuple-element.72), channel_id=1, source_target_pairs={{0,7},{1,0},{2,1},{3,2},{4,3},{5,4},{6,5},{7,6},{8,15},{9,8},{10,9... | collective-permute-start | bytes 688136 | tf_op jit(solution)/shard_map/ppermute | solution.py:590
  34.7 2.5 %collective-permute-start.9 = (f32[2,64,256]{2,1,0:T(8,128)S(1)}, f32[2,64,256]{2,1,0:T(8,128)S(1)}, u32[]{:S(2)}, u32[]{:S(2)}) collective-permute-start(f32[2,64,256]{2,1,0:T(8,128)S(1)} %shard_map.63.own_ref), channel_id=1, source_target_pairs={{0,24},{8,0},{16,8},{24,16},{1,25},{9,1},{17,9},{25,17},{2,26},{10... | collective-permute-start | bytes 393224 | tf_op jit(solution)/shard_map/ppermute | solution.py:590
  39.5 1.8 %collective-permute-done.7.refs_2_.refs_3_ = f32[112,512]{1,0:T(8,128)S(1)} collective-permute-done((f32[112,512]{1,0:T(8,128)S(1)}, f32[112,512]{1,0:T(8,128)S(1)}, u32[]{:S(2)}, u32[]{:S(2)}) %collective-permute-start.7) | collective-permute-done | bytes 229408 | tf_op jit(solution)/shard_map/ppermute | solution.py:590
  42.9 1.9 %collective-permute-start.10 = (f32[2,64,256]{2,1,0:T(8,128)S(1)}, f32[2,64,256]{2,1,0:T(8,128)S(1)}, u32[]{:S(2)}, u32[]{:S(2)}) collective-permute-start(f32[2,64,256]{2,1,0:T(8,128)S(1)} %shard_map.64.a_ref), channel_id=1, source_target_pairs={{0,24},{8,0},{16,8},{24,16},{1,25},{9,1},{17,9},{25,17},{2,26},{10... | collective-permute-start | bytes 393224 | tf_op jit(solution)/shard_map/ppermute | solution.py:590
  44.8 3.7 %collective-permute-done.10.b_ref.refs_5_ = f32[2,64,256]{2,1,0:T(8,128)S(1)} collective-permute-done((f32[2,64,256]{2,1,0:T(8,128)S(1)}, f32[2,64,256]{2,1,0:T(8,128)S(1)}, u32[]{:S(2)}, u32[]{:S(2)}) %collective-permute-start.10) | collective-permute-done | bytes 131104 | tf_op jit(solution)/shard_map/ppermute | solution.py:590
  48.7 1.7 %collective-permute-start.11 = (f32[128,256]{1,0:T(8,128)S(1)}, f32[128,256]{1,0:T(8,128)S(1)}, u32[]{:S(2)}, u32[]{:S(2)}) collective-permute-start(f32[128,256]{1,0:T(8,128)S(1)} %get-tuple-element.78), channel_id=1, source_target_pairs={{0,1},{2,3},{4,5},{6,7},{1,0},{3,2},{5,4},{7,6},{8,9},{10,11},{12,... | collective-permute-start | bytes 393224 | tf_op jit(solution)/shard_map/ppermute | solution.py:600
  50.4 2.3 %collective-permute-start.12 = (f32[128,256]{1,0:T(8,128)S(1)}, f32[128,256]{1,0:T(8,128)S(1)}, u32[]{:S(2)}, u32[]{:S(2)}) collective-permute-start(f32[128,256]{1,0:T(8,128)S(1)} %get-tuple-element.79), channel_id=1, source_target_pairs={{1,2},{3,4},{5,6},{7,0},{2,1},{4,3},{6,5},{0,7},{9,10},{11,12},{13... | collective-permute-start | bytes 393224 | tf_op jit(solution)/shard_map/ppermute | solution.py:600
  52.7 5.9 %collective-permute-done.13 = f32[2,24,256]{2,1,0:T(8,128)S(1)} collective-permute-done((f32[2,24,256]{2,1,0:T(8,128)S(1)}, f32[2,24,256]{2,1,0:T(8,128)S(1)}, u32[]{:S(2)}, u32[]{:S(2)}) %collective-permute-start.13) | collective-permute-done | bytes 49184 | tf_op jit(solution)/shard_map/ppermute | solution.py:590
  59.1 1.5 %collective-permute-start.17 = (f32[128,256]{1,0:T(8,128)S(1)}, f32[128,256]{1,0:T(8,128)S(1)}, u32[]{:S(2)}, u32[]{:S(2)}) collective-permute-start(f32[128,256]{1,0:T(8,128)S(1)} %get-tuple-element.87), channel_id=1, source_target_pairs={{1,2},{3,4},{5,6},{7,0},{2,1},{4,3},{6,5},{0,7},{9,10},{11,12},{13... | collective-permute-start | bytes 393224 | tf_op jit(solution)/shard_map/ppermute | solution.py:600
  60.6 4.7 %collective-permute-done.17.off_ref = f32[128,256]{1,0:T(8,128)S(1)} collective-permute-done((f32[128,256]{1,0:T(8,128)S(1)}, f32[128,256]{1,0:T(8,128)S(1)}, u32[]{:S(2)}, u32[]{:S(2)}) %collective-permute-start.17) | collective-permute-done | bytes 131104 | tf_op jit(solution)/shard_map/ppermute | solution.py:600
  66.9 4.5 %collective-permute-done.19.off_ref = f32[128,256]{1,0:T(8,128)S(1)} collective-permute-done((f32[128,256]{1,0:T(8,128)S(1)}, f32[128,256]{1,0:T(8,128)S(1)}, u32[]{:S(2)}, u32[]{:S(2)}) %collective-permute-start.19) | collective-permute-done | bytes 131104 | tf_op jit(solution)/shard_map/ppermute | solution.py:600
  71.6 1.2 %shard_map.69 = (f32[4,128,512]{2,1,0:T(8,128)}, f32[2,64,256]{2,1,0:T(8,128)}, f32[4,80,512]{2,1,0:T(8,128)S(1)}) custom-call(f32[4,48,512]{2,1,0:T(8,128)S(1)} %get-tuple-element.92.f_ref, f32[2,24,256]{2,1,0:T(8,128)S(1)} %get-tuple-element.73.b_ref.c_ref, f32[4,128,512]{2,1,0:T(8,128)S(1)} %bitcast.6, f32[2,64,256]{2,1,0:T(8,128)S(1)} %shard_map.68.e_ref), custom_call_target="tpu_custom_call" | custom-call | tf_op jit(solution)/shard_map/pallas_call | solution.py:44
  72.8 2.5 %collective-permute-done.15.f_ref = f32[4,80,512]{2,1,0:T(8,128)S(1)} collective-permute-done((f32[4,80,512]{2,1,0:T(8,128)S(1)}, f32[4,80,512]{2,1,0:T(8,128)S(1)}, u32[]{:S(2)}, u32[]{:S(2)}) %collective-permute-start.15) | collective-permute-done | bytes 655392 | tf_op jit(solution)/shard_map/ppermute | solution.py:590
  75.3 1.2 %shard_map.70 = (f32[4,128,512]{2,1,0:T(8,128)}, f32[2,64,256]{2,1,0:T(8,128)}) custom-call(f32[4,80,512]{2,1,0:T(8,128)S(1)} %collective-permute-done.15.f_ref, f32[2,64,256]{2,1,0:T(8,128)S(1)} %shard_map.68.e_ref, f32[4,80,512]{2,1,0:T(8,128)S(1)} %get-tuple-element.93.rest_ref, ...), custom_call_target="tpu_custom_call", output_to_operand_aliasing={{0}: (3, {}), {1}: (4, {})} | custom-call | tf_op jit(solution)/shard_map/pallas_call | solution.py:44
  (42 shorter events, 12.0 us)
Async XLA Ops:
  3.4 16.8 %collective-permute-start = (f32[304,512]{1,0:T(8,128)S(1)}, f32[304,512]{1,0:T(8,128)S(1)}, u32[]{:S(2)}, u32[]{:S(2)}) collective-permute-start(f32[304,512]{1,0:T(8,128)S(1)} %get-tuple-element.57), channel_id=1, source_target_pairs={{0,1},{1,2},{2,3},{3,4},{4,5},{5,6},{6,7},{7,0},{8,9},{9,10},{10,1... | collective-permute-start | bytes 1867784 | tf_op jit(solution)/shard_map/ppermute | solution.py:590
  5.0 15.1 %collective-permute-start.4 = (f32[4,56,512]{2,1,0:T(8,128)S(1)}, f32[4,56,512]{2,1,0:T(8,128)S(1)}, u32[]{:S(2)}, u32[]{:S(2)}) collective-permute-start(f32[4,56,512]{2,1,0:T(8,128)S(1)} %shard_map.57), channel_id=1, source_target_pairs={{0,8},{8,16},{16,24},{24,0},{1,9},{9,17},{17,25},{25,1},{2,10},{10... | collective-permute-start | bytes 1376264 | tf_op jit(solution)/shard_map/ppermute | solution.py:590
  7.7 16.1 %collective-permute-start.1 = (f32[304,512]{1,0:T(8,128)S(1)}, f32[304,512]{1,0:T(8,128)S(1)}, u32[]{:S(2)}, u32[]{:S(2)}) collective-permute-start(f32[304,512]{1,0:T(8,128)S(1)} %get-tuple-element.58), channel_id=1, source_target_pairs={{0,7},{1,0},{2,1},{3,2},{4,3},{5,4},{6,5},{7,6},{8,15},{9,8},{10,9... | collective-permute-start | bytes 1867784 | tf_op jit(solution)/shard_map/ppermute | solution.py:590
  20.5 7.6 %collective-permute-start.5 = (f32[144,512]{1,0:T(8,128)S(1)}, f32[144,512]{1,0:T(8,128)S(1)}, u32[]{:S(2)}, u32[]{:S(2)}) collective-permute-start(f32[144,512]{1,0:T(8,128)S(1)} %get-tuple-element.67), channel_id=1, source_target_pairs={{0,1},{1,2},{2,3},{3,4},{4,5},{5,6},{6,7},{7,0},{8,9},{9,10},{10,1... | collective-permute-start | bytes 884744 | tf_op jit(solution)/shard_map/ppermute | solution.py:590
  21.3 9.4 %collective-permute-start.6 = (f32[144,512]{1,0:T(8,128)S(1)}, f32[144,512]{1,0:T(8,128)S(1)}, u32[]{:S(2)}, u32[]{:S(2)}) collective-permute-start(f32[144,512]{1,0:T(8,128)S(1)} %get-tuple-element.68), channel_id=1, source_target_pairs={{0,7},{1,0},{2,1},{3,2},{4,3},{5,4},{6,5},{7,6},{8,15},{9,8},{10,9... | collective-permute-start | bytes 884744 | tf_op jit(solution)/shard_map/ppermute | solution.py:590
  24.7 13.5 %collective-permute-start.2 = (f32[176,512]{1,0:T(8,128)S(1)}, f32[176,512]{1,0:T(8,128)S(1)}, u32[]{:S(2)}, u32[]{:S(2)}) collective-permute-start(f32[176,512]{1,0:T(8,128)S(1)} %get-tuple-element.60), channel_id=1, source_target_pairs={{0,1},{1,2},{2,3},{3,4},{4,5},{5,6},{6,7},{7,0},{8,9},{9,10},{10,1... | collective-permute-start | bytes 1081352 | tf_op jit(solution)/shard_map/ppermute | solution.py:590
  24.7 13.7 %collective-permute-start.3 = (f32[176,512]{1,0:T(8,128)S(1)}, f32[176,512]{1,0:T(8,128)S(1)}, u32[]{:S(2)}, u32[]{:S(2)}) collective-permute-start(f32[176,512]{1,0:T(8,128)S(1)} %get-tuple-element.61), channel_id=1, source_target_pairs={{0,7},{1,0},{2,1},{3,2},{4,3},{5,4},{6,5},{7,6},{8,15},{9,8},{10,9... | collective-permute-start | bytes 1081352 | tf_op jit(solution)/shard_map/ppermute | solution.py:590
  30.7 3.5 %copy-start = (f32[1,4,128,512]{3,2,1,0:T(8,128)S(1)}, f32[1,4,128,512]{3,2,1,0:T(8,128)}, u32[]{:S(2)}) copy-start(f32[1,4,128,512]{3,2,1,0:T(8,128)} %param.4) | copy-start | bytes 3145732
  31.3 10.0 %collective-permute-start.7 = (f32[112,512]{1,0:T(8,128)S(1)}, f32[112,512]{1,0:T(8,128)S(1)}, u32[]{:S(2)}, u32[]{:S(2)}) collective-permute-start(f32[112,512]{1,0:T(8,128)S(1)} %get-tuple-element.71), channel_id=1, source_target_pairs={{0,1},{1,2},{2,3},{3,4},{4,5},{5,6},{6,7},{7,0},{8,9},{9,10},{10,1... | collective-permute-start | bytes 688136 | tf_op jit(solution)/shard_map/ppermute | solution.py:590
  32.9 9.1 %collective-permute-start.8 = (f32[112,512]{1,0:T(8,128)S(1)}, f32[112,512]{1,0:T(8,128)S(1)}, u32[]{:S(2)}, u32[]{:S(2)}) collective-permute-start(f32[112,512]{1,0:T(8,128)S(1)} %get-tuple-element.72), channel_id=1, source_target_pairs={{0,7},{1,0},{2,1},{3,2},{4,3},{5,4},{6,5},{7,6},{8,15},{9,8},{10,9... | collective-permute-start | bytes 688136 | tf_op jit(solution)/shard_map/ppermute | solution.py:590
  34.7 8.2 %collective-permute-start.9 = (f32[2,64,256]{2,1,0:T(8,128)S(1)}, f32[2,64,256]{2,1,0:T(8,128)S(1)}, u32[]{:S(2)}, u32[]{:S(2)}) collective-permute-start(f32[2,64,256]{2,1,0:T(8,128)S(1)} %shard_map.63.own_ref), channel_id=1, source_target_pairs={{0,24},{8,0},{16,8},{24,16},{1,25},{9,1},{17,9},{25,17},{2,26},{10... | collective-permute-start | bytes 393224 | tf_op jit(solution)/shard_map/ppermute | solution.py:590
  42.9 5.7 %collective-permute-start.10 = (f32[2,64,256]{2,1,0:T(8,128)S(1)}, f32[2,64,256]{2,1,0:T(8,128)S(1)}, u32[]{:S(2)}, u32[]{:S(2)}) collective-permute-start(f32[2,64,256]{2,1,0:T(8,128)S(1)} %shard_map.64.a_ref), channel_id=1, source_target_pairs={{0,24},{8,0},{16,8},{24,16},{1,25},{9,1},{17,9},{25,17},{2,26},{10... | collective-permute-start | bytes 393224 | tf_op jit(solution)/shard_map/ppermute | solution.py:590
  44.8 13.9 %collective-permute-start.14 = (f32[2,64,256]{2,1,0:T(8,128)S(1)}, f32[2,64,256]{2,1,0:T(8,128)S(1)}, u32[]{:S(2)}, u32[]{:S(2)}) collective-permute-start(f32[2,64,256]{2,1,0:T(8,128)S(1)} %shard_map.64.a_ref), channel_id=1, source_target_pairs={{0,16},{8,24},{16,0},{24,8},{1,17},{9,25},{17,1},{25,9},{2,18},{10... | collective-permute-start | bytes 393224 | tf_op jit(solution)/shard_map/ppermute | solution.py:590
  48.7 10.0 %collective-permute-start.11 = (f32[128,256]{1,0:T(8,128)S(1)}, f32[128,256]{1,0:T(8,128)S(1)}, u32[]{:S(2)}, u32[]{:S(2)}) collective-permute-start(f32[128,256]{1,0:T(8,128)S(1)} %get-tuple-element.78), channel_id=1, source_target_pairs={{0,1},{2,3},{4,5},{6,7},{1,0},{3,2},{5,4},{7,6},{8,9},{10,11},{12,... | collective-permute-start | bytes 393224 | tf_op jit(solution)/shard_map/ppermute | solution.py:600
  50.4 8.2 %collective-permute-start.12 = (f32[128,256]{1,0:T(8,128)S(1)}, f32[128,256]{1,0:T(8,128)S(1)}, u32[]{:S(2)}, u32[]{:S(2)}) collective-permute-start(f32[128,256]{1,0:T(8,128)S(1)} %get-tuple-element.79), channel_id=1, source_target_pairs={{1,2},{3,4},{5,6},{7,0},{2,1},{4,3},{6,5},{0,7},{9,10},{11,12},{13... | collective-permute-start | bytes 393224 | tf_op jit(solution)/shard_map/ppermute | solution.py:600
  52.7 5.9 %collective-permute-start.13 = (f32[2,24,256]{2,1,0:T(8,128)S(1)}, f32[2,24,256]{2,1,0:T(8,128)S(1)}, u32[]{:S(2)}, u32[]{:S(2)}) collective-permute-start(f32[2,24,256]{2,1,0:T(8,128)S(1)} %slice.8), channel_id=1, source_target_pairs={{0,8},{8,16},{16,24},{24,0},{1,9},{9,17},{17,25},{25,1},{2,10},{10... | collective-permute-start | bytes 147464 | tf_op jit(solution)/shard_map/ppermute | solution.py:590
  58.6 16.6 %collective-permute-start.15 = (f32[4,80,512]{2,1,0:T(8,128)S(1)}, f32[4,80,512]{2,1,0:T(8,128)S(1)}, u32[]{:S(2)}, u32[]{:S(2)}) collective-permute-start(f32[4,80,512]{2,1,0:T(8,128)S(1)} %get-tuple-element.81), channel_id=1, source_target_pairs={{0,8},{8,16},{16,24},{24,0},{1,9},{9,17},{17,25},{25,1},{2,10},{10... | collective-permute-start | bytes 1966088 | tf_op jit(solution)/shard_map/ppermute | solution.py:590
  59.0 1.6 %collective-permute-start.16 = (f32[128,256]{1,0:T(8,128)S(1)}, f32[128,256]{1,0:T(8,128)S(1)}, u32[]{:S(2)}, u32[]{:S(2)}) collective-permute-start(f32[128,256]{1,0:T(8,128)S(1)} %get-tuple-element.86), channel_id=1, source_target_pairs={{0,1},{2,3},{4,5},{6,7},{1,0},{3,2},{5,4},{7,6},{8,9},{10,11},{12,... | collective-permute-start | bytes 393224 | tf_op jit(solution)/shard_map/ppermute | solution.py:600
  59.1 6.2 %collective-permute-start.17 = (f32[128,256]{1,0:T(8,128)S(1)}, f32[128,256]{1,0:T(8,128)S(1)}, u32[]{:S(2)}, u32[]{:S(2)}) collective-permute-start(f32[128,256]{1,0:T(8,128)S(1)} %get-tuple-element.87), channel_id=1, source_target_pairs={{1,2},{3,4},{5,6},{7,0},{2,1},{4,3},{6,5},{0,7},{9,10},{11,12},{13... | collective-permute-start | bytes 393224 | tf_op jit(solution)/shard_map/ppermute | solution.py:600
  65.5 1.4 %collective-permute-start.18 = (f32[128,256]{1,0:T(8,128)S(1)}, f32[128,256]{1,0:T(8,128)S(1)}, u32[]{:S(2)}, u32[]{:S(2)}) collective-permute-start(f32[128,256]{1,0:T(8,128)S(1)} %get-tuple-element.90), channel_id=1, source_target_pairs={{0,1},{2,3},{4,5},{6,7},{1,0},{3,2},{5,4},{7,6},{8,9},{10,11},{12,... | collective-permute-start | bytes 393224 | tf_op jit(solution)/shard_map/ppermute | solution.py:600
  65.6 5.9 %collective-permute-start.19 = (f32[128,256]{1,0:T(8,128)S(1)}, f32[128,256]{1,0:T(8,128)S(1)}, u32[]{:S(2)}, u32[]{:S(2)}) collective-permute-start(f32[128,256]{1,0:T(8,128)S(1)} %get-tuple-element.91), channel_id=1, source_target_pairs={{1,2},{3,4},{5,6},{7,0},{2,1},{4,3},{6,5},{0,7},{9,10},{11,12},{13... | collective-permute-start | bytes 393224 | tf_op jit(solution)/shard_map/ppermute | solution.py:600

commit v8 on v7

--- a/solution.py
+++ b/solution.py
@@ -557,16 +557,19 @@
         out_specs=[HBM, HBM, VMEM])
 
 
-def finish_upper(fine, correction, rest, update, tail):
+def finish_upper(fine_first, fine, correction, rest, update, tail):
     nx, rows, nz = fine.shape
 
-    def body(f_ref, e_ref, rest_ref, *refs):
-        update, tail, out, tail_out, scratch, sems = refs[2:]
+    def body(first_ref, other_ref, e_ref, rest_ref, *refs):
+        update, tail, out, tail_out, f_ref, scratch, sems = refs[2:]
+        first = here().first
         copies = []
         for p in range(nx):
             for a in range(0, rows, TILE):
                 s = slice(a, a + TILE)
-                out[p, s] = f_ref[p, s] + rest_ref[p, s]
+                f = jnp.where(first, first_ref[p, s], other_ref[p, s])
+                f_ref[p, s] = f
+                out[p, s] = f + rest_ref[p, s]
             copies.append(pltpu.make_async_copy(out.at[p], update.at[p, pl.ds(0, rows)], sems.at[p]))
             copies[-1].start()
         matrix = pair_matrix(nz, nz // 2, 0.125)
@@ -578,11 +581,11 @@
             c.wait()
 
     return call(
-        body, [update.shape, tail.shape], [fine, correction, rest, update, tail],
-        [VMEM] * 3 + [HBM] * 2,
-        [pltpu.VMEM(fine.shape, F32), pltpu.VMEM((nx // 2, rows // 2, nz // 2), F32), lane_scratch(rows, nz // 2),
-         pltpu.SemaphoreType.DMA((nx + nx // 2,))],
-        [HBM, HBM], {3: 0, 4: 1})
+        body, [update.shape, tail.shape], [fine_first, fine, correction, rest, update, tail],
+        [VMEM] * 4 + [HBM] * 2,
+        [pltpu.VMEM(fine.shape, F32), pltpu.VMEM((nx // 2, rows // 2, nz // 2), F32), pltpu.VMEM(fine.shape, F32),
+         lane_scratch(rows, nz // 2), pltpu.SemaphoreType.DMA((nx + nx // 2,))],
+        [HBM, HBM], {4: 0, 5: 1})
 
 
 def ring(block, axis, distance):
@@ -647,16 +650,18 @@
     shifted = [jump] + [ring(jump, "tm", -j) for j in range(1, home)]
     shifted.append(jnp.concatenate([jump[:, :half_cut], lower], axis=1))
     sweep = sweep_start(shifted[0], shifted[1], half_cut, coarse_coef)
+    _, early = lax.optimization_barrier((sweep[0], moved))
+    moved_first = lax.ppermute(early, "tm", [(home, 0)])
     for j in range(home):
         state, part, on, off = sweep
         off, on = swapped(off, "space", 1), swapped(on, "space", 0)
         if j == 0:
             *_, moved = lax.optimization_barrier((on, off, lower, *shifted[2:home], moved))
-            moved = ring(moved, "tm", 1)
+            moved = lax.ppermute(moved, "tm", [(i, i + 1) for i in range(home)])
         more = (shifted[j + 1:j + 3], home - j - 1) if j < home - 1 else ()
         sweep = sweep_step(state, part, on, off, half_cut, coarse_coef, *more)
     update, tail, rest = finish_lower(own_fine, fine_coarse, own_prior, sweep[0])
-    update, tail = finish_upper(moved, sweep[0], rest, update, tail)
+    update, tail = finish_upper(moved_first, moved, sweep[0], rest, update, tail)
     return update[None], tail[None]
 
 

time: 76.7 us -> 75.7 us (0.987)
  waiting for transfers between devices: 36 us -> 32.3 us
  starting transfers between devices: 24.9 us -> 27.5 us
    ppermute x14 -> x13, waiting for transfers between devices: 26.4 us -> 23.2 us  [ring(): lax.ppermute(block, axis, [(i, (i + distance) % size) for i in range(size)])]
    ppermute x0 -> x2, starting transfers between devices: none -> 2.62 us  [the longest x1 1.33 us: shards(): moved = lax.ppermute(moved, 'tm', [(i, i + 1) for i in range(home)])]
    ppermute x14 -> x13, starting transfers between devices: 18.3 us -> 18.2 us  [ring(): lax.ppermute(block, axis, [(i, (i + distance) % size) for i in range(size)])]
  transfers between devices with their start and end apart: 20 -> 21, of which waited for: 12 -> 12; matrix products, arithmetic and copies ran while one was open for 0% -> 0% of each run, Pallas kernels for 14% -> 14%
where the time goes in v8:
time: 75.7 us; the launch traced here: 75.4 us
  waiting for transfers between devices  32.3 us (43%)
  starting transfers between devices  27.5 us (36%)
  Pallas kernels  14.7 us (19%)
  between operations  0.87 us (1%)
    ppermute x13, waiting for transfers between devices, ring(): lax.ppermute(block, axis, [(i, (i + distance) % size) for i in range(size)])  23.2 us
    ppermute x13, starting transfers between devices, ring(): lax.ppermute(block, axis, [(i, (i + distance) % size) for i in range(size)])  18.2 us
    pallas_call x21, Pallas kernels, call(): pl.pallas_call(body, out_shape=[jax.ShapeDtypeStruct(s, F32) for s in out...  14.7 us
    ppermute x6, waiting for transfers between devices, swapped(): return lax.ppermute(block, axis, pairs + [(j, i) for i, j in pairs])  9.08 us
    ppermute x6, starting transfers between devices, swapped(): return lax.ppermute(block, axis, pairs + [(j, i) for i, j in pairs])  6.67 us
  transfers between devices with their start and end apart: 21, of which 12 were waited for; matrix products, arithmetic and copies ran while one was open for 0% of the time, Pallas kernels for 14%

profile of v8, /device:TPU:0, one launch (start us, length us, event | category | flops | bytes accessed | tf_op | source)
XLA Modules:
  0.0 75.4 jit_solution(17553513341501008268)
XLA Ops:
  0.6 2.8 %shard_map.50 = (f32[4,128,512]{2,1,0:T(8,128)S(1)}, f32[4,88,512]{2,1,0:T(8,128)S(1)}, f32[304,512]{1,0:T(8,128)S(1)}, f32[304,512]{1,0:T(8,128)S(1)}) custom-call(f32[4,128,512]{2,1,0:T(8,128)} %i_ref.3, f32[4,128,512]{2,1,0:T(8,128)} %bitcast.3, f32[4,128,512]{2,1,0:T(8,128)} %k_hbm.1), custom_call_target="tpu_custom_call" | custom-call | tf_op jit(solution)/shard_map/pallas_call | solution.py:44
  5.0 2.6 %collective-permute-start.4 = (f32[4,56,512]{2,1,0:T(8,128)S(1)}, f32[4,56,512]{2,1,0:T(8,128)S(1)}, u32[]{:S(2)}, u32[]{:S(2)}) collective-permute-start(f32[4,56,512]{2,1,0:T(8,128)S(1)} %shard_map.57), channel_id=1, source_target_pairs={{0,8},{8,16},{16,24},{24,0},{1,9},{9,17},{17,25},{25,1},{2,10},{10... | collective-permute-start | bytes 1376264 | tf_op jit(solution)/shard_map/ppermute | solution.py:593
  7.7 2.3 %collective-permute-start.1 = (f32[304,512]{1,0:T(8,128)S(1)}, f32[304,512]{1,0:T(8,128)S(1)}, u32[]{:S(2)}, u32[]{:S(2)}) collective-permute-start(f32[304,512]{1,0:T(8,128)S(1)} %get-tuple-element.59), channel_id=1, source_target_pairs={{0,7},{1,0},{2,1},{3,2},{4,3},{5,4},{6,5},{7,6},{8,15},{9,8},{10,9... | collective-permute-start | bytes 1867784 | tf_op jit(solution)/shard_map/ppermute | solution.py:593
  12.0 8.2 %collective-permute-done.4.r_ref = f32[4,56,512]{2,1,0:T(8,128)S(1)} collective-permute-done((f32[4,56,512]{2,1,0:T(8,128)S(1)}, f32[4,56,512]{2,1,0:T(8,128)S(1)}, u32[]{:S(2)}, u32[]{:S(2)}) %collective-permute-start.4) | collective-permute-done | bytes 458784 | tf_op jit(solution)/shard_map/ppermute | solution.py:593
  21.3 2.0 %collective-permute-start.6 = (f32[144,512]{1,0:T(8,128)S(1)}, f32[144,512]{1,0:T(8,128)S(1)}, u32[]{:S(2)}, u32[]{:S(2)}) collective-permute-start(f32[144,512]{1,0:T(8,128)S(1)} %get-tuple-element.69), channel_id=1, source_target_pairs={{0,7},{1,0},{2,1},{3,2},{4,3},{5,4},{6,5},{7,6},{8,15},{9,8},{10,9... | collective-permute-start | bytes 884744 | tf_op jit(solution)/shard_map/ppermute | solution.py:593
  24.7 2.6 %collective-permute-start.3 = (f32[176,512]{1,0:T(8,128)S(1)}, f32[176,512]{1,0:T(8,128)S(1)}, u32[]{:S(2)}, u32[]{:S(2)}) collective-permute-start(f32[176,512]{1,0:T(8,128)S(1)} %get-tuple-element.62), channel_id=1, source_target_pairs={{0,7},{1,0},{2,1},{3,2},{4,3},{5,4},{6,5},{7,6},{8,15},{9,8},{10,9... | collective-permute-start | bytes 1081352 | tf_op jit(solution)/shard_map/ppermute | solution.py:593
  28.1 2.6 %collective-permute-done.6.refs_4_.refs_5_.hi = f32[144,512]{1,0:T(8,128)S(1)} collective-permute-done((f32[144,512]{1,0:T(8,128)S(1)}, f32[144,512]{1,0:T(8,128)S(1)}, u32[]{:S(2)}, u32[]{:S(2)}) %collective-permute-start.6) | collective-permute-done | bytes 294944 | tf_op jit(solution)/shard_map/ppermute | solution.py:593
  31.3 1.6 %collective-permute-start.7 = (f32[112,512]{1,0:T(8,128)S(1)}, f32[112,512]{1,0:T(8,128)S(1)}, u32[]{:S(2)}, u32[]{:S(2)}) collective-permute-start(f32[112,512]{1,0:T(8,128)S(1)} %get-tuple-element.72), channel_id=1, source_target_pairs={{0,1},{1,2},{2,3},{3,4},{4,5},{5,6},{6,7},{7,0},{8,9},{9,10},{10,1... | collective-permute-start | bytes 688136 | tf_op jit(solution)/shard_map/ppermute | solution.py:593
  32.9 1.3 %collective-permute-start.8 = (f32[112,512]{1,0:T(8,128)S(1)}, f32[112,512]{1,0:T(8,128)S(1)}, u32[]{:S(2)}, u32[]{:S(2)}) collective-permute-start(f32[112,512]{1,0:T(8,128)S(1)} %get-tuple-element.73), channel_id=1, source_target_pairs={{0,7},{1,0},{2,1},{3,2},{4,3},{5,4},{6,5},{7,6},{8,15},{9,8},{10,9... | collective-permute-start | bytes 688136 | tf_op jit(solution)/shard_map/ppermute | solution.py:593
  34.7 2.5 %collective-permute-start.9 = (f32[2,64,256]{2,1,0:T(8,128)S(1)}, f32[2,64,256]{2,1,0:T(8,128)S(1)}, u32[]{:S(2)}, u32[]{:S(2)}) collective-permute-start(f32[2,64,256]{2,1,0:T(8,128)S(1)} %shard_map.63.own_ref), channel_id=1, source_target_pairs={{0,24},{8,0},{16,8},{24,16},{1,25},{9,1},{17,9},{25,17},{2,26},{10... | collective-permute-start | bytes 393224 | tf_op jit(solution)/shard_map/ppermute | solution.py:593
  39.5 1.8 %collective-permute-done.7.refs_2_.refs_3_ = f32[112,512]{1,0:T(8,128)S(1)} collective-permute-done((f32[112,512]{1,0:T(8,128)S(1)}, f32[112,512]{1,0:T(8,128)S(1)}, u32[]{:S(2)}, u32[]{:S(2)}) %collective-permute-start.7) | collective-permute-done | bytes 229408 | tf_op jit(solution)/shard_map/ppermute | solution.py:593
  42.9 1.9 %collective-permute-start.10 = (f32[2,64,256]{2,1,0:T(8,128)S(1)}, f32[2,64,256]{2,1,0:T(8,128)S(1)}, u32[]{:S(2)}, u32[]{:S(2)}) collective-permute-start(f32[2,64,256]{2,1,0:T(8,128)S(1)} %shard_map.64.a_ref), channel_id=1, source_target_pairs={{0,24},{8,0},{16,8},{24,16},{1,25},{9,1},{17,9},{25,17},{2,26},{10... | collective-permute-start | bytes 393224 | tf_op jit(solution)/shard_map/ppermute | solution.py:593
  44.8 3.7 %collective-permute-done.10.b_ref.refs_5_ = f32[2,64,256]{2,1,0:T(8,128)S(1)} collective-permute-done((f32[2,64,256]{2,1,0:T(8,128)S(1)}, f32[2,64,256]{2,1,0:T(8,128)S(1)}, u32[]{:S(2)}, u32[]{:S(2)}) %collective-permute-start.10) | collective-permute-done | bytes 131104 | tf_op jit(solution)/shard_map/ppermute | solution.py:593
  48.7 1.7 %collective-permute-start.12 = (f32[128,256]{1,0:T(8,128)S(1)}, f32[128,256]{1,0:T(8,128)S(1)}, u32[]{:S(2)}, u32[]{:S(2)}) collective-permute-start(f32[128,256]{1,0:T(8,128)S(1)} %get-tuple-element.82), channel_id=1, source_target_pairs={{0,1},{2,3},{4,5},{6,7},{1,0},{3,2},{5,4},{7,6},{8,9},{10,11},{12,... | collective-permute-start | bytes 393224 | tf_op jit(solution)/shard_map/ppermute | solution.py:603
  50.4 2.3 %collective-permute-start.13 = (f32[128,256]{1,0:T(8,128)S(1)}, f32[128,256]{1,0:T(8,128)S(1)}, u32[]{:S(2)}, u32[]{:S(2)}) collective-permute-start(f32[128,256]{1,0:T(8,128)S(1)} %get-tuple-element.83), channel_id=1, source_target_pairs={{1,2},{3,4},{5,6},{7,0},{2,1},{4,3},{6,5},{0,7},{9,10},{11,12},{13... | collective-permute-start | bytes 393224 | tf_op jit(solution)/shard_map/ppermute | solution.py:603
  52.7 1.3 %collective-permute-start.11 = (f32[4,80,512]{2,1,0:T(8,128)S(1)}, f32[4,80,512]{2,1,0:T(8,128)S(1)}, u32[]{:S(2)}, u32[]{:S(2)}) collective-permute-start(f32[4,80,512]{2,1,0:T(8,128)S(1)} %get-tuple-element.84), channel_id=1, source_target_pairs={{24,0},{25,1},{26,2},{27,3},{28,4},{29,5},{30,6},{31,7}} | collective-permute-start | bytes 1966088 | tf_op jit(solution)/shard_map/ppermute | solution.py:654
  54.0 5.1 %collective-permute-done.14 = f32[2,24,256]{2,1,0:T(8,128)S(1)} collective-permute-done((f32[2,24,256]{2,1,0:T(8,128)S(1)}, f32[2,24,256]{2,1,0:T(8,128)S(1)}, u32[]{:S(2)}, u32[]{:S(2)}) %collective-permute-start.14) | collective-permute-done | bytes 49184 | tf_op jit(solution)/shard_map/ppermute | solution.py:593
  59.2 1.3 %collective-permute-start.16 = (f32[4,80,512]{2,1,0:T(8,128)S(1)}, f32[4,80,512]{2,1,0:T(8,128)S(1)}, u32[]{:S(2)}, u32[]{:S(2)}) collective-permute-start(f32[4,80,512]{2,1,0:T(8,128)S(1)} %get-tuple-element.84), channel_id=1, source_target_pairs={{0,8},{8,16},{16,24},{1,9},{9,17},{17,25},{2,10},{10,18},{18,26},{... | collective-permute-start | bytes 1966088 | tf_op jit(solution)/shard_map/ppermute | solution.py:660
  60.9 1.2 %collective-permute-start.18 = (f32[128,256]{1,0:T(8,128)S(1)}, f32[128,256]{1,0:T(8,128)S(1)}, u32[]{:S(2)}, u32[]{:S(2)}) collective-permute-start(f32[128,256]{1,0:T(8,128)S(1)} %get-tuple-element.89), channel_id=1, source_target_pairs={{1,2},{3,4},{5,6},{7,0},{2,1},{4,3},{6,5},{0,7},{9,10},{11,12},{13... | collective-permute-start | bytes 393224 | tf_op jit(solution)/shard_map/ppermute | solution.py:603
  62.2 4.3 %collective-permute-done.18.off_ref = f32[128,256]{1,0:T(8,128)S(1)} collective-permute-done((f32[128,256]{1,0:T(8,128)S(1)}, f32[128,256]{1,0:T(8,128)S(1)}, u32[]{:S(2)}, u32[]{:S(2)}) %collective-permute-start.18) | collective-permute-done | bytes 131104 | tf_op jit(solution)/shard_map/ppermute | solution.py:603
  66.9 1.3 %collective-permute-start.20 = (f32[128,256]{1,0:T(8,128)S(1)}, f32[128,256]{1,0:T(8,128)S(1)}, u32[]{:S(2)}, u32[]{:S(2)}) collective-permute-start(f32[128,256]{1,0:T(8,128)S(1)} %get-tuple-element.93), channel_id=1, source_target_pairs={{1,2},{3,4},{5,6},{7,0},{2,1},{4,3},{6,5},{0,7},{9,10},{11,12},{13... | collective-permute-start | bytes 393224 | tf_op jit(solution)/shard_map/ppermute | solution.py:603
  68.2 4.6 %collective-permute-done.20.off_ref = f32[128,256]{1,0:T(8,128)S(1)} collective-permute-done((f32[128,256]{1,0:T(8,128)S(1)}, f32[128,256]{1,0:T(8,128)S(1)}, u32[]{:S(2)}, u32[]{:S(2)}) %collective-permute-start.20) | collective-permute-done | bytes 131104 | tf_op jit(solution)/shard_map/ppermute | solution.py:603
  73.0 1.2 %shard_map.69 = (f32[4,128,512]{2,1,0:T(8,128)}, f32[2,64,256]{2,1,0:T(8,128)}, f32[4,80,512]{2,1,0:T(8,128)S(1)}) custom-call(f32[4,48,512]{2,1,0:T(8,128)S(1)} %get-tuple-element.94.f_ref, f32[2,24,256]{2,1,0:T(8,128)S(1)} %get-tuple-element.74.b_ref.c_ref, f32[4,128,512]{2,1,0:T(8,128)S(1)} %bitcast.6, f32[2,64,256]{2,1,0:T(8,128)S(1)} %shard_map.68.e_ref), custom_call_target="tpu_custom_call" | custom-call | tf_op jit(solution)/shard_map/pallas_call | solution.py:44
  74.2 1.2 %shard_map.70 = (f32[4,128,512]{2,1,0:T(8,128)}, f32[2,64,256]{2,1,0:T(8,128)}) custom-call(f32[4,80,512]{2,1,0:T(8,128)S(1)} %collective-permute-done.11.first_ref, f32[4,80,512]{2,1,0:T(8,128)S(1)} %collective-permute-done.16.other_ref, f32[2,64,256]{2,1,0:T(8,128)S(1)} %shard_map.68.e_ref, ...), custom_call_target="tpu_custom_call", output_to_operand_aliasing={{0}: (4, {}), {1}: (5, {})} | custom-call | tf_op jit(solution)/shard_map/pallas_call | solution.py:44
  (44 shorter events, 13.0 us)
Async XLA Ops:
  3.4 16.8 %collective-permute-start = (f32[304,512]{1,0:T(8,128)S(1)}, f32[304,512]{1,0:T(8,128)S(1)}, u32[]{:S(2)}, u32[]{:S(2)}) collective-permute-start(f32[304,512]{1,0:T(8,128)S(1)} %get-tuple-element.58), channel_id=1, source_target_pairs={{0,1},{1,2},{2,3},{3,4},{4,5},{5,6},{6,7},{7,0},{8,9},{9,10},{10,1... | collective-permute-start | bytes 1867784 | tf_op jit(solution)/shard_map/ppermute | solution.py:593
  5.0 15.1 %collective-permute-start.4 = (f32[4,56,512]{2,1,0:T(8,128)S(1)}, f32[4,56,512]{2,1,0:T(8,128)S(1)}, u32[]{:S(2)}, u32[]{:S(2)}) collective-permute-start(f32[4,56,512]{2,1,0:T(8,128)S(1)} %shard_map.57), channel_id=1, source_target_pairs={{0,8},{8,16},{16,24},{24,0},{1,9},{9,17},{17,25},{25,1},{2,10},{10... | collective-permute-start | bytes 1376264 | tf_op jit(solution)/shard_map/ppermute | solution.py:593
  7.7 16.1 %collective-permute-start.1 = (f32[304,512]{1,0:T(8,128)S(1)}, f32[304,512]{1,0:T(8,128)S(1)}, u32[]{:S(2)}, u32[]{:S(2)}) collective-permute-start(f32[304,512]{1,0:T(8,128)S(1)} %get-tuple-element.59), channel_id=1, source_target_pairs={{0,7},{1,0},{2,1},{3,2},{4,3},{5,4},{6,5},{7,6},{8,15},{9,8},{10,9... | collective-permute-start | bytes 1867784 | tf_op jit(solution)/shard_map/ppermute | solution.py:593
  20.5 7.6 %collective-permute-start.5 = (f32[144,512]{1,0:T(8,128)S(1)}, f32[144,512]{1,0:T(8,128)S(1)}, u32[]{:S(2)}, u32[]{:S(2)}) collective-permute-start(f32[144,512]{1,0:T(8,128)S(1)} %get-tuple-element.68), channel_id=1, source_target_pairs={{0,1},{1,2},{2,3},{3,4},{4,5},{5,6},{6,7},{7,0},{8,9},{9,10},{10,1... | collective-permute-start | bytes 884744 | tf_op jit(solution)/shard_map/ppermute | solution.py:593
  21.3 9.4 %collective-permute-start.6 = (f32[144,512]{1,0:T(8,128)S(1)}, f32[144,512]{1,0:T(8,128)S(1)}, u32[]{:S(2)}, u32[]{:S(2)}) collective-permute-start(f32[144,512]{1,0:T(8,128)S(1)} %get-tuple-element.69), channel_id=1, source_target_pairs={{0,7},{1,0},{2,1},{3,2},{4,3},{5,4},{6,5},{7,6},{8,15},{9,8},{10,9... | collective-permute-start | bytes 884744 | tf_op jit(solution)/shard_map/ppermute | solution.py:593
  24.7 13.5 %collective-permute-start.2 = (f32[176,512]{1,0:T(8,128)S(1)}, f32[176,512]{1,0:T(8,128)S(1)}, u32[]{:S(2)}, u32[]{:S(2)}) collective-permute-start(f32[176,512]{1,0:T(8,128)S(1)} %get-tuple-element.61), channel_id=1, source_target_pairs={{0,1},{1,2},{2,3},{3,4},{4,5},{5,6},{6,7},{7,0},{8,9},{9,10},{10,1... | collective-permute-start | bytes 1081352 | tf_op jit(solution)/shard_map/ppermute | solution.py:593
  24.7 13.7 %collective-permute-start.3 = (f32[176,512]{1,0:T(8,128)S(1)}, f32[176,512]{1,0:T(8,128)S(1)}, u32[]{:S(2)}, u32[]{:S(2)}) collective-permute-start(f32[176,512]{1,0:T(8,128)S(1)} %get-tuple-element.62), channel_id=1, source_target_pairs={{0,7},{1,0},{2,1},{3,2},{4,3},{5,4},{6,5},{7,6},{8,15},{9,8},{10,9... | collective-permute-start | bytes 1081352 | tf_op jit(solution)/shard_map/ppermute | solution.py:593
  30.7 3.5 %copy-start = (f32[1,4,128,512]{3,2,1,0:T(8,128)S(1)}, f32[1,4,128,512]{3,2,1,0:T(8,128)}, u32[]{:S(2)}) copy-start(f32[1,4,128,512]{3,2,1,0:T(8,128)} %param.4) | copy-start | bytes 3145732
  31.3 10.0 %collective-permute-start.7 = (f32[112,512]{1,0:T(8,128)S(1)}, f32[112,512]{1,0:T(8,128)S(1)}, u32[]{:S(2)}, u32[]{:S(2)}) collective-permute-start(f32[112,512]{1,0:T(8,128)S(1)} %get-tuple-element.72), channel_id=1, source_target_pairs={{0,1},{1,2},{2,3},{3,4},{4,5},{5,6},{6,7},{7,0},{8,9},{9,10},{10,1... | collective-permute-start | bytes 688136 | tf_op jit(solution)/shard_map/ppermute | solution.py:593
  32.9 9.1 %collective-permute-start.8 = (f32[112,512]{1,0:T(8,128)S(1)}, f32[112,512]{1,0:T(8,128)S(1)}, u32[]{:S(2)}, u32[]{:S(2)}) collective-permute-start(f32[112,512]{1,0:T(8,128)S(1)} %get-tuple-element.73), channel_id=1, source_target_pairs={{0,7},{1,0},{2,1},{3,2},{4,3},{5,4},{6,5},{7,6},{8,15},{9,8},{10,9... | collective-permute-start | bytes 688136 | tf_op jit(solution)/shard_map/ppermute | solution.py:593
  34.7 8.2 %collective-permute-start.9 = (f32[2,64,256]{2,1,0:T(8,128)S(1)}, f32[2,64,256]{2,1,0:T(8,128)S(1)}, u32[]{:S(2)}, u32[]{:S(2)}) collective-permute-start(f32[2,64,256]{2,1,0:T(8,128)S(1)} %shard_map.63.own_ref), channel_id=1, source_target_pairs={{0,24},{8,0},{16,8},{24,16},{1,25},{9,1},{17,9},{25,17},{2,26},{10... | collective-permute-start | bytes 393224 | tf_op jit(solution)/shard_map/ppermute | solution.py:593
  42.9 5.7 %collective-permute-start.10 = (f32[2,64,256]{2,1,0:T(8,128)S(1)}, f32[2,64,256]{2,1,0:T(8,128)S(1)}, u32[]{:S(2)}, u32[]{:S(2)}) collective-permute-start(f32[2,64,256]{2,1,0:T(8,128)S(1)} %shard_map.64.a_ref), channel_id=1, source_target_pairs={{0,24},{8,0},{16,8},{24,16},{1,25},{9,1},{17,9},{25,17},{2,26},{10... | collective-permute-start | bytes 393224 | tf_op jit(solution)/shard_map/ppermute | solution.py:593
  44.8 14.4 %collective-permute-start.15 = (f32[2,64,256]{2,1,0:T(8,128)S(1)}, f32[2,64,256]{2,1,0:T(8,128)S(1)}, u32[]{:S(2)}, u32[]{:S(2)}) collective-permute-start(f32[2,64,256]{2,1,0:T(8,128)S(1)} %shard_map.64.a_ref), channel_id=1, source_target_pairs={{0,16},{8,24},{16,0},{24,8},{1,17},{9,25},{17,1},{25,9},{2,18},{10... | collective-permute-start | bytes 393224 | tf_op jit(solution)/shard_map/ppermute | solution.py:593
  48.7 10.5 %collective-permute-start.12 = (f32[128,256]{1,0:T(8,128)S(1)}, f32[128,256]{1,0:T(8,128)S(1)}, u32[]{:S(2)}, u32[]{:S(2)}) collective-permute-start(f32[128,256]{1,0:T(8,128)S(1)} %get-tuple-element.82), channel_id=1, source_target_pairs={{0,1},{2,3},{4,5},{6,7},{1,0},{3,2},{5,4},{7,6},{8,9},{10,11},{12,... | collective-permute-start | bytes 393224 | tf_op jit(solution)/shard_map/ppermute | solution.py:603
  50.4 8.8 %collective-permute-start.13 = (f32[128,256]{1,0:T(8,128)S(1)}, f32[128,256]{1,0:T(8,128)S(1)}, u32[]{:S(2)}, u32[]{:S(2)}) collective-permute-start(f32[128,256]{1,0:T(8,128)S(1)} %get-tuple-element.83), channel_id=1, source_target_pairs={{1,2},{3,4},{5,6},{7,0},{2,1},{4,3},{6,5},{0,7},{9,10},{11,12},{13... | collective-permute-start | bytes 393224 | tf_op jit(solution)/shard_map/ppermute | solution.py:603
  52.7 6.4 %collective-permute-start.14 = (f32[2,24,256]{2,1,0:T(8,128)S(1)}, f32[2,24,256]{2,1,0:T(8,128)S(1)}, u32[]{:S(2)}, u32[]{:S(2)}) collective-permute-start(f32[2,24,256]{2,1,0:T(8,128)S(1)} %slice.8), channel_id=1, source_target_pairs={{0,8},{8,16},{16,24},{24,0},{1,9},{9,17},{17,25},{25,1},{2,10},{10... | collective-permute-start | bytes 147464 | tf_op jit(solution)/shard_map/ppermute | solution.py:593
  52.7 21.4 %collective-permute-start.11 = (f32[4,80,512]{2,1,0:T(8,128)S(1)}, f32[4,80,512]{2,1,0:T(8,128)S(1)}, u32[]{:S(2)}, u32[]{:S(2)}) collective-permute-start(f32[4,80,512]{2,1,0:T(8,128)S(1)} %get-tuple-element.84), channel_id=1, source_target_pairs={{24,0},{25,1},{26,2},{27,3},{28,4},{29,5},{30,6},{31,7}} | collective-permute-start | bytes 1966088 | tf_op jit(solution)/shard_map/ppermute | solution.py:654
  59.2 15.0 %collective-permute-start.16 = (f32[4,80,512]{2,1,0:T(8,128)S(1)}, f32[4,80,512]{2,1,0:T(8,128)S(1)}, u32[]{:S(2)}, u32[]{:S(2)}) collective-permute-start(f32[4,80,512]{2,1,0:T(8,128)S(1)} %get-tuple-element.84), channel_id=1, source_target_pairs={{0,8},{8,16},{16,24},{1,9},{9,17},{17,25},{2,10},{10,18},{18,26},{... | collective-permute-start | bytes 1966088 | tf_op jit(solution)/shard_map/ppermute | solution.py:660
  60.8 1.4 %collective-permute-start.17 = (f32[128,256]{1,0:T(8,128)S(1)}, f32[128,256]{1,0:T(8,128)S(1)}, u32[]{:S(2)}, u32[]{:S(2)}) collective-permute-start(f32[128,256]{1,0:T(8,128)S(1)} %get-tuple-element.88), channel_id=1, source_target_pairs={{0,1},{2,3},{4,5},{6,7},{1,0},{3,2},{5,4},{7,6},{8,9},{10,11},{12,... | collective-permute-start | bytes 393224 | tf_op jit(solution)/shard_map/ppermute | solution.py:603
  60.9 5.6 %collective-permute-start.18 = (f32[128,256]{1,0:T(8,128)S(1)}, f32[128,256]{1,0:T(8,128)S(1)}, u32[]{:S(2)}, u32[]{:S(2)}) collective-permute-start(f32[128,256]{1,0:T(8,128)S(1)} %get-tuple-element.89), channel_id=1, source_target_pairs={{1,2},{3,4},{5,6},{7,0},{2,1},{4,3},{6,5},{0,7},{9,10},{11,12},{13... | collective-permute-start | bytes 393224 | tf_op jit(solution)/shard_map/ppermute | solution.py:603
  66.8 1.4 %collective-permute-start.19 = (f32[128,256]{1,0:T(8,128)S(1)}, f32[128,256]{1,0:T(8,128)S(1)}, u32[]{:S(2)}, u32[]{:S(2)}) collective-permute-start(f32[128,256]{1,0:T(8,128)S(1)} %get-tuple-element.92), channel_id=1, source_target_pairs={{0,1},{2,3},{4,5},{6,7},{1,0},{3,2},{5,4},{7,6},{8,9},{10,11},{12,... | collective-permute-start | bytes 393224 | tf_op jit(solution)/shard_map/ppermute | solution.py:603
  66.9 5.9 %collective-permute-start.20 = (f32[128,256]{1,0:T(8,128)S(1)}, f32[128,256]{1,0:T(8,128)S(1)}, u32[]{:S(2)}, u32[]{:S(2)}) collective-permute-start(f32[128,256]{1,0:T(8,128)S(1)} %get-tuple-element.93), channel_id=1, source_target_pairs={{1,2},{3,4},{5,6},{7,0},{2,1},{4,3},{6,5},{0,7},{9,10},{11,12},{13... | collective-permute-start | bytes 393224 | tf_op jit(solution)/shard_map/ppermute | solution.py:603

commit v9 on v8

--- a/solution.py
+++ b/solution.py
@@ -210,14 +210,10 @@
     nx, ny, nz = cond.shape
 
     def body(i_ref, p_ref, k_hbm, k_ref, v_ref, down, up, sems):
-        def copy(ref):
-            run(row_copies(k_hbm, k_ref, (0, ny), 0, sems, 0, range(nx))
-                + row_copies(ref, v_ref, (0, end), 0, sems, nx, range(nx)))
-
-        chosen(here().last, copy, i_ref, p_ref)
         k = fields([(0, ny, 0)], [k_ref], nx, nz)
         v = fields([(0, end, 0)], [v_ref], nx, nz)
-        for out, own, inner in ((down, 0, 1), (up, nx - 1, nx - 2)):
+
+        def message(out, own, inner):
             for a in range(0, ny, TILE):
                 own_k = k[own].tile(a)
                 out[a:a + TILE] = own_k
@@ -229,6 +225,23 @@
                 c, stepped = row_step(v[own], u, d, r, 1.0 - (total + face), a)
                 out[ny + a:ny + a + TILE] = c
                 out[ny + end + a:ny + end + a + TILE] = stepped + face * v[inner].tile(a)
+
+        def copy(ref):
+            for x in k + v:
+                x.moved.clear()
+            conds = row_copies(k_hbm, k_ref, (0, ny), 0, sems, 0, range(nx))
+            states = row_copies(ref, v_ref, (0, end), 0, sems, nx, range(nx))
+            groups = [conds[:2] + states[:2], conds[2:] + states[2:]]
+            for c in groups[0] + groups[1]:
+                c.start()
+            for c in groups[0]:
+                c.wait()
+            message(down, 0, 1)
+            for c in groups[1]:
+                c.wait()
+            message(up, nx - 1, nx - 2)
+
+        chosen(here().last, copy, i_ref, p_ref)
 
     return call(
         body, [cond.shape, (nx, end, nz)] + [(ny + 2 * end, nz)] * 2, [initial, prior, cond], [HBM, HBM, HBM],

time: 75.7 us -> 75 us (level)
  no operation moved by 1% of the time
where the time goes in v9:
time: 75 us; the launch traced here: 74.8 us
  waiting for transfers between devices  32.2 us (43%)
  starting transfers between devices  27.6 us (37%)
  Pallas kernels  14.1 us (19%)
  between operations  0.87 us (1%)
    ppermute x13, waiting for transfers between devices, ring(): lax.ppermute(block, axis, [(i, (i + distance) % size) for i in range(size)])  23.2 us
    ppermute x13, starting transfers between devices, ring(): lax.ppermute(block, axis, [(i, (i + distance) % size) for i in range(size)])  18.2 us
    pallas_call x21, Pallas kernels, call(): pl.pallas_call(body, out_shape=[jax.ShapeDtypeStruct(s, F32) for s in out...  14.1 us
    ppermute x6, waiting for transfers between devices, swapped(): return lax.ppermute(block, axis, pairs + [(j, i) for i, j in pairs])  9.06 us
    ppermute x6, starting transfers between devices, swapped(): return lax.ppermute(block, axis, pairs + [(j, i) for i, j in pairs])  6.7 us
  transfers between devices with their start and end apart: 21, of which 12 were waited for; matrix products, arithmetic and copies ran while one was open for 0% of the time, Pallas kernels for 14%

profile of v9, /device:TPU:0, one launch (start us, length us, event | category | flops | bytes accessed | tf_op | source)
XLA Modules:
  0.0 74.8 jit_solution(11500092072954405074)
XLA Ops:
  0.6 2.1 %shard_map.50 = (f32[4,128,512]{2,1,0:T(8,128)S(1)}, f32[4,88,512]{2,1,0:T(8,128)S(1)}, f32[304,512]{1,0:T(8,128)S(1)}, f32[304,512]{1,0:T(8,128)S(1)}) custom-call(f32[4,128,512]{2,1,0:T(8,128)} %i_ref.3, f32[4,128,512]{2,1,0:T(8,128)} %bitcast.3, f32[4,128,512]{2,1,0:T(8,128)} %k_hbm.1), custom_call_target="tpu_custom_call" | custom-call | tf_op jit(solution)/shard_map/pallas_call | solution.py:44
  4.4 2.6 %collective-permute-start.4 = (f32[4,56,512]{2,1,0:T(8,128)S(1)}, f32[4,56,512]{2,1,0:T(8,128)S(1)}, u32[]{:S(2)}, u32[]{:S(2)}) collective-permute-start(f32[4,56,512]{2,1,0:T(8,128)S(1)} %shard_map.57), channel_id=1, source_target_pairs={{0,8},{8,16},{16,24},{24,0},{1,9},{9,17},{17,25},{25,1},{2,10},{10... | collective-permute-start | bytes 1376264 | tf_op jit(solution)/shard_map/ppermute | solution.py:606
  7.0 2.3 %collective-permute-start.1 = (f32[304,512]{1,0:T(8,128)S(1)}, f32[304,512]{1,0:T(8,128)S(1)}, u32[]{:S(2)}, u32[]{:S(2)}) collective-permute-start(f32[304,512]{1,0:T(8,128)S(1)} %get-tuple-element.59), channel_id=1, source_target_pairs={{0,7},{1,0},{2,1},{3,2},{4,3},{5,4},{6,5},{7,6},{8,15},{9,8},{10,9... | collective-permute-start | bytes 1867784 | tf_op jit(solution)/shard_map/ppermute | solution.py:606
  11.3 8.2 %collective-permute-done.4.r_ref = f32[4,56,512]{2,1,0:T(8,128)S(1)} collective-permute-done((f32[4,56,512]{2,1,0:T(8,128)S(1)}, f32[4,56,512]{2,1,0:T(8,128)S(1)}, u32[]{:S(2)}, u32[]{:S(2)}) %collective-permute-start.4) | collective-permute-done | bytes 458784 | tf_op jit(solution)/shard_map/ppermute | solution.py:606
  20.7 2.0 %collective-permute-start.6 = (f32[144,512]{1,0:T(8,128)S(1)}, f32[144,512]{1,0:T(8,128)S(1)}, u32[]{:S(2)}, u32[]{:S(2)}) collective-permute-start(f32[144,512]{1,0:T(8,128)S(1)} %get-tuple-element.69), channel_id=1, source_target_pairs={{0,7},{1,0},{2,1},{3,2},{4,3},{5,4},{6,5},{7,6},{8,15},{9,8},{10,9... | collective-permute-start | bytes 884744 | tf_op jit(solution)/shard_map/ppermute | solution.py:606
  24.1 2.6 %collective-permute-start.3 = (f32[176,512]{1,0:T(8,128)S(1)}, f32[176,512]{1,0:T(8,128)S(1)}, u32[]{:S(2)}, u32[]{:S(2)}) collective-permute-start(f32[176,512]{1,0:T(8,128)S(1)} %get-tuple-element.62), channel_id=1, source_target_pairs={{0,7},{1,0},{2,1},{3,2},{4,3},{5,4},{6,5},{7,6},{8,15},{9,8},{10,9... | collective-permute-start | bytes 1081352 | tf_op jit(solution)/shard_map/ppermute | solution.py:606
  27.5 2.6 %collective-permute-done.6.refs_4_.refs_5_.hi = f32[144,512]{1,0:T(8,128)S(1)} collective-permute-done((f32[144,512]{1,0:T(8,128)S(1)}, f32[144,512]{1,0:T(8,128)S(1)}, u32[]{:S(2)}, u32[]{:S(2)}) %collective-permute-start.6) | collective-permute-done | bytes 294944 | tf_op jit(solution)/shard_map/ppermute | solution.py:606
  30.6 1.6 %collective-permute-start.7 = (f32[112,512]{1,0:T(8,128)S(1)}, f32[112,512]{1,0:T(8,128)S(1)}, u32[]{:S(2)}, u32[]{:S(2)}) collective-permute-start(f32[112,512]{1,0:T(8,128)S(1)} %get-tuple-element.72), channel_id=1, source_target_pairs={{0,1},{1,2},{2,3},{3,4},{4,5},{5,6},{6,7},{7,0},{8,9},{9,10},{10,1... | collective-permute-start | bytes 688136 | tf_op jit(solution)/shard_map/ppermute | solution.py:606
  32.2 1.3 %collective-permute-start.8 = (f32[112,512]{1,0:T(8,128)S(1)}, f32[112,512]{1,0:T(8,128)S(1)}, u32[]{:S(2)}, u32[]{:S(2)}) collective-permute-start(f32[112,512]{1,0:T(8,128)S(1)} %get-tuple-element.73), channel_id=1, source_target_pairs={{0,7},{1,0},{2,1},{3,2},{4,3},{5,4},{6,5},{7,6},{8,15},{9,8},{10,9... | collective-permute-start | bytes 688136 | tf_op jit(solution)/shard_map/ppermute | solution.py:606
  34.0 2.5 %collective-permute-start.9 = (f32[2,64,256]{2,1,0:T(8,128)S(1)}, f32[2,64,256]{2,1,0:T(8,128)S(1)}, u32[]{:S(2)}, u32[]{:S(2)}) collective-permute-start(f32[2,64,256]{2,1,0:T(8,128)S(1)} %shard_map.63.own_ref), channel_id=1, source_target_pairs={{0,24},{8,0},{16,8},{24,16},{1,25},{9,1},{17,9},{25,17},{2,26},{10... | collective-permute-start | bytes 393224 | tf_op jit(solution)/shard_map/ppermute | solution.py:606
  38.9 1.8 %collective-permute-done.7.refs_2_.refs_3_ = f32[112,512]{1,0:T(8,128)S(1)} collective-permute-done((f32[112,512]{1,0:T(8,128)S(1)}, f32[112,512]{1,0:T(8,128)S(1)}, u32[]{:S(2)}, u32[]{:S(2)}) %collective-permute-start.7) | collective-permute-done | bytes 229408 | tf_op jit(solution)/shard_map/ppermute | solution.py:606
  42.2 1.9 %collective-permute-start.10 = (f32[2,64,256]{2,1,0:T(8,128)S(1)}, f32[2,64,256]{2,1,0:T(8,128)S(1)}, u32[]{:S(2)}, u32[]{:S(2)}) collective-permute-start(f32[2,64,256]{2,1,0:T(8,128)S(1)} %shard_map.64.a_ref), channel_id=1, source_target_pairs={{0,24},{8,0},{16,8},{24,16},{1,25},{9,1},{17,9},{25,17},{2,26},{10... | collective-permute-start | bytes 393224 | tf_op jit(solution)/shard_map/ppermute | solution.py:606
  44.1 3.7 %collective-permute-done.10.b_ref.refs_5_ = f32[2,64,256]{2,1,0:T(8,128)S(1)} collective-permute-done((f32[2,64,256]{2,1,0:T(8,128)S(1)}, f32[2,64,256]{2,1,0:T(8,128)S(1)}, u32[]{:S(2)}, u32[]{:S(2)}) %collective-permute-start.10) | collective-permute-done | bytes 131104 | tf_op jit(solution)/shard_map/ppermute | solution.py:606
  48.0 1.7 %collective-permute-start.12 = (f32[128,256]{1,0:T(8,128)S(1)}, f32[128,256]{1,0:T(8,128)S(1)}, u32[]{:S(2)}, u32[]{:S(2)}) collective-permute-start(f32[128,256]{1,0:T(8,128)S(1)} %get-tuple-element.82), channel_id=1, source_target_pairs={{0,1},{2,3},{4,5},{6,7},{1,0},{3,2},{5,4},{7,6},{8,9},{10,11},{12,... | collective-permute-start | bytes 393224 | tf_op jit(solution)/shard_map/ppermute | solution.py:616
  49.8 2.3 %collective-permute-start.13 = (f32[128,256]{1,0:T(8,128)S(1)}, f32[128,256]{1,0:T(8,128)S(1)}, u32[]{:S(2)}, u32[]{:S(2)}) collective-permute-start(f32[128,256]{1,0:T(8,128)S(1)} %get-tuple-element.83), channel_id=1, source_target_pairs={{1,2},{3,4},{5,6},{7,0},{2,1},{4,3},{6,5},{0,7},{9,10},{11,12},{13... | collective-permute-start | bytes 393224 | tf_op jit(solution)/shard_map/ppermute | solution.py:616
  52.1 1.3 %collective-permute-start.11 = (f32[4,80,512]{2,1,0:T(8,128)S(1)}, f32[4,80,512]{2,1,0:T(8,128)S(1)}, u32[]{:S(2)}, u32[]{:S(2)}) collective-permute-start(f32[4,80,512]{2,1,0:T(8,128)S(1)} %get-tuple-element.84), channel_id=1, source_target_pairs={{24,0},{25,1},{26,2},{27,3},{28,4},{29,5},{30,6},{31,7}} | collective-permute-start | bytes 1966088 | tf_op jit(solution)/shard_map/ppermute | solution.py:667
  53.4 5.1 %collective-permute-done.14 = f32[2,24,256]{2,1,0:T(8,128)S(1)} collective-permute-done((f32[2,24,256]{2,1,0:T(8,128)S(1)}, f32[2,24,256]{2,1,0:T(8,128)S(1)}, u32[]{:S(2)}, u32[]{:S(2)}) %collective-permute-start.14) | collective-permute-done | bytes 49184 | tf_op jit(solution)/shard_map/ppermute | solution.py:606
  58.5 1.3 %collective-permute-start.16 = (f32[4,80,512]{2,1,0:T(8,128)S(1)}, f32[4,80,512]{2,1,0:T(8,128)S(1)}, u32[]{:S(2)}, u32[]{:S(2)}) collective-permute-start(f32[4,80,512]{2,1,0:T(8,128)S(1)} %get-tuple-element.84), channel_id=1, source_target_pairs={{0,8},{8,16},{16,24},{1,9},{9,17},{17,25},{2,10},{10,18},{18,26},{... | collective-permute-start | bytes 1966088 | tf_op jit(solution)/shard_map/ppermute | solution.py:673
  60.3 1.2 %collective-permute-start.18 = (f32[128,256]{1,0:T(8,128)S(1)}, f32[128,256]{1,0:T(8,128)S(1)}, u32[]{:S(2)}, u32[]{:S(2)}) collective-permute-start(f32[128,256]{1,0:T(8,128)S(1)} %get-tuple-element.89), channel_id=1, source_target_pairs={{1,2},{3,4},{5,6},{7,0},{2,1},{4,3},{6,5},{0,7},{9,10},{11,12},{13... | collective-permute-start | bytes 393224 | tf_op jit(solution)/shard_map/ppermute | solution.py:616
  61.6 4.3 %collective-permute-done.18.off_ref = f32[128,256]{1,0:T(8,128)S(1)} collective-permute-done((f32[128,256]{1,0:T(8,128)S(1)}, f32[128,256]{1,0:T(8,128)S(1)}, u32[]{:S(2)}, u32[]{:S(2)}) %collective-permute-start.18) | collective-permute-done | bytes 131104 | tf_op jit(solution)/shard_map/ppermute | solution.py:616
  66.2 1.3 %collective-permute-start.20 = (f32[128,256]{1,0:T(8,128)S(1)}, f32[128,256]{1,0:T(8,128)S(1)}, u32[]{:S(2)}, u32[]{:S(2)}) collective-permute-start(f32[128,256]{1,0:T(8,128)S(1)} %get-tuple-element.93), channel_id=1, source_target_pairs={{1,2},{3,4},{5,6},{7,0},{2,1},{4,3},{6,5},{0,7},{9,10},{11,12},{13... | collective-permute-start | bytes 393224 | tf_op jit(solution)/shard_map/ppermute | solution.py:616
  67.6 4.6 %collective-permute-done.20.off_ref = f32[128,256]{1,0:T(8,128)S(1)} collective-permute-done((f32[128,256]{1,0:T(8,128)S(1)}, f32[128,256]{1,0:T(8,128)S(1)}, u32[]{:S(2)}, u32[]{:S(2)}) %collective-permute-start.20) | collective-permute-done | bytes 131104 | tf_op jit(solution)/shard_map/ppermute | solution.py:616
  72.3 1.2 %shard_map.69 = (f32[4,128,512]{2,1,0:T(8,128)}, f32[2,64,256]{2,1,0:T(8,128)}, f32[4,80,512]{2,1,0:T(8,128)S(1)}) custom-call(f32[4,48,512]{2,1,0:T(8,128)S(1)} %get-tuple-element.94.f_ref, f32[2,24,256]{2,1,0:T(8,128)S(1)} %get-tuple-element.74.b_ref.c_ref, f32[4,128,512]{2,1,0:T(8,128)S(1)} %bitcast.6, f32[2,64,256]{2,1,0:T(8,128)S(1)} %shard_map.68.e_ref), custom_call_target="tpu_custom_call" | custom-call | tf_op jit(solution)/shard_map/pallas_call | solution.py:44
  73.6 1.2 %shard_map.70 = (f32[4,128,512]{2,1,0:T(8,128)}, f32[2,64,256]{2,1,0:T(8,128)}) custom-call(f32[4,80,512]{2,1,0:T(8,128)S(1)} %collective-permute-done.11.first_ref, f32[4,80,512]{2,1,0:T(8,128)S(1)} %collective-permute-done.16.other_ref, f32[2,64,256]{2,1,0:T(8,128)S(1)} %shard_map.68.e_ref, ...), custom_call_target="tpu_custom_call", output_to_operand_aliasing={{0}: (4, {}), {1}: (5, {})} | custom-call | tf_op jit(solution)/shard_map/pallas_call | solution.py:44
  (44 shorter events, 13.0 us)
Async XLA Ops:
  2.8 16.8 %collective-permute-start = (f32[304,512]{1,0:T(8,128)S(1)}, f32[304,512]{1,0:T(8,128)S(1)}, u32[]{:S(2)}, u32[]{:S(2)}) collective-permute-start(f32[304,512]{1,0:T(8,128)S(1)} %get-tuple-element.58), channel_id=1, source_target_pairs={{0,1},{1,2},{2,3},{3,4},{4,5},{5,6},{6,7},{7,0},{8,9},{9,10},{10,1... | collective-permute-start | bytes 1867784 | tf_op jit(solution)/shard_map/ppermute | solution.py:606
  4.4 15.2 %collective-permute-start.4 = (f32[4,56,512]{2,1,0:T(8,128)S(1)}, f32[4,56,512]{2,1,0:T(8,128)S(1)}, u32[]{:S(2)}, u32[]{:S(2)}) collective-permute-start(f32[4,56,512]{2,1,0:T(8,128)S(1)} %shard_map.57), channel_id=1, source_target_pairs={{0,8},{8,16},{16,24},{24,0},{1,9},{9,17},{17,25},{25,1},{2,10},{10... | collective-permute-start | bytes 1376264 | tf_op jit(solution)/shard_map/ppermute | solution.py:606
  7.0 16.1 %collective-permute-start.1 = (f32[304,512]{1,0:T(8,128)S(1)}, f32[304,512]{1,0:T(8,128)S(1)}, u32[]{:S(2)}, u32[]{:S(2)}) collective-permute-start(f32[304,512]{1,0:T(8,128)S(1)} %get-tuple-element.59), channel_id=1, source_target_pairs={{0,7},{1,0},{2,1},{3,2},{4,3},{5,4},{6,5},{7,6},{8,15},{9,8},{10,9... | collective-permute-start | bytes 1867784 | tf_op jit(solution)/shard_map/ppermute | solution.py:606
  19.9 7.6 %collective-permute-start.5 = (f32[144,512]{1,0:T(8,128)S(1)}, f32[144,512]{1,0:T(8,128)S(1)}, u32[]{:S(2)}, u32[]{:S(2)}) collective-permute-start(f32[144,512]{1,0:T(8,128)S(1)} %get-tuple-element.68), channel_id=1, source_target_pairs={{0,1},{1,2},{2,3},{3,4},{4,5},{5,6},{6,7},{7,0},{8,9},{9,10},{10,1... | collective-permute-start | bytes 884744 | tf_op jit(solution)/shard_map/ppermute | solution.py:606
  20.7 9.4 %collective-permute-start.6 = (f32[144,512]{1,0:T(8,128)S(1)}, f32[144,512]{1,0:T(8,128)S(1)}, u32[]{:S(2)}, u32[]{:S(2)}) collective-permute-start(f32[144,512]{1,0:T(8,128)S(1)} %get-tuple-element.69), channel_id=1, source_target_pairs={{0,7},{1,0},{2,1},{3,2},{4,3},{5,4},{6,5},{7,6},{8,15},{9,8},{10,9... | collective-permute-start | bytes 884744 | tf_op jit(solution)/shard_map/ppermute | solution.py:606
  24.0 13.5 %collective-permute-start.2 = (f32[176,512]{1,0:T(8,128)S(1)}, f32[176,512]{1,0:T(8,128)S(1)}, u32[]{:S(2)}, u32[]{:S(2)}) collective-permute-start(f32[176,512]{1,0:T(8,128)S(1)} %get-tuple-element.61), channel_id=1, source_target_pairs={{0,1},{1,2},{2,3},{3,4},{4,5},{5,6},{6,7},{7,0},{8,9},{9,10},{10,1... | collective-permute-start | bytes 1081352 | tf_op jit(solution)/shard_map/ppermute | solution.py:606
  24.1 13.7 %collective-permute-start.3 = (f32[176,512]{1,0:T(8,128)S(1)}, f32[176,512]{1,0:T(8,128)S(1)}, u32[]{:S(2)}, u32[]{:S(2)}) collective-permute-start(f32[176,512]{1,0:T(8,128)S(1)} %get-tuple-element.62), channel_id=1, source_target_pairs={{0,7},{1,0},{2,1},{3,2},{4,3},{5,4},{6,5},{7,6},{8,15},{9,8},{10,9... | collective-permute-start | bytes 1081352 | tf_op jit(solution)/shard_map/ppermute | solution.py:606
  30.0 3.5 %copy-start = (f32[1,4,128,512]{3,2,1,0:T(8,128)S(1)}, f32[1,4,128,512]{3,2,1,0:T(8,128)}, u32[]{:S(2)}) copy-start(f32[1,4,128,512]{3,2,1,0:T(8,128)} %param.4) | copy-start | bytes 3145732
  30.6 10.0 %collective-permute-start.7 = (f32[112,512]{1,0:T(8,128)S(1)}, f32[112,512]{1,0:T(8,128)S(1)}, u32[]{:S(2)}, u32[]{:S(2)}) collective-permute-start(f32[112,512]{1,0:T(8,128)S(1)} %get-tuple-element.72), channel_id=1, source_target_pairs={{0,1},{1,2},{2,3},{3,4},{4,5},{5,6},{6,7},{7,0},{8,9},{9,10},{10,1... | collective-permute-start | bytes 688136 | tf_op jit(solution)/shard_map/ppermute | solution.py:606
  32.2 9.1 %collective-permute-start.8 = (f32[112,512]{1,0:T(8,128)S(1)}, f32[112,512]{1,0:T(8,128)S(1)}, u32[]{:S(2)}, u32[]{:S(2)}) collective-permute-start(f32[112,512]{1,0:T(8,128)S(1)} %get-tuple-element.73), channel_id=1, source_target_pairs={{0,7},{1,0},{2,1},{3,2},{4,3},{5,4},{6,5},{7,6},{8,15},{9,8},{10,9... | collective-permute-start | bytes 688136 | tf_op jit(solution)/shard_map/ppermute | solution.py:606
  34.0 8.2 %collective-permute-start.9 = (f32[2,64,256]{2,1,0:T(8,128)S(1)}, f32[2,64,256]{2,1,0:T(8,128)S(1)}, u32[]{:S(2)}, u32[]{:S(2)}) collective-permute-start(f32[2,64,256]{2,1,0:T(8,128)S(1)} %shard_map.63.own_ref), channel_id=1, source_target_pairs={{0,24},{8,0},{16,8},{24,16},{1,25},{9,1},{17,9},{25,17},{2,26},{10... | collective-permute-start | bytes 393224 | tf_op jit(solution)/shard_map/ppermute | solution.py:606
  42.2 5.7 %collective-permute-start.10 = (f32[2,64,256]{2,1,0:T(8,128)S(1)}, f32[2,64,256]{2,1,0:T(8,128)S(1)}, u32[]{:S(2)}, u32[]{:S(2)}) collective-permute-start(f32[2,64,256]{2,1,0:T(8,128)S(1)} %shard_map.64.a_ref), channel_id=1, source_target_pairs={{0,24},{8,0},{16,8},{24,16},{1,25},{9,1},{17,9},{25,17},{2,26},{10... | collective-permute-start | bytes 393224 | tf_op jit(solution)/shard_map/ppermute | solution.py:606
  44.1 14.4 %collective-permute-start.15 = (f32[2,64,256]{2,1,0:T(8,128)S(1)}, f32[2,64,256]{2,1,0:T(8,128)S(1)}, u32[]{:S(2)}, u32[]{:S(2)}) collective-permute-start(f32[2,64,256]{2,1,0:T(8,128)S(1)} %shard_map.64.a_ref), channel_id=1, source_target_pairs={{0,16},{8,24},{16,0},{24,8},{1,17},{9,25},{17,1},{25,9},{2,18},{10... | collective-permute-start | bytes 393224 | tf_op jit(solution)/shard_map/ppermute | solution.py:606
  48.0 10.5 %collective-permute-start.12 = (f32[128,256]{1,0:T(8,128)S(1)}, f32[128,256]{1,0:T(8,128)S(1)}, u32[]{:S(2)}, u32[]{:S(2)}) collective-permute-start(f32[128,256]{1,0:T(8,128)S(1)} %get-tuple-element.82), channel_id=1, source_target_pairs={{0,1},{2,3},{4,5},{6,7},{1,0},{3,2},{5,4},{7,6},{8,9},{10,11},{12,... | collective-permute-start | bytes 393224 | tf_op jit(solution)/shard_map/ppermute | solution.py:616
  49.8 8.8 %collective-permute-start.13 = (f32[128,256]{1,0:T(8,128)S(1)}, f32[128,256]{1,0:T(8,128)S(1)}, u32[]{:S(2)}, u32[]{:S(2)}) collective-permute-start(f32[128,256]{1,0:T(8,128)S(1)} %get-tuple-element.83), channel_id=1, source_target_pairs={{1,2},{3,4},{5,6},{7,0},{2,1},{4,3},{6,5},{0,7},{9,10},{11,12},{13... | collective-permute-start | bytes 393224 | tf_op jit(solution)/shard_map/ppermute | solution.py:616
  52.1 6.4 %collective-permute-start.14 = (f32[2,24,256]{2,1,0:T(8,128)S(1)}, f32[2,24,256]{2,1,0:T(8,128)S(1)}, u32[]{:S(2)}, u32[]{:S(2)}) collective-permute-start(f32[2,24,256]{2,1,0:T(8,128)S(1)} %slice.8), channel_id=1, source_target_pairs={{0,8},{8,16},{16,24},{24,0},{1,9},{9,17},{17,25},{25,1},{2,10},{10... | collective-permute-start | bytes 147464 | tf_op jit(solution)/shard_map/ppermute | solution.py:606
  52.1 21.4 %collective-permute-start.11 = (f32[4,80,512]{2,1,0:T(8,128)S(1)}, f32[4,80,512]{2,1,0:T(8,128)S(1)}, u32[]{:S(2)}, u32[]{:S(2)}) collective-permute-start(f32[4,80,512]{2,1,0:T(8,128)S(1)} %get-tuple-element.84), channel_id=1, source_target_pairs={{24,0},{25,1},{26,2},{27,3},{28,4},{29,5},{30,6},{31,7}} | collective-permute-start | bytes 1966088 | tf_op jit(solution)/shard_map/ppermute | solution.py:667
  58.5 15.0 %collective-permute-start.16 = (f32[4,80,512]{2,1,0:T(8,128)S(1)}, f32[4,80,512]{2,1,0:T(8,128)S(1)}, u32[]{:S(2)}, u32[]{:S(2)}) collective-permute-start(f32[4,80,512]{2,1,0:T(8,128)S(1)} %get-tuple-element.84), channel_id=1, source_target_pairs={{0,8},{8,16},{16,24},{1,9},{9,17},{17,25},{2,10},{10,18},{18,26},{... | collective-permute-start | bytes 1966088 | tf_op jit(solution)/shard_map/ppermute | solution.py:673
  60.2 1.4 %collective-permute-start.17 = (f32[128,256]{1,0:T(8,128)S(1)}, f32[128,256]{1,0:T(8,128)S(1)}, u32[]{:S(2)}, u32[]{:S(2)}) collective-permute-start(f32[128,256]{1,0:T(8,128)S(1)} %get-tuple-element.88), channel_id=1, source_target_pairs={{0,1},{2,3},{4,5},{6,7},{1,0},{3,2},{5,4},{7,6},{8,9},{10,11},{12,... | collective-permute-start | bytes 393224 | tf_op jit(solution)/shard_map/ppermute | solution.py:616
  60.3 5.6 %collective-permute-start.18 = (f32[128,256]{1,0:T(8,128)S(1)}, f32[128,256]{1,0:T(8,128)S(1)}, u32[]{:S(2)}, u32[]{:S(2)}) collective-permute-start(f32[128,256]{1,0:T(8,128)S(1)} %get-tuple-element.89), channel_id=1, source_target_pairs={{1,2},{3,4},{5,6},{7,0},{2,1},{4,3},{6,5},{0,7},{9,10},{11,12},{13... | collective-permute-start | bytes 393224 | tf_op jit(solution)/shard_map/ppermute | solution.py:616
  66.2 1.4 %collective-permute-start.19 = (f32[128,256]{1,0:T(8,128)S(1)}, f32[128,256]{1,0:T(8,128)S(1)}, u32[]{:S(2)}, u32[]{:S(2)}) collective-permute-start(f32[128,256]{1,0:T(8,128)S(1)} %get-tuple-element.92), channel_id=1, source_target_pairs={{0,1},{2,3},{4,5},{6,7},{1,0},{3,2},{5,4},{7,6},{8,9},{10,11},{12,... | collective-permute-start | bytes 393224 | tf_op jit(solution)/shard_map/ppermute | solution.py:616
  66.2 5.9 %collective-permute-start.20 = (f32[128,256]{1,0:T(8,128)S(1)}, f32[128,256]{1,0:T(8,128)S(1)}, u32[]{:S(2)}, u32[]{:S(2)}) collective-permute-start(f32[128,256]{1,0:T(8,128)S(1)} %get-tuple-element.93), channel_id=1, source_target_pairs={{1,2},{3,4},{5,6},{7,0},{2,1},{4,3},{6,5},{0,7},{9,10},{11,12},{13... | collective-permute-start | bytes 393224 | tf_op jit(solution)/shard_map/ppermute | solution.py:616
